TPU v7x, 32 devices: a whole 2x2x4 slice. The times are simulated.
32 devices in a mesh: dp: 2 (over x), expert: 16 (over z, y, core).
Axes of the slice: x: 2, y: 2, z: 4, core: 2. Of those that a mesh axis runs over, the one named last changes fastest.
Arguments:
- tokens: bfloat16 [768, 2048], P(('dp', 'expert')), may hold values from -6 to 6
- out_grad: bfloat16 [768, 2048], P(('dp', 'expert')), may hold values from -0.59765625 to 0.59765625
- expert_ids: int32 [768, 8], P(('dp', 'expert')), may hold values from 0 to 15, all different within a row; in each aligned block of 24 rows (0 to 23, 24 to 47, ...) at most 16 rows name the same one
- router_weight: bfloat16 [2048, 16], replicated, may hold values from -0.1875 to 0.1875
- w_gate: bfloat16 [16, 2048, 768], P('expert'), may hold values from -0.125 to 0.125
- w_up: bfloat16 [16, 2048, 768], P('expert'), may hold values from -0.125 to 0.125
- w_down: bfloat16 [16, 768, 2048], P('expert'), may hold values from -0.21875 to 0.21875
Outputs:
- grad_tokens: bfloat16 [768, 2048], P(('dp', 'expert'))
- grad_router: float32 [2048, 16], replicated
- grad_gate: bfloat16 [16, 2048, 768], P('expert', 'dp')
- grad_up: bfloat16 [16, 2048, 768], P('expert', 'dp')
- grad_down: bfloat16 [16, 768, 2048], P('expert', 'dp')
Inputs may be any that keep to these rules, and one draw needn't show every extreme that they name: `expert_ids`: each row names 8 different experts. Among the 24 tokens of one device (aligned blocks of rows), no expert is named by more than 16 tokens, and in some blocks one expert is named by exactly 16.
All inputs are finite; a program needn't handle non-finite values.
Results may differ from a plain program's by a relative error of at most 0.017.
Values may be sent and summed in bfloat16 or wider, within the bound.
No kernel may reach another device: no remote copies, remote signals or barrier semaphores. Data moves between devices by JAX's collectives and lax.ppermute only.
A program may use at most 128 MiB of HBM per device.

v0:
```python
import jax
import jax.numpy as jnp
from jax import lax
from jax.sharding import PartitionSpec as P

PASSES = 3


def expert_rows(rows_in, rows_grad, weight_gate, weight_up, weight_down):
    gate_pre = jnp.dot(rows_in, weight_gate, preferred_element_type=jnp.float32)
    up_pre = jnp.dot(rows_in, weight_up, preferred_element_type=jnp.float32)
    sigmoid_gate = jax.nn.sigmoid(gate_pre)
    activation = gate_pre * sigmoid_gate
    hidden = activation * up_pre
    contract_cols = (((1,), (1,)), ((), ()))
    hidden_grad = lax.dot_general(
        rows_grad, weight_down, contract_cols, preferred_element_type=jnp.float32
    )
    score_grad = jnp.sum(hidden_grad * hidden, axis=1).astype(jnp.bfloat16)
    gate_grad = (
        hidden_grad * up_pre * sigmoid_gate * (1.0 + gate_pre * (1.0 - sigmoid_gate))
    ).astype(jnp.bfloat16)
    up_grad = (hidden_grad * activation).astype(jnp.bfloat16)
    input_grad = lax.dot_general(
        gate_grad, weight_gate, contract_cols, preferred_element_type=jnp.float32
    )
    input_grad = input_grad + lax.dot_general(
        up_grad, weight_up, contract_cols, preferred_element_type=jnp.float32
    )
    return (
        hidden.astype(jnp.bfloat16),
        gate_grad,
        up_grad,
        input_grad.astype(jnp.bfloat16),
        score_grad,
    )


def scaled_rows(gate_values, rows_grad, gate_grad, up_grad):
    gate_scale = gate_values.astype(jnp.float32)[:, None]
    return (
        (gate_scale * rows_grad).astype(jnp.bfloat16),
        (gate_scale * gate_grad).astype(jnp.bfloat16),
        (gate_scale * up_grad).astype(jnp.bfloat16),
    )


def balancer_forward_pass(router_logit_rows):
    expert_density_rows = [jnp.exp(router_logit_rows)]
    division_ratios, column_totals, row_totals = ([], [], [])
    for repeat in range(PASSES):
        column_sum = lax.psum(jnp.sum(expert_density_rows[-1], axis=0), ("dp", "expert"))
        quotient = expert_density_rows[-1] / column_sum
        row_sum = jnp.sum(quotient, axis=1, keepdims=True)
        expert_density_rows.append(quotient / row_sum)
        division_ratios.append(quotient)
        column_totals.append(column_sum)
        row_totals.append(row_sum)
    return (expert_density_rows, division_ratios, column_totals, row_totals)


def balancer_adjoint_pass(
    density_gradient, expert_density_rows, division_ratios, column_totals, row_totals
):
    for repeat in reversed(range(PASSES)):
        density = expert_density_rows[repeat + 1]
        quotient_grad = (
            density_gradient - jnp.sum(density_gradient * density, axis=1, keepdims=True)
        ) / row_totals[repeat]
        shared = lax.psum(
            jnp.sum(quotient_grad * division_ratios[repeat], axis=0), ("dp", "expert")
        )
        density_gradient = (quotient_grad - shared) / column_totals[repeat]
    return density_gradient * expert_density_rows[0]


def column_product(operand_left, operand_right):
    return lax.dot_general(
        operand_left, operand_right, (((0,), (0,)), ((), ())), preferred_element_type=jnp.float32
    )


def per_device(tokens, out_grad, expert_ids, router_weight, w_gate, w_up, w_down):
    tok_rows, model_width = tokens.shape
    expert_blocks = router_weight.shape[1]
    top_picks = expert_ids.shape[1]
    capacity = min(tok_rows, 4 * tok_rows * top_picks // (3 * expert_blocks))
    sources = lax.axis_size("expert")
    slot_total = sources * capacity
    weight_gate, weight_up, weight_down = (w_gate[0], w_up[0], w_down[0])
    ff_width = weight_gate.shape[1]
    highest = lax.Precision.HIGHEST
    router_logit_rows = jnp.dot(tokens, router_weight, preferred_element_type=jnp.float32)
    expert_range = jnp.arange(expert_blocks, dtype=jnp.int32)
    picked = jnp.sum(
        (expert_ids[:, :, None] == expert_range[None, None, :]).astype(jnp.int32), axis=1
    )
    slot_rank = jnp.cumsum(picked, axis=0) - picked
    slot_range = jnp.arange(capacity, dtype=jnp.int32)
    selected = (slot_rank.T[:, None, :] == slot_range[None, :, None]) & (picked.T[:, None, :] > 0)
    select_half = selected.astype(jnp.bfloat16)
    select_full = selected.astype(jnp.float32)
    send_in = jnp.einsum(
        "ect,td->ecd", select_half, tokens, preferred_element_type=jnp.float32
    ).astype(jnp.bfloat16)
    send_grad = jnp.einsum(
        "ect,td->ecd", select_half, out_grad, preferred_element_type=jnp.float32
    ).astype(jnp.bfloat16)
    balancer_state = balancer_forward_pass(router_logit_rows)
    gate_matrix = expert_blocks * balancer_state[0][-1]
    send_gates = jnp.einsum("ect,te->ec", select_full, gate_matrix, precision=highest).astype(
        jnp.bfloat16
    )
    recv_in, recv_grad, recv_gates = (
        lax.all_to_all(send_in, "expert", split_axis=0, concat_axis=0, tiled=True),
        lax.all_to_all(send_grad, "expert", split_axis=0, concat_axis=0, tiled=True),
        lax.all_to_all(send_gates, "expert", split_axis=0, concat_axis=0, tiled=True),
    )
    flat_in = recv_in.reshape(slot_total, model_width)
    flat_grad = recv_grad.reshape(slot_total, model_width)
    hidden, gate_grad, up_grad, input_grad, score_grad = expert_rows(
        flat_in, flat_grad, weight_gate, weight_up, weight_down
    )
    input_slots, score_slots = (input_grad, score_grad)
    back_input, back_score = (
        lax.all_to_all(
            input_slots.reshape(sources, capacity, model_width),
            "expert",
            split_axis=0,
            concat_axis=0,
            tiled=True,
        ),
        lax.all_to_all(
            score_slots.reshape(sources, capacity),
            "expert",
            split_axis=0,
            concat_axis=0,
            tiled=True,
        ),
    )
    gate_values = recv_gates.reshape(slot_total)
    down_scaled, gate_scaled, up_scaled = scaled_rows(gate_values, flat_grad, gate_grad, up_grad)
    paired = jnp.concatenate([gate_scaled, up_scaled], axis=1)
    grad_pair = lax.psum_scatter(
        column_product(flat_in, paired).astype(jnp.bfloat16), "dp", scatter_dimension=0, tiled=True
    ).astype(jnp.float32)
    grad_down = lax.psum_scatter(
        column_product(hidden, down_scaled).astype(jnp.bfloat16),
        "dp",
        scatter_dimension=0,
        tiled=True,
    ).astype(jnp.float32)
    grad_gate = grad_pair[:, :ff_width].astype(jnp.bfloat16)[None]
    grad_up = grad_pair[:, ff_width:].astype(jnp.bfloat16)[None]
    grad_down = grad_down.astype(jnp.bfloat16)[None]
    route_weights = select_full * gate_matrix.T[:, None, :]
    expert_input = jnp.einsum(
        "ect,ecd->td", route_weights, back_input.astype(jnp.float32), precision=highest
    )
    density_gradient = expert_blocks * jnp.einsum(
        "ect,ec->te", select_full, back_score.astype(jnp.float32), precision=highest
    )
    expert_density_rows, division_ratios, column_totals, row_totals = balancer_state
    logit_gradient = balancer_adjoint_pass(
        density_gradient, expert_density_rows, division_ratios, column_totals, row_totals
    ).astype(jnp.bfloat16)
    router_term = lax.dot_general(
        tokens, logit_gradient, (((0,), (0,)), ((), ())), preferred_element_type=jnp.float32
    )
    grad_router = lax.psum(router_term, ("dp", "expert"))
    router_input = lax.dot_general(
        logit_gradient, router_weight, (((1,), (1,)), ((), ())), preferred_element_type=jnp.float32
    )
    grad_tokens = (expert_input + router_input).astype(jnp.bfloat16)
    return (grad_tokens, grad_router, grad_gate, grad_up, grad_down)


def solution(mesh):
    in_specs = (
        P(("dp", "expert"), None),
        P(("dp", "expert"), None),
        P(("dp", "expert"), None),
        P(),
        P("expert", None, None),
        P("expert", None, None),
        P("expert", None, None),
    )
    out_specs = (
        P(("dp", "expert"), None),
        P(),
        P("expert", "dp", None),
        P("expert", "dp", None),
        P("expert", "dp", None),
    )
    return jax.shard_map(
        per_device, mesh=mesh, in_specs=in_specs, out_specs=out_specs, check_vma=False
    )
```

profile of v0, /device:TPU:0, one launch (start us, length us, event | category | flops | bytes accessed | tf_op | source)
XLA Modules:
  0.0 508.1 jit_solution(5854701547444370432)
XLA Ops:
  8.0 0.0 copy-start
  8.0 0.9 convert_reduce_fusion
  8.9 1.3 fusion.58
  10.2 42.0 %psum.49 = f32[16]{0:T(128)S(1)} all-reduce(f32[16]{0:T(128)S(1)} %get-tuple-element.20), channel_id=1, replica_groups=mesh['dp'=2,'expert'=16] {'dp','expert'}, use_global_device_ids=true, to_apply=%region_3.4 | all-reduce | flops 16 | bytes 128 | tf_op jit(solution)/shard_map/psum | solution.py:52
  52.2 0.1 fusion.48
  52.3 0.2 fusion.49
  52.5 40.2 %psum.50 = f32[16]{0:T(128)S(1)} all-reduce(f32[16]{0:T(128)S(1)} %fusion.49), channel_id=1, replica_groups=mesh['dp'=2,'expert'=16] {'dp','expert'}, use_global_device_ids=true, to_apply=%region_6.7 | all-reduce | flops 16 | bytes 128 | tf_op jit(solution)/shard_map/psum | solution.py:52
  92.7 0.1 fusion.52
  92.8 0.2 fusion.53
  92.9 0.1 copy.39
  93.0 39.9 %psum.51 = f32[16]{0:T(128)S(1)} all-reduce(f32[16]{0:T(128)S(1)} %fusion.53), channel_id=1, replica_groups=mesh['dp'=2,'expert'=16] {'dp','expert'}, use_global_device_ids=true, to_apply=%region_9.10 | all-reduce | flops 16 | bytes 128 | tf_op jit(solution)/shard_map/psum | solution.py:52
  133.0 0.1 fusion.56
  133.0 0.1 broadcast_multiply_fusion
  133.2 0.1 copy.41
  133.3 0.2 fusion.32
  133.5 0.6 copy.46
  134.1 5.4 %all-to-all-start.4 = ((bf16[16,1,16]{2,1,0:T(2,128)(2,1)}), bf16[16,1,16]{2,1,0:T(2,128)(2,1)S(1)}, u32[]{:S(2)}, u32[]{:S(2)}) async-start(bf16[16,1,16]{2,1,0:T(2,128)(2,1)} %copy.46), calls=%async_computation.4 | async-start | bytes 16384 | tf_op jit(solution)/shard_map/all_to_all | solution.py:117
  139.6 2.3 convolution_convert_fusion.2
  141.8 4.0 all-to-all-done.4
  145.9 4.3 all-to-all-start.1
  150.2 1.4 convolution_convert_fusion.3
  151.6 21.5 %all-to-all-done.1 = bf16[16,16,2048]{2,1,0:T(8,128)(2,1)} async-done(((bf16[16,16,2048]{2,1,0:T(8,128)(2,1)}), bf16[16,16,2048]{2,1,0:T(8,128)(2,1)}, u32[]{:S(2)}, u32[]{:S(2)}) %all-to-all-start.1) | async-done | bytes 1048608 | tf_op jit(solution)/shard_map/all_to_all | solution.py:115
  173.2 6.9 %all-to-all-start = ((bf16[16,16,2048]{2,1,0:T(8,128)(2,1)}), bf16[16,16,2048]{2,1,0:T(8,128)(2,1)}, u32[]{:S(2)}, u32[]{:S(2)}) async-start(bf16[16,16,2048]{2,1,0:T(8,128)(2,1)} %convolution_convert_fusion.3), calls=%async_computation | async-start | bytes 2097152 | tf_op jit(solution)/shard_map/all_to_all | solution.py:116
  180.1 0.0 reduce-scatter.3.cloned.1.call-start
  180.1 0.1 reshape.65
  180.2 4.1 fusion.6
  184.3 18.8 %all-to-all-done = bf16[16,16,2048]{2,1,0:T(8,128)(2,1)} async-done(((bf16[16,16,2048]{2,1,0:T(8,128)(2,1)}), bf16[16,16,2048]{2,1,0:T(8,128)(2,1)}, u32[]{:S(2)}, u32[]{:S(2)}) %all-to-all-start) | async-done | bytes 1048608 | tf_op jit(solution)/shard_map/all_to_all | solution.py:116
  203.1 3.3 fusion.8
  206.4 3.6 multiply_convert_fusion.3
  210.0 5.7 %convolution_convert_fusion = bf16[2048,1536]{1,0:T(8,128)(2,1)} fusion(bf16[256,2048]{1,0:T(8,128)(2,1)} %bitcast.7, bf16[256,768]{1,0:T(8,128)(2,1)S(1)} %get-tuple-element.18, bf16[256,768]{1,0:T(8,128)(2,1)S(1)} %get-tuple-element.5), kind=kOutput, calls=%fused_computation | convolution fusion | flops 1615331328 | bytes 8126464 | tf_op jit(solution)/shard_map/dot_general | solution.py:78
  215.7 0.0 reduce-scatter.3.cloned.1.call-update
  215.8 0.0 all-reduce.2.cloned.1.call-start
  215.8 0.1 convert_element_type.110
  215.9 13.1 %all_to_all.33 = bf16[16,1,16]{2,1,0:T(2,128)(2,1)S(1)} all-to-all(bf16[16,1,16]{2,1,0:T(2,128)(2,1)S(1)} %convert_element_type.110), channel_id=1, replica_groups=mesh['dp'=2,'expert'=16] {'expert'}, dimensions={0} | all-to-all | bytes 1024 | tf_op jit(solution)/shard_map/all_to_all | solution.py:133
  229.0 0.1 fusion.34
  229.1 0.1 fusion.44
  229.2 0.1 multiply_reduce_fusion.5
  229.3 38.7 %psum.52 = f32[16]{0:T(128)S(1)} all-reduce(f32[16]{0:T(128)S(1)} %multiply_reduce_fusion.5), channel_id=1, replica_groups=mesh['dp'=2,'expert'=16] {'dp','expert'}, use_global_device_ids=true, to_apply=%region_14.15 | all-reduce | flops 16 | bytes 128 | tf_op jit(solution)/shard_map/psum | solution.py:70
  268.1 0.1 multiply_reduce_fusion.4
  268.2 0.2 multiply_reduce_fusion.3
  268.4 40.5 %psum.53 = f32[16]{0:T(128)S(1)} all-reduce(f32[16]{0:T(128)S(1)} %multiply_reduce_fusion.3), channel_id=1, replica_groups=mesh['dp'=2,'expert'=16] {'dp','expert'}, use_global_device_ids=true, to_apply=%region_17.18 | all-reduce | flops 16 | bytes 128 | tf_op jit(solution)/shard_map/psum | solution.py:70
  308.9 0.1 multiply_reduce_fusion.2
  309.0 0.2 multiply_reduce_fusion.1
  309.2 39.8 %psum.54 = f32[16]{0:T(128)S(1)} all-reduce(f32[16]{0:T(128)S(1)} %multiply_reduce_fusion.1), channel_id=1, replica_groups=mesh['dp'=2,'expert'=16] {'dp','expert'}, use_global_device_ids=true, to_apply=%region_20.21 | all-reduce | flops 16 | bytes 128 | tf_op jit(solution)/shard_map/psum | solution.py:70
  349.0 0.0 copy-start.25
  349.0 0.9 convolution_bitcast_fusion.1
  349.9 0.0 all-reduce.2.cloned.1.call-update
  349.9 0.2 reduce-scatter.5.cloned.1.call-start
  350.1 4.5 convolution_convert_fusion.1
  354.7 0.0 reduce-scatter.5.cloned.1.call-update
  354.7 0.0 copy-start.1
  354.7 0.9 copy-done.4
  355.7 1.0 fusion
  356.7 0.0 copy-done.1
  356.7 0.0 copy-done.3
  356.8 2.0 fusion.13
  358.8 5.0 all-to-all-start.2
  363.8 0.1 fusion.46
  363.9 22.9 %all-to-all-done.2 = bf16[16,16,2048]{2,1,0:T(8,128)(2,1)} async-done(((bf16[16,16,2048]{2,1,0:T(8,128)(2,1)}), bf16[16,16,2048]{2,1,0:T(8,128)(2,1)}, u32[]{:S(2)}, u32[]{:S(2)}) %all-to-all-start.2) | async-done | bytes 1048608 | tf_op jit(solution)/shard_map/all_to_all | solution.py:126
  386.8 2.2 convolution_bitcast_fusion
  389.1 0.9 fusion.16
  390.0 3.7 slice_bitcast_fusion
  393.7 105.3 %all-reduce.2.cloned.1.call-done = f32[2048,16]{0,1:T(8,128)} async-done(((f32[2048,16]{0,1:T(8,128)}), f32[2048,16]{0,1:T(8,128)}) %all-reduce.2.cloned.1.call-update) | async-done | bytes 131088 | tf_op jit(solution)/shard_map/psum | solution.py:170
  499.1 1.6 copy.62
  (58 shorter events, 0.2 us)
Async XLA Ops:
  8.0 198.4 %copy-start = (bf16[1,2048,768]{2,1,0:T(8,128)(2,1)S(1)}, bf16[1,2048,768]{2,1,0:T(8,128)(2,1)}, u32[]{:S(2)}) copy-start(bf16[1,2048,768]{2,1,0:T(8,128)(2,1)} %param.11) | copy-start | bytes 9437188
  8.0 142.2 %copy-start.10 = (bf16[24,2048]{1,0:T(8,128)(2,1)S(1)}, bf16[24,2048]{1,0:T(8,128)(2,1)}, u32[]{:S(2)}) copy-start(bf16[24,2048]{1,0:T(8,128)(2,1)} %param.8) | copy-start | bytes 294916
  52.2 296.8 %copy-start.6 = (f32[16]{0:T(128)}, f32[16]{0:T(128)S(1)}, u32[]{:S(2)}) copy-start(f32[16]{0:T(128)S(1)} %psum.49) | copy-start | bytes 196
  52.3 296.7 %copy-start.8 = (f32[24]{0:T(128)}, f32[24]{0:T(128)S(1)}, u32[]{:S(2)}) copy-start(f32[24]{0:T(128)S(1)} %fusion.48) | copy-start | bytes 292
  52.5 120.7 %copy-start.17 = (pred[16,24]{1,0:T(8,128)(4,1)}, pred[16,24]{1,0:T(8,128)(4,1)S(1)}, u32[]{:S(2)}) copy-start(pred[16,24]{1,0:T(8,128)(4,1)S(1)} %compare_bitcast_fusion) | copy-start | bytes 1156
  92.7 216.2 %copy-start.13 = (f32[16]{0:T(128)}, f32[16]{0:T(128)S(1)}, u32[]{:S(2)}) copy-start(f32[16]{0:T(128)S(1)} %psum.50) | copy-start | bytes 196
  92.8 216.1 %copy-start.15 = (f32[24]{0:T(128)}, f32[24]{0:T(128)S(1)}, u32[]{:S(2)}) copy-start(f32[24]{0:T(128)S(1)} %fusion.52) | copy-start | bytes 292
  132.9 135.1 %copy-start.21 = (f32[16]{0:T(128)}, f32[16]{0:T(128)S(1)}, u32[]{:S(2)}) copy-start(f32[16]{0:T(128)S(1)} %psum.51) | copy-start | bytes 196
  133.0 135.0 %copy-start.19 = (f32[24]{0:T(128)}, f32[24]{0:T(128)S(1)}, u32[]{:S(2)}) copy-start(f32[24]{0:T(128)S(1)} %get-tuple-element.13) | copy-start | bytes 292
  133.3 39.9 %copy-start.11 = (s32[16,24]{1,0:T(8,128)}, s32[16,24]{1,0:T(8,128)S(1)}, u32[]{:S(2)}) copy-start(s32[16,24]{1,0:T(8,128)S(1)} %copy.41) | copy-start | bytes 4612
  134.1 11.8 %all-to-all-start.4 = ((bf16[16,1,16]{2,1,0:T(2,128)(2,1)}), bf16[16,1,16]{2,1,0:T(2,128)(2,1)S(1)}, u32[]{:S(2)}, u32[]{:S(2)}) async-start(bf16[16,1,16]{2,1,0:T(2,128)(2,1)} %copy.46), calls=%async_computation.4 | async-start | bytes 16384 | tf_op jit(solution)/shard_map/all_to_all | solution.py:117
  145.9 27.3 %all-to-all-start.1 = ((bf16[16,16,2048]{2,1,0:T(8,128)(2,1)}), bf16[16,16,2048]{2,1,0:T(8,128)(2,1)}, u32[]{:S(2)}, u32[]{:S(2)}) async-start(bf16[16,16,2048]{2,1,0:T(8,128)(2,1)} %convolution_convert_fusion.2), calls=%async_computation.1 | async-start | bytes 2097152 | tf_op jit(solution)/shard_map/all_to_all | solution.py:115
  173.2 29.9 %all-to-all-start = ((bf16[16,16,2048]{2,1,0:T(8,128)(2,1)}), bf16[16,16,2048]{2,1,0:T(8,128)(2,1)}, u32[]{:S(2)}, u32[]{:S(2)}) async-start(bf16[16,16,2048]{2,1,0:T(8,128)(2,1)} %convolution_convert_fusion.3), calls=%async_computation | async-start | bytes 2097152 | tf_op jit(solution)/shard_map/all_to_all | solution.py:116
  180.1 209.9 %reduce-scatter.3.cloned.1.call-start = ((), (), s32[]{:S(2)}) async-start(), calls=%async_computation.8 | async-start | bytes 9437184 | tf_op jit(solution)/shard_map/reduce_scatter | solution.py:144
  203.1 3.3 copy-start.27
  215.7 133.2 %copy-start.2 = (bf16[24,2048]{1,0:T(8,128)(2,1)S(1)}, bf16[24,2048]{1,0:T(8,128)(2,1)}, u32[]{:S(2)}) copy-start(bf16[24,2048]{1,0:T(8,128)(2,1)} %param.7) | copy-start | bytes 294916
  215.8 283.3 %all-reduce.2.cloned.1.call-start = ((), (), s32[]{:S(2)}) async-start(), calls=%async_computation.7 | async-start | bytes 262144 | tf_op jit(solution)/shard_map/psum | solution.py:170
  309.0 41.1 %copy-start.23 = (f32[24]{0:T(128)}, f32[24]{0:T(128)S(1)}, u32[]{:S(2)}) copy-start(f32[24]{0:T(128)S(1)} %get-tuple-element.9) | copy-start | bytes 292
  349.0 1.2 copy-start.25
  349.9 149.2 %reduce-scatter.5.cloned.1.call-start = ((), (), s32[]{:S(2)}) async-start(), calls=%async_computation.9 | async-start | bytes 4718592 | tf_op jit(solution)/shard_map/reduce_scatter | solution.py:147
  354.7 1.0 copy-start.4
  354.7 2.0 copy-start.1
  354.7 2.0 copy-start.3
  356.7 7.0 %copy-start.7 = (f32[16]{0:T(128)S(1)}, f32[16]{0:T(128)}, u32[]{:S(2)}) copy-start(f32[16]{0:T(128)} %copy-done.6) | copy-start | bytes 196
  356.7 7.0 %copy-start.9 = (f32[24]{0:T(128)S(1)}, f32[24]{0:T(128)}, u32[]{:S(2)}) copy-start(f32[24]{0:T(128)} %copy-done.8) | copy-start | bytes 292
  356.7 7.1 %copy-start.14 = (f32[16]{0:T(128)S(1)}, f32[16]{0:T(128)}, u32[]{:S(2)}) copy-start(f32[16]{0:T(128)} %copy-done.13) | copy-start | bytes 196
  356.7 7.1 %copy-start.16 = (f32[24]{0:T(128)S(1)}, f32[24]{0:T(128)}, u32[]{:S(2)}) copy-start(f32[24]{0:T(128)} %copy-done.15) | copy-start | bytes 292
  356.7 7.1 %copy-start.20 = (f32[24]{0:T(128)S(1)}, f32[24]{0:T(128)}, u32[]{:S(2)}) copy-start(f32[24]{0:T(128)} %copy-done.19) | copy-start | bytes 292
  356.8 7.1 %copy-start.22 = (f32[16]{0:T(128)S(1)}, f32[16]{0:T(128)}, u32[]{:S(2)}) copy-start(f32[16]{0:T(128)} %copy-done.21) | copy-start | bytes 196
  356.8 30.0 %copy-start.12 = (s32[16,24]{1,0:T(8,128)S(1)}, s32[16,24]{1,0:T(8,128)}, u32[]{:S(2)}) copy-start(s32[16,24]{1,0:T(8,128)} %copy-done.11) | copy-start | bytes 4612
  356.8 30.0 %copy-start.18 = (pred[16,24]{1,0:T(8,128)(4,1)S(1)}, pred[16,24]{1,0:T(8,128)(4,1)}, u32[]{:S(2)}) copy-start(pred[16,24]{1,0:T(8,128)(4,1)} %copy-done.17) | copy-start | bytes 1156
  358.8 30.2 %copy-start.5 = (bf16[2048,16]{0,1:T(8,128)(2,1)S(1)}, bf16[2048,16]{0,1:T(8,128)(2,1)}, u32[]{:S(2)}) copy-start(bf16[2048,16]{0,1:T(8,128)(2,1)} %param.10) | copy-start | bytes 196612
  358.8 30.3 %copy-start.24 = (f32[24]{0:T(128)S(1)}, f32[24]{0:T(128)}, u32[]{:S(2)}) copy-start(f32[24]{0:T(128)} %copy-done.23) | copy-start | bytes 292
  358.8 30.3 %copy-start.26 = (f32[16]{0:T(128)S(1)}, f32[16]{0:T(128)}, u32[]{:S(2)}) copy-start(f32[16]{0:T(128)} %copy-done.25) | copy-start | bytes 196
  358.8 28.0 %all-to-all-start.2 = ((bf16[16,16,2048]{2,1,0:T(8,128)(2,1)}), bf16[16,16,2048]{2,1,0:T(8,128)(2,1)}, u32[]{:S(2)}, u32[]{:S(2)}) async-start(bf16[16,16,2048]{2,1,0:T(8,128)(2,1)} %bitcast.80), calls=%async_computation.2 | async-start | bytes 2097152 | tf_op jit(solution)/shard_map/all_to_all | solution.py:126
Sparse Core Ops, SparseCore 0:
  215.9 80.4 reduce-scatter.2
  354.8 42.6 reduce-scatter.4
Sparse Core Ops, SparseCore 1:
  350.0 149.0 all-reduce.1
where the time goes:
time: 509 us; the launch traced here: 508 us
  blocking collectives  254 us (50%)
  waiting for transfers between devices  173 us (34%)
  matrix products  33.6 us (7%)
  starting transfers between devices  21.9 us (4%)
  between operations  15.8 us (3%)
  local copies, waits for them, and re-layouts  7.35 us (1%)
    psum x3, blocking collectives, balancer_forward_pass(): lax.psum(jnp.sum(expert_density_rows[-1], axis=0), ('dp', 'expert'))  122 us
    psum x3, blocking collectives, balancer_adjoint_pass(): lax.psum(jnp.sum(quotient_grad * division_ratios[repeat], axis=0), ('dp',...  119 us
    psum x1, waiting for transfers between devices, per_device(): grad_router = lax.psum(router_term, ('dp', 'expert'))  105 us
    all_to_all x1, waiting for transfers between devices, per_device(): lax.all_to_all(input_slots.reshape(sources, capacity, model_width), 'expe...  22.9 us
    all_to_all x1, waiting for transfers between devices, per_device(): lax.all_to_all(send_in, 'expert', split_axis=0, concat_axis=0, tiled=True)  21.5 us
    all_to_all x1, waiting for transfers between devices, per_device(): lax.all_to_all(send_grad, 'expert', split_axis=0, concat_axis=0, tiled=True)  18.8 us
    all_to_all x1, blocking collectives, per_device(): lax.all_to_all(score_slots.reshape(sources, capacity), 'expert', split_ax...  13.1 us
    dot_general x2, matrix products, column_product(): lax.dot_general(operand_left, operand_right, (((0,), (0,)), ((), ())), pr...  10.2 us
  transfers between devices with their start and end apart: 7, of which 5 were waited for; matrix products, arithmetic and copies ran while one was open for 5% of the time, Pallas kernels for 0%

commit v1 on v0

v1 whole, which is shorter than its diff:
```python
import jax
import jax.numpy as jnp
from jax import lax
from jax.sharding import PartitionSpec as P

PASSES = 3
LANES = 128


def swap_expert(array, offset):
    size = lax.axis_size("expert")
    return lax.ppermute(array, "expert", [(i, i ^ offset) for i in range(size)])


def swap_group(array, offset):
    size = lax.axis_size("dp")
    return lax.ppermute(array, "dp", [(i, i ^ offset) for i in range(size)])


def contract(left, right, left_dim, right_dim):
    return lax.dot_general(
        left, right, (((left_dim,), (right_dim,)), ((), ())), preferred_element_type=jnp.float32
    )


def expert_rows(rows_in, rows_grad, weight_gate, weight_up, weight_down):
    gate_pre = contract(rows_in, weight_gate, 1, 0)
    up_pre = contract(rows_in, weight_up, 1, 0)
    sigmoid_gate = jax.nn.sigmoid(gate_pre)
    activation = gate_pre * sigmoid_gate
    hidden = activation * up_pre
    hidden_grad = contract(rows_grad, weight_down, 1, 1)
    score = jnp.sum(hidden_grad * hidden, axis=1)
    gate_grad = hidden_grad * up_pre * sigmoid_gate * (1.0 + gate_pre * (1.0 - sigmoid_gate))
    up_grad = hidden_grad * activation
    return (
        hidden.astype(jnp.bfloat16),
        gate_grad.astype(jnp.bfloat16),
        up_grad.astype(jnp.bfloat16),
        score,
    )


def balancer_forward_pass(logits):
    densities = [jnp.exp(logits)]
    quotients, column_totals, row_totals = ([], [], [])
    for _ in range(PASSES):
        column_sum = jnp.sum(densities[-1], axis=1, keepdims=True)
        quotient = densities[-1] / column_sum
        row_sum = jnp.sum(quotient, axis=0, keepdims=True)
        densities.append(quotient / row_sum)
        quotients.append(quotient)
        column_totals.append(column_sum)
        row_totals.append(row_sum)
    return (densities, quotients, column_totals, row_totals)


def balancer_adjoint_pass(density_gradient, densities, quotients, column_totals, row_totals):
    for repeat in reversed(range(PASSES)):
        inner = jnp.sum(density_gradient * densities[repeat + 1], axis=0, keepdims=True)
        quotient_grad = (density_gradient - inner) / row_totals[repeat]
        shared = jnp.sum(quotient_grad * quotients[repeat], axis=1, keepdims=True)
        density_gradient = (quotient_grad - shared) / column_totals[repeat]
    return density_gradient * densities[0]


def per_device(tokens, out_grad, expert_ids, router_weight, w_gate, w_up, w_down):
    tok_rows, model_width = tokens.shape
    experts = router_weight.shape[1]
    groups = lax.axis_size("dp")
    far = lax.axis_size("expert") // 4
    chunk = 2 * far * tok_rows
    me = lax.axis_index("expert")
    my_group = lax.axis_index("dp")
    weight_gate, weight_up, weight_down = (w_gate[0], w_up[0], w_down[0])
    ff_width = weight_gate.shape[1]

    lane = jnp.arange(LANES, dtype=jnp.int32)
    picked = jnp.any(expert_ids[:, :, None] == lane[None, None, :], axis=1)
    packed = jnp.concatenate([tokens, out_grad, picked.astype(jnp.bfloat16)], axis=1)

    line = jnp.concatenate([packed] + [swap_expert(packed, k * 4) for k in range(1, far)], axis=0)
    line_next = swap_expert(line, 2)
    own = [
        jnp.concatenate([line, swap_expert(line, 1)], axis=0),
        jnp.concatenate([line_next, swap_expert(line_next, 1)], axis=0),
    ]
    logits_own = jnp.concatenate(
        [contract(router_weight, rows[:, :model_width], 0, 1) for rows in own], axis=1
    )
    logits = jnp.concatenate(
        [logits_own] + [swap_group(logits_own, offset) for offset in range(1, groups)], axis=1
    )
    state = balancer_forward_pass(logits)
    gates = experts * state[0][-1]
    my_gate = lax.dynamic_slice_in_dim(gates, me, 1, axis=0)[0]

    sums, scores, token_rows = ([], [], [])
    half = model_width // groups
    half_ff = ff_width // groups
    tie = None
    for index in range(2 * groups):
        if index < 2:
            rows = own[index]
        else:
            source = (line, line_next)[index % 2]
            if groups > 2 and tie is not None:
                source, tie = lax.optimization_barrier((source, tie))
            moved = swap_group(source, index // 2)
            rows = jnp.concatenate([moved, swap_expert(moved, 1)], axis=0)
        rows_in = rows[:, :model_width]
        rows_grad = rows[:, model_width : 2 * model_width]
        mask = jnp.sum(
            jnp.where(lane[None, :] == me, rows[:, 2 * model_width :].astype(jnp.float32), 0.0), axis=1
        )
        hidden, gate_grad, up_grad, score = expert_rows(
            rows_in, rows_grad, weight_gate, weight_up, weight_down
        )
        gate = (mask * my_gate[index * chunk : (index + 1) * chunk])[:, None]
        if index < 2:
            scores.append((score * mask).astype(jnp.bfloat16))
            part = contract(gate_grad, weight_gate, 1, 1) + contract(up_grad, weight_up, 1, 1)
            part = (gate * part).astype(jnp.bfloat16).reshape(2, far, tok_rows, model_width)
            near = part[0].astype(jnp.float32) + swap_expert(part[1], 1).astype(jnp.float32)
            total = near[0]
            near = near.astype(jnp.bfloat16)
            for k in range(1, far):
                total = total + swap_expert(near[k], k * 4).astype(jnp.float32)
            sums.append(total)
        sent = gate.astype(jnp.bfloat16).astype(jnp.float32)
        rows_half = lax.dynamic_slice_in_dim(rows_in, my_group * half, half, axis=1)
        hidden_half = lax.dynamic_slice_in_dim(hidden, my_group * half_ff, half_ff, axis=1)
        terms = (
            contract(rows_half, (sent * gate_grad).astype(jnp.bfloat16), 0, 0),
            contract(rows_half, (sent * up_grad).astype(jnp.bfloat16), 0, 0),
            contract(hidden_half, (sent * rows_grad).astype(jnp.bfloat16), 0, 0),
        )
        totals = terms if index == 0 else tuple(t + u for t, u in zip(totals, terms))
        token_rows.append(rows_in)
        tie = totals[0]
    row_sum = sums[0] + swap_expert(sums[1].astype(jnp.bfloat16), 2).astype(jnp.float32)

    grad_gate, grad_up, grad_down = (t.astype(jnp.bfloat16)[None] for t in totals)

    score = jnp.stack(scores).reshape(2, 2, far, tok_rows)
    from_far = [score]
    for k in range(1, far):
        got = swap_expert(score, k * 4)
        from_far.append(jnp.stack([got[:, :, j ^ k] for j in range(far)], axis=2))
    score = jnp.stack(from_far)
    score = jnp.stack([score, jnp.flip(swap_expert(score, 2), axis=1)], axis=1)
    score = jnp.stack([score, jnp.flip(swap_expert(score, 1), axis=3)], axis=2)
    score = score.reshape(experts, 2 * chunk)
    score = jnp.concatenate(
        [score] + [swap_group(score, offset) for offset in range(1, groups)], axis=1
    )
    order = jnp.arange(experts, dtype=jnp.int32)
    unswap = ((order[:, None] ^ me) == order[None, :]).astype(jnp.bfloat16)
    score = contract(unswap, score, 1, 0)
    logit_grad = balancer_adjoint_pass(experts * score, *state).astype(jnp.bfloat16)
    grad_router = sum(
        contract(rows, logit_grad[:, i * chunk : (i + 1) * chunk], 0, 1)
        for i, rows in enumerate(token_rows)
    )
    mine = logit_grad[:, :tok_rows]
    grad_tokens = (row_sum + contract(mine, router_weight, 0, 1)).astype(jnp.bfloat16)
    return (grad_tokens, grad_router, grad_gate, grad_up, grad_down)


def solution(mesh):
    in_specs = (
        P(("dp", "expert"), None),
        P(("dp", "expert"), None),
        P(("dp", "expert"), None),
        P(),
        P("expert", None, None),
        P("expert", None, None),
        P("expert", None, None),
    )
    out_specs = (
        P(("dp", "expert"), None),
        P(),
        P("expert", "dp", None),
        P("expert", "dp", None),
        P("expert", "dp", None),
    )
    return jax.shard_map(
        per_device, mesh=mesh, in_specs=in_specs, out_specs=out_specs, check_vma=False
    )
```

time: 509 us -> 153 us (0.30)
  blocking collectives: 254 us -> 0 us
  waiting for transfers between devices: 173 us -> 40.1 us
  local copies, waits for them, and re-layouts: 7.35 us -> 25.6 us
  between operations: 15.8 us -> 1.38 us
  matrix products: 33.6 us -> 46.4 us
  starting transfers between devices: 21.9 us -> 31.3 us
  other arithmetic: 2.59 us -> 7.81 us
    psum x6 -> x0, blocking collectives: 241 us -> none  [the longest x3 122 us: balancer_forward_pass(): lax.psum(jnp.sum(expert_density_rows[-1], axis=0), ('dp', 'expert'))]
    psum x1 -> x0, waiting for transfers between devices: 105 us -> none  [per_device(): grad_router = lax.psum(router_term, ('dp', 'expert'))]
    all_to_all x4 -> x0, waiting for transfers between devices: 67.2 us -> none  [the longest x1 22.9 us: per_device(): lax.all_to_all(input_slots.reshape(sources, capacity, model_width), 'expe...]
    ppermute x0 -> x26, waiting for transfers between devices: none -> 40.1 us  [the longest x22 38 us: swap_expert(): return lax.ppermute(array, 'expert', [(i, i ^ offset) for i in range(size)])]
    ppermute x0 -> x26, starting transfers between devices: none -> 31.3 us  [the longest x22 27.1 us: swap_expert(): return lax.ppermute(array, 'expert', [(i, i ^ offset) for i in range(size)])]
    all_to_all x4 -> x0, starting transfers between devices: 21.6 us -> none  [the longest x1 6.87 us: per_device(): lax.all_to_all(send_grad, 'expert', split_axis=0, concat_axis=0, tiled=True)]
    all_to_all x1 -> x0, blocking collectives: 13.1 us -> none  [per_device(): lax.all_to_all(score_slots.reshape(sources, capacity), 'expert', split_ax...]
    dot_general x15 -> x36, matrix products: 33.6 us -> 46.4 us  [contract(): lax.dot_general(left, right, (((left_dim,), (right_dim,)), ((), ())), pre...]
  transfers between devices with their start and end apart: 7 -> 26, of which waited for: 5 -> 10; matrix products, arithmetic and copies ran while one was open for 5% -> 34% of each run, Pallas kernels for 0% -> 0%
where the time goes in v1:
time: 153 us
  matrix products  46.4 us (30%)
  waiting for transfers between devices  40.1 us (26%)
  starting transfers between devices  31.3 us (20%)
  local copies, waits for them, and re-layouts  25.6 us (17%)
  other arithmetic  7.81 us (5%)
    dot_general x36, matrix products, contract(): lax.dot_general(left, right, (((left_dim,), (right_dim,)), ((), ())), pre...  46.4 us
    ppermute x22, waiting for transfers between devices, swap_expert(): return lax.ppermute(array, 'expert', [(i, i ^ offset) for i in range(size)])  38 us
    ppermute x22, starting transfers between devices, swap_expert(): return lax.ppermute(array, 'expert', [(i, i ^ offset) for i in range(size)])  27.1 us
    unnamed x108, local copies, waits for them, and re-layouts  14.8 us
    ppermute x4, starting transfers between devices, swap_group(): return lax.ppermute(array, 'dp', [(i, i ^ offset) for i in range(size)])  4.2 us
    convert_element_type x4, local copies, waits for them, and re-layouts, per_device(): scores.append((score * mask).astype(jnp.bfloat16))  4.04 us
  transfers between devices with their start and end apart: 26, of which 10 were waited for; matrix products, arithmetic and copies ran while one was open for 34% of the time, Pallas kernels for 0%

profile of v1, /device:TPU:0, one launch (start us, length us, event | category | flops | bytes accessed | tf_op | source)
XLA Modules:
  0.0 152.6 jit_solution(13153852967509644692)
XLA Ops:
  0.6 0.9 copy.16
  1.7 1.7 %pad_maximum_fusion.1 = (bf16[24,4224]{1,0:T(8,128)(2,1)}, bf16[192,4224]{1,0:T(8,128)(2,1)}) fusion(bf16[24,128]{1,0:T(8,128)(2,1)S(1)} %convert_element_type.305, bf16[24,2048]{1,0:T(8,128)(2,1)} %param.8, bf16[24,2048]{1,0:T(8,128)(2,1)} %param.7), kind=kLoop, calls=%fused_computation.126 | loop fusion | flops 608255 | bytes 608256 | tf_op jit(solution)/shard_map/concatenate | solution.py:80
  3.4 4.0 %collective-permute-start.1 = (bf16[24,4224]{1,0:T(8,128)(2,1)}, bf16[24,4224]{1,0:T(8,128)(2,1)S(1)}, u32[]{:S(2)}, u32[]{:S(2)}) collective-permute-start(bf16[24,4224]{1,0:T(8,128)(2,1)} %get-tuple-element.43), channel_id=1, source_target_pairs={{0,8},{1,9},{2,10},{3,11},{4,12},{5,13},{6,14},{7,15},{8,0},{9,1},... | collective-permute-start | bytes 608264 | tf_op jit(solution)/shard_map/ppermute | solution.py:12
  7.5 1.6 %collective-permute-start = (bf16[24,4224]{1,0:T(8,128)(2,1)}, bf16[24,4224]{1,0:T(8,128)(2,1)}, u32[]{:S(2)}, u32[]{:S(2)}) collective-permute-start(bf16[24,4224]{1,0:T(8,128)(2,1)} %get-tuple-element.43), channel_id=1, source_target_pairs={{0,4},{1,5},{2,6},{3,7},{4,0},{5,1},{6,2},{7,3},{8,12},{9,13},{10,... | collective-permute-start | bytes 608264 | tf_op jit(solution)/shard_map/ppermute | solution.py:12
  9.6 9.2 %collective-permute-done.1 = bf16[24,4224]{1,0:T(8,128)(2,1)S(1)} collective-permute-done((bf16[24,4224]{1,0:T(8,128)(2,1)}, bf16[24,4224]{1,0:T(8,128)(2,1)S(1)}, u32[]{:S(2)}, u32[]{:S(2)}) %collective-permute-start.1) | collective-permute-done | bytes 202784 | tf_op jit(solution)/shard_map/ppermute | solution.py:12
  18.8 3.8 %collective-permute-done.2 = bf16[24,4224]{1,0:T(8,128)(2,1)S(1)} collective-permute-done((bf16[24,4224]{1,0:T(8,128)(2,1)}, bf16[24,4224]{1,0:T(8,128)(2,1)S(1)}, u32[]{:S(2)}, u32[]{:S(2)}) %collective-permute-start.2) | collective-permute-done | bytes 202784 | tf_op jit(solution)/shard_map/ppermute | solution.py:12
  22.6 1.3 pad_maximum_fusion
  23.9 1.6 %collective-permute-start.22 = (bf16[96,4224]{1,0:T(8,128)(2,1)S(1)}, bf16[96,4224]{1,0:T(8,128)(2,1)S(1)}, u32[]{:S(2)}, u32[]{:S(2)}) collective-permute-start(bf16[96,4224]{1,0:T(8,128)(2,1)S(1)} %pad_maximum_fusion), channel_id=1, source_target_pairs={{0,16},{16,0},{1,17},{17,1},{2,18},{18,2},{3,19},{19,3},{4,20},{20... | collective-permute-start | bytes 2433032 | tf_op jit(solution)/shard_map/ppermute | solution.py:17
  25.4 1.5 collective-permute-start.4
  27.0 1.6 %constant_dynamic-update-slice_fusion.3 = bf16[192,4224]{1,0:T(8,128)(2,1)} fusion(bf16[192,4224]{1,0:T(8,128)(2,1)} %get-tuple-element.44, bf16[24,4224]{1,0:T(8,128)(2,1)} %collective-permute-done), kind=kLoop, calls=%fused_computation.181 | loop fusion | bytes 405504
  28.6 0.7 constant_dynamic-update-slice_fusion.2
  30.0 0.9 constant_dynamic-update-slice_fusion
  31.0 2.0 %fusion.22 = f32[192,768]{1,0:T(8,128)S(1)} fusion(bf16[1,2048,768]{2,1,0:T(8,128)(2,1)S(1)} %copy-done.2, bf16[192,4224]{1,0:T(8,128)(2,1)} %constant_dynamic-update-slice_fusion), kind=kOutput, calls=%fused_computation.22 | convolution fusion | flops 603979776 | bytes 4521984 | tf_op jit(solution)/shard_map/dot_general | solution.py:21
  33.0 1.0 slice.199
  34.0 0.8 fusion.10
  34.8 1.1 copy-done.11
  35.9 2.1 %multiply_reduce_fusion.1 = (f32[192]{0:T(256)S(1)}, bf16[192,768]{1,0:T(8,128)(2,1)}, bf16[192,768]{1,0:T(8,128)(2,1)S(1)}, bf16[192,768]{1,0:T(8,128)(2,1)S(1)}) fusion(f32[192,768]{1,0:T(8,128)S(1)} %fusion.22, f32[192,768]{1,0:T(8,128)S(1)} %fusion.10, bf16[1,768,2048]{2,1,0:T(8,128)(2,1)S(1)} %copy-done.11, bf16[192,4224]{1,0:T(8,128)(2,1)S(1)} %copy-done.12), kind=kOutput, calls=%fused_computation.89 | convolution fusion | flops 606486336 | bytes 5997312 | tf_op jit(solution)/shard_map/dot_general | solution.py:21
  38.0 6.0 %collective-permute-done.4 = bf16[96,4224]{1,0:T(8,128)(2,1)S(1)} collective-permute-done((bf16[96,4224]{1,0:T(8,128)(2,1)S(1)}, bf16[96,4224]{1,0:T(8,128)(2,1)S(1)}, u32[]{:S(2)}, u32[]{:S(2)}) %collective-permute-start.4) | collective-permute-done | bytes 811040 | tf_op jit(solution)/shard_map/ppermute | solution.py:12
  44.6 2.3 %fusion.8 = f32[192,2048]{1,0:T(8,128)} fusion(bf16[192,768]{1,0:T(8,128)(2,1)S(1)} %get-tuple-element.26, bf16[1,2048,768]{2,1,0:T(8,128)(2,1)S(1)} %copy-done), kind=kOutput, calls=%fused_computation.8 | convolution fusion | flops 603979776 | bytes 5013504 | tf_op jit(solution)/shard_map/dot_general | solution.py:21
  48.6 0.8 fusion.18
  49.5 1.5 collective-permute-start.6
  50.9 0.8 fusion.6
  51.8 2.2 %multiply_reduce_fusion = (f32[192]{0:T(256)S(1)}, bf16[192,768]{1,0:T(8,128)(2,1)}, bf16[192,768]{1,0:T(8,128)(2,1)S(1)}, bf16[192,768]{1,0:T(8,128)(2,1)}) fusion(f32[192,768]{1,0:T(8,128)S(1)} %fusion.18, f32[192,768]{1,0:T(8,128)S(1)} %fusion.6, bf16[1,768,2048]{2,1,0:T(8,128)(2,1)S(1)} %copy-done.11, ...), kind=kOutput, calls=%fused_computation.88 | convolution fusion | flops 606486336 | bytes 5997312 | tf_op jit(solution)/shard_map/dot_general | solution.py:21
  54.1 1.7 %fusion.14 = f32[192,768]{1,0:T(8,128)} fusion(bf16[1,2048,768]{2,1,0:T(8,128)(2,1)S(1)} %copy-done.2, bf16[192,4224]{1,0:T(8,128)(2,1)S(1)} %constant_dynamic-update-slice_fusion.9), kind=kOutput, calls=%fused_computation.14 | convolution fusion | flops 603979776 | bytes 4521984 | tf_op jit(solution)/shard_map/dot_general | solution.py:21
  55.8 2.3 %fusion.4 = f32[192,2048]{1,0:T(8,128)} fusion(bf16[192,768]{1,0:T(8,128)(2,1)S(1)} %get-tuple-element.25, bf16[1,2048,768]{2,1,0:T(8,128)(2,1)S(1)} %copy-done), kind=kOutput, calls=%fused_computation.4 | convolution fusion | flops 603979776 | bytes 5013504 | tf_op jit(solution)/shard_map/dot_general | solution.py:21
  58.1 1.8 %fusion.69 = (f32[192,768]{1,0:T(8,128)}, f32[192,768]{1,0:T(8,128)}) fusion(bf16[1,2048,768]{2,1,0:T(8,128)(2,1)S(1)} %copy-done, bf16[192,4224]{1,0:T(8,128)(2,1)S(1)} %constant_dynamic-update-slice_fusion.9), kind=kOutput, calls=%fused_computation.85 | convolution fusion | flops 604569600 | bytes 5111808 | tf_op jit(solution)/shard_map/dot_general | solution.py:21
  59.9 2.1 %collective-permute-done.24 = bf16[96,4224]{1,0:T(8,128)(2,1)S(1)} collective-permute-done((bf16[96,4224]{1,0:T(8,128)(2,1)S(1)}, bf16[96,4224]{1,0:T(8,128)(2,1)S(1)}, u32[]{:S(2)}, u32[]{:S(2)}) %collective-permute-start.24) | collective-permute-done | bytes 811040 | tf_op jit(solution)/shard_map/ppermute | solution.py:17
  62.1 2.0 %fusion.26 = f32[192,768]{1,0:T(8,128)} fusion(bf16[1,768,2048]{2,1,0:T(8,128)(2,1)S(1)} %copy-done.11, bf16[192,4224]{1,0:T(8,128)(2,1)S(1)} %constant_dynamic-update-slice_fusion.9), kind=kOutput, calls=%fused_computation.26 | convolution fusion | flops 603979776 | bytes 4521984 | tf_op jit(solution)/shard_map/dot_general | solution.py:21
  64.1 1.1 slice.200
  65.2 1.0 slice.232
  67.0 0.7 fusion.175
  67.8 1.2 copy-done.4
  70.8 1.3 convert_element_type.335
  72.2 1.3 convert_element_type.334
  73.4 1.3 constant_dynamic-update-slice_fusion.8
  74.7 1.3 constant_dynamic-update-slice_fusion.7
  75.9 8.0 %collective-permute-start.17 = (bf16[2,2,4,24]{3,2,1,0:T(4,128)(2,1)}, bf16[2,2,4,24]{3,2,1,0:T(4,128)(2,1)}, u32[]{:S(2)}, u32[]{:S(2)}) collective-permute-start(bf16[2,2,4,24]{3,2,1,0:T(4,128)(2,1)} %constant_dynamic-update-slice_fusion.7), channel_id=1, source_target_pairs={{0,8},{1,9},{2,10},{3,11},{4,12},{5,13},{6,14},{7,15},{8,0},{9,1},... | collective-permute-start | bytes 2312 | tf_op jit(solution)/shard_map/ppermute | solution.py:12
  83.9 2.9 %fusion.68 = (f32[192,768]{1,0:T(8,128)}, f32[192,768]{1,0:T(8,128)}) fusion(bf16[1,2048,768]{2,1,0:T(8,128)(2,1)S(1)} %copy-done, bf16[192,4224]{1,0:T(8,128)(2,1)} %copy-done.4), kind=kOutput, calls=%fused_computation.81 | convolution fusion | flops 604569600 | bytes 5111808 | tf_op jit(solution)/shard_map/dot_general | solution.py:21
  86.9 0.7 convert_element_type.333
  88.9 0.8 fusion.180
  89.6 4.3 %collective-permute-done.18 = bf16[2,2,4,24]{3,2,1,0:T(4,128)(2,1)S(1)} collective-permute-done((bf16[2,2,4,24]{3,2,1,0:T(4,128)(2,1)}, bf16[2,2,4,24]{3,2,1,0:T(4,128)(2,1)S(1)}, u32[]{:S(2)}, u32[]{:S(2)}) %collective-permute-start.18) | collective-permute-done | bytes 800 | tf_op jit(solution)/shard_map/ppermute | solution.py:12
  94.0 1.6 %collective-permute-start.19 = (bf16[4,2,2,4,24]{4,3,2,1,0:T(4,128)(2,1)S(1)}, bf16[4,2,2,4,24]{4,3,2,1,0:T(4,128)(2,1)S(1)}, u32[]{:S(2)}, u32[]{:S(2)}) collective-permute-start(bf16[4,2,2,4,24]{4,3,2,1,0:T(4,128)(2,1)S(1)} %pad_maximum_fusion.5), channel_id=1, source_target_pairs={{0,2},{1,3},{2,0},{3,1},{4,6},{5,7},{6,4},{7,5},{8,10},{9,11},{10,... | collective-permute-start | bytes 9224 | tf_op jit(solution)/shard_map/ppermute | solution.py:12
  95.6 2.2 %collective-permute-done.19 = bf16[4,2,2,4,24]{4,3,2,1,0:T(4,128)(2,1)S(1)} collective-permute-done((bf16[4,2,2,4,24]{4,3,2,1,0:T(4,128)(2,1)S(1)}, bf16[4,2,2,4,24]{4,3,2,1,0:T(4,128)(2,1)S(1)}, u32[]{:S(2)}, u32[]{:S(2)}) %collective-permute-start.19) | collective-permute-done | bytes 3104 | tf_op jit(solution)/shard_map/ppermute | solution.py:12
  98.0 4.0 %fusion.12 = f32[192,768]{1,0:T(8,128)} fusion(bf16[1,2048,768]{2,1,0:T(8,128)(2,1)} %param.12, bf16[192,4224]{1,0:T(8,128)(2,1)} %copy-done.4), kind=kOutput, calls=%fused_computation.12 | convolution fusion | flops 603979776 | bytes 4521984 | tf_op jit(solution)/shard_map/dot_general | solution.py:21
  102.9 3.1 %fusion.24 = f32[192,768]{1,0:T(8,128)S(1)} fusion(bf16[1,768,2048]{2,1,0:T(8,128)(2,1)} %param.13, bf16[192,4224]{1,0:T(8,128)(2,1)S(1)} %copy-done.5), kind=kOutput, calls=%fused_computation.24 | convolution fusion | flops 603979776 | bytes 4521984 | tf_op jit(solution)/shard_map/dot_general | solution.py:21
  108.8 1.3 copy-done.3
  110.1 1.2 fusion.45
  111.4 1.0 copy-done.19
  113.9 0.7 copy-done.14
  114.6 1.2 fusion.48
  119.6 0.8 fusion.76
  123.7 1.8 %fusion.52 = bf16[1,1024,768]{2,1,0:T(8,128)(2,1)} fusion(f32[1024,768]{1,0:T(8,128)S(1)} %fusion.74, f32[1024,768]{1,0:T(8,128)S(1)} %fusion.82, f32[1024,768]{1,0:T(8,128)S(1)} %fusion.78, bf16[192,2048]{1,0:T(8,128)(2,1)S(1)} %slice.234, s32[]{:T(128)S(6)} %select_n.31, f32[192,768]{1,0:T(8,128)S(1)} %fusion.24, f32[192]{0:T(256)S(1)} %fusion.146, ...), kind=kOutput, calls=%fused_computation.50 | convolution fusion | flops 306462720 | bytes 12583940 | tf_op jit(solution)/shard_map/dot_general | solution.py:21
  125.5 1.9 %fusion.51 = bf16[1,1024,768]{2,1,0:T(8,128)(2,1)} fusion(f32[1024,768]{1,0:T(8,128)S(1)} %fusion.76, f32[1024,768]{1,0:T(8,128)S(1)} %fusion.84, f32[1024,768]{1,0:T(8,128)S(1)} %fusion.80, bf16[192,2048]{1,0:T(8,128)(2,1)S(1)} %slice.234, s32[]{:T(128)S(6)} %select_n.31, f32[192]{0:T(256)S(1)} %fusion.146, f32[192,768]{1,0:T(8,128)S(1)} %copy-done.23, ...), kind=kOutput, calls=%fused_computation.49 | convolution fusion | flops 307052544 | bytes 13173764 | tf_op jit(solution)/shard_map/dot_general | solution.py:21
  127.4 1.9 %fusion.32 = bf16[1,384,2048]{2,1,0:T(8,128)(2,1)} fusion(f32[384,2048]{1,0:T(8,128)S(1)} %fusion.55, f32[384,2048]{1,0:T(8,128)S(1)} %fusion.53, f32[384,2048]{1,0:T(8,128)S(1)} %fusion.54, f32[192]{0:T(256)S(1)} %fusion.146, bf16[192,4224]{1,0:T(8,128)(2,1)S(1)} %copy-done.6, f32[192,768]{1,0:T(8,128)S(1)} %copy-done.18, s32[]{:T(128)S(6)} %select_n.34, ...), kind=kOutput, calls=%fused_computation.35 | convolution fusion | flops 306462720 | bytes 12387332 | tf_op jit(solution)/shard_map/dot_general | solution.py:21
  129.5 2.0 %collective-permute-start.14 = (bf16[24,2048]{1,0:T(8,128)(2,1)S(1)}, bf16[24,2048]{1,0:T(8,128)(2,1)S(1)}, u32[]{:S(2)}, u32[]{:S(2)}) collective-permute-start(bf16[24,2048]{1,0:T(8,128)(2,1)S(1)} %get-tuple-element.41), channel_id=1, source_target_pairs={{0,12},{1,13},{2,14},{3,15},{4,8},{5,9},{6,10},{7,11},{8,4},{9,5},... | collective-permute-start | bytes 294920 | tf_op jit(solution)/shard_map/ppermute | solution.py:12
  131.6 1.4 collective-permute-start.13
  133.2 1.0 collective-permute-start.8
  134.2 2.0 %collective-permute-start.10 = (bf16[24,2048]{1,0:T(8,128)(2,1)S(1)}, bf16[24,2048]{1,0:T(8,128)(2,1)S(1)}, u32[]{:S(2)}, u32[]{:S(2)}) collective-permute-start(bf16[24,2048]{1,0:T(8,128)(2,1)S(1)} %get-tuple-element.38), channel_id=1, source_target_pairs={{0,12},{1,13},{2,14},{3,15},{4,8},{5,9},{6,10},{7,11},{8,4},{9,5},... | collective-permute-start | bytes 294920 | tf_op jit(solution)/shard_map/ppermute | solution.py:12
  137.3 9.7 %collective-permute-done.13 = bf16[24,2048]{1,0:T(8,128)(2,1)S(1)} collective-permute-done((bf16[24,2048]{1,0:T(8,128)(2,1)S(1)}, bf16[24,2048]{1,0:T(8,128)(2,1)S(1)}, u32[]{:S(2)}, u32[]{:S(2)}) %collective-permute-start.13) | collective-permute-done | bytes 98336 | tf_op jit(solution)/shard_map/ppermute | solution.py:12
  147.1 1.6 %collective-permute-start.15 = (bf16[24,2048]{1,0:T(8,128)(2,1)S(1)}, bf16[24,2048]{1,0:T(8,128)(2,1)S(1)}, u32[]{:S(2)}, u32[]{:S(2)}) collective-permute-start(bf16[24,2048]{1,0:T(8,128)(2,1)S(1)} %fusion.99), channel_id=1, source_target_pairs={{0,2},{1,3},{2,0},{3,1},{4,6},{5,7},{6,4},{7,5},{8,10},{9,11},{10,... | collective-permute-start | bytes 294920 | tf_op jit(solution)/shard_map/ppermute | solution.py:12
  148.7 0.9 convolution_add_fusion
  149.6 0.7 collective-permute-done.9
  150.4 1.4 collective-permute-done.15
  151.8 0.8 fusion.105
  (192 shorter events, 21.5 us)
Async XLA Ops:
  0.6 33.4 %copy-start = (bf16[1,2048,768]{2,1,0:T(8,128)(2,1)S(1)}, bf16[1,2048,768]{2,1,0:T(8,128)(2,1)}, u32[]{:S(2)}) copy-start(bf16[1,2048,768]{2,1,0:T(8,128)(2,1)} %param.11) | copy-start | bytes 9437188
  1.7 5.8 %copy-start.37 = (bf16[24,128]{1,0:T(8,128)(2,1)}, bf16[24,128]{1,0:T(8,128)(2,1)S(1)}, u32[]{:S(2)}) copy-start(bf16[24,128]{1,0:T(8,128)(2,1)S(1)} %convert_element_type.305) | copy-start | bytes 18436
  3.4 15.4 %collective-permute-start.1 = (bf16[24,4224]{1,0:T(8,128)(2,1)}, bf16[24,4224]{1,0:T(8,128)(2,1)S(1)}, u32[]{:S(2)}, u32[]{:S(2)}) collective-permute-start(bf16[24,4224]{1,0:T(8,128)(2,1)} %get-tuple-element.43), channel_id=1, source_target_pairs={{0,8},{1,9},{2,10},{3,11},{4,12},{5,13},{6,14},{7,15},{8,0},{9,1},... | collective-permute-start | bytes 608264 | tf_op jit(solution)/shard_map/ppermute | solution.py:12
  7.5 11.3 %collective-permute-start = (bf16[24,4224]{1,0:T(8,128)(2,1)}, bf16[24,4224]{1,0:T(8,128)(2,1)}, u32[]{:S(2)}, u32[]{:S(2)}) collective-permute-start(bf16[24,4224]{1,0:T(8,128)(2,1)} %get-tuple-element.43), channel_id=1, source_target_pairs={{0,4},{1,5},{2,6},{3,7},{4,0},{5,1},{6,2},{7,3},{8,12},{9,13},{10,... | collective-permute-start | bytes 608264 | tf_op jit(solution)/shard_map/ppermute | solution.py:12
  9.0 13.6 %collective-permute-start.2 = (bf16[24,4224]{1,0:T(8,128)(2,1)}, bf16[24,4224]{1,0:T(8,128)(2,1)S(1)}, u32[]{:S(2)}, u32[]{:S(2)}) collective-permute-start(bf16[24,4224]{1,0:T(8,128)(2,1)} %get-tuple-element.43), channel_id=1, source_target_pairs={{0,12},{1,13},{2,14},{3,15},{4,8},{5,9},{6,10},{7,11},{8,4},{9,5},... | collective-permute-start | bytes 608264 | tf_op jit(solution)/shard_map/ppermute | solution.py:12
  22.6 8.4 %copy-start.2 = (bf16[1,2048,768]{2,1,0:T(8,128)(2,1)S(1)}, bf16[1,2048,768]{2,1,0:T(8,128)(2,1)}, u32[]{:S(2)}) copy-start(bf16[1,2048,768]{2,1,0:T(8,128)(2,1)} %param.12) | copy-start | bytes 9437188
  23.9 23.1 %collective-permute-start.22 = (bf16[96,4224]{1,0:T(8,128)(2,1)S(1)}, bf16[96,4224]{1,0:T(8,128)(2,1)S(1)}, u32[]{:S(2)}, u32[]{:S(2)}) collective-permute-start(bf16[96,4224]{1,0:T(8,128)(2,1)S(1)} %pad_maximum_fusion), channel_id=1, source_target_pairs={{0,16},{16,0},{1,17},{17,1},{2,18},{18,2},{3,19},{19,3},{4,20},{20... | collective-permute-start | bytes 2433032 | tf_op jit(solution)/shard_map/ppermute | solution.py:17
  25.4 18.6 %collective-permute-start.4 = (bf16[96,4224]{1,0:T(8,128)(2,1)S(1)}, bf16[96,4224]{1,0:T(8,128)(2,1)S(1)}, u32[]{:S(2)}, u32[]{:S(2)}) collective-permute-start(bf16[96,4224]{1,0:T(8,128)(2,1)S(1)} %pad_maximum_fusion), channel_id=1, source_target_pairs={{0,2},{1,3},{2,0},{3,1},{4,6},{5,7},{6,4},{7,5},{8,10},{9,11},{10,... | collective-permute-start | bytes 2433032 | tf_op jit(solution)/shard_map/ppermute | solution.py:12
  27.0 3.0 %collective-permute-start.3 = (bf16[96,4224]{1,0:T(8,128)(2,1)S(1)}, bf16[96,4224]{1,0:T(8,128)(2,1)S(1)}, u32[]{:S(2)}, u32[]{:S(2)}) collective-permute-start(bf16[96,4224]{1,0:T(8,128)(2,1)S(1)} %pad_maximum_fusion), channel_id=1, source_target_pairs={{0,1},{1,0},{2,3},{3,2},{4,5},{5,4},{6,7},{7,6},{8,9},{9,8},{10,11... | collective-permute-start | bytes 2433032 | tf_op jit(solution)/shard_map/ppermute | solution.py:12
  31.0 2.1 %copy-start.12 = (bf16[192,4224]{1,0:T(8,128)(2,1)S(1)}, bf16[192,4224]{1,0:T(8,128)(2,1)}, u32[]{:S(2)}) copy-start(bf16[192,4224]{1,0:T(8,128)(2,1)} %constant_dynamic-update-slice_fusion) | copy-start | bytes 4866052
  34.0 1.9 %copy-start.11 = (bf16[1,768,2048]{2,1,0:T(8,128)(2,1)S(1)}, bf16[1,768,2048]{2,1,0:T(8,128)(2,1)}, u32[]{:S(2)}) copy-start(bf16[1,768,2048]{2,1,0:T(8,128)(2,1)} %param.13) | copy-start | bytes 9437188
  38.0 6.6 %copy-start.24 = (bf16[192,768]{1,0:T(8,128)(2,1)}, bf16[192,768]{1,0:T(8,128)(2,1)S(1)}, u32[]{:S(2)}) copy-start(bf16[192,768]{1,0:T(8,128)(2,1)S(1)} %get-tuple-element.26) | copy-start | bytes 884740
  44.1 18.0 %collective-permute-start.24 = (bf16[96,4224]{1,0:T(8,128)(2,1)S(1)}, bf16[96,4224]{1,0:T(8,128)(2,1)S(1)}, u32[]{:S(2)}, u32[]{:S(2)}) collective-permute-start(bf16[96,4224]{1,0:T(8,128)(2,1)S(1)} %collective-permute-done.4), channel_id=1, source_target_pairs={{0,16},{16,0},{1,17},{17,1},{2,18},{18,2},{3,19},{19,3},{4,20},{20... | collective-permute-start | bytes 2433032 | tf_op jit(solution)/shard_map/ppermute | solution.py:17
  44.6 3.6 %collective-permute-start.5 = (bf16[96,4224]{1,0:T(8,128)(2,1)S(1)}, bf16[96,4224]{1,0:T(8,128)(2,1)S(1)}, u32[]{:S(2)}, u32[]{:S(2)}) collective-permute-start(bf16[96,4224]{1,0:T(8,128)(2,1)S(1)} %collective-permute-done.4), channel_id=1, source_target_pairs={{0,1},{1,0},{2,3},{3,2},{4,5},{5,4},{6,7},{7,6},{8,9},{9,8},{10,11... | collective-permute-start | bytes 2433032 | tf_op jit(solution)/shard_map/ppermute | solution.py:12
  47.0 7.0 %collective-permute-start.23 = (bf16[96,4224]{1,0:T(8,128)(2,1)S(1)}, bf16[96,4224]{1,0:T(8,128)(2,1)S(1)}, u32[]{:S(2)}, u32[]{:S(2)}) collective-permute-start(bf16[96,4224]{1,0:T(8,128)(2,1)S(1)} %collective-permute-done.22), channel_id=1, source_target_pairs={{0,1},{1,0},{2,3},{3,2},{4,5},{5,4},{6,7},{7,6},{8,9},{9,8},{10,11... | collective-permute-start | bytes 2433032 | tf_op jit(solution)/shard_map/ppermute | solution.py:12
  48.3 19.5 %copy-start.7 = (bf16[192,4224]{1,0:T(8,128)(2,1)}, bf16[192,4224]{1,0:T(8,128)(2,1)S(1)}, u32[]{:S(2)}) copy-start(bf16[192,4224]{1,0:T(8,128)(2,1)S(1)} %constant_dynamic-update-slice_fusion.5) | copy-start | bytes 4866052
  49.5 16.7 %collective-permute-start.6 = (f32[16,384]{1,0:T(8,128)S(1)}, f32[16,384]{1,0:T(8,128)S(1)}, u32[]{:S(2)}, u32[]{:S(2)}) collective-permute-start(f32[16,384]{1,0:T(8,128)S(1)} %pad_maximum_fusion.4), channel_id=1, source_target_pairs={{0,16},{16,0},{1,17},{17,1},{2,18},{18,2},{3,19},{19,3},{4,20},{20... | collective-permute-start | bytes 73736 | tf_op jit(solution)/shard_map/ppermute | solution.py:17
  54.0 1.8 %copy-start.27 = (bf16[192,768]{1,0:T(8,128)(2,1)}, bf16[192,768]{1,0:T(8,128)(2,1)S(1)}, u32[]{:S(2)}) copy-start(bf16[192,768]{1,0:T(8,128)(2,1)S(1)} %get-tuple-element.25) | copy-start | bytes 884740
  54.1 13.7 %copy-start.9 = (bf16[192,4224]{1,0:T(8,128)(2,1)}, bf16[192,4224]{1,0:T(8,128)(2,1)S(1)}, u32[]{:S(2)}) copy-start(bf16[192,4224]{1,0:T(8,128)(2,1)S(1)} %constant_dynamic-update-slice_fusion.9) | copy-start | bytes 4866052
  62.0 5.7 %collective-permute-start.25 = (bf16[96,4224]{1,0:T(8,128)(2,1)S(1)}, bf16[96,4224]{1,0:T(8,128)(2,1)S(1)}, u32[]{:S(2)}, u32[]{:S(2)}) collective-permute-start(bf16[96,4224]{1,0:T(8,128)(2,1)S(1)} %collective-permute-done.24), channel_id=1, source_target_pairs={{0,1},{1,0},{2,3},{3,2},{4,5},{5,4},{6,7},{7,6},{8,9},{9,8},{10,11... | collective-permute-start | bytes 2433032 | tf_op jit(solution)/shard_map/ppermute | solution.py:12
  66.4 3.3 %copy-start.35 = (f32[16]{0:T(128)}, f32[16]{0:T(128)S(1)}, u32[]{:S(2)}) copy-start(f32[16]{0:T(128)S(1)} %fusion.155) | copy-start | bytes 196
  66.7 3.0 %copy-start.39 = (f32[16]{0:T(128)}, f32[16]{0:T(128)S(1)}, u32[]{:S(2)}) copy-start(f32[16]{0:T(128)S(1)} %fusion.132) | copy-start | bytes 196
  67.0 3.8 %copy-start.45 = (f32[16]{0:T(128)}, f32[16]{0:T(128)S(1)}, u32[]{:S(2)}) copy-start(f32[16]{0:T(128)S(1)} %fusion.151) | copy-start | bytes 196
  67.8 1.2 copy-start.4
  69.7 1.2 copy-start.43
  75.9 12.9 %collective-permute-start.17 = (bf16[2,2,4,24]{3,2,1,0:T(4,128)(2,1)}, bf16[2,2,4,24]{3,2,1,0:T(4,128)(2,1)}, u32[]{:S(2)}, u32[]{:S(2)}) collective-permute-start(bf16[2,2,4,24]{3,2,1,0:T(4,128)(2,1)} %constant_dynamic-update-slice_fusion.7), channel_id=1, source_target_pairs={{0,8},{1,9},{2,10},{3,11},{4,12},{5,13},{6,14},{7,15},{8,0},{9,1},... | collective-permute-start | bytes 2312 | tf_op jit(solution)/shard_map/ppermute | solution.py:12
  88.3 5.6 %collective-permute-start.18 = (bf16[2,2,4,24]{3,2,1,0:T(4,128)(2,1)}, bf16[2,2,4,24]{3,2,1,0:T(4,128)(2,1)S(1)}, u32[]{:S(2)}, u32[]{:S(2)}) collective-permute-start(bf16[2,2,4,24]{3,2,1,0:T(4,128)(2,1)} %constant_dynamic-update-slice_fusion.7), channel_id=1, source_target_pairs={{0,12},{1,13},{2,14},{3,15},{4,8},{5,9},{6,10},{7,11},{8,4},{9,5},... | collective-permute-start | bytes 2312 | tf_op jit(solution)/shard_map/ppermute | solution.py:12
  88.8 5.1 %collective-permute-start.16 = (bf16[2,2,4,24]{3,2,1,0:T(4,128)(2,1)}, bf16[2,2,4,24]{3,2,1,0:T(4,128)(2,1)S(1)}, u32[]{:S(2)}, u32[]{:S(2)}) collective-permute-start(bf16[2,2,4,24]{3,2,1,0:T(4,128)(2,1)} %constant_dynamic-update-slice_fusion.7), channel_id=1, source_target_pairs={{0,4},{1,5},{2,6},{3,7},{4,0},{5,1},{6,2},{7,3},{8,12},{9,13},{10,... | collective-permute-start | bytes 2312 | tf_op jit(solution)/shard_map/ppermute | solution.py:12
  94.0 3.8 %collective-permute-start.19 = (bf16[4,2,2,4,24]{4,3,2,1,0:T(4,128)(2,1)S(1)}, bf16[4,2,2,4,24]{4,3,2,1,0:T(4,128)(2,1)S(1)}, u32[]{:S(2)}, u32[]{:S(2)}) collective-permute-start(bf16[4,2,2,4,24]{4,3,2,1,0:T(4,128)(2,1)S(1)} %pad_maximum_fusion.5), channel_id=1, source_target_pairs={{0,2},{1,3},{2,0},{3,1},{4,6},{5,7},{6,4},{7,5},{8,10},{9,11},{10,... | collective-permute-start | bytes 9224 | tf_op jit(solution)/shard_map/ppermute | solution.py:12
  97.9 5.0 %copy-start.5 = (bf16[192,4224]{1,0:T(8,128)(2,1)S(1)}, bf16[192,4224]{1,0:T(8,128)(2,1)}, u32[]{:S(2)}) copy-start(bf16[192,4224]{1,0:T(8,128)(2,1)} %copy-done.4) | copy-start | bytes 4866052
  97.9 4.1 %collective-permute-start.20 = (bf16[4,2,2,2,4,24]{5,4,3,2,1,0:T(4,128)(2,1)S(1)}, bf16[4,2,2,2,4,24]{5,4,3,2,1,0:T(4,128)(2,1)S(1)}, u32[]{:S(2)}, u32[]{:S(2)}) collective-permute-start(bf16[4,2,2,2,4,24]{5,4,3,2,1,0:T(4,128)(2,1)S(1)} %get-tuple-element.46), channel_id=1, source_target_pairs={{0,1},{1,0},{2,3},{3,2},{4,5},{5,4},{6,7},{7,6},{8,9},{9,8},{10,11... | collective-permute-start | bytes 18440 | tf_op jit(solution)/shard_map/ppermute | solution.py:12
  102.2 3.9 %copy-start.36 = (f32[16]{0:T(128)S(1)}, f32[16]{0:T(128)}, u32[]{:S(2)}) copy-start(f32[16]{0:T(128)} %copy-done.35) | copy-start | bytes 196
  102.2 3.9 %copy-start.38 = (f32[768]{0:T(1024)S(1)}, f32[768]{0:T(1024)}, u32[]{:S(2)}) copy-start(f32[768]{0:T(1024)} %get-tuple-element.23) | copy-start | bytes 9220
  102.2 3.9 %copy-start.40 = (f32[16]{0:T(128)S(1)}, f32[16]{0:T(128)}, u32[]{:S(2)}) copy-start(f32[16]{0:T(128)} %copy-done.39) | copy-start | bytes 196
  102.3 3.9 %copy-start.46 = (f32[16]{0:T(128)S(1)}, f32[16]{0:T(128)}, u32[]{:S(2)}) copy-start(f32[16]{0:T(128)} %copy-done.45) | copy-start | bytes 196
  102.3 3.9 %copy-start.49 = (s32[16]{0:T(128)S(1)}, s32[16]{0:T(128)}, u32[]{:S(2)}) copy-start(s32[16]{0:T(128)} %iota_xor_fusion) | copy-start | bytes 196
  102.3 3.8 %collective-permute-start.21 = (bf16[16,384]{1,0:T(8,128)(2,1)S(1)}, bf16[16,384]{1,0:T(8,128)(2,1)S(1)}, u32[]{:S(2)}, u32[]{:S(2)}) collective-permute-start(bf16[16,384]{1,0:T(8,128)(2,1)S(1)} %reshape.205), channel_id=1, source_target_pairs={{0,16},{16,0},{1,17},{17,1},{2,18},{18,2},{3,19},{19,3},{4,20},{20... | collective-permute-start | bytes 36872 | tf_op jit(solution)/shard_map/ppermute | solution.py:17
  106.0 1.2 copy-start.28
  107.2 1.6 %copy-start.15 = (f32[192,2048]{1,0:T(8,128)S(1)}, f32[192,2048]{1,0:T(8,128)}, u32[]{:S(2)}) copy-start(f32[192,2048]{1,0:T(8,128)} %fusion.4) | copy-start | bytes 4718596
  108.1 2.0 %copy-start.3 = (bf16[1,2048,768]{2,1,0:T(8,128)(2,1)S(1)}, bf16[1,2048,768]{2,1,0:T(8,128)(2,1)}, u32[]{:S(2)}) copy-start(bf16[1,2048,768]{2,1,0:T(8,128)(2,1)} %param.12) | copy-start | bytes 9437188
  110.1 1.3 copy-start.42
  111.3 1.2 copy-start.25
  113.2 1.4 copy-start.14
  114.6 2.2 %copy-start.13 = (bf16[192,4224]{1,0:T(8,128)(2,1)S(1)}, bf16[192,4224]{1,0:T(8,128)(2,1)}, u32[]{:S(2)}) copy-start(bf16[192,4224]{1,0:T(8,128)(2,1)} %constant_dynamic-update-slice_fusion) | copy-start | bytes 4866052
  115.8 1.5 copy-start.8
  115.9 1.9 %copy-start.10 = (bf16[192,4224]{1,0:T(8,128)(2,1)S(1)}, bf16[192,4224]{1,0:T(8,128)(2,1)}, u32[]{:S(2)}) copy-start(bf16[192,4224]{1,0:T(8,128)(2,1)} %copy-done.9) | copy-start | bytes 4866052
  116.6 1.9 %copy-start.48 = (f32[192]{0:T(256)S(1)}, f32[192]{0:T(256)}, u32[]{:S(2)}) copy-start(f32[192]{0:T(256)} %get-tuple-element.7) | copy-start | bytes 2308
  116.6 1.9 %copy-start.16 = (f32[192,768]{1,0:T(8,128)S(1)}, f32[192,768]{1,0:T(8,128)}, u32[]{:S(2)}) copy-start(f32[192,768]{1,0:T(8,128)} %fusion.26) | copy-start | bytes 1769476
  116.6 1.9 %copy-start.21 = (bf16[192,2048]{1,0:T(8,128)(2,1)S(1)}, bf16[192,2048]{1,0:T(8,128)(2,1)}, u32[]{:S(2)}) copy-start(bf16[192,2048]{1,0:T(8,128)(2,1)} %slice.232) | copy-start | bytes 2359300
  116.7 1.9 %copy-start.22 = (f32[192,768]{1,0:T(8,128)S(1)}, f32[192,768]{1,0:T(8,128)}, u32[]{:S(2)}) copy-start(f32[192,768]{1,0:T(8,128)} %get-tuple-element.63) | copy-start | bytes 1769476
  118.0 15.1 %collective-permute-start.7 = (bf16[4,24,2048]{2,1,0:T(8,128)(2,1)S(1)}, bf16[4,24,2048]{2,1,0:T(8,128)(2,1)S(1)}, u32[]{:S(2)}, u32[]{:S(2)}) collective-permute-start(bf16[4,24,2048]{2,1,0:T(8,128)(2,1)S(1)} %bitcast.138), channel_id=1, source_target_pairs={{0,1},{1,0},{2,3},{3,2},{4,5},{5,4},{6,7},{7,6},{8,9},{9,8},{10,11... | collective-permute-start | bytes 1179656 | tf_op jit(solution)/shard_map/ppermute | solution.py:12
  118.1 11.2 %collective-permute-start.11 = (bf16[4,24,2048]{2,1,0:T(8,128)(2,1)S(1)}, bf16[4,24,2048]{2,1,0:T(8,128)(2,1)S(1)}, u32[]{:S(2)}, u32[]{:S(2)}) collective-permute-start(bf16[4,24,2048]{2,1,0:T(8,128)(2,1)S(1)} %bitcast.139), channel_id=1, source_target_pairs={{0,1},{1,0},{2,3},{3,2},{4,5},{5,4},{6,7},{7,6},{8,9},{9,8},{10,11... | collective-permute-start | bytes 1179656 | tf_op jit(solution)/shard_map/ppermute | solution.py:12
  123.7 1.8 %copy-start.18 = (f32[192,768]{1,0:T(8,128)S(1)}, f32[192,768]{1,0:T(8,128)}, u32[]{:S(2)}) copy-start(f32[192,768]{1,0:T(8,128)} %fusion.12) | copy-start | bytes 1769476
  125.5 1.9 %copy-start.6 = (bf16[192,4224]{1,0:T(8,128)(2,1)S(1)}, bf16[192,4224]{1,0:T(8,128)(2,1)}, u32[]{:S(2)}) copy-start(bf16[192,4224]{1,0:T(8,128)(2,1)} %copy-done.4) | copy-start | bytes 4866052
  125.5 1.9 %copy-start.29 = (f32[192,768]{1,0:T(8,128)S(1)}, f32[192,768]{1,0:T(8,128)}, u32[]{:S(2)}) copy-start(f32[192,768]{1,0:T(8,128)} %get-tuple-element.64) | copy-start | bytes 1769476
  129.5 6.7 %collective-permute-start.12 = (bf16[24,2048]{1,0:T(8,128)(2,1)S(1)}, bf16[24,2048]{1,0:T(8,128)(2,1)S(1)}, u32[]{:S(2)}, u32[]{:S(2)}) collective-permute-start(bf16[24,2048]{1,0:T(8,128)(2,1)S(1)} %get-tuple-element.40), channel_id=1, source_target_pairs={{0,4},{1,5},{2,6},{3,7},{4,0},{5,1},{6,2},{7,3},{8,12},{9,13},{10,... | collective-permute-start | bytes 294920 | tf_op jit(solution)/shard_map/ppermute | solution.py:12
  129.5 7.8 %collective-permute-start.14 = (bf16[24,2048]{1,0:T(8,128)(2,1)S(1)}, bf16[24,2048]{1,0:T(8,128)(2,1)S(1)}, u32[]{:S(2)}, u32[]{:S(2)}) collective-permute-start(bf16[24,2048]{1,0:T(8,128)(2,1)S(1)} %get-tuple-element.41), channel_id=1, source_target_pairs={{0,12},{1,13},{2,14},{3,15},{4,8},{5,9},{6,10},{7,11},{8,4},{9,5},... | collective-permute-start | bytes 294920 | tf_op jit(solution)/shard_map/ppermute | solution.py:12
  131.6 15.5 %collective-permute-start.13 = (bf16[24,2048]{1,0:T(8,128)(2,1)S(1)}, bf16[24,2048]{1,0:T(8,128)(2,1)S(1)}, u32[]{:S(2)}, u32[]{:S(2)}) collective-permute-start(bf16[24,2048]{1,0:T(8,128)(2,1)S(1)} %get-tuple-element.42), channel_id=1, source_target_pairs={{0,8},{1,9},{2,10},{3,11},{4,12},{5,13},{6,14},{7,15},{8,0},{9,1},... | collective-permute-start | bytes 294920 | tf_op jit(solution)/shard_map/ppermute | solution.py:12
  133.0 18.8 %copy-start.34 = (bf16[2048,16]{0,1:T(8,128)(2,1)S(1)}, bf16[2048,16]{0,1:T(8,128)(2,1)}, u32[]{:S(2)}) copy-start(bf16[2048,16]{0,1:T(8,128)(2,1)} %param.10) | copy-start | bytes 196612
  133.0 19.6 %copy-start.1 = (bf16[1,2048,768]{2,1,0:T(8,128)(2,1)S(1)}, bf16[1,2048,768]{2,1,0:T(8,128)(2,1)}, u32[]{:S(2)}) copy-start(bf16[1,2048,768]{2,1,0:T(8,128)(2,1)} %param.11) | copy-start | bytes 9437188
  133.2 16.4 %collective-permute-start.8 = (bf16[24,2048]{1,0:T(8,128)(2,1)S(1)}, bf16[24,2048]{1,0:T(8,128)(2,1)S(1)}, u32[]{:S(2)}, u32[]{:S(2)}) collective-permute-start(bf16[24,2048]{1,0:T(8,128)(2,1)S(1)} %get-tuple-element.37), channel_id=1, source_target_pairs={{0,4},{1,5},{2,6},{3,7},{4,0},{5,1},{6,2},{7,3},{8,12},{9,13},{10,... | collective-permute-start | bytes 294920 | tf_op jit(solution)/shard_map/ppermute | solution.py:12
  134.2 15.4 %collective-permute-start.10 = (bf16[24,2048]{1,0:T(8,128)(2,1)S(1)}, bf16[24,2048]{1,0:T(8,128)(2,1)S(1)}, u32[]{:S(2)}, u32[]{:S(2)}) collective-permute-start(bf16[24,2048]{1,0:T(8,128)(2,1)S(1)} %get-tuple-element.38), channel_id=1, source_target_pairs={{0,12},{1,13},{2,14},{3,15},{4,8},{5,9},{6,10},{7,11},{8,4},{9,5},... | collective-permute-start | bytes 294920 | tf_op jit(solution)/shard_map/ppermute | solution.py:12
  136.2 14.2 %collective-permute-start.9 = (bf16[24,2048]{1,0:T(8,128)(2,1)S(1)}, bf16[24,2048]{1,0:T(8,128)(2,1)S(1)}, u32[]{:S(2)}, u32[]{:S(2)}) collective-permute-start(bf16[24,2048]{1,0:T(8,128)(2,1)S(1)} %get-tuple-element.39), channel_id=1, source_target_pairs={{0,8},{1,9},{2,10},{3,11},{4,12},{5,13},{6,14},{7,15},{8,0},{9,1},... | collective-permute-start | bytes 294920 | tf_op jit(solution)/shard_map/ppermute | solution.py:12
  147.1 4.7 %collective-permute-start.15 = (bf16[24,2048]{1,0:T(8,128)(2,1)S(1)}, bf16[24,2048]{1,0:T(8,128)(2,1)S(1)}, u32[]{:S(2)}, u32[]{:S(2)}) collective-permute-start(bf16[24,2048]{1,0:T(8,128)(2,1)S(1)} %fusion.99), channel_id=1, source_target_pairs={{0,2},{1,3},{2,0},{3,1},{4,6},{5,7},{6,4},{7,5},{8,10},{9,11},{10,... | collective-permute-start | bytes 294920 | tf_op jit(solution)/shard_map/ppermute | solution.py:12
  (12 other events, 11.1 us)

commit v2 on v1

v2 whole, which is shorter than its diff:
```python
import functools

import jax
import jax.numpy as jnp
from jax import lax
from jax.experimental import pallas as pl
from jax.experimental.pallas import tpu as pltpu
from jax.sharding import PartitionSpec as P

PASSES = 3
LANES = 128
SUBLANES = 8
FF_TILE = 256
MIB = 1 << 20
ROWS_AT_ONCE = 1024


def swap_expert(array, offset):
    size = lax.axis_size("expert")
    return lax.ppermute(array, "expert", [(i, i ^ offset) for i in range(size)])


def swap_group(array, offset):
    size = lax.axis_size("dp")
    return lax.ppermute(array, "dp", [(i, i ^ offset) for i in range(size)])


def contract(left, right, left_dim, right_dim):
    return lax.dot_general(
        left, right, (((left_dim,), (right_dim,)), ((), ())), preferred_element_type=jnp.float32
    )


def balancer_forward_pass(logits):
    densities = [jnp.exp(logits)]
    quotients, column_totals, row_totals = ([], [], [])
    for _ in range(PASSES):
        column_sum = jnp.sum(densities[-1], axis=1, keepdims=True)
        quotient = densities[-1] / column_sum
        row_sum = jnp.sum(quotient, axis=0, keepdims=True)
        densities.append(quotient / row_sum)
        quotients.append(quotient)
        column_totals.append(column_sum)
        row_totals.append(row_sum)
    return (densities, quotients, column_totals, row_totals)


def balancer_adjoint_pass(density_gradient, densities, quotients, column_totals, row_totals):
    for repeat in reversed(range(PASSES)):
        inner = jnp.sum(density_gradient * densities[repeat + 1], axis=0, keepdims=True)
        quotient_grad = (density_gradient - inner) / row_totals[repeat]
        shared = jnp.sum(quotient_grad * quotients[repeat], axis=1, keepdims=True)
        density_gradient = (quotient_grad - shared) / column_totals[repeat]
    return density_gradient * densities[0]


def gate_kernel(me_ref, logits_ref, gate_ref):
    logits = logits_ref[...]
    experts, count = logits.shape
    gates = experts * balancer_forward_pass(logits)[0][-1]
    row = lax.broadcasted_iota(jnp.int32, gates.shape, 0)
    mine = jnp.sum(jnp.where(row == me_ref[0], gates, 0.0), axis=0, keepdims=True)
    gate_ref[...] = jnp.transpose(jnp.broadcast_to(mine, (LANES, count)))


def adjoint_kernel(me_ref, logits_ref, score_ref, grad_ref):
    logits = logits_ref[...]
    experts = logits.shape[0]
    row = lax.broadcasted_iota(jnp.int32, (experts, experts), 0)
    column = lax.broadcasted_iota(jnp.int32, (experts, experts), 1)
    unswap = jnp.where((row ^ me_ref[0]) == column, 1.0, 0.0).astype(jnp.bfloat16)
    score = contract(unswap, score_ref[...], 1, 0)
    state = balancer_forward_pass(logits)
    grad_ref[...] = balancer_adjoint_pass(experts * score, *state).astype(jnp.bfloat16)


def small_call(kernel, me, operands, out_shape):
    whole = pl.BlockSpec(memory_space=pltpu.VMEM)
    return pl.pallas_call(
        kernel,
        in_specs=[pl.BlockSpec(memory_space=pltpu.SMEM)] + [whole] * len(operands),
        out_specs=whole,
        out_shape=out_shape,
        compiler_params=pltpu.CompilerParams(vmem_limit_bytes=32 * MIB),
        cost_estimate=pl.CostEstimate(flops=10**6, bytes_accessed=10**6, transcendentals=10**4),
    )(me, *operands)


def rows_kernel(parts, own, me_ref, *refs):
    tok_refs, grad_refs = (refs[:parts], refs[parts : 2 * parts])
    gate_ref, wg_ref, wu_ref, wd_ref = refs[2 * parts : 2 * parts + 4]
    tok_ref, grad_ref, hidden_ref, gs_ref, us_ref = refs[2 * parts + 4 : 2 * parts + 9]
    width = tok_ref.shape[1]
    if own:
        keep_ref, send_ref, score_ref, total_ref, mask_ref = refs[2 * parts + 9 :]
    else:
        (mask_ref,) = refs[2 * parts + 9 :]
    step = pl.program_id(0)

    @pl.when(step == 0)
    def _():
        at = 0
        for tok_part, grad_part in zip(tok_refs, grad_refs):
            rows = tok_part.shape[0]
            tok_ref[at : at + rows, :] = tok_part[...]
            grad_ref[at : at + rows, :] = grad_part[:, :width]
            picked = grad_part[:, width:].astype(jnp.float32)
            lane = lax.broadcasted_iota(jnp.int32, picked.shape, 1)
            mask = jnp.sum(jnp.where(lane == me_ref[0], picked, 0.0), axis=1, keepdims=True)
            mask_ref[at : at + rows, :] = jnp.broadcast_to(mask, (rows, LANES))
            at += rows

    rows_in, rows_grad = (tok_ref[...], grad_ref[...])
    wg, wu, wd = (wg_ref[0], wu_ref[0], wd_ref[0])
    gate_pre = contract(rows_in, wg, 1, 0)
    up_pre = contract(rows_in, wu, 1, 0)
    hidden_grad = contract(rows_grad, wd, 1, 1)
    sigmoid_gate = jax.nn.sigmoid(gate_pre)
    activation = gate_pre * sigmoid_gate
    hidden = activation * up_pre
    gate_grad = (
        hidden_grad * up_pre * sigmoid_gate * (1.0 + gate_pre * (1.0 - sigmoid_gate))
    ).astype(jnp.bfloat16)
    up_grad = (hidden_grad * activation).astype(jnp.bfloat16)
    mask = mask_ref[:, :1]
    gate = mask * gate_ref[:, :1]
    sent = gate.astype(jnp.bfloat16).astype(jnp.float32)
    hidden_ref[...] = (sent * hidden).astype(jnp.bfloat16)
    gs_ref[...] = (sent * gate_grad).astype(jnp.bfloat16)
    us_ref[...] = (sent * up_grad).astype(jnp.bfloat16)
    if own:
        product = hidden_grad * hidden * mask
        high = product.astype(jnp.bfloat16)
        low = (product - high).astype(jnp.bfloat16)
        ones = jnp.ones((SUBLANES, product.shape[1]), jnp.bfloat16)
        score = contract(ones, high, 1, 1) + contract(ones, low, 1, 1)
        part = contract(gate_grad, wg, 1, 1) + contract(up_grad, wu, 1, 1)

        @pl.when(step == 0)
        def _():
            total_ref[...] = part
            score_ref[...] = score

        @pl.when(step > 0)
        def _():
            total_ref[...] += part
            score_ref[...] += score

        @pl.when(step == pl.num_programs(0) - 1)
        def _():
            half = keep_ref.shape[0]
            scaled = (gate * total_ref[...]).astype(jnp.bfloat16)
            keep_ref[...] = scaled[:half]
            send_ref[...] = scaled[half:]


def rows_call(me, tok_parts, grad_parts, gate, w_gate, w_up, w_down, own):
    parts = len(tok_parts)
    width = tok_parts[0].shape[1]
    ff_width = w_gate.shape[2]
    tile = FF_TILE if ff_width % FF_TILE == 0 else ff_width
    rows = sum(part.shape[0] for part in tok_parts)
    half = jnp.bfloat16

    def whole(array):
        return pl.BlockSpec(array.shape, lambda j: (0, 0))

    def fixed(shape):
        return pl.BlockSpec(shape, lambda j: (0, 0))

    out_shape = [
        jax.ShapeDtypeStruct((rows, width), half),
        jax.ShapeDtypeStruct((rows, width), half),
    ] + [jax.ShapeDtypeStruct((rows, ff_width), half)] * 3
    out_specs = [fixed((rows, width))] * 2 + [pl.BlockSpec((rows, tile), lambda j: (0, j))] * 3
    scratch = []
    if own:
        out_shape += [jax.ShapeDtypeStruct((rows // 2, width), half)] * 2
        out_shape += [jax.ShapeDtypeStruct((SUBLANES, rows), jnp.float32)]
        out_specs += [fixed((rows // 2, width))] * 2 + [fixed((SUBLANES, rows))]
        scratch = [pltpu.VMEM((rows, width), jnp.float32)]
    scratch += [pltpu.VMEM((rows, LANES), jnp.float32)]
    products = 5 if own else 3
    return pl.pallas_call(
        functools.partial(rows_kernel, parts, own),
        grid=(ff_width // tile,),
        in_specs=[pl.BlockSpec(memory_space=pltpu.SMEM)]
        + [whole(part) for part in tok_parts]
        + [whole(part) for part in grad_parts]
        + [
            fixed((rows, LANES)),
            pl.BlockSpec((1, width, tile), lambda j: (0, 0, j)),
            pl.BlockSpec((1, width, tile), lambda j: (0, 0, j)),
            pl.BlockSpec((1, tile, width), lambda j: (0, j, 0)),
        ],
        out_specs=out_specs,
        out_shape=out_shape,
        scratch_shapes=scratch,
        compiler_params=pltpu.CompilerParams(vmem_limit_bytes=56 * MIB),
        cost_estimate=pl.CostEstimate(
            flops=2 * products * rows * width * ff_width,
            bytes_accessed=6 * width * ff_width,
            transcendentals=rows * ff_width,
        ),
    )(me, *tok_parts, *grad_parts, gate, w_gate, w_up, w_down)


def weights_kernel(blocks, group_ref, *refs):
    tok, grad, hidden, gates, ups = (refs[i * blocks : (i + 1) * blocks] for i in range(5))
    out_gate, out_up, out_down = refs[5 * blocks :]
    for out, lefts, rights in ((out_gate, tok, gates), (out_up, tok, ups), (out_down, hidden, grad)):
        total = contract(lefts[0][...], rights[0][...], 0, 0)
        for left, right in zip(lefts[1:], rights[1:]):
            total += contract(left[...], right[...], 0, 0)
        out[0] = total.astype(out.dtype)


def weights_call(group, groups, tok, grad, hidden, gates, ups, dtype):
    width, ff_width = (tok[0].shape[1], gates[0].shape[1])
    half, half_ff = (width // groups, ff_width // groups)
    steps = max(s for s in (4, 2, 1) if half % (s * LANES) == 0)
    if half_ff % LANES:
        hidden = [lax.dynamic_slice_in_dim(h, group[0] * half_ff, half_ff, axis=1) for h in hidden]

    def rows(array):
        return array.shape[0]

    def hidden_block(j, group_ref):
        return (0, 0 if half_ff % LANES else group_ref[0])

    in_specs = (
        [pl.BlockSpec((rows(a), half // steps), lambda j, g: (0, g[0] * steps + j)) for a in tok]
        + [pl.BlockSpec((rows(a), width // steps), lambda j, g: (0, j)) for a in grad]
        + [pl.BlockSpec((rows(a), half_ff), hidden_block) for a in hidden]
        + [pl.BlockSpec((rows(a), ff_width), lambda j, g: (0, 0)) for a in gates + ups]
    )
    return pl.pallas_call(
        functools.partial(weights_kernel, len(tok)),
        grid_spec=pltpu.PrefetchScalarGridSpec(
            num_scalar_prefetch=1,
            grid=(steps,),
            in_specs=in_specs,
            out_specs=[
                pl.BlockSpec((1, half // steps, ff_width), lambda j, g: (0, j, 0)),
                pl.BlockSpec((1, half // steps, ff_width), lambda j, g: (0, j, 0)),
                pl.BlockSpec((1, half_ff, width // steps), lambda j, g: (0, 0, j)),
            ],
        ),
        out_shape=[
            jax.ShapeDtypeStruct((1, half, ff_width), dtype),
            jax.ShapeDtypeStruct((1, half, ff_width), dtype),
            jax.ShapeDtypeStruct((1, half_ff, width), dtype),
        ],
        compiler_params=pltpu.CompilerParams(vmem_limit_bytes=48 * MIB),
        cost_estimate=pl.CostEstimate(
            flops=6 * sum(rows(a) for a in tok) * half * ff_width,
            bytes_accessed=6 * half * ff_width,
            transcendentals=0,
        ),
    )(group, *tok, *grad, *hidden, *gates, *ups)


def per_device(tokens, out_grad, expert_ids, router_weight, w_gate, w_up, w_down):
    tok_rows, width = tokens.shape
    experts = router_weight.shape[1]
    groups = lax.axis_size("dp")
    far = lax.axis_size("expert") // 4
    chunk = 2 * far * tok_rows
    me = lax.axis_index("expert").astype(jnp.int32)[None]
    group = lax.axis_index("dp").astype(jnp.int32)[None]

    def along(array):
        return jnp.concatenate([array] + [swap_expert(array, 4 * k) for k in range(1, far)], axis=0)

    tok_line = along(tokens)
    lane = jnp.arange(LANES, dtype=jnp.int32)
    picked = jnp.any(expert_ids[:, :, None] == lane[None, None, :], axis=1)
    grad_line = along(jnp.concatenate([out_grad, picked.astype(jnp.bfloat16)], axis=1))
    tok_next = swap_expert(tok_line, 2)
    grad_next = swap_expert(grad_line, 2)
    tok_own = [(tok_line, swap_expert(tok_line, 1)), (tok_next, swap_expert(tok_next, 1))]
    grad_own = [(grad_line, swap_expert(grad_line, 1)), (grad_next, swap_expert(grad_next, 1))]

    logits_own = jnp.concatenate(
        [contract(router_weight, rows, 0, 1) for pair in tok_own for rows in pair], axis=1
    )
    logits = jnp.concatenate(
        [logits_own] + [swap_group(logits_own, offset) for offset in range(1, groups)], axis=1
    )
    gate = small_call(
        gate_kernel, me, (logits,), jax.ShapeDtypeStruct((logits.shape[1], LANES), jnp.float32)
    )

    done, sums, scores = ([], [], [])
    row_sum = 0.0
    for index in range(2):
        *rows, keep, send, score = rows_call(
            me, tok_own[index], grad_own[index], gate[index * chunk : (index + 1) * chunk],
            w_gate, w_up, w_down, True,
        )
        done.append(rows)
        scores.append(score[0].astype(jnp.bfloat16))
        got = swap_expert(send, 1)
        for k in range(far):
            cut = slice(k * tok_rows, (k + 1) * tok_rows)
            near = keep[cut].astype(jnp.float32) + got[cut].astype(jnp.float32)
            if index or k:
                near = swap_expert(near.astype(jnp.bfloat16), 4 * k + 2 * index).astype(jnp.float32)
            row_sum = row_sum + near

    score = jnp.stack(scores).reshape(2, 2, far, tok_rows)
    from_far = [score]
    for k in range(1, far):
        got = swap_expert(score, k * 4)
        from_far.append(jnp.stack([got[:, :, j ^ k] for j in range(far)], axis=2))
    score = jnp.stack(from_far)
    score = jnp.stack([score, jnp.flip(swap_expert(score, 2), axis=1)], axis=1)
    score = jnp.stack([score, jnp.flip(swap_expert(score, 1), axis=3)], axis=2)
    score = score.reshape(experts, 2 * chunk)
    score = jnp.concatenate(
        [score] + [swap_group(score, offset) for offset in range(1, groups)], axis=1
    )
    logit_grad = small_call(
        adjoint_kernel, me, (logits, score), jax.ShapeDtypeStruct(logits.shape, jnp.bfloat16)
    )

    token_rows = [rows[0] for rows in done]
    at_once = 2 * groups * chunk <= ROWS_AT_ONCE
    totals = None
    tie = None
    for offset in range(1, groups):
        sources = (tok_line, grad_line, tok_next, grad_next)
        if not at_once:
            terms = weights_call(group, groups, *map(list, zip(*done)), jnp.float32)
            totals = terms if totals is None else [t + u for t, u in zip(totals, terms)]
            done = []
            sources, totals = lax.optimization_barrier((sources, totals))
        moved = [swap_group(part, offset) for part in sources]
        parts = []
        for part in moved:
            parts += [part, swap_expert(part, 1)]
        rows = rows_call(
            me, parts[0:2] + parts[4:6], parts[2:4] + parts[6:8],
            gate[2 * chunk * offset : 2 * chunk * (offset + 1)], w_gate, w_up, w_down, False,
        )
        done.append(rows)
        token_rows.append(rows[0])
    final = weights_call(
        group, groups, *map(list, zip(*done)), jnp.bfloat16 if totals is None else jnp.float32
    )
    if totals is not None:
        final = [(t + u).astype(jnp.bfloat16) for t, u in zip(totals, final)]

    grad_router = 0.0
    at = 0
    for rows in token_rows:
        grad_router += contract(rows, logit_grad[:, at : at + rows.shape[0]], 0, 1)
        at += rows.shape[0]
    row_sum = row_sum + contract(logit_grad[:, :tok_rows], router_weight, 0, 1)
    return (row_sum.astype(jnp.bfloat16), grad_router, *final)


def solution(mesh):
    in_specs = (
        P(("dp", "expert"), None),
        P(("dp", "expert"), None),
        P(("dp", "expert"), None),
        P(),
        P("expert", None, None),
        P("expert", None, None),
        P("expert", None, None),
    )
    out_specs = (
        P(("dp", "expert"), None),
        P(),
        P("expert", "dp", None),
        P("expert", "dp", None),
        P("expert", "dp", None),
    )
    return jax.shard_map(
        per_device, mesh=mesh, in_specs=in_specs, out_specs=out_specs, check_vma=False
    )
```

time: 153 us -> 144 us (0.941)
  matrix products: 46.4 us -> 3.16 us
  Pallas kernels: 0 us -> 42.7 us
  local copies, waits for them, and re-layouts: 25.6 us -> 10 us
  starting transfers between devices: 31.3 us -> 41.3 us
  other arithmetic: 7.81 us -> 2.39 us
  waiting for transfers between devices: 40.1 us -> 42.4 us
    dot_general x36 -> x8, matrix products: 46.4 us -> 3.16 us  [contract(): lax.dot_general(left, right, (((left_dim,), (right_dim,)), ((), ())), pre...]
    pallas_call x0 -> x6, Pallas kernels: none -> 42.7 us  [the longest x3 33.4 us: rows_call(): pl.pallas_call(functools.partial(rows_kernel, parts, own), grid=(ff_width...]
    ppermute x4 -> x6, waiting for transfers between devices: 2.12 us -> 16.4 us  [swap_group(): return lax.ppermute(array, 'dp', [(i, i ^ offset) for i in range(size)])]
    ppermute x22 -> x30, waiting for transfers between devices: 38 us -> 26.1 us  [swap_expert(): return lax.ppermute(array, 'expert', [(i, i ^ offset) for i in range(size)])]
    unnamed x108 -> x67, local copies, waits for them, and re-layouts: 14.8 us -> 6.48 us
    ppermute x22 -> x30, starting transfers between devices: 27.1 us -> 34.1 us  [swap_expert(): return lax.ppermute(array, 'expert', [(i, i ^ offset) for i in range(size)])]
    convert_element_type x4 -> x0, local copies, waits for them, and re-layouts: 4.04 us -> none  [per_device(): scores.append((score * mask).astype(jnp.bfloat16))]
    ppermute x4 -> x6, starting transfers between devices: 4.2 us -> 7.19 us  [swap_group(): return lax.ppermute(array, 'dp', [(i, i ^ offset) for i in range(size)])]
  transfers between devices with their start and end apart: 26 -> 36, of which waited for: 10 -> 14; matrix products, arithmetic and copies ran while one was open for 34% -> 6% of each run, Pallas kernels for 0% -> 21%
where the time goes in v2:
time: 144 us; the launch traced here: 143 us
  Pallas kernels  42.7 us (30%)
  waiting for transfers between devices  42.4 us (29%)
  starting transfers between devices  41.3 us (29%)
  local copies, waits for them, and re-layouts  10 us (7%)
  matrix products  3.16 us (2%)
  other arithmetic  2.39 us (2%)
    ppermute x30, starting transfers between devices, swap_expert(): return lax.ppermute(array, 'expert', [(i, i ^ offset) for i in range(size)])  34.1 us
    pallas_call x3, Pallas kernels, rows_call(): pl.pallas_call(functools.partial(rows_kernel, parts, own), grid=(ff_width...  33.4 us
    ppermute x30, waiting for transfers between devices, swap_expert(): return lax.ppermute(array, 'expert', [(i, i ^ offset) for i in range(size)])  26.1 us
    ppermute x6, waiting for transfers between devices, swap_group(): return lax.ppermute(array, 'dp', [(i, i ^ offset) for i in range(size)])  16.4 us
    pallas_call x1, Pallas kernels, weights_call(): pl.pallas_call(functools.partial(weights_kernel, len(tok)), grid_spec=plt...  8.23 us
    ppermute x6, starting transfers between devices, swap_group(): return lax.ppermute(array, 'dp', [(i, i ^ offset) for i in range(size)])  7.19 us
    unnamed x67, local copies, waits for them, and re-layouts  6.48 us
    dot_general x8, matrix products, contract(): lax.dot_general(left, right, (((left_dim,), (right_dim,)), ((), ())), pre...  3.16 us
  transfers between devices with their start and end apart: 36, of which 14 were waited for; matrix products, arithmetic and copies ran while one was open for 6% of the time, Pallas kernels for 21%

profile of v2, /device:TPU:0, one launch (start us, length us, event | category | flops | bytes accessed | tf_op | source)
XLA Modules:
  0.0 143.1 jit_solution(18178485722987751434)
XLA Ops:
  0.6 3.1 %collective-permute-start = (bf16[24,2048]{1,0:T(8,128)(2,1)}, bf16[24,2048]{1,0:T(8,128)(2,1)S(1)}, u32[]{:S(2)}, u32[]{:S(2)}) collective-permute-start(bf16[24,2048]{1,0:T(8,128)(2,1)} %param.7), channel_id=1, source_target_pairs={{0,4},{1,5},{2,6},{3,7},{4,0},{5,1},{6,2},{7,3},{8,12},{9,13},{10,... | collective-permute-start | bytes 294920 | tf_op jit(solution)/shard_map/ppermute | solution.py:20
  3.7 2.6 %collective-permute-start.1 = (bf16[24,2048]{1,0:T(8,128)(2,1)}, bf16[24,2048]{1,0:T(8,128)(2,1)S(1)}, u32[]{:S(2)}, u32[]{:S(2)}) collective-permute-start(bf16[24,2048]{1,0:T(8,128)(2,1)} %param.7), channel_id=1, source_target_pairs={{0,8},{1,9},{2,10},{3,11},{4,12},{5,13},{6,14},{7,15},{8,0},{9,1},... | collective-permute-start | bytes 294920 | tf_op jit(solution)/shard_map/ppermute | solution.py:20
  6.3 0.8 copy.15
  7.2 0.9 pad_maximum_fusion.1
  8.1 3.8 %collective-permute-start.6 = (bf16[24,2176]{1,0:T(8,128)(2,1)S(1)}, bf16[24,2176]{1,0:T(8,128)(2,1)S(1)}, u32[]{:S(2)}, u32[]{:S(2)}) collective-permute-start(bf16[24,2176]{1,0:T(8,128)(2,1)S(1)} %pad_maximum_fusion.1), channel_id=1, source_target_pairs={{0,12},{1,13},{2,14},{3,15},{4,8},{5,9},{6,10},{7,11},{8,4},{9,5},... | collective-permute-start | bytes 313352 | tf_op jit(solution)/shard_map/ppermute | solution.py:20
  11.9 0.9 constant_dynamic-update-slice_fusion.3
  12.8 0.7 collective-permute-start.4
  13.6 5.4 %collective-permute-done.1 = bf16[24,2048]{1,0:T(8,128)(2,1)S(1)} collective-permute-done((bf16[24,2048]{1,0:T(8,128)(2,1)}, bf16[24,2048]{1,0:T(8,128)(2,1)S(1)}, u32[]{:S(2)}, u32[]{:S(2)}) %collective-permute-start.1) | collective-permute-done | bytes 98336 | tf_op jit(solution)/shard_map/ppermute | solution.py:20
  19.0 1.6 %collective-permute-start.8 = (bf16[96,2048]{1,0:T(8,128)(2,1)S(1)}, bf16[96,2048]{1,0:T(8,128)(2,1)S(1)}, u32[]{:S(2)}, u32[]{:S(2)}) collective-permute-start(bf16[96,2048]{1,0:T(8,128)(2,1)S(1)} %constant_dynamic-update-slice_fusion.refs_0_), channel_id=1, source_target_pairs={{0,2},{1,3},{2,0},{3,1},{4,6},{5,7},{6,4},{7,5},{8,10},{9,11},{10,... | collective-permute-start | bytes 1179656 | tf_op jit(solution)/shard_map/ppermute | solution.py:20
  20.6 0.2 convolution_bitcast_fusion.3
  20.8 3.6 %collective-permute-done.5 = bf16[24,2176]{1,0:T(8,128)(2,1)S(1)} collective-permute-done((bf16[24,2176]{1,0:T(8,128)(2,1)S(1)}, bf16[24,2176]{1,0:T(8,128)(2,1)S(1)}, u32[]{:S(2)}, u32[]{:S(2)}) %collective-permute-start.5) | collective-permute-done | bytes 104480 | tf_op jit(solution)/shard_map/ppermute | solution.py:20
  24.4 0.9 pad_maximum_fusion.refs_2_
  25.3 1.6 %collective-permute-start.15 = (bf16[96,2176]{1,0:T(8,128)(2,1)S(1)}, bf16[96,2176]{1,0:T(8,128)(2,1)S(1)}, u32[]{:S(2)}, u32[]{:S(2)}) collective-permute-start(bf16[96,2176]{1,0:T(8,128)(2,1)S(1)} %pad_maximum_fusion.refs_2_), channel_id=1, source_target_pairs={{0,2},{1,3},{2,0},{3,1},{4,6},{5,7},{6,4},{7,5},{8,10},{9,11},{10,... | collective-permute-start | bytes 1253384 | tf_op jit(solution)/shard_map/ppermute | solution.py:20
  26.9 0.5 collective-permute-start.9
  27.6 0.2 convolution_bitcast_fusion.2
  27.9 1.4 collective-permute-done.9.refs_1_
  29.2 0.8 copy-done.21
  30.0 0.2 convolution_bitcast_fusion
  30.3 1.5 %collective-permute-start.10 = (f32[16,384]{1,0:T(8,128)S(1)}, f32[16,384]{1,0:T(8,128)S(1)}, u32[]{:S(2)}, u32[]{:S(2)}) collective-permute-start(f32[16,384]{1,0:T(8,128)S(1)} %pad_maximum_fusion.4), channel_id=1, source_target_pairs={{0,16},{16,0},{1,17},{17,1},{2,18},{18,2},{3,19},{19,3},{4,20},{20... | collective-permute-start | bytes 73736 | tf_op jit(solution)/shard_map/ppermute | solution.py:25
  31.8 4.0 %collective-permute-done.15.refs_2_ = bf16[96,2176]{1,0:T(8,128)(2,1)S(1)} collective-permute-done((bf16[96,2176]{1,0:T(8,128)(2,1)S(1)}, bf16[96,2176]{1,0:T(8,128)(2,1)S(1)}, u32[]{:S(2)}, u32[]{:S(2)}) %collective-permute-start.15) | collective-permute-done | bytes 417824 | tf_op jit(solution)/shard_map/ppermute | solution.py:20
  35.9 0.5 shard_map.110
  36.4 0.7 fusion.12
  37.1 0.7 copy-done.27
  37.8 12.0 %shard_map.111 = (bf16[192,2048]{1,0:T(8,128)(2,1)}, bf16[192,2048]{1,0:T(8,128)(2,1)}, bf16[192,768]{1,0:T(8,128)(2,1)}, bf16[192,768]{1,0:T(8,128)(2,1)}, bf16...) custom-call(s32[1]{0:T(128)} %bitcast.me_ref, ...), custom_call_target="tpu_custom_call" | custom-call | flops 3019898880 | bytes 9437184 | tf_op jit(solution)/shard_map/pallas_call | solution.py:184
  49.8 0.7 fusion.10
  50.7 12.1 %shard_map.112 = (bf16[192,2048]{1,0:T(8,128)(2,1)}, bf16[192,2048]{1,0:T(8,128)(2,1)}, bf16[192,768]{1,0:T(8,128)(2,1)}, bf16[192,768]{1,0:T(8,128)(2,1)}, bf16...) custom-call(s32[1]{0:T(128)} %bitcast.me_ref, ...), custom_call_target="tpu_custom_call" | custom-call | flops 3019898880 | bytes 9437184 | tf_op jit(solution)/shard_map/pallas_call | solution.py:184
  62.8 0.8 fusion.9
  63.7 2.5 %collective-permute-start.24 = (bf16[2,2,4,24]{3,2,1,0:T(4,128)(2,1)S(1)}, bf16[2,2,4,24]{3,2,1,0:T(4,128)(2,1)S(1)}, u32[]{:S(2)}, u32[]{:S(2)}) collective-permute-start(bf16[2,2,4,24]{3,2,1,0:T(4,128)(2,1)S(1)} %constant_dynamic-update-slice_fusion.4), channel_id=1, source_target_pairs={{0,12},{1,13},{2,14},{3,15},{4,8},{5,9},{6,10},{7,11},{8,4},{9,5},... | collective-permute-start | bytes 2312 | tf_op jit(solution)/shard_map/ppermute | solution.py:20
  66.2 1.5 %collective-permute-start.28 = (bf16[96,2048]{1,0:T(8,128)(2,1)S(1)}, bf16[96,2048]{1,0:T(8,128)(2,1)}, u32[]{:S(2)}, u32[]{:S(2)}) collective-permute-start(bf16[96,2048]{1,0:T(8,128)(2,1)S(1)} %copy-done.15), channel_id=1, source_target_pairs={{0,16},{16,0},{1,17},{17,1},{2,18},{18,2},{3,19},{19,3},{4,20},{20... | collective-permute-start | bytes 1179656 | tf_op jit(solution)/shard_map/ppermute | solution.py:25
  67.7 0.5 collective-permute-start.32
  68.3 1.5 %collective-permute-start.30 = (bf16[96,2048]{1,0:T(8,128)(2,1)}, bf16[96,2048]{1,0:T(8,128)(2,1)}, u32[]{:S(2)}, u32[]{:S(2)}) collective-permute-start(bf16[96,2048]{1,0:T(8,128)(2,1)} %copy-done.19), channel_id=1, source_target_pairs={{0,16},{16,0},{1,17},{17,1},{2,18},{18,2},{3,19},{19,3},{4,20},{20... | collective-permute-start | bytes 1179656 | tf_op jit(solution)/shard_map/ppermute | solution.py:25
  69.9 3.3 %collective-permute-start.22 = (bf16[2,2,4,24]{3,2,1,0:T(4,128)(2,1)S(1)}, bf16[2,2,4,24]{3,2,1,0:T(4,128)(2,1)S(1)}, u32[]{:S(2)}, u32[]{:S(2)}) collective-permute-start(bf16[2,2,4,24]{3,2,1,0:T(4,128)(2,1)S(1)} %constant_dynamic-update-slice_fusion.4), channel_id=1, source_target_pairs={{0,4},{1,5},{2,6},{3,7},{4,0},{5,1},{6,2},{7,3},{8,12},{9,13},{10,... | collective-permute-start | bytes 2312 | tf_op jit(solution)/shard_map/ppermute | solution.py:20
  73.3 1.4 collective-permute-done.22
  74.8 3.0 %collective-permute-done.23 = bf16[2,2,4,24]{3,2,1,0:T(4,128)(2,1)S(1)} collective-permute-done((bf16[2,2,4,24]{3,2,1,0:T(4,128)(2,1)S(1)}, bf16[2,2,4,24]{3,2,1,0:T(4,128)(2,1)S(1)}, u32[]{:S(2)}, u32[]{:S(2)}) %collective-permute-start.23) | collective-permute-done | bytes 800 | tf_op jit(solution)/shard_map/ppermute | solution.py:20
  77.9 2.0 %collective-permute-start.25 = (bf16[4,2,2,4,24]{4,3,2,1,0:T(4,128)(2,1)S(1)}, bf16[4,2,2,4,24]{4,3,2,1,0:T(4,128)(2,1)S(1)}, u32[]{:S(2)}, u32[]{:S(2)}) collective-permute-start(bf16[4,2,2,4,24]{4,3,2,1,0:T(4,128)(2,1)S(1)} %pad_maximum_fusion.6), channel_id=1, source_target_pairs={{0,2},{1,3},{2,0},{3,1},{4,6},{5,7},{6,4},{7,5},{8,10},{9,11},{10,... | collective-permute-start | bytes 9224 | tf_op jit(solution)/shard_map/ppermute | solution.py:20
  79.9 1.8 %collective-permute-done.25 = bf16[4,2,2,4,24]{4,3,2,1,0:T(4,128)(2,1)S(1)} collective-permute-done((bf16[4,2,2,4,24]{4,3,2,1,0:T(4,128)(2,1)S(1)}, bf16[4,2,2,4,24]{4,3,2,1,0:T(4,128)(2,1)S(1)}, u32[]{:S(2)}, u32[]{:S(2)}) %collective-permute-start.25) | collective-permute-done | bytes 3104 | tf_op jit(solution)/shard_map/ppermute | solution.py:20
  81.8 1.2 collective-permute-done.26
  83.2 0.6 collective-permute-start.27
  83.8 1.6 %collective-permute-start.34 = (bf16[96,2176]{1,0:T(8,128)(2,1)}, bf16[96,2176]{1,0:T(8,128)(2,1)S(1)}, u32[]{:S(2)}, u32[]{:S(2)}) collective-permute-start(bf16[96,2176]{1,0:T(8,128)(2,1)} %copy-done.23), channel_id=1, source_target_pairs={{0,16},{16,0},{1,17},{17,1},{2,18},{18,2},{3,19},{19,3},{4,20},{20... | collective-permute-start | bytes 1253384 | tf_op jit(solution)/shard_map/ppermute | solution.py:25
  85.4 1.9 %collective-permute-done.32.refs_4_ = bf16[96,2176]{1,0:T(8,128)(2,1)} collective-permute-done((bf16[96,2176]{1,0:T(8,128)(2,1)S(1)}, bf16[96,2176]{1,0:T(8,128)(2,1)}, u32[]{:S(2)}, u32[]{:S(2)}) %collective-permute-start.32) | collective-permute-done | bytes 417824 | tf_op jit(solution)/shard_map/ppermute | solution.py:25
  87.3 8.4 %collective-permute-done.30.refs_2_ = bf16[96,2048]{1,0:T(8,128)(2,1)} collective-permute-done((bf16[96,2048]{1,0:T(8,128)(2,1)}, bf16[96,2048]{1,0:T(8,128)(2,1)}, u32[]{:S(2)}, u32[]{:S(2)}) %collective-permute-start.30) | collective-permute-done | bytes 393248 | tf_op jit(solution)/shard_map/ppermute | solution.py:25
  95.7 0.7 slice.172.refs_8_
  96.4 0.5 collective-permute-start.11
  96.9 0.6 shard_map.113
  97.5 0.2 fusion.3
  97.7 0.3 convolution_add_fusion.1
  98.0 6.1 %collective-permute-done.34.refs_6_ = bf16[96,2176]{1,0:T(8,128)(2,1)S(1)} collective-permute-done((bf16[96,2176]{1,0:T(8,128)(2,1)}, bf16[96,2176]{1,0:T(8,128)(2,1)S(1)}, u32[]{:S(2)}, u32[]{:S(2)}) %collective-permute-start.34) | collective-permute-done | bytes 417824 | tf_op jit(solution)/shard_map/ppermute | solution.py:25
  104.1 0.5 collective-permute-start.35
  104.7 1.1 collective-permute-done.17
  105.8 1.3 collective-permute-start.14
  107.3 3.0 %collective-permute-start.13 = (bf16[24,2048]{1,0:T(8,128)(2,1)S(1)}, bf16[24,2048]{1,0:T(8,128)(2,1)S(1)}, u32[]{:S(2)}, u32[]{:S(2)}) collective-permute-start(bf16[24,2048]{1,0:T(8,128)(2,1)S(1)} %get-tuple-element.55), channel_id=1, source_target_pairs={{0,8},{1,9},{2,10},{3,11},{4,12},{5,13},{6,14},{7,15},{8,0},{9,1},... | collective-permute-start | bytes 294920 | tf_op jit(solution)/shard_map/ppermute | solution.py:20
  110.4 2.3 %collective-permute-start.21 = (bf16[24,2048]{1,0:T(8,128)(2,1)S(1)}, bf16[24,2048]{1,0:T(8,128)(2,1)S(1)}, u32[]{:S(2)}, u32[]{:S(2)}) collective-permute-start(bf16[24,2048]{1,0:T(8,128)(2,1)S(1)} %get-tuple-element.57), channel_id=1, source_target_pairs={{0,14},{1,15},{2,12},{3,13},{4,10},{5,11},{6,8},{7,9},{8,6},{9,7},... | collective-permute-start | bytes 294920 | tf_op jit(solution)/shard_map/ppermute | solution.py:20
  112.8 1.9 %collective-permute-start.20 = (bf16[24,2048]{1,0:T(8,128)(2,1)S(1)}, bf16[24,2048]{1,0:T(8,128)(2,1)S(1)}, u32[]{:S(2)}, u32[]{:S(2)}) collective-permute-start(bf16[24,2048]{1,0:T(8,128)(2,1)S(1)} %get-tuple-element.58), channel_id=1, source_target_pairs={{0,10},{1,11},{2,8},{3,9},{4,14},{5,15},{6,12},{7,13},{8,2},{9,3},... | collective-permute-start | bytes 294920 | tf_op jit(solution)/shard_map/ppermute | solution.py:20
  114.8 9.4 %shard_map.114 = (bf16[384,2048]{1,0:T(8,128)(2,1)}, bf16[384,2048]{1,0:T(8,128)(2,1)}, bf16[384,768]{1,0:T(8,128)(2,1)}, bf16[384,768]{1,0:T(8,128)(2,1)}, bf16[384,768]{1,0:T(8,128)(2,1)}) custom-call(s32[1]{0:T(128)} %bitcast.me_ref, bf16[96,2048]{1,0:T(8,128)(2,1)} %collective-permute-done.28.refs_0_, bf16[96,2048]{1,0:T(8,128)(2,1)} %copy-done.29, ...), custom_call_target="tpu_custom_call" | custom-call | flops 3623878656 | bytes 9437184 | tf_op jit(solution)/shard_map/pallas_call | solution.py:184
  124.2 1.1 copy-done.10
  125.3 1.1 copy-done.11
  126.3 1.1 copy-done.12
  127.4 8.2 %shard_map.115 = (bf16[1,1024,768]{2,1,0:T(8,128)(2,1)}, bf16[1,1024,768]{2,1,0:T(8,128)(2,1)}, bf16[1,384,2048]{2,1,0:T(8,128)(2,1)}) custom-call(s32[1]{0:T(128)} %bitcast.14.group_ref, bf16[192,2048]{1,0:T(8,128)(2,1)S(1)} %copy-done.1, bf16[192,2048]{1,0:T(8,128)(2,1)S(1)} %copy-done.2, bf16[384,2048]{1,0:T(8,128)(2,1)} %get-tuple-element.37.refs_2_, ...), custom_call_target="tpu_custom_call" | custom-call | flops 3623878656 | bytes 4718592 | tf_op jit(solution)/shard_map/pallas_call | solution.py:237
  135.6 2.0 %collective-permute-start.19 = (bf16[24,2048]{1,0:T(8,128)(2,1)S(1)}, bf16[24,2048]{1,0:T(8,128)(2,1)S(1)}, u32[]{:S(2)}, u32[]{:S(2)}) collective-permute-start(bf16[24,2048]{1,0:T(8,128)(2,1)S(1)} %get-tuple-element.59), channel_id=1, source_target_pairs={{0,6},{1,7},{2,4},{3,5},{4,2},{5,3},{6,0},{7,1},{8,14},{9,15},{10,... | collective-permute-start | bytes 294920 | tf_op jit(solution)/shard_map/ppermute | solution.py:20
  137.7 0.5 collective-permute-start.18
  138.2 1.0 convolution_add_fusion
  139.2 2.0 %collective-permute-done.19 = bf16[24,2048]{1,0:T(8,128)(2,1)S(1)} collective-permute-done((bf16[24,2048]{1,0:T(8,128)(2,1)S(1)}, bf16[24,2048]{1,0:T(8,128)(2,1)S(1)}, u32[]{:S(2)}, u32[]{:S(2)}) %collective-permute-start.19) | collective-permute-done | bytes 98336 | tf_op jit(solution)/shard_map/ppermute | solution.py:20
  141.2 1.1 collective-permute-done.18
  142.3 0.9 add_convert_fusion
  (120 shorter events, 1.9 us)
Async XLA Ops:
  0.6 20.0 %copy-start = (bf16[2048,16]{0,1:T(8,128)(2,1)S(1)}, bf16[2048,16]{0,1:T(8,128)(2,1)}, u32[]{:S(2)}) copy-start(bf16[2048,16]{0,1:T(8,128)(2,1)} %param.10) | copy-start | bytes 196612
  0.6 12.2 %collective-permute-start = (bf16[24,2048]{1,0:T(8,128)(2,1)}, bf16[24,2048]{1,0:T(8,128)(2,1)S(1)}, u32[]{:S(2)}, u32[]{:S(2)}) collective-permute-start(bf16[24,2048]{1,0:T(8,128)(2,1)} %param.7), channel_id=1, source_target_pairs={{0,4},{1,5},{2,6},{3,7},{4,0},{5,1},{6,2},{7,3},{8,12},{9,13},{10,... | collective-permute-start | bytes 294920 | tf_op jit(solution)/shard_map/ppermute | solution.py:20
  3.7 15.2 %collective-permute-start.1 = (bf16[24,2048]{1,0:T(8,128)(2,1)}, bf16[24,2048]{1,0:T(8,128)(2,1)S(1)}, u32[]{:S(2)}, u32[]{:S(2)}) collective-permute-start(bf16[24,2048]{1,0:T(8,128)(2,1)} %param.7), channel_id=1, source_target_pairs={{0,8},{1,9},{2,10},{3,11},{4,12},{5,13},{6,14},{7,15},{8,0},{9,1},... | collective-permute-start | bytes 294920 | tf_op jit(solution)/shard_map/ppermute | solution.py:20
  6.3 12.6 %collective-permute-start.2 = (bf16[24,2048]{1,0:T(8,128)(2,1)}, bf16[24,2048]{1,0:T(8,128)(2,1)S(1)}, u32[]{:S(2)}, u32[]{:S(2)}) collective-permute-start(bf16[24,2048]{1,0:T(8,128)(2,1)} %param.7), channel_id=1, source_target_pairs={{0,12},{1,13},{2,14},{3,15},{4,8},{5,9},{6,10},{7,11},{8,4},{9,5},... | collective-permute-start | bytes 294920 | tf_op jit(solution)/shard_map/ppermute | solution.py:20
  8.1 12.7 %collective-permute-start.6 = (bf16[24,2176]{1,0:T(8,128)(2,1)S(1)}, bf16[24,2176]{1,0:T(8,128)(2,1)S(1)}, u32[]{:S(2)}, u32[]{:S(2)}) collective-permute-start(bf16[24,2176]{1,0:T(8,128)(2,1)S(1)} %pad_maximum_fusion.1), channel_id=1, source_target_pairs={{0,12},{1,13},{2,14},{3,15},{4,8},{5,9},{6,10},{7,11},{8,4},{9,5},... | collective-permute-start | bytes 313352 | tf_op jit(solution)/shard_map/ppermute | solution.py:20
  11.9 12.5 %collective-permute-start.5 = (bf16[24,2176]{1,0:T(8,128)(2,1)S(1)}, bf16[24,2176]{1,0:T(8,128)(2,1)S(1)}, u32[]{:S(2)}, u32[]{:S(2)}) collective-permute-start(bf16[24,2176]{1,0:T(8,128)(2,1)S(1)} %pad_maximum_fusion.1), channel_id=1, source_target_pairs={{0,8},{1,9},{2,10},{3,11},{4,12},{5,13},{6,14},{7,15},{8,0},{9,1},... | collective-permute-start | bytes 313352 | tf_op jit(solution)/shard_map/ppermute | solution.py:20
  12.8 11.5 %collective-permute-start.4 = (bf16[24,2176]{1,0:T(8,128)(2,1)S(1)}, bf16[24,2176]{1,0:T(8,128)(2,1)S(1)}, u32[]{:S(2)}, u32[]{:S(2)}) collective-permute-start(bf16[24,2176]{1,0:T(8,128)(2,1)S(1)} %pad_maximum_fusion.1), channel_id=1, source_target_pairs={{0,4},{1,5},{2,6},{3,7},{4,0},{5,1},{6,2},{7,3},{8,12},{9,13},{10,... | collective-permute-start | bytes 313352 | tf_op jit(solution)/shard_map/ppermute | solution.py:20
  19.0 17.4 %copy-start.14 = (bf16[96,2048]{1,0:T(8,128)(2,1)}, bf16[96,2048]{1,0:T(8,128)(2,1)S(1)}, u32[]{:S(2)}) copy-start(bf16[96,2048]{1,0:T(8,128)(2,1)S(1)} %constant_dynamic-update-slice_fusion.refs_0_) | copy-start | bytes 1179652
  19.0 7.9 %collective-permute-start.8 = (bf16[96,2048]{1,0:T(8,128)(2,1)S(1)}, bf16[96,2048]{1,0:T(8,128)(2,1)S(1)}, u32[]{:S(2)}, u32[]{:S(2)}) collective-permute-start(bf16[96,2048]{1,0:T(8,128)(2,1)S(1)} %constant_dynamic-update-slice_fusion.refs_0_), channel_id=1, source_target_pairs={{0,2},{1,3},{2,0},{3,1},{4,6},{5,7},{6,4},{7,5},{8,10},{9,11},{10,... | collective-permute-start | bytes 1179656 | tf_op jit(solution)/shard_map/ppermute | solution.py:20
  20.6 7.1 %collective-permute-start.3 = (bf16[96,2048]{1,0:T(8,128)(2,1)S(1)}, bf16[96,2048]{1,0:T(8,128)(2,1)S(1)}, u32[]{:S(2)}, u32[]{:S(2)}) collective-permute-start(bf16[96,2048]{1,0:T(8,128)(2,1)S(1)} %constant_dynamic-update-slice_fusion.refs_0_), channel_id=1, source_target_pairs={{0,1},{1,0},{2,3},{3,2},{4,5},{5,4},{6,7},{7,6},{8,9},{9,8},{10,11... | collective-permute-start | bytes 1179656 | tf_op jit(solution)/shard_map/ppermute | solution.py:20
  25.3 11.8 %copy-start.16 = (bf16[96,2176]{1,0:T(8,128)(2,1)}, bf16[96,2176]{1,0:T(8,128)(2,1)S(1)}, u32[]{:S(2)}) copy-start(bf16[96,2176]{1,0:T(8,128)(2,1)S(1)} %pad_maximum_fusion.refs_2_) | copy-start | bytes 1253380
  25.3 10.5 %collective-permute-start.15 = (bf16[96,2176]{1,0:T(8,128)(2,1)S(1)}, bf16[96,2176]{1,0:T(8,128)(2,1)S(1)}, u32[]{:S(2)}, u32[]{:S(2)}) collective-permute-start(bf16[96,2176]{1,0:T(8,128)(2,1)S(1)} %pad_maximum_fusion.refs_2_), channel_id=1, source_target_pairs={{0,2},{1,3},{2,0},{3,1},{4,6},{5,7},{6,4},{7,5},{8,10},{9,11},{10,... | collective-permute-start | bytes 1253384 | tf_op jit(solution)/shard_map/ppermute | solution.py:20
  26.9 10.2 %collective-permute-start.7 = (bf16[96,2176]{1,0:T(8,128)(2,1)S(1)}, bf16[96,2176]{1,0:T(8,128)(2,1)S(1)}, u32[]{:S(2)}, u32[]{:S(2)}) collective-permute-start(bf16[96,2176]{1,0:T(8,128)(2,1)S(1)} %pad_maximum_fusion.refs_2_), channel_id=1, source_target_pairs={{0,1},{1,0},{2,3},{3,2},{4,5},{5,4},{6,7},{7,6},{8,9},{9,8},{10,11... | collective-permute-start | bytes 1253384 | tf_op jit(solution)/shard_map/ppermute | solution.py:20
  26.9 22.9 %copy-start.19 = (bf16[96,2048]{1,0:T(8,128)(2,1)}, bf16[96,2048]{1,0:T(8,128)(2,1)S(1)}, u32[]{:S(2)}) copy-start(bf16[96,2048]{1,0:T(8,128)(2,1)S(1)} %collective-permute-done.8.refs_0_) | copy-start | bytes 1179652
  26.9 2.3 %collective-permute-start.9 = (bf16[96,2048]{1,0:T(8,128)(2,1)S(1)}, bf16[96,2048]{1,0:T(8,128)(2,1)S(1)}, u32[]{:S(2)}, u32[]{:S(2)}) collective-permute-start(bf16[96,2048]{1,0:T(8,128)(2,1)S(1)} %collective-permute-done.8.refs_0_), channel_id=1, source_target_pairs={{0,1},{1,0},{2,3},{3,2},{4,5},{5,4},{6,7},{7,6},{8,9},{9,8},{10,11... | collective-permute-start | bytes 1179656 | tf_op jit(solution)/shard_map/ppermute | solution.py:20
  27.6 9.5 %copy-start.20 = (bf16[96,2048]{1,0:T(8,128)(2,1)}, bf16[96,2048]{1,0:T(8,128)(2,1)S(1)}, u32[]{:S(2)}) copy-start(bf16[96,2048]{1,0:T(8,128)(2,1)S(1)} %collective-permute-done.3.refs_1_) | copy-start | bytes 1179652
  30.3 5.5 %collective-permute-start.10 = (f32[16,384]{1,0:T(8,128)S(1)}, f32[16,384]{1,0:T(8,128)S(1)}, u32[]{:S(2)}, u32[]{:S(2)}) collective-permute-start(f32[16,384]{1,0:T(8,128)S(1)} %pad_maximum_fusion.4), channel_id=1, source_target_pairs={{0,16},{16,0},{1,17},{17,1},{2,18},{18,2},{3,19},{19,3},{4,20},{20... | collective-permute-start | bytes 73736 | tf_op jit(solution)/shard_map/ppermute | solution.py:25
  35.8 14.0 %copy-start.23 = (bf16[96,2176]{1,0:T(8,128)(2,1)}, bf16[96,2176]{1,0:T(8,128)(2,1)S(1)}, u32[]{:S(2)}) copy-start(bf16[96,2176]{1,0:T(8,128)(2,1)S(1)} %collective-permute-done.15.refs_2_) | copy-start | bytes 1253380
  35.8 14.8 %collective-permute-start.16 = (bf16[96,2176]{1,0:T(8,128)(2,1)S(1)}, bf16[96,2176]{1,0:T(8,128)(2,1)}, u32[]{:S(2)}, u32[]{:S(2)}) collective-permute-start(bf16[96,2176]{1,0:T(8,128)(2,1)S(1)} %collective-permute-done.15.refs_2_), channel_id=1, source_target_pairs={{0,1},{1,0},{2,3},{3,2},{4,5},{5,4},{6,7},{7,6},{8,9},{9,8},{10,11... | collective-permute-start | bytes 1253384 | tf_op jit(solution)/shard_map/ppermute | solution.py:20
  50.6 15.6 %copy-start.15 = (bf16[96,2048]{1,0:T(8,128)(2,1)S(1)}, bf16[96,2048]{1,0:T(8,128)(2,1)}, u32[]{:S(2)}) copy-start(bf16[96,2048]{1,0:T(8,128)(2,1)} %copy-done.14) | copy-start | bytes 1179652
  50.7 17.1 %copy-start.17 = (bf16[96,2176]{1,0:T(8,128)(2,1)S(1)}, bf16[96,2176]{1,0:T(8,128)(2,1)}, u32[]{:S(2)}) copy-start(bf16[96,2176]{1,0:T(8,128)(2,1)} %copy-done.16) | copy-start | bytes 1253380
  50.7 46.8 %copy-start.1 = (bf16[192,2048]{1,0:T(8,128)(2,1)S(1)}, bf16[192,2048]{1,0:T(8,128)(2,1)}, u32[]{:S(2)}) copy-start(bf16[192,2048]{1,0:T(8,128)(2,1)} %get-tuple-element.35.refs_0_) | copy-start | bytes 2359300
  62.8 35.0 %copy-start.2 = (bf16[192,2048]{1,0:T(8,128)(2,1)S(1)}, bf16[192,2048]{1,0:T(8,128)(2,1)}, u32[]{:S(2)}) copy-start(bf16[192,2048]{1,0:T(8,128)(2,1)} %get-tuple-element.36.refs_1_) | copy-start | bytes 2359300
  62.8 41.8 %copy-start.18 = (bf16[96,2048]{1,0:T(8,128)(2,1)S(1)}, bf16[96,2048]{1,0:T(8,128)(2,1)}, u32[]{:S(2)}) copy-start(bf16[96,2048]{1,0:T(8,128)(2,1)} %get-tuple-element.29) | copy-start | bytes 1179652
  63.7 9.5 %collective-permute-start.24 = (bf16[2,2,4,24]{3,2,1,0:T(4,128)(2,1)S(1)}, bf16[2,2,4,24]{3,2,1,0:T(4,128)(2,1)S(1)}, u32[]{:S(2)}, u32[]{:S(2)}) collective-permute-start(bf16[2,2,4,24]{3,2,1,0:T(4,128)(2,1)S(1)} %constant_dynamic-update-slice_fusion.4), channel_id=1, source_target_pairs={{0,12},{1,13},{2,14},{3,15},{4,8},{5,9},{6,10},{7,11},{8,4},{9,5},... | collective-permute-start | bytes 2312 | tf_op jit(solution)/shard_map/ppermute | solution.py:20
  66.2 17.6 %collective-permute-start.28 = (bf16[96,2048]{1,0:T(8,128)(2,1)S(1)}, bf16[96,2048]{1,0:T(8,128)(2,1)}, u32[]{:S(2)}, u32[]{:S(2)}) collective-permute-start(bf16[96,2048]{1,0:T(8,128)(2,1)S(1)} %copy-done.15), channel_id=1, source_target_pairs={{0,16},{16,0},{1,17},{17,1},{2,18},{18,2},{3,19},{19,3},{4,20},{20... | collective-permute-start | bytes 1179656 | tf_op jit(solution)/shard_map/ppermute | solution.py:25
  67.7 19.5 %collective-permute-start.32 = (bf16[96,2176]{1,0:T(8,128)(2,1)S(1)}, bf16[96,2176]{1,0:T(8,128)(2,1)}, u32[]{:S(2)}, u32[]{:S(2)}) collective-permute-start(bf16[96,2176]{1,0:T(8,128)(2,1)S(1)} %copy-done.17), channel_id=1, source_target_pairs={{0,16},{16,0},{1,17},{17,1},{2,18},{18,2},{3,19},{19,3},{4,20},{20... | collective-permute-start | bytes 1253384 | tf_op jit(solution)/shard_map/ppermute | solution.py:25
  68.3 27.4 %collective-permute-start.30 = (bf16[96,2048]{1,0:T(8,128)(2,1)}, bf16[96,2048]{1,0:T(8,128)(2,1)}, u32[]{:S(2)}, u32[]{:S(2)}) collective-permute-start(bf16[96,2048]{1,0:T(8,128)(2,1)} %copy-done.19), channel_id=1, source_target_pairs={{0,16},{16,0},{1,17},{17,1},{2,18},{18,2},{3,19},{19,3},{4,20},{20... | collective-permute-start | bytes 1179656 | tf_op jit(solution)/shard_map/ppermute | solution.py:25
  69.9 4.9 %collective-permute-start.22 = (bf16[2,2,4,24]{3,2,1,0:T(4,128)(2,1)S(1)}, bf16[2,2,4,24]{3,2,1,0:T(4,128)(2,1)S(1)}, u32[]{:S(2)}, u32[]{:S(2)}) collective-permute-start(bf16[2,2,4,24]{3,2,1,0:T(4,128)(2,1)S(1)} %constant_dynamic-update-slice_fusion.4), channel_id=1, source_target_pairs={{0,4},{1,5},{2,6},{3,7},{4,0},{5,1},{6,2},{7,3},{8,12},{9,13},{10,... | collective-permute-start | bytes 2312 | tf_op jit(solution)/shard_map/ppermute | solution.py:20
  73.2 4.6 %collective-permute-start.23 = (bf16[2,2,4,24]{3,2,1,0:T(4,128)(2,1)S(1)}, bf16[2,2,4,24]{3,2,1,0:T(4,128)(2,1)S(1)}, u32[]{:S(2)}, u32[]{:S(2)}) collective-permute-start(bf16[2,2,4,24]{3,2,1,0:T(4,128)(2,1)S(1)} %constant_dynamic-update-slice_fusion.4), channel_id=1, source_target_pairs={{0,8},{1,9},{2,10},{3,11},{4,12},{5,13},{6,14},{7,15},{8,0},{9,1},... | collective-permute-start | bytes 2312 | tf_op jit(solution)/shard_map/ppermute | solution.py:20
  77.9 3.8 %collective-permute-start.25 = (bf16[4,2,2,4,24]{4,3,2,1,0:T(4,128)(2,1)S(1)}, bf16[4,2,2,4,24]{4,3,2,1,0:T(4,128)(2,1)S(1)}, u32[]{:S(2)}, u32[]{:S(2)}) collective-permute-start(bf16[4,2,2,4,24]{4,3,2,1,0:T(4,128)(2,1)S(1)} %pad_maximum_fusion.6), channel_id=1, source_target_pairs={{0,2},{1,3},{2,0},{3,1},{4,6},{5,7},{6,4},{7,5},{8,10},{9,11},{10,... | collective-permute-start | bytes 9224 | tf_op jit(solution)/shard_map/ppermute | solution.py:20
  81.7 1.3 collective-permute-start.26
  83.2 13.2 %collective-permute-start.27 = (bf16[16,384]{1,0:T(8,128)(2,1)S(1)}, bf16[16,384]{1,0:T(8,128)(2,1)S(1)}, u32[]{:S(2)}, u32[]{:S(2)}) collective-permute-start(bf16[16,384]{1,0:T(8,128)(2,1)S(1)} %reshape.19), channel_id=1, source_target_pairs={{0,16},{16,0},{1,17},{17,1},{2,18},{18,2},{3,19},{19,3},{4,20},{20... | collective-permute-start | bytes 36872 | tf_op jit(solution)/shard_map/ppermute | solution.py:25
  83.8 20.3 %copy-start.28 = (bf16[96,2048]{1,0:T(8,128)(2,1)S(1)}, bf16[96,2048]{1,0:T(8,128)(2,1)}, u32[]{:S(2)}) copy-start(bf16[96,2048]{1,0:T(8,128)(2,1)} %get-tuple-element.32) | copy-start | bytes 1179652
  83.8 23.4 %collective-permute-start.29 = (bf16[96,2048]{1,0:T(8,128)(2,1)}, bf16[96,2048]{1,0:T(8,128)(2,1)S(1)}, u32[]{:S(2)}, u32[]{:S(2)}) collective-permute-start(bf16[96,2048]{1,0:T(8,128)(2,1)} %collective-permute-done.28.refs_0_), channel_id=1, source_target_pairs={{0,1},{1,0},{2,3},{3,2},{4,5},{5,4},{6,7},{7,6},{8,9},{9,8},{10,11... | collective-permute-start | bytes 1179656 | tf_op jit(solution)/shard_map/ppermute | solution.py:20
  83.8 20.3 %collective-permute-start.34 = (bf16[96,2176]{1,0:T(8,128)(2,1)}, bf16[96,2176]{1,0:T(8,128)(2,1)S(1)}, u32[]{:S(2)}, u32[]{:S(2)}) collective-permute-start(bf16[96,2176]{1,0:T(8,128)(2,1)} %copy-done.23), channel_id=1, source_target_pairs={{0,16},{16,0},{1,17},{17,1},{2,18},{18,2},{3,19},{19,3},{4,20},{20... | collective-permute-start | bytes 1253384 | tf_op jit(solution)/shard_map/ppermute | solution.py:25
  87.2 23.0 %collective-permute-start.33 = (bf16[96,2176]{1,0:T(8,128)(2,1)}, bf16[96,2176]{1,0:T(8,128)(2,1)S(1)}, u32[]{:S(2)}, u32[]{:S(2)}) collective-permute-start(bf16[96,2176]{1,0:T(8,128)(2,1)} %collective-permute-done.32.refs_4_), channel_id=1, source_target_pairs={{0,1},{1,0},{2,3},{3,2},{4,5},{5,4},{6,7},{7,6},{8,9},{9,8},{10,11... | collective-permute-start | bytes 1253384 | tf_op jit(solution)/shard_map/ppermute | solution.py:20
  95.7 14.7 %collective-permute-start.31 = (bf16[96,2048]{1,0:T(8,128)(2,1)}, bf16[96,2048]{1,0:T(8,128)(2,1)S(1)}, u32[]{:S(2)}, u32[]{:S(2)}) collective-permute-start(bf16[96,2048]{1,0:T(8,128)(2,1)} %collective-permute-done.30.refs_2_), channel_id=1, source_target_pairs={{0,1},{1,0},{2,3},{3,2},{4,5},{5,4},{6,7},{7,6},{8,9},{9,8},{10,11... | collective-permute-start | bytes 1179656 | tf_op jit(solution)/shard_map/ppermute | solution.py:20
  96.4 10.8 %copy-start.22 = (bf16[96,2048]{1,0:T(8,128)(2,1)S(1)}, bf16[96,2048]{1,0:T(8,128)(2,1)}, u32[]{:S(2)}) copy-start(bf16[96,2048]{1,0:T(8,128)(2,1)} %get-tuple-element.31) | copy-start | bytes 1179652
  96.4 7.7 %collective-permute-start.11 = (bf16[96,2048]{1,0:T(8,128)(2,1)}, bf16[96,2048]{1,0:T(8,128)(2,1)S(1)}, u32[]{:S(2)}, u32[]{:S(2)}) collective-permute-start(bf16[96,2048]{1,0:T(8,128)(2,1)} %get-tuple-element.30), channel_id=1, source_target_pairs={{0,1},{1,0},{2,3},{3,2},{4,5},{5,4},{6,7},{7,6},{8,9},{9,8},{10,11... | collective-permute-start | bytes 1179656 | tf_op jit(solution)/shard_map/ppermute | solution.py:20
  104.1 10.7 %copy-start.24 = (bf16[96,2176]{1,0:T(8,128)(2,1)}, bf16[96,2176]{1,0:T(8,128)(2,1)S(1)}, u32[]{:S(2)}) copy-start(bf16[96,2176]{1,0:T(8,128)(2,1)S(1)} %collective-permute-done.34.refs_6_) | copy-start | bytes 1253380
  104.1 1.7 %collective-permute-start.17 = (bf16[96,2048]{1,0:T(8,128)(2,1)S(1)}, bf16[96,2048]{1,0:T(8,128)(2,1)S(1)}, u32[]{:S(2)}, u32[]{:S(2)}) collective-permute-start(bf16[96,2048]{1,0:T(8,128)(2,1)S(1)} %copy-done.28), channel_id=1, source_target_pairs={{0,1},{1,0},{2,3},{3,2},{4,5},{5,4},{6,7},{7,6},{8,9},{9,8},{10,11... | collective-permute-start | bytes 1179656 | tf_op jit(solution)/shard_map/ppermute | solution.py:20
  104.1 8.6 %collective-permute-start.35 = (bf16[96,2176]{1,0:T(8,128)(2,1)S(1)}, bf16[96,2176]{1,0:T(8,128)(2,1)S(1)}, u32[]{:S(2)}, u32[]{:S(2)}) collective-permute-start(bf16[96,2176]{1,0:T(8,128)(2,1)S(1)} %collective-permute-done.34.refs_6_), channel_id=1, source_target_pairs={{0,1},{1,0},{2,3},{3,2},{4,5},{5,4},{6,7},{7,6},{8,9},{9,8},{10,11... | collective-permute-start | bytes 1253384 | tf_op jit(solution)/shard_map/ppermute | solution.py:20
  105.8 29.8 %collective-permute-start.14 = (bf16[24,2048]{1,0:T(8,128)(2,1)S(1)}, bf16[24,2048]{1,0:T(8,128)(2,1)S(1)}, u32[]{:S(2)}, u32[]{:S(2)}) collective-permute-start(bf16[24,2048]{1,0:T(8,128)(2,1)S(1)} %get-tuple-element.54), channel_id=1, source_target_pairs={{0,12},{1,13},{2,14},{3,15},{4,8},{5,9},{6,10},{7,11},{8,4},{9,5},... | collective-permute-start | bytes 294920 | tf_op jit(solution)/shard_map/ppermute | solution.py:20
  107.3 7.5 %copy-start.29 = (bf16[96,2048]{1,0:T(8,128)(2,1)}, bf16[96,2048]{1,0:T(8,128)(2,1)S(1)}, u32[]{:S(2)}) copy-start(bf16[96,2048]{1,0:T(8,128)(2,1)S(1)} %collective-permute-done.29.refs_1_) | copy-start | bytes 1179652
  107.3 30.4 %collective-permute-start.13 = (bf16[24,2048]{1,0:T(8,128)(2,1)S(1)}, bf16[24,2048]{1,0:T(8,128)(2,1)S(1)}, u32[]{:S(2)}, u32[]{:S(2)}) collective-permute-start(bf16[24,2048]{1,0:T(8,128)(2,1)S(1)} %get-tuple-element.55), channel_id=1, source_target_pairs={{0,8},{1,9},{2,10},{3,11},{4,12},{5,13},{6,14},{7,15},{8,0},{9,1},... | collective-permute-start | bytes 294920 | tf_op jit(solution)/shard_map/ppermute | solution.py:20
  110.2 4.5 %copy-start.25 = (bf16[96,2176]{1,0:T(8,128)(2,1)}, bf16[96,2176]{1,0:T(8,128)(2,1)S(1)}, u32[]{:S(2)}) copy-start(bf16[96,2176]{1,0:T(8,128)(2,1)S(1)} %collective-permute-done.33.refs_5_) | copy-start | bytes 1253380
  110.2 28.9 %collective-permute-start.12 = (bf16[24,2048]{1,0:T(8,128)(2,1)S(1)}, bf16[24,2048]{1,0:T(8,128)(2,1)S(1)}, u32[]{:S(2)}, u32[]{:S(2)}) collective-permute-start(bf16[24,2048]{1,0:T(8,128)(2,1)S(1)} %get-tuple-element.53), channel_id=1, source_target_pairs={{0,4},{1,5},{2,6},{3,7},{4,0},{5,1},{6,2},{7,3},{8,12},{9,13},{10,... | collective-permute-start | bytes 294920 | tf_op jit(solution)/shard_map/ppermute | solution.py:20
  110.4 2.4 %copy-start.30 = (bf16[96,2048]{1,0:T(8,128)(2,1)}, bf16[96,2048]{1,0:T(8,128)(2,1)S(1)}, u32[]{:S(2)}) copy-start(bf16[96,2048]{1,0:T(8,128)(2,1)S(1)} %collective-permute-done.31.refs_3_) | copy-start | bytes 1179652
  110.4 28.7 %collective-permute-start.21 = (bf16[24,2048]{1,0:T(8,128)(2,1)S(1)}, bf16[24,2048]{1,0:T(8,128)(2,1)S(1)}, u32[]{:S(2)}, u32[]{:S(2)}) collective-permute-start(bf16[24,2048]{1,0:T(8,128)(2,1)S(1)} %get-tuple-element.57), channel_id=1, source_target_pairs={{0,14},{1,15},{2,12},{3,13},{4,10},{5,11},{6,8},{7,9},{8,6},{9,7},... | collective-permute-start | bytes 294920 | tf_op jit(solution)/shard_map/ppermute | solution.py:20
  112.8 2.0 %copy-start.26 = (bf16[96,2176]{1,0:T(8,128)(2,1)}, bf16[96,2176]{1,0:T(8,128)(2,1)S(1)}, u32[]{:S(2)}) copy-start(bf16[96,2176]{1,0:T(8,128)(2,1)S(1)} %collective-permute-done.35.refs_7_) | copy-start | bytes 1253380
  112.8 11.4 %copy-start.3 = (bf16[192,2048]{1,0:T(8,128)(2,1)S(1)}, bf16[192,2048]{1,0:T(8,128)(2,1)}, u32[]{:S(2)}) copy-start(bf16[192,2048]{1,0:T(8,128)(2,1)} %get-tuple-element.38.refs_3_) | copy-start | bytes 2359300
  112.8 11.4 %copy-start.4 = (bf16[192,768]{1,0:T(8,128)(2,1)S(1)}, bf16[192,768]{1,0:T(8,128)(2,1)}, u32[]{:S(2)}) copy-start(bf16[192,768]{1,0:T(8,128)(2,1)} %get-tuple-element.41.refs_6_) | copy-start | bytes 884740
  112.8 11.4 %copy-start.5 = (bf16[192,768]{1,0:T(8,128)(2,1)S(1)}, bf16[192,768]{1,0:T(8,128)(2,1)}, u32[]{:S(2)}) copy-start(bf16[192,768]{1,0:T(8,128)(2,1)} %get-tuple-element.44.refs_9_) | copy-start | bytes 884740
  112.8 11.4 %copy-start.6 = (bf16[192,768]{1,0:T(8,128)(2,1)S(1)}, bf16[192,768]{1,0:T(8,128)(2,1)}, u32[]{:S(2)}) copy-start(bf16[192,768]{1,0:T(8,128)(2,1)} %get-tuple-element.47.refs_12_) | copy-start | bytes 884740
  112.8 11.4 %copy-start.7 = (bf16[192,768]{1,0:T(8,128)(2,1)S(1)}, bf16[192,768]{1,0:T(8,128)(2,1)}, u32[]{:S(2)}) copy-start(bf16[192,768]{1,0:T(8,128)(2,1)} %get-tuple-element.42.refs_7_) | copy-start | bytes 884740
  112.8 11.4 %copy-start.8 = (bf16[192,768]{1,0:T(8,128)(2,1)S(1)}, bf16[192,768]{1,0:T(8,128)(2,1)}, u32[]{:S(2)}) copy-start(bf16[192,768]{1,0:T(8,128)(2,1)} %get-tuple-element.45.refs_10_) | copy-start | bytes 884740
  112.8 11.4 %copy-start.9 = (bf16[192,768]{1,0:T(8,128)(2,1)S(1)}, bf16[192,768]{1,0:T(8,128)(2,1)}, u32[]{:S(2)}) copy-start(bf16[192,768]{1,0:T(8,128)(2,1)} %get-tuple-element.48.refs_13_) | copy-start | bytes 884740
  112.8 26.3 %collective-permute-start.20 = (bf16[24,2048]{1,0:T(8,128)(2,1)S(1)}, bf16[24,2048]{1,0:T(8,128)(2,1)S(1)}, u32[]{:S(2)}, u32[]{:S(2)}) collective-permute-start(bf16[24,2048]{1,0:T(8,128)(2,1)S(1)} %get-tuple-element.58), channel_id=1, source_target_pairs={{0,10},{1,11},{2,8},{3,9},{4,14},{5,15},{6,12},{7,13},{8,2},{9,3},... | collective-permute-start | bytes 294920 | tf_op jit(solution)/shard_map/ppermute | solution.py:20
  124.2 1.1 copy-start.10
  125.3 1.1 copy-start.11
  127.4 10.8 %copy-start.13 = (bf16[384,2048]{1,0:T(8,128)(2,1)S(1)}, bf16[384,2048]{1,0:T(8,128)(2,1)}, u32[]{:S(2)}) copy-start(bf16[384,2048]{1,0:T(8,128)(2,1)} %get-tuple-element.37.refs_2_) | copy-start | bytes 4718596
  135.6 5.5 %collective-permute-start.19 = (bf16[24,2048]{1,0:T(8,128)(2,1)S(1)}, bf16[24,2048]{1,0:T(8,128)(2,1)S(1)}, u32[]{:S(2)}, u32[]{:S(2)}) collective-permute-start(bf16[24,2048]{1,0:T(8,128)(2,1)S(1)} %get-tuple-element.59), channel_id=1, source_target_pairs={{0,6},{1,7},{2,4},{3,5},{4,2},{5,3},{6,0},{7,1},{8,14},{9,15},{10,... | collective-permute-start | bytes 294920 | tf_op jit(solution)/shard_map/ppermute | solution.py:20
  137.7 4.6 %collective-permute-start.18 = (bf16[24,2048]{1,0:T(8,128)(2,1)S(1)}, bf16[24,2048]{1,0:T(8,128)(2,1)S(1)}, u32[]{:S(2)}, u32[]{:S(2)}) collective-permute-start(bf16[24,2048]{1,0:T(8,128)(2,1)S(1)} %get-tuple-element.56), channel_id=1, source_target_pairs={{0,2},{1,3},{2,0},{3,1},{4,6},{5,7},{6,4},{7,5},{8,10},{9,11},{10,... | collective-permute-start | bytes 294920 | tf_op jit(solution)/shard_map/ppermute | solution.py:20
  (3 other events, 2.6 us)

commit v3 on v1

v3 whole, which is shorter than its diff:
```python
import functools

import jax
import jax.numpy as jnp
from jax import lax
from jax.experimental import pallas as pl
from jax.experimental.pallas import tpu as pltpu
from jax.sharding import PartitionSpec as P

PASSES = 3
LANES = 128
SUBLANES = 8
FF_TILE = 256
GRANT = 56 << 20
ROWS_AT_ONCE = 1024


def swap_expert(array, offset):
    size = lax.axis_size("expert")
    return lax.ppermute(array, "expert", [(i, i ^ offset) for i in range(size)])


def swap_group(array, offset):
    size = lax.axis_size("dp")
    return lax.ppermute(array, "dp", [(i, i ^ offset) for i in range(size)])


def contract(left, right, left_dim, right_dim):
    return lax.dot_general(
        left, right, (((left_dim,), (right_dim,)), ((), ())), preferred_element_type=jnp.float32
    )


def balancer_forward_pass(logits):
    densities = [jnp.exp(logits)]
    quotients, column_totals, row_totals = ([], [], [])
    for _ in range(PASSES):
        column_sum = jnp.sum(densities[-1], axis=1, keepdims=True)
        quotient = densities[-1] / column_sum
        row_sum = jnp.sum(quotient, axis=0, keepdims=True)
        densities.append(quotient / row_sum)
        quotients.append(quotient)
        column_totals.append(column_sum)
        row_totals.append(row_sum)
    return (densities, quotients, column_totals, row_totals)


def balancer_adjoint_pass(density_gradient, densities, quotients, column_totals, row_totals):
    for repeat in reversed(range(PASSES)):
        inner = jnp.sum(density_gradient * densities[repeat + 1], axis=0, keepdims=True)
        quotient_grad = (density_gradient - inner) / row_totals[repeat]
        shared = jnp.sum(quotient_grad * quotients[repeat], axis=1, keepdims=True)
        density_gradient = (quotient_grad - shared) / column_totals[repeat]
    return density_gradient * densities[0]


def gate_kernel(me_ref, logits_ref, gate_ref):
    logits = logits_ref[...]
    experts, count = logits.shape
    gates = experts * balancer_forward_pass(logits)[0][-1]
    row = lax.broadcasted_iota(jnp.int32, gates.shape, 0)
    mine = jnp.sum(jnp.where(row == me_ref[0], gates, 0.0), axis=0, keepdims=True)
    gate_ref[...] = jnp.transpose(jnp.broadcast_to(mine, (LANES, count)))


def kernel_call(
    kernel, scalars, small, large, out_shape, scratch, copies, large_outs=0, after=(), macs=10**6
):
    whole = pl.BlockSpec(memory_space=pltpu.VMEM)
    outside = pl.BlockSpec(memory_space=pltpu.HBM)
    inputs = len(scalars) + len(small) + len(large)

    def body(*refs):
        kernel(*refs[:inputs], *refs[inputs + len(after) :])

    return pl.pallas_call(
        body,
        in_specs=[pl.BlockSpec(memory_space=pltpu.SMEM)] * len(scalars)
        + [whole] * len(small)
        + [outside] * (len(large) + len(after)),
        out_specs=[outside] * large_outs + [whole] * (len(out_shape) - large_outs),
        out_shape=out_shape,
        scratch_shapes=[*scratch] + [pltpu.SemaphoreType.DMA((copies,))] * (copies > 0),
        compiler_params=pltpu.CompilerParams(vmem_limit_bytes=GRANT),
        cost_estimate=pl.CostEstimate(
            flops=2 * macs, bytes_accessed=macs // 200, transcendentals=macs // 10000
        ),
    )(*scalars, *small, *large, *after)


def shape(rows, columns, dtype=jnp.bfloat16):
    return jax.ShapeDtypeStruct((rows, columns), dtype)


def tiles(extent, tile):
    tile = tile if extent % tile == 0 else extent
    return [slice(at, at + tile) for at in range(0, extent, tile)]


class Copies:
    def __init__(self, sems):
        self.sems, self.count = (sems, 0)

    def start(self, source, target):
        copy = pltpu.make_async_copy(source, target, self.sems.at[self.count])
        self.count += 1
        copy.start()
        return copy

    def stack(self, parts, target, columns=slice(None)):
        started, at = ([], 0)
        for part in parts:
            rows = part.shape[0]
            started.append(self.start(part.at[:, columns], target.at[pl.ds(at, rows), :]))
            at += rows
        return started


def wait(copies):
    for copy in copies:
        copy.wait()


def column_of(me_ref, picked):
    picked = picked.astype(jnp.float32)
    lane = lax.broadcasted_iota(jnp.int32, picked.shape, 1)
    return jnp.sum(jnp.where(lane == me_ref[0], picked, 0.0), axis=1, keepdims=True)


def hidden_tile(rows_in, rows_grad, wg, wu, wd):
    gate_pre = contract(rows_in, wg, 1, 0)
    up_pre = contract(rows_in, wu, 1, 0)
    hidden_grad = contract(rows_grad, wd, 1, 1)
    sigmoid_gate = jax.nn.sigmoid(gate_pre)
    activation = gate_pre * sigmoid_gate
    hidden = activation * up_pre
    gate_grad = hidden_grad * up_pre * sigmoid_gate * (1.0 + gate_pre * (1.0 - sigmoid_gate))
    up_grad = hidden_grad * activation
    half = jnp.bfloat16
    return hidden, gate_grad.astype(half), up_grad.astype(half), hidden_grad * hidden


def start_weights(copies, sources, targets):
    (wg, wu, wd), (wg_to, wu_to, wd_to) = (sources, targets)
    started = []
    for cut in tiles(wg.shape[2], FF_TILE):
        here = pl.ds(cut.start, cut.stop - cut.start)
        started.append(
            [
                copies.start(wg.at[0, :, here], wg_to.at[:, here]),
                copies.start(wu.at[0, :, here], wu_to.at[:, here]),
                copies.start(wd.at[0, here, :], wd_to.at[here, :]),
            ]
        )
    return started


def logits_kernel(parts, *refs):
    router, *tok, out, rows, sems = refs
    copies = Copies(sems)
    wait(copies.stack(tok, rows))
    out[...] = contract(router[...], rows[...], 1, 1)


def expert_kernel(parts, me_ref, gate_ref, *refs):
    tok, grad, sources = (refs[:parts], refs[parts : 2 * parts], refs[2 * parts : 2 * parts + 3])
    refs = refs[2 * parts + 3 :]
    sum_outs, scaled_outs, score_ref, refs = (refs[:parts], refs[parts : parts + 3], refs[parts + 3], refs[parts + 4 :])
    rows_in, rows_grad, wg, wu, wd, gate_grad, up_grad, hs, gs, us, sums, sems = refs
    copies = Copies(sems)
    width = rows_in.shape[1]
    tok_here = copies.stack(tok, rows_in)
    weights_here = start_weights(copies, sources, (wg, wu, wd))
    grad_here = copies.stack(grad, rows_grad)
    wait(tok_here)
    wait(grad_here)
    mask = column_of(me_ref, rows_grad[:, width:])
    gate = mask * gate_ref[: rows_in.shape[0], :1]
    sent = gate.astype(jnp.bfloat16).astype(jnp.float32)
    score = jnp.zeros(score_ref.shape, jnp.float32)
    results = []
    for cut, here in zip(tiles(wg.shape[1], FF_TILE), weights_here):
        wait(here)
        hidden, gate_part, up_part, product = hidden_tile(
            rows_in[...], rows_grad[:, :width], wg[:, cut], wu[:, cut], wd[cut, :]
        )
        gate_grad[:, cut] = gate_part
        up_grad[:, cut] = up_part
        here = pl.ds(cut.start, cut.stop - cut.start)
        for value, target, out in zip((hidden, gate_part, up_part), (hs, gs, us), scaled_outs):
            target[:, cut] = (sent * value).astype(jnp.bfloat16)
            results.append(copies.start(target.at[:, here], out.at[:, here]))
        product = product * mask
        high = product.astype(jnp.bfloat16)
        low = (product - high).astype(jnp.bfloat16)
        ones = jnp.ones((SUBLANES, product.shape[1]), jnp.bfloat16)
        score += contract(ones, high, 1, 1) + contract(ones, low, 1, 1)
    score_ref[...] = score
    for cut in tiles(width, 2 * FF_TILE):
        part = contract(gate_grad[...], wg[cut, :], 1, 1)
        part += contract(up_grad[...], wu[cut, :], 1, 1)
        sums[:, cut] = (gate * part).astype(jnp.bfloat16)
        at = 0
        here = pl.ds(cut.start, cut.stop - cut.start)
        for out in sum_outs:
            source = sums.at[pl.ds(at, out.shape[0]), here]
            results.append(copies.start(source, out.at[:, here]))
            at += out.shape[0]
    wait(results)


def expert_call(me, gate, tok, grad, weights, after):
    rows = sum(part.shape[0] for part in tok)
    width, ff_width = weights[0].shape[1:]
    half = jnp.bfloat16
    wide, narrow = (pltpu.VMEM((rows, width), half), pltpu.VMEM((rows, ff_width), half))
    return kernel_call(
        functools.partial(expert_kernel, len(tok)), (me,), (gate,), (*tok, *grad, *weights),
        [shape(part.shape[0], width) for part in tok]
        + [shape(rows, ff_width)] * 3 + [shape(SUBLANES, rows, jnp.float32)],
        [wide, pltpu.VMEM((rows, grad[0].shape[1]), half)]
        + [pltpu.VMEM((width, ff_width), half)] * 2 + [pltpu.VMEM((ff_width, width), half)]
        + [narrow] * 5 + [wide],
        2 * len(tok) + 6 * len(tiles(ff_width, FF_TILE))
        + len(tok) * len(tiles(width, 2 * FF_TILE)),
        len(tok) + 3, after, 5 * rows * width * ff_width,
    )


def add_kernel(left, right, out, left_here, right_here, total, sems):
    copies = Copies(sems)
    wait([copies.start(left, left_here), copies.start(right, right_here)])
    total[...] = (
        left_here[...].astype(jnp.float32) + right_here[...].astype(jnp.float32)
    ).astype(total.dtype)
    wait([copies.start(total, out)])


def weights_kernel(parts, fresh, given, start, steps, me_ref, group_ref, *refs):
    gate_ref, refs = (refs[0], refs[1:])
    tok, grad, sources = (refs[:parts], refs[parts : 2 * parts], refs[2 * parts : 2 * parts + 3])
    refs = refs[2 * parts + 3 :]
    given_refs, outs, refs = (refs[: 3 * given], refs[3 * given :][:3], refs[3 * given + 3 :])
    hs, gs, us, tok_half, grad_all, hidden_half, *refs = refs
    tile_out, rows_in, picked, wg, wu, wd, sems = (refs[:3], *refs[3:])
    copies = Copies(sems)
    width = tok[0].shape[1]
    half = outs[0].shape[1]
    half_ff = outs[2].shape[1]
    plain = pl.ds(0, width)
    known = sum(ref.shape[0] for ref in given_refs[:given])
    fresh_here = weights_here = []
    if fresh:
        fresh_here = copies.stack(tok[parts - fresh :], rows_in)
        fresh_here += copies.stack(grad[parts - fresh :], picked, pl.ds(width, LANES))
    first = sum(ref.shape[0] for ref in grad[: parts - fresh])
    new_here = []
    if fresh:
        fresh_rows = pl.ds(first, grad_all.shape[0] - first)
        new_here = copies.stack(grad[parts - fresh :], grad_all.at[fresh_rows, :], plain)
        weights_here = start_weights(copies, sources, (wg, wu, wd))
    grad_here = copies.stack(grad[: parts - fresh], grad_all, plain)
    mine = pl.ds(pl.multiple_of(group_ref[0] * half, LANES), half)
    rest_here = copies.stack(tok, tok_half, mine)
    for kind, target in enumerate((hs, gs, us)):
        if given:
            rest_here += copies.stack(
                given_refs[kind * given : (kind + 1) * given], target
            )
    wait(fresh_here)
    wait(new_here)
    if fresh:
        count = rows_in.shape[0]
        gate = column_of(me_ref, picked[...]) * gate_ref[start : start + count, :1]
        sent = gate.astype(jnp.bfloat16).astype(jnp.float32)
        new = slice(known, known + count)
        for cut, here in zip(tiles(wg.shape[1], FF_TILE), weights_here):
            wait(here)
            hidden, gate_grad, up_grad, _ = hidden_tile(
                rows_in[...], grad_all[new, :], wg[:, cut], wu[:, cut], wd[cut, :]
            )
            hs[new, cut] = (sent * hidden).astype(jnp.bfloat16)
            gs[new, cut] = (sent * gate_grad).astype(jnp.bfloat16)
            us[new, cut] = (sent * up_grad).astype(jnp.bfloat16)
    wait(rest_here)
    wait(grad_here)
    if half_ff % LANES == 0:
        hidden_half[...] = hs[:, pl.ds(pl.multiple_of(group_ref[0] * half_ff, LANES), half_ff)]
    else:
        for index in range(hs.shape[1] // half_ff):

            @pl.when(group_ref[0] == index)
            def _():
                hidden_half[...] = hs[:, index * half_ff : (index + 1) * half_ff]

    results = []
    for which, left, right in ((0, tok_half, gs), (1, tok_half, us), (2, hidden_half, grad_all)):
        for step in range(steps):
            if which < 2:
                size = half // steps
                cut = slice(step * size, (step + 1) * size)
                value = contract(left[:, cut], right[...], 0, 0)
                target = outs[which].at[0, pl.ds(step * size, size), :]
            else:
                size = width // steps
                cut = slice(step * size, (step + 1) * size)
                value = contract(left[...], right[:, cut], 0, 0)
                target = outs[which].at[0, :, pl.ds(step * size, size)]
            tile_out[which][step] = value.astype(tile_out[which].dtype)
            results.append(copies.start(tile_out[which].at[step], target))
    wait(results)


def weights_call(me, group, groups, tok, grad, gate, weights, given, fresh, start, dtype):
    width, ff_width = weights[0].shape[1:]
    half, half_ff = (width // groups, ff_width // groups)
    rows = sum(part.shape[0] for part in tok)
    new_rows = sum(part.shape[0] for part in tok[len(tok) - fresh :]) if fresh else SUBLANES * 2
    steps = max(s for s in (4, 2, 1) if half % (s * LANES) == 0)
    low = jnp.bfloat16
    scratch = [pltpu.VMEM((rows, ff_width), low)] * 3
    scratch += [
        pltpu.VMEM((rows, half), low),
        pltpu.VMEM((rows, width), low),
        pltpu.VMEM((rows, half_ff), low),
        pltpu.VMEM((steps, half // steps, ff_width), dtype),
        pltpu.VMEM((steps, half // steps, ff_width), dtype),
        pltpu.VMEM((steps, half_ff, width // steps), dtype),
        pltpu.VMEM((new_rows, width), low),
        pltpu.VMEM((new_rows, LANES), low),
        pltpu.VMEM((width, ff_width), low),
        pltpu.VMEM((width, ff_width), low),
        pltpu.VMEM((ff_width, width), low),
    ]
    count = 2 * len(tok) + 2 * fresh + 3 * len(given) + 3 * steps
    count += 3 * len(tiles(ff_width, FF_TILE)) if fresh else 0
    return kernel_call(
        functools.partial(weights_kernel, len(tok), fresh, len(given), start, steps),
        (me, group), (gate,),
        (*tok, *grad, *weights, *(block[kind] for kind in range(3) for block in given)),
        [
            jax.ShapeDtypeStruct((1, half, ff_width), dtype),
            jax.ShapeDtypeStruct((1, half, ff_width), dtype),
            jax.ShapeDtypeStruct((1, half_ff, width), dtype),
        ],
        scratch, count, 3, (), 3 * (rows * half + new_rows * width) * ff_width,
    )


def router_kernel(parts, me_ref, *refs):
    logits_ref, score_ref, *tok = refs[: 2 + parts]
    grad_ref, router_ref, rows, sems = refs[2 + parts :]
    copies = Copies(sems)
    rows_here = copies.stack(tok, rows)
    logits = logits_ref[...]
    experts = logits.shape[0]
    row = lax.broadcasted_iota(jnp.int32, (experts, experts), 0)
    column = lax.broadcasted_iota(jnp.int32, (experts, experts), 1)
    unswap = jnp.where((row ^ me_ref[0]) == column, 1.0, 0.0).astype(jnp.bfloat16)
    score = contract(unswap, score_ref[...], 1, 0)
    state = balancer_forward_pass(logits)
    grad = balancer_adjoint_pass(experts * score, *state).astype(jnp.bfloat16)
    grad_ref[...] = grad
    wait(rows_here)
    router_ref[...] = contract(grad, rows[...], 1, 0)


def per_device(tokens, out_grad, expert_ids, router_weight, w_gate, w_up, w_down):
    tok_rows, width = tokens.shape
    experts = router_weight.shape[1]
    groups = lax.axis_size("dp")
    far = lax.axis_size("expert") // 4
    chunk = 2 * far * tok_rows
    me = lax.axis_index("expert").astype(jnp.int32)[None]
    group = lax.axis_index("dp").astype(jnp.int32)[None]

    def along(array):
        return jnp.concatenate([array] + [swap_expert(array, 4 * k) for k in range(1, far)], axis=0)

    tok_line = along(tokens)
    lane = jnp.arange(LANES, dtype=jnp.int32)
    picked = jnp.any(expert_ids[:, :, None] == lane[None, None, :], axis=1)
    grad_line = along(jnp.concatenate([out_grad, picked.astype(jnp.bfloat16)], axis=1))
    tok_next = swap_expert(tok_line, 2)
    grad_next = swap_expert(grad_line, 2)
    tok_own = [(tok_line, swap_expert(tok_line, 1)), (tok_next, swap_expert(tok_next, 1))]
    grad_own = [(grad_line, swap_expert(grad_line, 1)), (grad_next, swap_expert(grad_next, 1))]

    tok_parts = [rows for pair in tok_own for rows in pair]
    grad_parts = [rows for pair in grad_own for rows in pair]
    weights = (w_gate, w_up, w_down)
    ff_width = w_gate.shape[2]

    at_once = 2 * groups * chunk <= ROWS_AT_ONCE

    def moved(parts, offset):
        out = []
        for part in parts:
            part = swap_group(part, offset)
            out += [part, swap_expert(part, 1)]
        return out

    moved_tok = moved((tok_line, tok_next), 1) if at_once else []
    (logits_own,) = kernel_call(
        functools.partial(logits_kernel, len(tok_parts)), (), (router_weight.T,), tok_parts,
        [shape(experts, 2 * chunk, jnp.float32)],
        [pltpu.VMEM((2 * chunk, width), jnp.bfloat16)], len(tok_parts), 0, moved_tok[:1],
    )
    moved_grad = moved((grad_line, grad_next), 1) if at_once else []
    logits = jnp.concatenate(
        [logits_own] + [swap_group(logits_own, offset) for offset in range(1, groups)], axis=1
    )
    (gate,) = kernel_call(
        gate_kernel, (me,), (logits,), (), [shape(logits.shape[1], LANES, jnp.float32)], (), 0
    )

    keep0, send0, keep1, send1, *scaled, score = expert_call(
        me, gate, tok_parts, grad_parts, weights, moved_tok[2:3]
    )
    given = [scaled]
    got1, got0 = (swap_expert(send1, 1), swap_expert(send0, 1))
    (near,) = kernel_call(
        add_kernel, (), (), (keep1, got1), [shape(*keep1.shape)],
        [pltpu.VMEM(keep1.shape, keep1.dtype)] * 3, 3, 1, moved_grad,
    )
    near = swap_expert(near, 2)
    row_sum = 0.0
    for k in range(far):
        cut = slice(k * tok_rows, (k + 1) * tok_rows)
        total = sum(array[cut].astype(jnp.float32) for array in (keep0, got0, near))
        if k:
            total = swap_expert(total.astype(jnp.bfloat16), 4 * k).astype(jnp.float32)
        row_sum = row_sum + total

    score = score[0].astype(jnp.bfloat16).reshape(2, 2, far, tok_rows)
    from_far = [score]
    for k in range(1, far):
        got = swap_expert(score, k * 4)
        from_far.append(jnp.stack([got[:, :, j ^ k] for j in range(far)], axis=2))
    score = jnp.stack(from_far)
    score = jnp.stack([score, jnp.flip(swap_expert(score, 2), axis=1)], axis=1)
    score = jnp.stack([score, jnp.flip(swap_expert(score, 1), axis=3)], axis=2)
    score = score.reshape(experts, 2 * chunk)
    score = jnp.concatenate(
        [score] + [swap_group(score, offset) for offset in range(1, groups)], axis=1
    )
    token_rows = list(tok_parts)
    totals = None
    if not at_once:
        totals = weights_call(
            me, group, groups, tok_parts, grad_parts, gate, weights, given, 0, 0, jnp.float32
        )
        tok_parts, grad_parts, given = ([], [], [])
    for offset in range(1, groups):
        if not at_once:
            (tok_line, tok_next, grad_line, grad_next), totals = lax.optimization_barrier(
                ((tok_line, tok_next, grad_line, grad_next), totals)
            )
            moved_tok = moved((tok_line, tok_next), offset)
            moved_grad = moved((grad_line, grad_next), offset)
        token_rows += moved_tok
        terms = weights_call(
            me, group, groups, tok_parts + moved_tok, grad_parts + moved_grad, gate, weights, given,
            4, 2 * chunk * offset, jnp.bfloat16 if at_once else jnp.float32,
        )
        totals = terms if totals is None else [t + u for t, u in zip(totals, terms)]
    final = [t.astype(jnp.bfloat16) for t in totals]

    logit_grad, grad_router = kernel_call(
        functools.partial(router_kernel, len(token_rows)), (me,), (logits, score), token_rows,
        [shape(*logits.shape), shape(experts, width, jnp.float32)],
        [pltpu.VMEM((logits.shape[1], width), jnp.bfloat16)], len(token_rows),
    )
    row_sum = row_sum + contract(logit_grad[:, :tok_rows], router_weight, 0, 1)
    return (row_sum.astype(jnp.bfloat16), grad_router.T, *final)


def solution(mesh):
    in_specs = (
        P(("dp", "expert"), None),
        P(("dp", "expert"), None),
        P(("dp", "expert"), None),
        P(),
        P("expert", None, None),
        P("expert", None, None),
        P("expert", None, None),
    )
    out_specs = (
        P(("dp", "expert"), None),
        P(),
        P("expert", "dp", None),
        P("expert", "dp", None),
        P("expert", "dp", None),
    )
    return jax.shard_map(
        per_device, mesh=mesh, in_specs=in_specs, out_specs=out_specs, check_vma=False
    )
```

time: 153 us -> 124 us (0.81)
  matrix products: 46.4 us -> 1.52 us
  Pallas kernels: 0 us -> 42.8 us
  local copies, waits for them, and re-layouts: 25.6 us -> 6.1 us
  waiting for transfers between devices: 40.1 us -> 30.2 us
  starting transfers between devices: 31.3 us -> 37.7 us
  other arithmetic: 7.81 us -> 4.21 us
    dot_general x36 -> x1, matrix products: 46.4 us -> 1.52 us  [contract(): lax.dot_general(left, right, (((left_dim,), (right_dim,)), ((), ())), pre...]
    pallas_call x0 -> x6, Pallas kernels: none -> 42.8 us  [kernel_call(): pl.pallas_call(body, in_specs=[pl.BlockSpec(memory_space=pltpu.SMEM)] * l...]
    ppermute x22 -> x27, waiting for transfers between devices: 38 us -> 22.4 us  [swap_expert(): return lax.ppermute(array, 'expert', [(i, i ^ offset) for i in range(size)])]
    unnamed x108 -> x38, local copies, waits for them, and re-layouts: 14.8 us -> 5 us
    ppermute x4 -> x6, waiting for transfers between devices: 2.12 us -> 7.75 us  [swap_group(): return lax.ppermute(array, 'dp', [(i, i ^ offset) for i in range(size)])]
    ppermute x22 -> x27, starting transfers between devices: 27.1 us -> 30.5 us  [swap_expert(): return lax.ppermute(array, 'expert', [(i, i ^ offset) for i in range(size)])]
    slice x7 -> x0, local copies, waits for them, and re-layouts: 3.29 us -> none  [the longest x2 2.05 us: per_device(): rows[:, :model_width]]
    convert_element_type x4 -> x3, local copies, waits for them, and re-layouts: 4.04 us -> 0.91 us  [per_device(): score = score[0].astype(jnp.bfloat16).reshape(2, 2, far, tok_rows)]
  transfers between devices with their start and end apart: 26 -> 33, of which waited for: 10 -> 9; matrix products, arithmetic and copies ran while one was open for 34% -> 6% of each run, Pallas kernels for 0% -> 35%
where the time goes in v3:
time: 124 us
  Pallas kernels  42.8 us (35%)
  starting transfers between devices  37.7 us (30%)
  waiting for transfers between devices  30.2 us (24%)
  local copies, waits for them, and re-layouts  6.1 us (5%)
  other arithmetic  4.21 us (3%)
  matrix products  1.52 us (1%)
    pallas_call x6, Pallas kernels, kernel_call(): pl.pallas_call(body, in_specs=[pl.BlockSpec(memory_space=pltpu.SMEM)] * l...  42.8 us
    ppermute x27, starting transfers between devices, swap_expert(): return lax.ppermute(array, 'expert', [(i, i ^ offset) for i in range(size)])  30.5 us
    ppermute x27, waiting for transfers between devices, swap_expert(): return lax.ppermute(array, 'expert', [(i, i ^ offset) for i in range(size)])  22.4 us
    ppermute x6, waiting for transfers between devices, swap_group(): return lax.ppermute(array, 'dp', [(i, i ^ offset) for i in range(size)])  7.75 us
    ppermute x6, starting transfers between devices, swap_group(): return lax.ppermute(array, 'dp', [(i, i ^ offset) for i in range(size)])  7.23 us
    unnamed x38, local copies, waits for them, and re-layouts  5 us
  transfers between devices with their start and end apart: 33, of which 9 were waited for; matrix products, arithmetic and copies ran while one was open for 6% of the time, Pallas kernels for 35%

profile of v3, /device:TPU:0, one launch (start us, length us, event | category | flops | bytes accessed | tf_op | source)
XLA Modules:
  0.0 123.5 jit_solution(15891642596500550690)
XLA Ops:
  0.6 3.1 %collective-permute-start = (bf16[24,2048]{1,0:T(8,128)(2,1)}, bf16[24,2048]{1,0:T(8,128)(2,1)S(1)}, u32[]{:S(2)}, u32[]{:S(2)}) collective-permute-start(bf16[24,2048]{1,0:T(8,128)(2,1)} %param.7), channel_id=1, source_target_pairs={{0,4},{1,5},{2,6},{3,7},{4,0},{5,1},{6,2},{7,3},{8,12},{9,13},{10,... | collective-permute-start | bytes 294920 | tf_op jit(solution)/shard_map/ppermute | solution.py:20
  3.7 2.6 %collective-permute-start.1 = (bf16[24,2048]{1,0:T(8,128)(2,1)}, bf16[24,2048]{1,0:T(8,128)(2,1)S(1)}, u32[]{:S(2)}, u32[]{:S(2)}) collective-permute-start(bf16[24,2048]{1,0:T(8,128)(2,1)} %param.7), channel_id=1, source_target_pairs={{0,8},{1,9},{2,10},{3,11},{4,12},{5,13},{6,14},{7,15},{8,0},{9,1},... | collective-permute-start | bytes 294920 | tf_op jit(solution)/shard_map/ppermute | solution.py:20
  6.3 0.8 copy.15
  7.1 0.1 fusion.1
  7.2 0.9 pad_maximum_fusion.1
  8.1 3.8 %collective-permute-start.10 = (bf16[24,2176]{1,0:T(8,128)(2,1)S(1)}, bf16[24,2176]{1,0:T(8,128)(2,1)S(1)}, u32[]{:S(2)}, u32[]{:S(2)}) collective-permute-start(bf16[24,2176]{1,0:T(8,128)(2,1)S(1)} %pad_maximum_fusion.1), channel_id=1, source_target_pairs={{0,12},{1,13},{2,14},{3,15},{4,8},{5,9},{6,10},{7,11},{8,4},{9,5},... | collective-permute-start | bytes 313352 | tf_op jit(solution)/shard_map/ppermute | solution.py:20
  11.9 0.9 constant_dynamic-update-slice_fusion.3
  12.8 0.7 collective-permute-start.8
  13.5 5.4 %collective-permute-done.1 = bf16[24,2048]{1,0:T(8,128)(2,1)S(1)} collective-permute-done((bf16[24,2048]{1,0:T(8,128)(2,1)}, bf16[24,2048]{1,0:T(8,128)(2,1)S(1)}, u32[]{:S(2)}, u32[]{:S(2)}) %collective-permute-start.1) | collective-permute-done | bytes 98336 | tf_op jit(solution)/shard_map/ppermute | solution.py:20
  18.9 0.0 collective-permute-done.2
  19.0 1.6 %collective-permute-start.4 = (bf16[96,2048]{1,0:T(8,128)(2,1)S(1)}, bf16[96,2048]{1,0:T(8,128)(2,1)S(1)}, u32[]{:S(2)}, u32[]{:S(2)}) collective-permute-start(bf16[96,2048]{1,0:T(8,128)(2,1)S(1)} %constant_dynamic-update-slice_fusion.refs_1_.refs_2_.refs_3_), channel_id=1, source_target_pairs={{0,2},{1,3},{2,0},{3,1},{4,6},{5,7},{6,4},{7,5},{8,10},{9,11},{10,... | collective-permute-start | bytes 1179656 | tf_op jit(solution)/shard_map/ppermute | solution.py:20
  20.6 0.0 collective-permute-done.10
  20.6 3.8 %collective-permute-done.9 = bf16[24,2176]{1,0:T(8,128)(2,1)S(1)} collective-permute-done((bf16[24,2176]{1,0:T(8,128)(2,1)S(1)}, bf16[24,2176]{1,0:T(8,128)(2,1)S(1)}, u32[]{:S(2)}, u32[]{:S(2)}) %collective-permute-start.9) | collective-permute-done | bytes 104480 | tf_op jit(solution)/shard_map/ppermute | solution.py:20
  24.4 0.9 pad_maximum_fusion.refs_6_.refs_11_
  25.3 1.6 %collective-permute-start.12 = (bf16[96,2176]{1,0:T(8,128)(2,1)S(1)}, bf16[96,2176]{1,0:T(8,128)(2,1)S(1)}, u32[]{:S(2)}, u32[]{:S(2)}) collective-permute-start(bf16[96,2176]{1,0:T(8,128)(2,1)S(1)} %pad_maximum_fusion.refs_6_.refs_11_), channel_id=1, source_target_pairs={{0,2},{1,3},{2,0},{3,1},{4,6},{5,7},{6,4},{7,5},{8,10},{9,11},{10,... | collective-permute-start | bytes 1253384 | tf_op jit(solution)/shard_map/ppermute | solution.py:20
  26.9 1.5 %collective-permute-start.6 = (bf16[96,2048]{1,0:T(8,128)(2,1)S(1)}, bf16[96,2048]{1,0:T(8,128)(2,1)S(1)}, u32[]{:S(2)}, u32[]{:S(2)}) collective-permute-start(bf16[96,2048]{1,0:T(8,128)(2,1)S(1)} %constant_dynamic-update-slice_fusion.refs_1_.refs_2_.refs_3_), channel_id=1, source_target_pairs={{0,16},{16,0},{1,17},{17,1},{2,18},{18,2},{3,19},{19,3},{4,20},{20... | collective-permute-start | bytes 1179656 | tf_op jit(solution)/shard_map/ppermute | solution.py:25
  28.4 0.2 collective-permute-start.5
  28.6 0.3 collective-permute-start.11
  28.9 6.9 %collective-permute-done.12.refs_8_.refs_13_ = bf16[96,2176]{1,0:T(8,128)(2,1)S(1)} collective-permute-done((bf16[96,2176]{1,0:T(8,128)(2,1)S(1)}, bf16[96,2176]{1,0:T(8,128)(2,1)S(1)}, u32[]{:S(2)}, u32[]{:S(2)}) %collective-permute-start.12) | collective-permute-done | bytes 417824 | tf_op jit(solution)/shard_map/ppermute | solution.py:20
  35.8 1.6 %collective-permute-start.14 = (bf16[96,2048]{1,0:T(8,128)(2,1)S(1)}, bf16[96,2048]{1,0:T(8,128)(2,1)S(1)}, u32[]{:S(2)}, u32[]{:S(2)}) collective-permute-start(bf16[96,2048]{1,0:T(8,128)(2,1)S(1)} %collective-permute-done.4.refs_3_.refs_4_.refs_5_), channel_id=1, source_target_pairs={{0,16},{16,0},{1,17},{17,1},{2,18},{18,2},{3,19},{19,3},{4,20},{20... | collective-permute-start | bytes 1179656 | tf_op jit(solution)/shard_map/ppermute | solution.py:25
  37.4 1.1 collective-permute-done.6.refs_5_.refs_7_
  38.5 0.7 copy-done.3
  39.2 0.2 copy-done.5
  39.3 3.4 %shard_map.110 = f32[16,384]{1,0:T(8,128)} custom-call(bf16[16,2048]{1,0:T(8,128)(2,1)} %bitcast.23, bf16[96,2048]{1,0:T(8,128)(2,1)} %copy-done, bf16[96,2048]{1,0:T(8,128)(2,1)} %copy-done.2, bf16[96,2048]{1,0:T(8,128)(2,1)} %copy-done.1, bf16[96,2048]{1,0:T(8,128)(2,1)} %copy-done.5, bf16[96,2048]{1,0:T(8,128)(2,1)} %copy-done.3), custom_call_target="tpu_custom_call" | custom-call | flops 2000000 | bytes 5000 | tf_op jit(solution)/shard_map/pallas_call | solution.py:76
  42.7 1.6 %collective-permute-start.7 = (f32[16,384]{1,0:T(8,128)}, f32[16,384]{1,0:T(8,128)S(1)}, u32[]{:S(2)}, u32[]{:S(2)}) collective-permute-start(f32[16,384]{1,0:T(8,128)} %shard_map.110), channel_id=1, source_target_pairs={{0,16},{16,0},{1,17},{17,1},{2,18},{18,2},{3,19},{19,3},{4,20},{20... | collective-permute-start | bytes 73736 | tf_op jit(solution)/shard_map/ppermute | solution.py:25
  44.3 0.5 collective-permute-start.17
  44.8 3.5 %collective-permute-done.7 = f32[16,384]{1,0:T(8,128)S(1)} collective-permute-done((f32[16,384]{1,0:T(8,128)}, f32[16,384]{1,0:T(8,128)S(1)}, u32[]{:S(2)}, u32[]{:S(2)}) %collective-permute-start.7) | collective-permute-done | bytes 24608 | tf_op jit(solution)/shard_map/ppermute | solution.py:25
  48.3 1.5 %collective-permute-start.19 = (bf16[96,2176]{1,0:T(8,128)(2,1)S(1)}, bf16[96,2176]{1,0:T(8,128)(2,1)S(1)}, u32[]{:S(2)}, u32[]{:S(2)}) collective-permute-start(bf16[96,2176]{1,0:T(8,128)(2,1)S(1)} %collective-permute-done.12.refs_8_.refs_13_), channel_id=1, source_target_pairs={{0,16},{16,0},{1,17},{17,1},{2,18},{18,2},{3,19},{19,3},{4,20},{20... | collective-permute-start | bytes 1253384 | tf_op jit(solution)/shard_map/ppermute | solution.py:25
  49.8 1.4 %pad_maximum_fusion.3.refs_1_ = f32[16,768]{1,0:T(8,128)} fusion(f32[16,384]{1,0:T(8,128)S(1)} %collective-permute-done.7, f32[16,384]{1,0:T(8,128)} %shard_map.110), kind=kLoop, calls=%fused_computation.10 | loop fusion | flops 12288 | bytes 98304 | tf_op jit(solution)/shard_map/concatenate | solution.py:410
  51.2 2.1 %shard_map.111.refs_1_.refs_2_ = f32[768,128]{1,0:T(8,128)} custom-call(s32[1]{0:T(128)} %bitcast.refs_0_, f32[16,768]{1,0:T(8,128)} %pad_maximum_fusion.3.refs_1_), custom_call_target="tpu_custom_call" | custom-call | flops 2000000 | bytes 5000 | tf_op jit(solution)/shard_map/pallas_call | solution.py:76
  53.3 0.8 copy-done.12
  54.0 16.2 %shard_map.112 = (bf16[96,2048]{1,0:T(8,128)(2,1)}, bf16[96,2048]{1,0:T(8,128)(2,1)}, bf16[96,2048]{1,0:T(8,128)(2,1)}, bf16[96,2048]{1,0:T(8,128)(2,1)}, bf16[3...) custom-call(s32[1]{0:T(128)} %bitcast.refs_0_, ...), custom_call_target="tpu_custom_call" | custom-call | flops 6039797760 | bytes 15099494 | tf_op jit(solution)/shard_map/pallas_call | solution.py:76
  70.2 0.7 convert_reduce_fusion
  70.9 0.1 convert_element_type.98
  71.0 3.8 %collective-permute-start.25 = (bf16[2,2,4,24]{3,2,1,0:T(4,128)(2,1)S(1)}, bf16[2,2,4,24]{3,2,1,0:T(4,128)(2,1)S(1)}, u32[]{:S(2)}, u32[]{:S(2)}) collective-permute-start(bf16[2,2,4,24]{3,2,1,0:T(4,128)(2,1)S(1)} %convert_element_type.98), channel_id=1, source_target_pairs={{0,4},{1,5},{2,6},{3,7},{4,0},{5,1},{6,2},{7,3},{8,12},{9,13},{10,... | collective-permute-start | bytes 2312 | tf_op jit(solution)/shard_map/ppermute | solution.py:20
  74.8 0.5 collective-permute-start.18
  75.3 2.4 %collective-permute-start.27 = (bf16[2,2,4,24]{3,2,1,0:T(4,128)(2,1)S(1)}, bf16[2,2,4,24]{3,2,1,0:T(4,128)(2,1)S(1)}, u32[]{:S(2)}, u32[]{:S(2)}) collective-permute-start(bf16[2,2,4,24]{3,2,1,0:T(4,128)(2,1)S(1)} %convert_element_type.98), channel_id=1, source_target_pairs={{0,12},{1,13},{2,14},{3,15},{4,8},{5,9},{6,10},{7,11},{8,4},{9,5},... | collective-permute-start | bytes 2312 | tf_op jit(solution)/shard_map/ppermute | solution.py:20
  77.7 0.1 convert_element_type.97
  77.9 1.5 %collective-permute-start.26 = (bf16[2,2,4,24]{3,2,1,0:T(4,128)(2,1)S(1)}, bf16[2,2,4,24]{3,2,1,0:T(4,128)(2,1)S(1)}, u32[]{:S(2)}, u32[]{:S(2)}) collective-permute-start(bf16[2,2,4,24]{3,2,1,0:T(4,128)(2,1)S(1)} %convert_element_type.98), channel_id=1, source_target_pairs={{0,8},{1,9},{2,10},{3,11},{4,12},{5,13},{6,14},{7,15},{8,0},{9,1},... | collective-permute-start | bytes 2312 | tf_op jit(solution)/shard_map/ppermute | solution.py:20
  79.4 0.1 collective-permute-start.16
  79.5 2.9 %collective-permute-done.26 = bf16[2,2,4,24]{3,2,1,0:T(4,128)(2,1)S(1)} collective-permute-done((bf16[2,2,4,24]{3,2,1,0:T(4,128)(2,1)S(1)}, bf16[2,2,4,24]{3,2,1,0:T(4,128)(2,1)S(1)}, u32[]{:S(2)}, u32[]{:S(2)}) %collective-permute-start.26) | collective-permute-done | bytes 800 | tf_op jit(solution)/shard_map/ppermute | solution.py:20
  82.6 1.6 %collective-permute-start.28 = (bf16[4,2,2,4,24]{4,3,2,1,0:T(4,128)(2,1)S(1)}, bf16[4,2,2,4,24]{4,3,2,1,0:T(4,128)(2,1)S(1)}, u32[]{:S(2)}, u32[]{:S(2)}) collective-permute-start(bf16[4,2,2,4,24]{4,3,2,1,0:T(4,128)(2,1)S(1)} %pad_maximum_fusion.6), channel_id=1, source_target_pairs={{0,2},{1,3},{2,0},{3,1},{4,6},{5,7},{6,4},{7,5},{8,10},{9,11},{10,... | collective-permute-start | bytes 9224 | tf_op jit(solution)/shard_map/ppermute | solution.py:20
  84.2 2.2 %collective-permute-done.28 = bf16[4,2,2,4,24]{4,3,2,1,0:T(4,128)(2,1)S(1)} collective-permute-done((bf16[4,2,2,4,24]{4,3,2,1,0:T(4,128)(2,1)S(1)}, bf16[4,2,2,4,24]{4,3,2,1,0:T(4,128)(2,1)S(1)}, u32[]{:S(2)}, u32[]{:S(2)}) %collective-permute-start.28) | collective-permute-done | bytes 3104 | tf_op jit(solution)/shard_map/ppermute | solution.py:20
  86.4 0.6 collective-permute-start.15
  87.0 0.2 copy-done.9
  87.2 0.6 copy-done.14
  87.7 0.2 copy-done.10
  87.9 2.0 %shard_map.113 = bf16[96,2048]{1,0:T(8,128)(2,1)} custom-call(bf16[96,2048]{1,0:T(8,128)(2,1)} %get-tuple-element.20.refs_0_, bf16[96,2048]{1,0:T(8,128)(2,1)} %copy-done.14, bf16[96,2176]{1,0:T(8,128)(2,1)} %copy-done.7, bf16[96,2176]{1,0:T(8,128)(2,1)} %copy-done.9, bf16[96,2176]{1,0:T(8,128)(2,1)} %copy-done.8, bf16[96,2176]{1,0:T(8,128)(2,1)} %copy-done.10), custom_call_target="tpu_custom_call" | custom-call | flops 2000000 | bytes 5000 | tf_op jit(solution)/shard_map/pallas_call | solution.py:76
  89.9 1.6 %collective-permute-start.21 = (bf16[96,2048]{1,0:T(8,128)(2,1)}, bf16[96,2048]{1,0:T(8,128)(2,1)S(1)}, u32[]{:S(2)}, u32[]{:S(2)}) collective-permute-start(bf16[96,2048]{1,0:T(8,128)(2,1)} %shard_map.113), channel_id=1, source_target_pairs={{0,2},{1,3},{2,0},{3,1},{4,6},{5,7},{6,4},{7,5},{8,10},{9,11},{10,... | collective-permute-start | bytes 1179656 | tf_op jit(solution)/shard_map/ppermute | solution.py:20
  91.5 0.1 collective-permute-start.29
  91.6 1.2 collective-permute-done.29
  92.8 0.1 pad_maximum_fusion.2
  92.9 0.1 reshape.28
  93.0 0.6 collective-permute-start.30
  93.6 3.2 %collective-permute-done.30 = bf16[16,384]{1,0:T(8,128)(2,1)S(1)} collective-permute-done((bf16[16,384]{1,0:T(8,128)(2,1)S(1)}, bf16[16,384]{1,0:T(8,128)(2,1)S(1)}, u32[]{:S(2)}, u32[]{:S(2)}) %collective-permute-start.30) | collective-permute-done | bytes 12320 | tf_op jit(solution)/shard_map/ppermute | solution.py:25
  96.8 0.6 pad_maximum_fusion.5.refs_2_
  97.4 0.8 copy-done.13
  98.2 4.0 %shard_map.114 = (bf16[16,768]{1,0:T(8,128)(2,1)}, f32[16,2048]{1,0:T(8,128)}) custom-call(s32[1]{0:T(128)} %bitcast.refs_0_, f32[16,768]{1,0:T(8,128)} %pad_maximum_fusion.3.refs_1_, bf16[16,768]{1,0:T(8,128)(2,1)} %pad_maximum_fusion.5.refs_2_, bf16[96,2048]{1,0:T(8,128)(2,1)} %copy-done, bf16[96,2048]{1,0:T(8,128)(2,1)} %copy-done.2, ...), custom_call_target="tpu_custom_call" | custom-call | flops 2000000 | bytes 5000 | tf_op jit(solution)/shard_map/pallas_call | solution.py:76
  102.2 0.1 add_convert_fusion.2
  102.3 1.5 %collective-permute-start.24 = (bf16[24,2048]{1,0:T(8,128)(2,1)S(1)}, bf16[24,2048]{1,0:T(8,128)(2,1)S(1)}, u32[]{:S(2)}, u32[]{:S(2)}) collective-permute-start(bf16[24,2048]{1,0:T(8,128)(2,1)S(1)} %get-tuple-element.32), channel_id=1, source_target_pairs={{0,12},{1,13},{2,14},{3,15},{4,8},{5,9},{6,10},{7,11},{8,4},{9,5},... | collective-permute-start | bytes 294920 | tf_op jit(solution)/shard_map/ppermute | solution.py:20
  103.8 0.6 collective-permute-start.23
  104.3 2.4 %collective-permute-start.22 = (bf16[24,2048]{1,0:T(8,128)(2,1)S(1)}, bf16[24,2048]{1,0:T(8,128)(2,1)S(1)}, u32[]{:S(2)}, u32[]{:S(2)}) collective-permute-start(bf16[24,2048]{1,0:T(8,128)(2,1)S(1)} %get-tuple-element.31), channel_id=1, source_target_pairs={{0,4},{1,5},{2,6},{3,7},{4,0},{5,1},{6,2},{7,3},{8,12},{9,13},{10,... | collective-permute-start | bytes 294920 | tf_op jit(solution)/shard_map/ppermute | solution.py:20
  106.8 15.2 %shard_map.115 = (bf16[1,1024,768]{2,1,0:T(8,128)(2,1)}, bf16[1,1024,768]{2,1,0:T(8,128)(2,1)}, bf16[1,384,2048]{2,1,0:T(8,128)(2,1)}) custom-call(s32[1]{0:T(128)} %bitcast.refs_0_, s32[1]{0:T(128)} %bitcast.12.refs_1_, f32[768,128]{1,0:T(8,128)} %shard_map.111.refs_1_.refs_2_, bf16[96,2048]{1,0:T(8,128)(2,1)} %copy-done, bf16[96,2048]{1,0:T(8,128)(2,1)} %copy-done.2, ...), custom_call_target="tpu_custom_call" | custom-call | flops 7247757312 | bytes 18119392 | tf_op jit(solution)/shard_map/pallas_call | solution.py:76
  122.0 1.5 %fusion = bf16[24,2048]{1,0:T(8,128)(2,1)} fusion(bf16[2048,16]{0,1:T(8,128)(2,1)S(1)} %copy-done.15, bf16[24,2048]{1,0:T(8,128)(2,1)S(1)} %collective-permute-done.24, bf16[24,2048]{1,0:T(8,128)(2,1)S(1)} %collective-permute-done.23, bf16[24,2048]{1,0:T(8,128)(2,1)S(1)} %collective-permute-done.22, bf16[96,2048]{1,0:T(8,128)(2,1)S(1)} %collective-permute-done.21, ...), kind=kOutput, calls=%fused_computation.1 | convolution fusion | flops 2211840 | bytes 757760 | tf_op jit(solution)/shard_map/dot_general | solution.py:29
  (70 shorter events, 0.3 us)
Async XLA Ops:
  0.6 12.2 %collective-permute-start = (bf16[24,2048]{1,0:T(8,128)(2,1)}, bf16[24,2048]{1,0:T(8,128)(2,1)S(1)}, u32[]{:S(2)}, u32[]{:S(2)}) collective-permute-start(bf16[24,2048]{1,0:T(8,128)(2,1)} %param.7), channel_id=1, source_target_pairs={{0,4},{1,5},{2,6},{3,7},{4,0},{5,1},{6,2},{7,3},{8,12},{9,13},{10,... | collective-permute-start | bytes 294920 | tf_op jit(solution)/shard_map/ppermute | solution.py:20
  3.7 15.2 %collective-permute-start.1 = (bf16[24,2048]{1,0:T(8,128)(2,1)}, bf16[24,2048]{1,0:T(8,128)(2,1)S(1)}, u32[]{:S(2)}, u32[]{:S(2)}) collective-permute-start(bf16[24,2048]{1,0:T(8,128)(2,1)} %param.7), channel_id=1, source_target_pairs={{0,8},{1,9},{2,10},{3,11},{4,12},{5,13},{6,14},{7,15},{8,0},{9,1},... | collective-permute-start | bytes 294920 | tf_op jit(solution)/shard_map/ppermute | solution.py:20
  6.3 12.6 %collective-permute-start.2 = (bf16[24,2048]{1,0:T(8,128)(2,1)}, bf16[24,2048]{1,0:T(8,128)(2,1)S(1)}, u32[]{:S(2)}, u32[]{:S(2)}) collective-permute-start(bf16[24,2048]{1,0:T(8,128)(2,1)} %param.7), channel_id=1, source_target_pairs={{0,12},{1,13},{2,14},{3,15},{4,8},{5,9},{6,10},{7,11},{8,4},{9,5},... | collective-permute-start | bytes 294920 | tf_op jit(solution)/shard_map/ppermute | solution.py:20
  8.1 12.5 %collective-permute-start.10 = (bf16[24,2176]{1,0:T(8,128)(2,1)S(1)}, bf16[24,2176]{1,0:T(8,128)(2,1)S(1)}, u32[]{:S(2)}, u32[]{:S(2)}) collective-permute-start(bf16[24,2176]{1,0:T(8,128)(2,1)S(1)} %pad_maximum_fusion.1), channel_id=1, source_target_pairs={{0,12},{1,13},{2,14},{3,15},{4,8},{5,9},{6,10},{7,11},{8,4},{9,5},... | collective-permute-start | bytes 313352 | tf_op jit(solution)/shard_map/ppermute | solution.py:20
  11.9 12.5 %collective-permute-start.9 = (bf16[24,2176]{1,0:T(8,128)(2,1)S(1)}, bf16[24,2176]{1,0:T(8,128)(2,1)S(1)}, u32[]{:S(2)}, u32[]{:S(2)}) collective-permute-start(bf16[24,2176]{1,0:T(8,128)(2,1)S(1)} %pad_maximum_fusion.1), channel_id=1, source_target_pairs={{0,8},{1,9},{2,10},{3,11},{4,12},{5,13},{6,14},{7,15},{8,0},{9,1},... | collective-permute-start | bytes 313352 | tf_op jit(solution)/shard_map/ppermute | solution.py:20
  12.8 11.5 %collective-permute-start.8 = (bf16[24,2176]{1,0:T(8,128)(2,1)S(1)}, bf16[24,2176]{1,0:T(8,128)(2,1)S(1)}, u32[]{:S(2)}, u32[]{:S(2)}) collective-permute-start(bf16[24,2176]{1,0:T(8,128)(2,1)S(1)} %pad_maximum_fusion.1), channel_id=1, source_target_pairs={{0,4},{1,5},{2,6},{3,7},{4,0},{5,1},{6,2},{7,3},{8,12},{9,13},{10,... | collective-permute-start | bytes 313352 | tf_op jit(solution)/shard_map/ppermute | solution.py:20
  19.0 19.5 %copy-start = (bf16[96,2048]{1,0:T(8,128)(2,1)}, bf16[96,2048]{1,0:T(8,128)(2,1)S(1)}, u32[]{:S(2)}) copy-start(bf16[96,2048]{1,0:T(8,128)(2,1)S(1)} %constant_dynamic-update-slice_fusion.refs_1_.refs_2_.refs_3_) | copy-start | bytes 1179652
  19.0 9.4 %collective-permute-start.4 = (bf16[96,2048]{1,0:T(8,128)(2,1)S(1)}, bf16[96,2048]{1,0:T(8,128)(2,1)S(1)}, u32[]{:S(2)}, u32[]{:S(2)}) collective-permute-start(bf16[96,2048]{1,0:T(8,128)(2,1)S(1)} %constant_dynamic-update-slice_fusion.refs_1_.refs_2_.refs_3_), channel_id=1, source_target_pairs={{0,2},{1,3},{2,0},{3,1},{4,6},{5,7},{6,4},{7,5},{8,10},{9,11},{10,... | collective-permute-start | bytes 1179656 | tf_op jit(solution)/shard_map/ppermute | solution.py:20
  25.3 27.9 %copy-start.6 = (bf16[96,2176]{1,0:T(8,128)(2,1)}, bf16[96,2176]{1,0:T(8,128)(2,1)S(1)}, u32[]{:S(2)}) copy-start(bf16[96,2176]{1,0:T(8,128)(2,1)S(1)} %pad_maximum_fusion.refs_6_.refs_11_) | copy-start | bytes 1253380
  25.3 10.5 %collective-permute-start.12 = (bf16[96,2176]{1,0:T(8,128)(2,1)S(1)}, bf16[96,2176]{1,0:T(8,128)(2,1)S(1)}, u32[]{:S(2)}, u32[]{:S(2)}) collective-permute-start(bf16[96,2176]{1,0:T(8,128)(2,1)S(1)} %pad_maximum_fusion.refs_6_.refs_11_), channel_id=1, source_target_pairs={{0,2},{1,3},{2,0},{3,1},{4,6},{5,7},{6,4},{7,5},{8,10},{9,11},{10,... | collective-permute-start | bytes 1253384 | tf_op jit(solution)/shard_map/ppermute | solution.py:20
  26.9 8.9 %collective-permute-start.3 = (bf16[96,2048]{1,0:T(8,128)(2,1)S(1)}, bf16[96,2048]{1,0:T(8,128)(2,1)S(1)}, u32[]{:S(2)}, u32[]{:S(2)}) collective-permute-start(bf16[96,2048]{1,0:T(8,128)(2,1)S(1)} %constant_dynamic-update-slice_fusion.refs_1_.refs_2_.refs_3_), channel_id=1, source_target_pairs={{0,1},{1,0},{2,3},{3,2},{4,5},{5,4},{6,7},{7,6},{8,9},{9,8},{10,11... | collective-permute-start | bytes 1179656 | tf_op jit(solution)/shard_map/ppermute | solution.py:20
  26.9 11.5 %collective-permute-start.6 = (bf16[96,2048]{1,0:T(8,128)(2,1)S(1)}, bf16[96,2048]{1,0:T(8,128)(2,1)S(1)}, u32[]{:S(2)}, u32[]{:S(2)}) collective-permute-start(bf16[96,2048]{1,0:T(8,128)(2,1)S(1)} %constant_dynamic-update-slice_fusion.refs_1_.refs_2_.refs_3_), channel_id=1, source_target_pairs={{0,16},{16,0},{1,17},{17,1},{2,18},{18,2},{3,19},{19,3},{4,20},{20... | collective-permute-start | bytes 1179656 | tf_op jit(solution)/shard_map/ppermute | solution.py:25
  28.4 10.0 %copy-start.1 = (bf16[96,2048]{1,0:T(8,128)(2,1)}, bf16[96,2048]{1,0:T(8,128)(2,1)S(1)}, u32[]{:S(2)}) copy-start(bf16[96,2048]{1,0:T(8,128)(2,1)S(1)} %collective-permute-done.4.refs_3_.refs_4_.refs_5_) | copy-start | bytes 1179652
  28.4 10.0 %collective-permute-start.5 = (bf16[96,2048]{1,0:T(8,128)(2,1)S(1)}, bf16[96,2048]{1,0:T(8,128)(2,1)S(1)}, u32[]{:S(2)}, u32[]{:S(2)}) collective-permute-start(bf16[96,2048]{1,0:T(8,128)(2,1)S(1)} %collective-permute-done.4.refs_3_.refs_4_.refs_5_), channel_id=1, source_target_pairs={{0,1},{1,0},{2,3},{3,2},{4,5},{5,4},{6,7},{7,6},{8,9},{9,8},{10,11... | collective-permute-start | bytes 1179656 | tf_op jit(solution)/shard_map/ppermute | solution.py:20
  28.6 24.6 %collective-permute-start.11 = (bf16[96,2176]{1,0:T(8,128)(2,1)S(1)}, bf16[96,2176]{1,0:T(8,128)(2,1)}, u32[]{:S(2)}, u32[]{:S(2)}) collective-permute-start(bf16[96,2176]{1,0:T(8,128)(2,1)S(1)} %pad_maximum_fusion.refs_6_.refs_11_), channel_id=1, source_target_pairs={{0,1},{1,0},{2,3},{3,2},{4,5},{5,4},{6,7},{7,6},{8,9},{9,8},{10,11... | collective-permute-start | bytes 1253384 | tf_op jit(solution)/shard_map/ppermute | solution.py:20
  35.8 17.5 %copy-start.16 = (bf16[96,2176]{1,0:T(8,128)(2,1)}, bf16[96,2176]{1,0:T(8,128)(2,1)S(1)}, u32[]{:S(2)}) copy-start(bf16[96,2176]{1,0:T(8,128)(2,1)S(1)} %collective-permute-done.12.refs_8_.refs_13_) | copy-start | bytes 1253380
  35.8 17.5 %collective-permute-start.13 = (bf16[96,2176]{1,0:T(8,128)(2,1)S(1)}, bf16[96,2176]{1,0:T(8,128)(2,1)}, u32[]{:S(2)}, u32[]{:S(2)}) collective-permute-start(bf16[96,2176]{1,0:T(8,128)(2,1)S(1)} %collective-permute-done.12.refs_8_.refs_13_), channel_id=1, source_target_pairs={{0,1},{1,0},{2,3},{3,2},{4,5},{5,4},{6,7},{7,6},{8,9},{9,8},{10,11... | collective-permute-start | bytes 1253384 | tf_op jit(solution)/shard_map/ppermute | solution.py:20
  35.8 2.7 %copy-start.2 = (bf16[96,2048]{1,0:T(8,128)(2,1)}, bf16[96,2048]{1,0:T(8,128)(2,1)S(1)}, u32[]{:S(2)}) copy-start(bf16[96,2048]{1,0:T(8,128)(2,1)S(1)} %collective-permute-done.3.refs_2_.refs_3_.refs_4_) | copy-start | bytes 1179652
  35.8 17.4 %collective-permute-start.14 = (bf16[96,2048]{1,0:T(8,128)(2,1)S(1)}, bf16[96,2048]{1,0:T(8,128)(2,1)S(1)}, u32[]{:S(2)}, u32[]{:S(2)}) collective-permute-start(bf16[96,2048]{1,0:T(8,128)(2,1)S(1)} %collective-permute-done.4.refs_3_.refs_4_.refs_5_), channel_id=1, source_target_pairs={{0,16},{16,0},{1,17},{17,1},{2,18},{18,2},{3,19},{19,3},{4,20},{20... | collective-permute-start | bytes 1179656 | tf_op jit(solution)/shard_map/ppermute | solution.py:25
  38.4 0.7 copy-start.3
  38.4 0.9 copy-start.5
  42.7 5.6 %collective-permute-start.7 = (f32[16,384]{1,0:T(8,128)}, f32[16,384]{1,0:T(8,128)S(1)}, u32[]{:S(2)}, u32[]{:S(2)}) collective-permute-start(f32[16,384]{1,0:T(8,128)} %shard_map.110), channel_id=1, source_target_pairs={{0,16},{16,0},{1,17},{17,1},{2,18},{18,2},{3,19},{19,3},{4,20},{20... | collective-permute-start | bytes 73736 | tf_op jit(solution)/shard_map/ppermute | solution.py:25
  44.3 30.5 %collective-permute-start.17 = (bf16[96,2176]{1,0:T(8,128)(2,1)S(1)}, bf16[96,2176]{1,0:T(8,128)(2,1)S(1)}, u32[]{:S(2)}, u32[]{:S(2)}) collective-permute-start(bf16[96,2176]{1,0:T(8,128)(2,1)S(1)} %pad_maximum_fusion.refs_6_.refs_11_), channel_id=1, source_target_pairs={{0,16},{16,0},{1,17},{17,1},{2,18},{18,2},{3,19},{19,3},{4,20},{20... | collective-permute-start | bytes 1253384 | tf_op jit(solution)/shard_map/ppermute | solution.py:25
  48.3 31.1 %collective-permute-start.19 = (bf16[96,2176]{1,0:T(8,128)(2,1)S(1)}, bf16[96,2176]{1,0:T(8,128)(2,1)S(1)}, u32[]{:S(2)}, u32[]{:S(2)}) collective-permute-start(bf16[96,2176]{1,0:T(8,128)(2,1)S(1)} %collective-permute-done.12.refs_8_.refs_13_), channel_id=1, source_target_pairs={{0,16},{16,0},{1,17},{17,1},{2,18},{18,2},{3,19},{19,3},{4,20},{20... | collective-permute-start | bytes 1253384 | tf_op jit(solution)/shard_map/ppermute | solution.py:25
  53.2 21.6 %copy-start.4 = (bf16[96,2048]{1,0:T(8,128)(2,1)S(1)}, bf16[96,2048]{1,0:T(8,128)(2,1)}, u32[]{:S(2)}) copy-start(bf16[96,2048]{1,0:T(8,128)(2,1)} %copy-done.3) | copy-start | bytes 1179652
  53.2 0.8 copy-start.12
  71.0 6.8 %collective-permute-start.25 = (bf16[2,2,4,24]{3,2,1,0:T(4,128)(2,1)S(1)}, bf16[2,2,4,24]{3,2,1,0:T(4,128)(2,1)S(1)}, u32[]{:S(2)}, u32[]{:S(2)}) collective-permute-start(bf16[2,2,4,24]{3,2,1,0:T(4,128)(2,1)S(1)} %convert_element_type.98), channel_id=1, source_target_pairs={{0,4},{1,5},{2,6},{3,7},{4,0},{5,1},{6,2},{7,3},{8,12},{9,13},{10,... | collective-permute-start | bytes 2312 | tf_op jit(solution)/shard_map/ppermute | solution.py:20
  74.8 22.6 %collective-permute-start.31 = (bf16[96,2048]{1,0:T(8,128)(2,1)S(1)}, bf16[96,2048]{1,0:T(8,128)(2,1)S(1)}, u32[]{:S(2)}, u32[]{:S(2)}) collective-permute-start(bf16[96,2048]{1,0:T(8,128)(2,1)S(1)} %copy-done.4), channel_id=1, source_target_pairs={{0,1},{1,0},{2,3},{3,2},{4,5},{5,4},{6,7},{7,6},{8,9},{9,8},{10,11... | collective-permute-start | bytes 1179656 | tf_op jit(solution)/shard_map/ppermute | solution.py:20
  74.8 12.2 %copy-start.7 = (bf16[96,2176]{1,0:T(8,128)(2,1)}, bf16[96,2176]{1,0:T(8,128)(2,1)S(1)}, u32[]{:S(2)}) copy-start(bf16[96,2176]{1,0:T(8,128)(2,1)S(1)} %collective-permute-done.17.refs_2_.refs_15_) | copy-start | bytes 1253380
  74.8 11.6 %collective-permute-start.18 = (bf16[96,2176]{1,0:T(8,128)(2,1)S(1)}, bf16[96,2176]{1,0:T(8,128)(2,1)S(1)}, u32[]{:S(2)}, u32[]{:S(2)}) collective-permute-start(bf16[96,2176]{1,0:T(8,128)(2,1)S(1)} %collective-permute-done.17.refs_2_.refs_15_), channel_id=1, source_target_pairs={{0,1},{1,0},{2,3},{3,2},{4,5},{5,4},{6,7},{7,6},{8,9},{9,8},{10,11... | collective-permute-start | bytes 1253384 | tf_op jit(solution)/shard_map/ppermute | solution.py:20
  75.3 7.2 %collective-permute-start.27 = (bf16[2,2,4,24]{3,2,1,0:T(4,128)(2,1)S(1)}, bf16[2,2,4,24]{3,2,1,0:T(4,128)(2,1)S(1)}, u32[]{:S(2)}, u32[]{:S(2)}) collective-permute-start(bf16[2,2,4,24]{3,2,1,0:T(4,128)(2,1)S(1)} %convert_element_type.98), channel_id=1, source_target_pairs={{0,12},{1,13},{2,14},{3,15},{4,8},{5,9},{6,10},{7,11},{8,4},{9,5},... | collective-permute-start | bytes 2312 | tf_op jit(solution)/shard_map/ppermute | solution.py:20
  77.9 4.6 %collective-permute-start.26 = (bf16[2,2,4,24]{3,2,1,0:T(4,128)(2,1)S(1)}, bf16[2,2,4,24]{3,2,1,0:T(4,128)(2,1)S(1)}, u32[]{:S(2)}, u32[]{:S(2)}) collective-permute-start(bf16[2,2,4,24]{3,2,1,0:T(4,128)(2,1)S(1)} %convert_element_type.98), channel_id=1, source_target_pairs={{0,8},{1,9},{2,10},{3,11},{4,12},{5,13},{6,14},{7,15},{8,0},{9,1},... | collective-permute-start | bytes 2312 | tf_op jit(solution)/shard_map/ppermute | solution.py:20
  79.4 7.6 %copy-start.8 = (bf16[96,2176]{1,0:T(8,128)(2,1)}, bf16[96,2176]{1,0:T(8,128)(2,1)S(1)}, u32[]{:S(2)}) copy-start(bf16[96,2176]{1,0:T(8,128)(2,1)S(1)} %collective-permute-done.19.refs_4_.refs_17_) | copy-start | bytes 1253380
  79.4 7.6 %collective-permute-start.16 = (bf16[96,2048]{1,0:T(8,128)(2,1)}, bf16[96,2048]{1,0:T(8,128)(2,1)S(1)}, u32[]{:S(2)}, u32[]{:S(2)}) collective-permute-start(bf16[96,2048]{1,0:T(8,128)(2,1)} %get-tuple-element.21), channel_id=1, source_target_pairs={{0,1},{1,0},{2,3},{3,2},{4,5},{5,4},{6,7},{7,6},{8,9},{9,8},{10,11... | collective-permute-start | bytes 1179656 | tf_op jit(solution)/shard_map/ppermute | solution.py:20
  82.4 4.6 %collective-permute-start.20 = (bf16[96,2176]{1,0:T(8,128)(2,1)S(1)}, bf16[96,2176]{1,0:T(8,128)(2,1)S(1)}, u32[]{:S(2)}, u32[]{:S(2)}) collective-permute-start(bf16[96,2176]{1,0:T(8,128)(2,1)S(1)} %collective-permute-done.19.refs_4_.refs_17_), channel_id=1, source_target_pairs={{0,1},{1,0},{2,3},{3,2},{4,5},{5,4},{6,7},{7,6},{8,9},{9,8},{10,11... | collective-permute-start | bytes 1253384 | tf_op jit(solution)/shard_map/ppermute | solution.py:20
  82.6 3.8 %collective-permute-start.28 = (bf16[4,2,2,4,24]{4,3,2,1,0:T(4,128)(2,1)S(1)}, bf16[4,2,2,4,24]{4,3,2,1,0:T(4,128)(2,1)S(1)}, u32[]{:S(2)}, u32[]{:S(2)}) collective-permute-start(bf16[4,2,2,4,24]{4,3,2,1,0:T(4,128)(2,1)S(1)} %pad_maximum_fusion.6), channel_id=1, source_target_pairs={{0,2},{1,3},{2,0},{3,1},{4,6},{5,7},{6,4},{7,5},{8,10},{9,11},{10,... | collective-permute-start | bytes 9224 | tf_op jit(solution)/shard_map/ppermute | solution.py:20
  86.4 11.0 %collective-permute-start.32 = (bf16[96,2048]{1,0:T(8,128)(2,1)}, bf16[96,2048]{1,0:T(8,128)(2,1)}, u32[]{:S(2)}, u32[]{:S(2)}) collective-permute-start(bf16[96,2048]{1,0:T(8,128)(2,1)} %copy-done.12), channel_id=1, source_target_pairs={{0,1},{1,0},{2,3},{3,2},{4,5},{5,4},{6,7},{7,6},{8,9},{9,8},{10,11... | collective-permute-start | bytes 1179656 | tf_op jit(solution)/shard_map/ppermute | solution.py:20
  86.4 0.8 copy-start.9
  86.4 15.8 %collective-permute-start.15 = (bf16[96,2048]{1,0:T(8,128)(2,1)}, bf16[96,2048]{1,0:T(8,128)(2,1)S(1)}, u32[]{:S(2)}, u32[]{:S(2)}) collective-permute-start(bf16[96,2048]{1,0:T(8,128)(2,1)} %get-tuple-element.19), channel_id=1, source_target_pairs={{0,1},{1,0},{2,3},{3,2},{4,5},{5,4},{6,7},{7,6},{8,9},{9,8},{10,11... | collective-permute-start | bytes 1179656 | tf_op jit(solution)/shard_map/ppermute | solution.py:20
  87.0 0.8 copy-start.14
  87.0 0.9 copy-start.10
  87.9 14.3 %copy-start.11 = (bf16[96,2048]{1,0:T(8,128)(2,1)S(1)}, bf16[96,2048]{1,0:T(8,128)(2,1)}, u32[]{:S(2)}) copy-start(bf16[96,2048]{1,0:T(8,128)(2,1)} %get-tuple-element.18) | copy-start | bytes 1179652
  89.9 12.2 %collective-permute-start.21 = (bf16[96,2048]{1,0:T(8,128)(2,1)}, bf16[96,2048]{1,0:T(8,128)(2,1)S(1)}, u32[]{:S(2)}, u32[]{:S(2)}) collective-permute-start(bf16[96,2048]{1,0:T(8,128)(2,1)} %shard_map.113), channel_id=1, source_target_pairs={{0,2},{1,3},{2,0},{3,1},{4,6},{5,7},{6,4},{7,5},{8,10},{9,11},{10,... | collective-permute-start | bytes 1179656 | tf_op jit(solution)/shard_map/ppermute | solution.py:20
  91.5 1.3 %collective-permute-start.29 = (bf16[4,2,2,2,4,24]{5,4,3,2,1,0:T(4,128)(2,1)S(1)}, bf16[4,2,2,2,4,24]{5,4,3,2,1,0:T(4,128)(2,1)S(1)}, u32[]{:S(2)}, u32[]{:S(2)}) collective-permute-start(bf16[4,2,2,2,4,24]{5,4,3,2,1,0:T(4,128)(2,1)S(1)} %get-tuple-element.35), channel_id=1, source_target_pairs={{0,1},{1,0},{2,3},{3,2},{4,5},{5,4},{6,7},{7,6},{8,9},{9,8},{10,11... | collective-permute-start | bytes 18440 | tf_op jit(solution)/shard_map/ppermute | solution.py:20
  93.0 3.8 %collective-permute-start.30 = (bf16[16,384]{1,0:T(8,128)(2,1)S(1)}, bf16[16,384]{1,0:T(8,128)(2,1)S(1)}, u32[]{:S(2)}, u32[]{:S(2)}) collective-permute-start(bf16[16,384]{1,0:T(8,128)(2,1)S(1)} %reshape.28), channel_id=1, source_target_pairs={{0,16},{16,0},{1,17},{17,1},{2,18},{18,2},{3,19},{19,3},{4,20},{20... | collective-permute-start | bytes 36872 | tf_op jit(solution)/shard_map/ppermute | solution.py:25
  97.4 0.8 copy-start.13
  102.3 19.7 %collective-permute-start.24 = (bf16[24,2048]{1,0:T(8,128)(2,1)S(1)}, bf16[24,2048]{1,0:T(8,128)(2,1)S(1)}, u32[]{:S(2)}, u32[]{:S(2)}) collective-permute-start(bf16[24,2048]{1,0:T(8,128)(2,1)S(1)} %get-tuple-element.32), channel_id=1, source_target_pairs={{0,12},{1,13},{2,14},{3,15},{4,8},{5,9},{6,10},{7,11},{8,4},{9,5},... | collective-permute-start | bytes 294920 | tf_op jit(solution)/shard_map/ppermute | solution.py:20
  103.8 18.2 %collective-permute-start.23 = (bf16[24,2048]{1,0:T(8,128)(2,1)S(1)}, bf16[24,2048]{1,0:T(8,128)(2,1)S(1)}, u32[]{:S(2)}, u32[]{:S(2)}) collective-permute-start(bf16[24,2048]{1,0:T(8,128)(2,1)S(1)} %get-tuple-element.33), channel_id=1, source_target_pairs={{0,8},{1,9},{2,10},{3,11},{4,12},{5,13},{6,14},{7,15},{8,0},{9,1},... | collective-permute-start | bytes 294920 | tf_op jit(solution)/shard_map/ppermute | solution.py:20
  104.3 17.7 %collective-permute-start.22 = (bf16[24,2048]{1,0:T(8,128)(2,1)S(1)}, bf16[24,2048]{1,0:T(8,128)(2,1)S(1)}, u32[]{:S(2)}, u32[]{:S(2)}) collective-permute-start(bf16[24,2048]{1,0:T(8,128)(2,1)S(1)} %get-tuple-element.31), channel_id=1, source_target_pairs={{0,4},{1,5},{2,6},{3,7},{4,0},{5,1},{6,2},{7,3},{8,12},{9,13},{10,... | collective-permute-start | bytes 294920 | tf_op jit(solution)/shard_map/ppermute | solution.py:20
  106.8 15.2 %copy-start.15 = (bf16[2048,16]{0,1:T(8,128)(2,1)S(1)}, bf16[2048,16]{0,1:T(8,128)(2,1)}, u32[]{:S(2)}) copy-start(bf16[2048,16]{0,1:T(8,128)(2,1)} %param.10) | copy-start | bytes 196612

commit v4 on v3

v4 whole, which is shorter than its diff:
```python
import functools

import jax
import jax.numpy as jnp
from jax import lax
from jax.experimental import pallas as pl
from jax.experimental.pallas import tpu as pltpu
from jax.sharding import PartitionSpec as P

PASSES = 3
LANES = 128
SUBLANES = 8
FF_TILE = 256
ROW_TILE = 32
GRANT = 56 << 20
ROWS_AT_ONCE = 1024


def swap_expert(array, offset):
    size = lax.axis_size("expert")
    return lax.ppermute(array, "expert", [(i, i ^ offset) for i in range(size)])


def swap_group(array, offset):
    size = lax.axis_size("dp")
    return lax.ppermute(array, "dp", [(i, i ^ offset) for i in range(size)])


def contract(left, right, left_dim, right_dim):
    return lax.dot_general(
        left, right, (((left_dim,), (right_dim,)), ((), ())), preferred_element_type=jnp.float32
    )


def balancer_forward_pass(logits):
    densities = [jnp.exp(logits)]
    quotients, column_totals, row_totals = ([], [], [])
    for _ in range(PASSES):
        column_sum = jnp.sum(densities[-1], axis=1, keepdims=True)
        quotient = densities[-1] / column_sum
        row_sum = jnp.sum(quotient, axis=0, keepdims=True)
        densities.append(quotient / row_sum)
        quotients.append(quotient)
        column_totals.append(column_sum)
        row_totals.append(row_sum)
    return (densities, quotients, column_totals, row_totals)


def balancer_adjoint_pass(density_gradient, densities, quotients, column_totals, row_totals):
    for repeat in reversed(range(PASSES)):
        inner = jnp.sum(density_gradient * densities[repeat + 1], axis=0, keepdims=True)
        quotient_grad = (density_gradient - inner) / row_totals[repeat]
        shared = jnp.sum(quotient_grad * quotients[repeat], axis=1, keepdims=True)
        density_gradient = (quotient_grad - shared) / column_totals[repeat]
    return density_gradient * densities[0]


def round_up(value, unit):
    return -(-value // unit) * unit


def pack_kernel(ids_ref, tok_ref, router_ref, out):
    experts = router_ref.shape[0]
    rest = contract(tok_ref[...], router_ref[...], 1, 1)
    lane = lax.broadcasted_iota(jnp.int32, out.shape, 1)
    packed = jnp.zeros(out.shape, jnp.float32)
    for pick in range(ids_ref.shape[1]):
        packed += jnp.where(lane == ids_ref[:, pick : pick + 1], 1.0, 0.0)
    row = lax.broadcasted_iota(jnp.int32, (experts, out.shape[1]), 0)
    column = lax.broadcasted_iota(jnp.int32, (experts, out.shape[1]), 1)
    for term in range(1, 4):
        part = rest.astype(jnp.bfloat16)
        rest = rest - part.astype(jnp.float32)
        place = jnp.where(column == row + term * experts, 1.0, 0.0).astype(jnp.bfloat16)
        packed += contract(part, place, 1, 0)
    out[...] = packed.astype(jnp.bfloat16)


def gate_kernel(parts, experts, me_ref, *refs):
    grad, gate_ref, logits_ref, packed, sems = (refs[:parts], *refs[parts:])
    copies = Copies(sems)
    extra = packed.shape[1]
    wait(copies.stack(grad, packed, pl.ds(grad[0].shape[1] - extra, extra)))
    turned = jnp.transpose(packed[...].astype(jnp.float32))
    columns = []
    for group in range(logits_ref.shape[1] // packed.shape[0]):
        at = (3 * group + 1) * experts
        terms = [turned[at + i * experts : at + (i + 1) * experts] for i in range(3)]
        columns.append(terms[0] + terms[1] + terms[2])
    logits = jnp.concatenate(columns, axis=1)
    logits_ref[...] = logits
    gates = experts * balancer_forward_pass(logits)[0][-1]
    row = lax.broadcasted_iota(jnp.int32, gates.shape, 0)
    mine = jnp.sum(jnp.where(row == me_ref[0], gates, 0.0), axis=0, keepdims=True)
    gate_ref[...] = jnp.transpose(jnp.broadcast_to(mine, (LANES, gates.shape[1])))


def kernel_call(
    kernel, scalars, small, large, out_shape, scratch, copies, large_outs=0, after=(), macs=10**6
):
    whole = pl.BlockSpec(memory_space=pltpu.VMEM)
    outside = pl.BlockSpec(memory_space=pltpu.HBM)
    inputs = len(scalars) + len(small) + len(large)

    def body(*refs):
        kernel(*refs[:inputs], *refs[inputs + len(after) :])

    return pl.pallas_call(
        body,
        in_specs=[pl.BlockSpec(memory_space=pltpu.SMEM)] * len(scalars)
        + [whole] * len(small)
        + [outside] * (len(large) + len(after)),
        out_specs=[outside] * large_outs + [whole] * (len(out_shape) - large_outs),
        out_shape=out_shape,
        scratch_shapes=[*scratch] + [pltpu.SemaphoreType.DMA((copies,))] * (copies > 0),
        compiler_params=pltpu.CompilerParams(vmem_limit_bytes=GRANT),
        cost_estimate=pl.CostEstimate(
            flops=2 * macs, bytes_accessed=macs // 200, transcendentals=macs // 10000
        ),
    )(*scalars, *small, *large, *after)


def shape(rows, columns, dtype=jnp.bfloat16):
    return jax.ShapeDtypeStruct((rows, columns), dtype)


def tiles(extent, tile):
    tile = tile if extent % tile == 0 else extent
    return [slice(at, at + tile) for at in range(0, extent, tile)]


class Copies:
    def __init__(self, sems):
        self.sems, self.count = (sems, 0)

    def start(self, source, target):
        copy = pltpu.make_async_copy(source, target, self.sems.at[self.count])
        self.count += 1
        copy.start()
        return copy

    def stack(self, parts, target, columns=slice(None)):
        started, at = ([], 0)
        for part in parts:
            rows = part.shape[0]
            started.append(self.start(part.at[:, columns], target.at[pl.ds(at, rows), :]))
            at += rows
        return started


def wait(copies):
    for copy in copies:
        copy.wait()


def loop(count, body, rolled=True):
    if not rolled:
        for index in range(count):
            body(index)
        return

    def step(index, carry):
        body(index)
        return carry

    lax.fori_loop(0, count, step, 0)


class Tiles:
    def __init__(self, copies, source, target, dim, tile):
        extent = target.shape[dim]
        self.tile = tile if extent % tile == 0 else extent
        self.count = extent // self.tile
        self.source, self.target, self.dim = (source, target, dim)
        self.sems, self.base = (copies.sems, copies.count)
        copies.count += self.count
        for index in range(self.count):
            self.copy(index).start()

    def here(self, index):
        start = index * self.tile
        if not isinstance(index, int):
            start = pl.multiple_of(start, self.tile)
        cut = pl.ds(start, self.tile)
        return (cut, slice(None)) if self.dim == 0 else (slice(None), cut)

    def copy(self, index):
        here = self.here(index)
        return pltpu.make_async_copy(
            self.source.at[here], self.target.at[here], self.sems.at[self.base + index]
        )


def mask_of(me_ref, picked):
    row = lax.broadcasted_iota(jnp.int32, (LANES, LANES), 0)
    mine = jnp.where(row == me_ref[0], 1.0, 0.0).astype(jnp.bfloat16)
    return contract(picked, mine, 1, 0)


def spread(lanes, width):
    return jnp.concatenate([lanes] * (width // LANES), axis=1)


def rounded(array):
    return array.astype(jnp.bfloat16).astype(jnp.float32)


def inner_terms(gate_pre, up_pre, hidden_grad):
    sigmoid_gate = jax.nn.sigmoid(gate_pre)
    activation = gate_pre * sigmoid_gate
    hidden = activation * up_pre
    gate_grad = hidden_grad * up_pre * sigmoid_gate * (1.0 + gate_pre * (1.0 - sigmoid_gate))
    up_grad = hidden_grad * activation
    half = jnp.bfloat16
    return hidden, gate_grad.astype(half), up_grad.astype(half)


def project_start(copies, tok, rows_in, sources, weights):
    width = rows_in.shape[1]
    tile = 2 * FF_TILE if width % (2 * FF_TILE) == 0 else width
    blocks = []
    for start in range(0, width, tile):
        cut = pl.ds(start, tile)
        here, at = ([], 0)
        for part in tok:
            rows = pl.ds(at, part.shape[0])
            here.append(copies.start(part.at[:, cut], rows_in.at[rows, cut]))
            at += part.shape[0]
        for source, weight in zip(sources, weights):
            here.append(copies.start(source.at[0, cut, :], weight.at[cut, :]))
        blocks.append((slice(start, start + tile), here))
    return blocks


def project(blocks, rows_in, targets, weights):
    for cut, here in blocks:
        wait(here)
        for target, weight in zip(targets, weights):
            value = contract(rows_in[:, cut], weight[cut, :], 1, 0)
            if cut.start == 0:
                target[...] = value
            else:
                target[...] += value


def backward(grad_here, rows_grad, hidden_grad, weight):
    wait(grad_here)

    def body(index):
        weight.copy(index).wait()
        cut = weight.here(index)[0]
        rows = rows_grad[:, : weight.target.shape[1]]
        hidden_grad[:, cut] = contract(rows, weight.target[cut, :], 1, 1)

    loop(weight.count, body)


def row_cut(index):
    start = index * ROW_TILE
    return pl.ds(start if isinstance(index, int) else pl.multiple_of(start, ROW_TILE), ROW_TILE)


def expert_kernel(parts, me_ref, gate_ref, place_ref, *refs):
    tok, grad, sources = (refs[:parts], refs[parts : 2 * parts], refs[2 * parts : 2 * parts + 3])
    refs = refs[2 * parts + 3 :]
    sum_outs, scaled_outs = (refs[:parts], refs[parts : parts + 3])
    rows_in, rows_grad, gate_pre, up_pre, hidden_grad, *refs = refs[parts + 3 :]
    wg, wu, wd, gate_grad, up_grad, hs, gs, us, sums, column, gate, sems = refs
    copies = Copies(sems)
    width = wg.shape[0]
    rows = gate_pre.shape[0]
    ff_width = wd.shape[0]
    blocks = project_start(copies, tok, rows_in, sources, (wg, wu))
    grad_here = copies.stack(grad, rows_grad)
    down = Tiles(copies, sources[2].at[0], wd, 0, FF_TILE)
    project(blocks, rows_in, (gate_pre, up_pre), (wg, wu))
    backward(grad_here, rows_grad, hidden_grad, down)
    gate[...] = mask_of(me_ref, rows_grad[:, width : width + LANES])
    column[...] = gate[...]
    gate[...] *= gate_ref[:rows, :]

    def terms(index):
        cut = row_cut(index)
        values = inner_terms(gate_pre[cut, :], up_pre[cut, :], hidden_grad[cut, :])
        gate_grad[cut, :] = values[1]
        up_grad[cut, :] = values[2]
        sent = spread(rounded(gate[cut, :]), ff_width)
        for value, target in zip(values, (hs, gs, us)):
            target[cut, :] = (sent * value).astype(jnp.bfloat16)
        product = hidden_grad[cut, :] * values[0]
        column[cut, :] *= sum(product[:, at] for at in tiles(ff_width, LANES))

    loop(rows // ROW_TILE, terms)
    results = [copies.start(source, out) for source, out in zip((hs, gs, us), scaled_outs)]
    ones = jnp.ones((SUBLANES, LANES), jnp.bfloat16)
    high = column[...].astype(jnp.bfloat16)
    low = (column[...] - high.astype(jnp.float32)).astype(jnp.bfloat16)
    score = (contract(ones, high, 1, 1) + contract(ones, low, 1, 1)).astype(jnp.bfloat16)
    score = contract(score, order_matrix(place_ref, round_up(rows, LANES)), 1, 1)
    block = placed([score[:1, at] for at in tiles(score.shape[1], LANES)], sums.shape[0])
    sums[:, width:] = block.astype(sums.dtype)
    chunk = sum_outs[0].shape[0]
    for at in range(0, rows, chunk):
        sums[at : at + chunk, width:] = sums[:chunk, width:]

    tile = 2 * FF_TILE if width % (2 * FF_TILE) == 0 else width

    def products(index):
        cut = pl.ds(pl.multiple_of(index * tile, tile), tile)
        part = contract(gate_grad[...], wg[cut, :], 1, 1)
        part += contract(up_grad[...], wu[cut, :], 1, 1)
        sums[:, cut] = (spread(gate[...], tile) * part).astype(jnp.bfloat16)

    loop(width // tile, products)
    at = 0
    for out in sum_outs:
        here = sums.at[pl.ds(at, out.shape[0]), pl.ds(0, out.shape[1])]
        results.append(copies.start(here, out))
        at += out.shape[0]
    wait(results)


def expert_call(me, gate, place, tok, grad, weights, after):
    rows = sum(part.shape[0] for part in tok)
    width, ff_width = weights[0].shape[1:]
    half = jnp.bfloat16
    narrow = pltpu.VMEM((rows, ff_width), half)
    return kernel_call(
        functools.partial(expert_kernel, len(tok)), (me,), (gate, place),
        (*tok, *grad, *weights),
        [shape(part.shape[0], width + LANES * (at > 1)) for at, part in enumerate(tok)]
        + [shape(rows, ff_width)] * 3,
        [pltpu.VMEM((rows, width), half), pltpu.VMEM((rows, grad[0].shape[1]), half)]
        + [pltpu.VMEM((rows, ff_width), jnp.float32)] * 3
        + [pltpu.VMEM((width, ff_width), half)] * 2 + [pltpu.VMEM((ff_width, width), half)]
        + [narrow] * 5 + [pltpu.VMEM((rows, width + LANES), half)]
        + [pltpu.VMEM((rows, LANES), jnp.float32)] * 2,
        2 * len(tok) + (len(tok) + 2) * len(tiles(width, 2 * FF_TILE))
        + len(tiles(ff_width, FF_TILE)) + 3,
        len(tok) + 3, after, 5 * rows * width * ff_width,
    )


def placed(rows, height):
    index = lax.broadcasted_iota(jnp.int32, (height, LANES), 0)
    block = jnp.zeros((height, LANES), jnp.float32)
    for at, row in enumerate(rows):
        block = jnp.where(index == at, jnp.broadcast_to(row, block.shape), block)
    return block


def first_rows(block, count):
    block = block.astype(jnp.float32)
    return [block[at : at + 1, :] for at in range(count)]


def order_matrix(place_ref, height):
    count = place_ref.shape[1]
    row = lax.broadcasted_iota(jnp.int32, (height, count), 0)
    return jnp.where(row == place_ref[...], 1.0, 0.0).astype(jnp.bfloat16)


def near_kernel(pieces, keep, got, out, keep_here, got_here, total, sems):
    copies = Copies(sems)
    wait([copies.start(keep, keep_here), copies.start(got, got_here)])
    width = total.shape[1] - LANES
    total[:, :width] = (
        keep_here[:, :width].astype(jnp.float32) + got_here[:, :width].astype(jnp.float32)
    ).astype(total.dtype)
    scores = first_rows(keep_here[: 2 * SUBLANES, width:], pieces)
    scores += first_rows(got_here[: 2 * SUBLANES, width:], pieces)
    total[:, width:] = placed(scores, total.shape[0]).astype(total.dtype)
    wait([copies.start(total, out)])


def ready_kernel(pieces, keep, got, near, across, *refs):
    outs, refs = (refs[: len(refs) - 6], refs[len(refs) - 6 :])
    keep_here, got_here, near_here, across_here, made, sems = refs
    copies = Copies(sems)
    wait(
        [
            copies.start(keep, keep_here), copies.start(got, got_here),
            copies.start(near, near_here), copies.start(across, across_here),
        ]
    )
    far = made.shape[0]
    rows = made.shape[1]
    width = keep_here.shape[1]
    scores = first_rows(near_here[: 4 * SUBLANES, width:], 2 * pieces)
    scores += first_rows(across_here[: 4 * SUBLANES, width:], 2 * pieces)
    block = placed(scores, rows)
    total = keep_here[...].astype(jnp.float32) + got_here[...].astype(jnp.float32)
    total += across_here[:, :width].astype(jnp.float32)
    results = []
    for k in range(far):
        made[k, :, :width] = total[k * rows : (k + 1) * rows, :].astype(made.dtype)
        made[k, :, width:] = block.astype(made.dtype)
        results.append(copies.start(made.at[k], outs[k]))
    wait(results)


def others_kernel(parts, start, me_ref, gate_ref, *refs):
    tok, grad, sources = (refs[:parts], refs[parts : 2 * parts], refs[2 * parts : 2 * parts + 3])
    outs, refs = (refs[2 * parts + 3 : 2 * parts + 6], refs[2 * parts + 6 :])
    rows_in, rows_grad, gate_pre, up_pre, hidden_grad, wg, wu, wd, hs, gs, us, gate, sems = refs
    copies = Copies(sems)
    rows, width = rows_in.shape
    ff_width = wd.shape[0]
    blocks = project_start(copies, tok, rows_in, sources, (wg, wu))
    grad_here = copies.stack(grad, rows_grad)
    down = Tiles(copies, sources[2].at[0], wd, 0, FF_TILE)
    project(blocks, rows_in, (gate_pre, up_pre), (wg, wu))
    backward(grad_here, rows_grad, hidden_grad, down)
    gate[...] = mask_of(me_ref, rows_grad[:, width : width + LANES])
    gate[...] *= gate_ref[start : start + rows, :]

    def terms(index):
        cut = row_cut(index)
        values = inner_terms(gate_pre[cut, :], up_pre[cut, :], hidden_grad[cut, :])
        sent = spread(rounded(gate[cut, :]), ff_width)
        for value, target in zip(values, (hs, gs, us)):
            target[cut, :] = (sent * value).astype(jnp.bfloat16)

    loop(rows // ROW_TILE, terms)
    wait([copies.start(source, out) for source, out in zip((hs, gs, us), outs)])


def others_call(me, gate, tok, grad, weights, start, after=()):
    rows = sum(part.shape[0] for part in tok)
    width, ff_width = weights[0].shape[1:]
    half = jnp.bfloat16
    return kernel_call(
        functools.partial(others_kernel, len(tok), start), (me,), (gate,), (*tok, *grad, *weights),
        [shape(rows, ff_width)] * 3,
        [pltpu.VMEM((rows, width), half), pltpu.VMEM((rows, grad[0].shape[1]), half)]
        + [pltpu.VMEM((rows, ff_width), jnp.float32)] * 3
        + [pltpu.VMEM((width, ff_width), half)] * 2 + [pltpu.VMEM((ff_width, width), half)]
        + [pltpu.VMEM((rows, ff_width), half)] * 3 + [pltpu.VMEM((rows, LANES), jnp.float32)],
        len(tok) + (len(tok) + 2) * len(tiles(width, 2 * FF_TILE))
        + len(tiles(ff_width, FF_TILE)) + 3,
        3, after, 3 * rows * width * ff_width,
    )


def weights_kernel(parts, given, steps, group_ref, *refs):
    tok, grad, given_refs = (refs[:parts], refs[parts : 2 * parts], refs[2 * parts :][: 3 * given])
    outs, refs = (refs[2 * parts + 3 * given :][:3], refs[2 * parts + 3 * given + 3 :])
    hs, gs, us, tok_half, grad_all, hidden_half, *tile_out, sems = refs
    copies = Copies(sems)
    width = grad_all.shape[1]
    half = outs[0].shape[1]
    half_ff = outs[2].shape[1]
    blocks = [given_refs[kind * given : (kind + 1) * given] for kind in range(3)]
    mine = pl.ds(pl.multiple_of(group_ref[0] * half, LANES), half)
    gate_here = copies.stack(tok, tok_half, mine) + copies.stack(blocks[1], gs)
    up_here = copies.stack(blocks[2], us)
    down_here = copies.stack(blocks[0], hs) + copies.stack(grad, grad_all, pl.ds(0, width))
    base = copies.count

    def result(which, step):
        tile = tile_out[which].shape[1 if which < 2 else 2]
        at = step * tile if isinstance(step, int) else pl.multiple_of(step * tile, tile)
        cut = pl.ds(at, tile)
        target = outs[which].at[0, cut, :] if which < 2 else outs[which].at[0, :, cut]
        return cut, pltpu.make_async_copy(
            tile_out[which].at[step], target, sems.at[base + which * steps + step]
        )

    def form(which, left, right):
        def body(step):
            cut, copy = result(which, step)
            sides = (left[:, cut], right[...]) if which < 2 else (left[...], right[:, cut])
            tile_out[which][step] = contract(*sides, 0, 0).astype(tile_out[which].dtype)
            copy.start()

        loop(steps, body, rolled=False)

    wait(gate_here)
    form(0, tok_half, gs)
    wait(up_here)
    form(1, tok_half, us)
    wait(down_here)
    if half_ff % LANES == 0:
        place = pl.ds(pl.multiple_of(group_ref[0] * half_ff, LANES), half_ff)
        hidden_half[...] = hs[:, place]
    else:
        for index in range(hs.shape[1] // half_ff):

            @pl.when(group_ref[0] == index)
            def _():
                hidden_half[...] = hs[:, index * half_ff : (index + 1) * half_ff]

    form(2, hidden_half, grad_all)
    wait([result(which, step)[1] for which in range(3) for step in range(steps)])


def weights_call(group, groups, tok, grad, given, dtype, after=()):
    width, ff_width = (tok[0].shape[1], given[0][0].shape[1])
    half, half_ff = (width // groups, ff_width // groups)
    rows = sum(part.shape[0] for part in tok)
    steps = max(s for s in (4, 2, 1) if half % (s * LANES) == 0)
    low = jnp.bfloat16
    scratch = [pltpu.VMEM((rows, ff_width), low)] * 3
    scratch += [
        pltpu.VMEM((rows, half), low),
        pltpu.VMEM((rows, width), low),
        pltpu.VMEM((rows, half_ff), low),
        pltpu.VMEM((steps, half // steps, ff_width), dtype),
        pltpu.VMEM((steps, half // steps, ff_width), dtype),
        pltpu.VMEM((steps, half_ff, width // steps), dtype),
    ]
    return kernel_call(
        functools.partial(weights_kernel, len(tok), len(given), steps), (group,), (),
        (*tok, *grad, *(block[kind] for kind in range(3) for block in given)),
        [
            jax.ShapeDtypeStruct((1, half, ff_width), dtype),
            jax.ShapeDtypeStruct((1, half, ff_width), dtype),
            jax.ShapeDtypeStruct((1, half_ff, width), dtype),
        ],
        scratch, 2 * len(tok) + 3 * len(given) + 3 * steps, 3, after, 3 * rows * half * ff_width,
    )


def router_kernel(parts, me_ref, *refs):
    logits_ref, score_ref, place_ref, *tok = refs[: 3 + parts]
    grad_ref, router_ref, rows, sems = refs[3 + parts :]
    copies = Copies(sems)
    rows_here = copies.stack(tok, rows)
    logits = logits_ref[...]
    experts = logits.shape[0]
    row = lax.broadcasted_iota(jnp.int32, (experts, experts), 0)
    column = lax.broadcasted_iota(jnp.int32, (experts, experts), 1)
    unswap = jnp.where((row ^ me_ref[0]) == column, 1.0, 0.0).astype(jnp.bfloat16)
    group = score_ref.shape[2]
    order = order_matrix(place_ref, group)
    score = jnp.concatenate(
        [contract(score_ref[at], order, 1, 0) for at in range(score_ref.shape[0])], axis=1
    )
    score = contract(unswap, score.astype(jnp.bfloat16), 1, 0)
    state = balancer_forward_pass(logits)
    grad = balancer_adjoint_pass(experts * score, *state).astype(jnp.bfloat16)
    grad_ref[...] = grad
    wait(rows_here)
    router_ref[...] = contract(grad, rows[...], 1, 0)


def per_device(tokens, out_grad, expert_ids, router_weight, w_gate, w_up, w_down):
    tok_rows, width = tokens.shape
    experts = router_weight.shape[1]
    groups = lax.axis_size("dp")
    far = lax.axis_size("expert") // 4
    chunk = 2 * far * tok_rows
    me = lax.axis_index("expert").astype(jnp.int32)[None]
    group = lax.axis_index("dp").astype(jnp.int32)[None]

    def along(array):
        return jnp.concatenate([array] + [swap_expert(array, 4 * k) for k in range(1, far)], axis=0)

    tok_line = along(tokens)
    (packed,) = kernel_call(
        pack_kernel, (), (expert_ids, tokens, router_weight.T), (),
        [shape(tok_rows, round_up(4 * experts, LANES))], (), 0,
    )
    columns = [out_grad, packed[:, : 4 * experts]]
    for offset in range(1, groups):
        columns.append(swap_group(packed, offset)[:, experts : 4 * experts])
    extra = (3 * groups + 1) * experts
    columns.append(jnp.zeros((tok_rows, round_up(extra, LANES) - extra), jnp.bfloat16))
    grad_line = along(jnp.concatenate(columns, axis=1))
    tok_next = swap_expert(tok_line, 2)
    grad_next = swap_expert(grad_line, 2)
    tok_own = [(tok_line, swap_expert(tok_line, 1)), (tok_next, swap_expert(tok_next, 1))]
    grad_own = [(grad_line, swap_expert(grad_line, 1)), (grad_next, swap_expert(grad_next, 1))]

    tok_parts = [rows for pair in tok_own for rows in pair]
    grad_parts = [rows for pair in grad_own for rows in pair]
    weights = (w_gate, w_up, w_down)

    at_once = 2 * groups * chunk <= ROWS_AT_ONCE

    def moved(parts, offset):
        out = []
        for part in parts:
            part = swap_group(part, offset)
            out += [part, swap_expert(part, 1)]
        return out

    moved_tok = moved((tok_line, tok_next), 1) if at_once else []
    moved_grad = moved((grad_line, grad_next), 1) if at_once else []
    early = []
    if at_once:
        for part, hops in ((moved_tok[1], 2), (tok_parts[3], 3)):
            corner = part[: 2 * SUBLANES, :LANES]
            for _ in range(hops):
                corner = swap_expert(corner, 1)
            early.append(corner)
    extra = grad_line.shape[1] - width
    gate, logits = kernel_call(
        functools.partial(gate_kernel, len(grad_parts), experts), (me,), (), grad_parts,
        [shape(2 * chunk * groups, LANES, jnp.float32), shape(experts, 2 * chunk * groups, jnp.float32)],
        [pltpu.VMEM((2 * chunk, extra), jnp.bfloat16)], len(grad_parts), 0, early,
    )
    slots = [4 * j + 2 * i + k for i in range(2) for k in range(2) for j in range(far)]
    slots = jnp.array(slots, jnp.int32) ^ me
    place = slots[:, None] * tok_rows + jnp.arange(tok_rows, dtype=jnp.int32)[None, :]
    place = place.reshape(1, 2 * chunk)
    pieces = round_up(2 * chunk, LANES) // LANES

    keep0, send0, keep1, send1, *scaled = expert_call(
        me, gate, place, tok_parts, grad_parts, weights, moved_tok[2:3]
    )
    given = [scaled]
    got1, got0 = (swap_expert(send1, 1), swap_expert(send0, 1))
    (near,) = kernel_call(
        functools.partial(near_kernel, pieces), (), (), (keep1, got1), [shape(*keep1.shape)],
        [pltpu.VMEM(keep1.shape, keep1.dtype)] * 3, 3, 1, moved_grad[0::2],
    )
    across = swap_expert(near, 2)
    ready = kernel_call(
        functools.partial(ready_kernel, pieces), (), (), (keep0, got0, near, across),
        [shape(tok_rows, width + LANES)] * far,
        [pltpu.VMEM(keep0.shape, keep0.dtype)] * 2 + [pltpu.VMEM(near.shape, near.dtype)] * 2
        + [pltpu.VMEM((far, tok_rows, width + LANES), near.dtype)], 4 + far, far,
    )
    arrived = [ready[0]] + [swap_expert(ready[k], 4 * k) for k in range(1, far)]
    row_sum = sum(part[:, :width].astype(jnp.float32) for part in arrived)
    score = jnp.stack([part[: 4 * pieces, width:] for part in arrived])
    score = score.reshape(experts, pieces * LANES)
    score = jnp.stack([score] + [swap_group(score, offset) for offset in range(1, groups)])
    to_send = ready[1:]

    token_rows = list(tok_parts)
    totals = None
    if not at_once:
        totals = weights_call(group, groups, tok_parts, grad_parts, given, jnp.float32)
        tok_parts, grad_parts, given = ([], [], [])
    for offset in range(1, groups):
        if not at_once:
            (tok_line, tok_next, grad_line, grad_next), totals = lax.optimization_barrier(
                ((tok_line, tok_next, grad_line, grad_next), totals)
            )
            moved_tok = moved((tok_line, tok_next), offset)
            moved_grad = moved((grad_line, grad_next), offset)
        token_rows += moved_tok
        fresh = others_call(me, gate, moved_tok, moved_grad, weights, 2 * chunk * offset)
        terms = weights_call(
            group, groups, tok_parts + moved_tok, grad_parts + moved_grad, given + [fresh],
            jnp.bfloat16 if at_once else jnp.float32, to_send,
        )
        totals = terms if totals is None else [t + u for t, u in zip(totals, terms)]
    final = [t.astype(jnp.bfloat16) for t in totals]

    logit_grad, grad_router = kernel_call(
        functools.partial(router_kernel, len(token_rows)), (me,), (logits, score, place), token_rows,
        [shape(*logits.shape), shape(experts, width, jnp.float32)],
        [pltpu.VMEM((logits.shape[1], width), jnp.bfloat16)], len(token_rows),
    )
    row_sum = row_sum + contract(logit_grad[:, :tok_rows], router_weight, 0, 1)
    return (row_sum.astype(jnp.bfloat16), grad_router.T, *final)


def solution(mesh):
    in_specs = (
        P(("dp", "expert"), None),
        P(("dp", "expert"), None),
        P(("dp", "expert"), None),
        P(),
        P("expert", None, None),
        P("expert", None, None),
        P("expert", None, None),
    )
    out_specs = (
        P(("dp", "expert"), None),
        P(),
        P("expert", "dp", None),
        P("expert", "dp", None),
        P("expert", "dp", None),
    )
    return jax.shard_map(
        per_device, mesh=mesh, in_specs=in_specs, out_specs=out_specs, check_vma=False
    )
```

time: 124 us -> 111 us (0.90)
  starting transfers between devices: 37.7 us -> 30.6 us
  waiting for transfers between devices: 30.2 us -> 25.1 us
  other arithmetic: 4.21 us -> 1.38 us
  local copies, waits for them, and re-layouts: 6.1 us -> 8.01 us
    ppermute x27, starting transfers between devices: 30.5 us -> 22.3 us  [swap_expert(): return lax.ppermute(array, 'expert', [(i, i ^ offset) for i in range(size)])]
    ppermute x27, waiting for transfers between devices: 22.4 us -> 19.2 us  [swap_expert(): return lax.ppermute(array, 'expert', [(i, i ^ offset) for i in range(size)])]
    concatenate x3 -> x0, other arithmetic: 2.87 us -> none  [the longest x1 1.36 us: per_device(): jnp.concatenate([logits_own] + [swap_group(logits_own, offset) for offset...]
    ppermute x6, waiting for transfers between devices: 7.75 us -> 5.88 us  [swap_group(): return lax.ppermute(array, 'dp', [(i, i ^ offset) for i in range(size)])]
    unnamed x38 -> x42, local copies, waits for them, and re-layouts: 5 us -> 5.53 us
    pallas_call x6 -> x8, Pallas kernels: 42.8 us -> 42.8 us  [kernel_call(): pl.pallas_call(body, in_specs=[pl.BlockSpec(memory_space=pltpu.SMEM)] * l...]
  transfers between devices with their start and end apart: 33 -> 33, of which waited for: 9 -> 11; matrix products, arithmetic and copies ran while one was open for 6% -> 5% of each run, Pallas kernels for 35% -> 33%
where the time goes in v4:
time: 111 us; the launch traced here: 110 us
  Pallas kernels  42.8 us (39%)
  starting transfers between devices  30.6 us (28%)
  waiting for transfers between devices  25.1 us (23%)
  local copies, waits for them, and re-layouts  8.01 us (7%)
  matrix products  1.53 us (1%)
  other arithmetic  1.38 us (1%)
    pallas_call x8, Pallas kernels, kernel_call(): pl.pallas_call(body, in_specs=[pl.BlockSpec(memory_space=pltpu.SMEM)] * l...  42.8 us
    ppermute x27, starting transfers between devices, swap_expert(): return lax.ppermute(array, 'expert', [(i, i ^ offset) for i in range(size)])  22.3 us
    ppermute x27, waiting for transfers between devices, swap_expert(): return lax.ppermute(array, 'expert', [(i, i ^ offset) for i in range(size)])  19.2 us
    ppermute x6, starting transfers between devices, swap_group(): return lax.ppermute(array, 'dp', [(i, i ^ offset) for i in range(size)])  8.33 us
    ppermute x6, waiting for transfers between devices, swap_group(): return lax.ppermute(array, 'dp', [(i, i ^ offset) for i in range(size)])  5.88 us
    unnamed x42, local copies, waits for them, and re-layouts  5.53 us
  transfers between devices with their start and end apart: 33, of which 11 were waited for; matrix products, arithmetic and copies ran while one was open for 5% of the time, Pallas kernels for 33%

profile of v4, /device:TPU:0, one launch (start us, length us, event | category | flops | bytes accessed | tf_op | source)
XLA Modules:
  0.0 110.5 jit_solution(1492298008319833026)
XLA Ops:
  0.6 4.1 %collective-permute-start.8 = (bf16[24,2048]{1,0:T(8,128)(2,1)}, bf16[24,2048]{1,0:T(8,128)(2,1)S(1)}, u32[]{:S(2)}, u32[]{:S(2)}) collective-permute-start(bf16[24,2048]{1,0:T(8,128)(2,1)} %refs_1_.1), channel_id=1, source_target_pairs={{0,8},{1,9},{2,10},{3,11},{4,12},{5,13},{6,14},{7,15},{8,0},{9,1},... | collective-permute-start | bytes 294920 | tf_op jit(solution)/shard_map/ppermute | solution.py:21
  4.7 1.6 %collective-permute-start.7 = (bf16[24,2048]{1,0:T(8,128)(2,1)}, bf16[24,2048]{1,0:T(8,128)(2,1)S(1)}, u32[]{:S(2)}, u32[]{:S(2)}) collective-permute-start(bf16[24,2048]{1,0:T(8,128)(2,1)} %refs_1_.1), channel_id=1, source_target_pairs={{0,4},{1,5},{2,6},{3,7},{4,0},{5,1},{6,2},{7,3},{8,12},{9,13},{10,... | collective-permute-start | bytes 294920 | tf_op jit(solution)/shard_map/ppermute | solution.py:21
  6.3 1.4 %copy.14.refs_0_ = s32[24,8]{1,0:T(8,128)} copy(s32[24,8]{0,1:T(8,128)} %param.10) | data formatting | bytes 1536 | tf_op args[2]
  7.7 1.8 %shard_map.119 = bf16[24,128]{1,0:T(8,128)(2,1)} custom-call(s32[24,8]{1,0:T(8,128)} %copy.14.refs_0_, bf16[24,2048]{1,0:T(8,128)(2,1)} %refs_1_.1, bf16[16,2048]{1,0:T(8,128)(2,1)} %bitcast.15), custom_call_target="tpu_custom_call" | custom-call | flops 2000000 | bytes 5000 | tf_op jit(solution)/shard_map/pallas_call | solution.py:108
  9.5 1.7 %collective-permute-start = (bf16[24,128]{1,0:T(8,128)(2,1)}, bf16[24,128]{1,0:T(8,128)(2,1)S(1)}, u32[]{:S(2)}, u32[]{:S(2)}) collective-permute-start(bf16[24,128]{1,0:T(8,128)(2,1)} %shard_map.119), channel_id=1, source_target_pairs={{0,16},{16,0},{1,17},{17,1},{2,18},{18,2},{3,19},{19,3},{4,20},{20... | collective-permute-start | bytes 18440 | tf_op jit(solution)/shard_map/ppermute | solution.py:26
  11.2 0.9 constant_dynamic-update-slice_fusion.3
  12.1 1.2 %collective-permute-done = bf16[24,128]{1,0:T(8,128)(2,1)S(1)} collective-permute-done((bf16[24,128]{1,0:T(8,128)(2,1)}, bf16[24,128]{1,0:T(8,128)(2,1)S(1)}, u32[]{:S(2)}, u32[]{:S(2)}) %collective-permute-start) | collective-permute-done | bytes 6176 | tf_op jit(solution)/shard_map/ppermute | solution.py:26
  13.3 0.1 slice.53
  13.4 1.0 concatenate.9
  14.4 3.9 %collective-permute-start.3 = (bf16[24,2176]{1,0:T(8,128)(2,1)S(1)}, bf16[24,2176]{1,0:T(8,128)(2,1)S(1)}, u32[]{:S(2)}, u32[]{:S(2)}) collective-permute-start(bf16[24,2176]{1,0:T(8,128)(2,1)S(1)} %concatenate.9), channel_id=1, source_target_pairs={{0,12},{1,13},{2,14},{3,15},{4,8},{5,9},{6,10},{7,11},{8,4},{9,5},... | collective-permute-start | bytes 313352 | tf_op jit(solution)/shard_map/ppermute | solution.py:21
  18.2 0.6 collective-permute-start.1
  18.9 1.7 %collective-permute-start.14 = (bf16[96,2048]{1,0:T(8,128)(2,1)S(1)}, bf16[96,2048]{1,0:T(8,128)(2,1)}, u32[]{:S(2)}, u32[]{:S(2)}) collective-permute-start(bf16[96,2048]{1,0:T(8,128)(2,1)S(1)} %constant_dynamic-update-slice_fusion.refs_3_.refs_4_.refs_1_), channel_id=1, source_target_pairs={{0,2},{1,3},{2,0},{3,1},{4,6},{5,7},{6,4},{7,5},{8,10},{9,11},{10,... | collective-permute-start | bytes 1179656 | tf_op jit(solution)/shard_map/ppermute | solution.py:21
  20.7 1.5 %collective-permute-start.10 = (bf16[96,2048]{1,0:T(8,128)(2,1)S(1)}, bf16[96,2048]{1,0:T(8,128)(2,1)S(1)}, u32[]{:S(2)}, u32[]{:S(2)}) collective-permute-start(bf16[96,2048]{1,0:T(8,128)(2,1)S(1)} %constant_dynamic-update-slice_fusion.refs_3_.refs_4_.refs_1_), channel_id=1, source_target_pairs={{0,16},{16,0},{1,17},{17,1},{2,18},{18,2},{3,19},{19,3},{4,20},{20... | collective-permute-start | bytes 1179656 | tf_op jit(solution)/shard_map/ppermute | solution.py:26
  22.2 2.9 %collective-permute-done.2 = bf16[24,2176]{1,0:T(8,128)(2,1)S(1)} collective-permute-done((bf16[24,2176]{1,0:T(8,128)(2,1)S(1)}, bf16[24,2176]{1,0:T(8,128)(2,1)S(1)}, u32[]{:S(2)}, u32[]{:S(2)}) %collective-permute-start.2) | collective-permute-done | bytes 104480 | tf_op jit(solution)/shard_map/ppermute | solution.py:21
  25.2 1.5 %collective-permute-start.5 = (bf16[96,2176]{1,0:T(8,128)(2,1)S(1)}, bf16[96,2176]{1,0:T(8,128)(2,1)S(1)}, u32[]{:S(2)}, u32[]{:S(2)}) collective-permute-start(bf16[96,2176]{1,0:T(8,128)(2,1)S(1)} %pad_maximum_fusion.refs_1_.refs_7_.refs_9_), channel_id=1, source_target_pairs={{0,2},{1,3},{2,0},{3,1},{4,6},{5,7},{6,4},{7,5},{8,10},{9,11},{10,... | collective-permute-start | bytes 1253384 | tf_op jit(solution)/shard_map/ppermute | solution.py:21
  26.7 1.6 %collective-permute-done.14.refs_5_.refs_6_.refs_3_ = bf16[96,2048]{1,0:T(8,128)(2,1)} collective-permute-done((bf16[96,2048]{1,0:T(8,128)(2,1)S(1)}, bf16[96,2048]{1,0:T(8,128)(2,1)}, u32[]{:S(2)}, u32[]{:S(2)}) %collective-permute-start.14) | collective-permute-done | bytes 393248 | tf_op jit(solution)/shard_map/ppermute | solution.py:21
  28.3 0.5 collective-permute-done.10.refs_8_.refs_2_.refs_5_
  28.9 1.4 %collective-permute-done.15.refs_6_.refs_7_.refs_4_ = bf16[96,2048]{1,0:T(8,128)(2,1)S(1)} collective-permute-done((bf16[96,2048]{1,0:T(8,128)(2,1)}, bf16[96,2048]{1,0:T(8,128)(2,1)S(1)}, u32[]{:S(2)}, u32[]{:S(2)}) %collective-permute-start.15) | collective-permute-done | bytes 393248 | tf_op jit(solution)/shard_map/ppermute | solution.py:21
  30.3 0.1 collective-permute-start.16
  30.4 0.4 collective-permute-start.19
  30.8 5.8 %collective-permute-done.5.refs_3_.refs_9_.refs_11_ = bf16[96,2176]{1,0:T(8,128)(2,1)S(1)} collective-permute-done((bf16[96,2176]{1,0:T(8,128)(2,1)S(1)}, bf16[96,2176]{1,0:T(8,128)(2,1)S(1)}, u32[]{:S(2)}, u32[]{:S(2)}) %collective-permute-start.5) | collective-permute-done | bytes 417824 | tf_op jit(solution)/shard_map/ppermute | solution.py:21
  36.6 1.5 %collective-permute-start.20 = (bf16[96,2048]{1,0:T(8,128)(2,1)}, bf16[96,2048]{1,0:T(8,128)(2,1)}, u32[]{:S(2)}, u32[]{:S(2)}) collective-permute-start(bf16[96,2048]{1,0:T(8,128)(2,1)} %collective-permute-done.14.refs_5_.refs_6_.refs_3_), channel_id=1, source_target_pairs={{0,16},{16,0},{1,17},{17,1},{2,18},{18,2},{3,19},{19,3},{4,20},{20... | collective-permute-start | bytes 1179656 | tf_op jit(solution)/shard_map/ppermute | solution.py:26
  38.1 0.1 collective-permute-start.6
  38.2 0.5 collective-permute-start.12
  38.7 0.1 collective-permute-start.17
  38.8 0.7 xor_multiply_fusion
  39.5 0.4 collective-permute-done.12
  39.9 0.1 collective-permute-start.13
  40.0 0.4 collective-permute-start.18
  40.4 0.1 iota_add_fusion
  40.5 0.7 add.38.refs_2_.refs_3_
  41.2 0.6 collective-permute-start.23
  41.8 1.5 %collective-permute-start.24 = (bf16[96,2176]{1,0:T(8,128)(2,1)S(1)}, bf16[96,2176]{1,0:T(8,128)(2,1)S(1)}, u32[]{:S(2)}, u32[]{:S(2)}) collective-permute-start(bf16[96,2176]{1,0:T(8,128)(2,1)S(1)} %collective-permute-done.5.refs_3_.refs_9_.refs_11_), channel_id=1, source_target_pairs={{0,16},{16,0},{1,17},{17,1},{2,18},{18,2},{3,19},{19,3},{4,20},{20... | collective-permute-start | bytes 1253384 | tf_op jit(solution)/shard_map/ppermute | solution.py:26
  43.3 0.7 copy-done.4
  44.0 2.2 %shard_map.120 = (f32[768,128]{1,0:T(8,128)}, f32[16,768]{1,0:T(8,128)}) custom-call(s32[1]{0:T(128)} %bitcast.refs_0_, bf16[96,2176]{1,0:T(8,128)(2,1)} %copy-done, bf16[96,2176]{1,0:T(8,128)(2,1)} %copy-done.3, bf16[96,2176]{1,0:T(8,128)(2,1)} %copy-done.2, bf16[96,2176]{1,0:T(8,128)(2,1)} %copy-done.4, bf16[16,128]{1,0:T(8,128)(2,1)} %copy-done.15, ...), custom_call_target="tpu_custom_call" | custom-call | flops 2000000 | bytes 5000 | tf_op jit(solution)/shard_map/pallas_call | solution.py:108
  46.2 2.7 %collective-permute-done.20.refs_14_.refs_10_.refs_4_.refs_7_ = bf16[96,2048]{1,0:T(8,128)(2,1)} collective-permute-done((bf16[96,2048]{1,0:T(8,128)(2,1)}, bf16[96,2048]{1,0:T(8,128)(2,1)}, u32[]{:S(2)}, u32[]{:S(2)}) %collective-permute-start.20) | collective-permute-done | bytes 393248 | tf_op jit(solution)/shard_map/ppermute | solution.py:26
  48.9 13.7 %shard_map.121 = (bf16[96,2048]{1,0:T(8,128)(2,1)}, bf16[96,2048]{1,0:T(8,128)(2,1)}, bf16[96,2176]{1,0:T(8,128)(2,1)}, bf16[96,2176]{1,0:T(8,128)(2,1)}, bf16[3...) custom-call(s32[1]{0:T(128)} %bitcast.refs_0_, f32[768,128]{1,0:T(8,128)} %get-tuple-element.26.refs_1_, ...), custom_call_target="tpu_custom_call" | custom-call | flops 6039797760 | bytes 15099494 | tf_op jit(solution)/shard_map/pallas_call | solution.py:108
  62.6 0.1 collective-permute-start.22
  62.7 0.5 collective-permute-start.31
  63.2 1.4 %collective-permute-done.24.refs_3_.refs_8_.refs_15_ = bf16[96,2176]{1,0:T(8,128)(2,1)S(1)} collective-permute-done((bf16[96,2176]{1,0:T(8,128)(2,1)S(1)}, bf16[96,2176]{1,0:T(8,128)(2,1)S(1)}, u32[]{:S(2)}, u32[]{:S(2)}) %collective-permute-start.24) | collective-permute-done | bytes 417824 | tf_op jit(solution)/shard_map/ppermute | solution.py:26
  64.6 0.5 collective-permute-start.30
  65.1 0.2 copy-done.7
  65.3 0.5 copy-done.8
  65.9 2.0 %shard_map.122.refs_2_ = bf16[96,2176]{1,0:T(8,128)(2,1)} custom-call(bf16[96,2176]{1,0:T(8,128)(2,1)} %get-tuple-element.29.refs_0_, bf16[96,2176]{1,0:T(8,128)(2,1)} %copy-done.8, bf16[96,2176]{1,0:T(8,128)(2,1)} %copy-done.6, bf16[96,2176]{1,0:T(8,128)(2,1)} %copy-done.7), custom_call_target="tpu_custom_call" | custom-call | flops 2000000 | bytes 5000 | tf_op jit(solution)/shard_map/pallas_call | solution.py:108
  67.9 1.6 %collective-permute-start.25 = (bf16[96,2176]{1,0:T(8,128)(2,1)}, bf16[96,2176]{1,0:T(8,128)(2,1)S(1)}, u32[]{:S(2)}, u32[]{:S(2)}) collective-permute-start(bf16[96,2176]{1,0:T(8,128)(2,1)} %shard_map.122.refs_2_), channel_id=1, source_target_pairs={{0,2},{1,3},{2,0},{3,1},{4,6},{5,7},{6,4},{7,5},{8,10},{9,11},{10,... | collective-permute-start | bytes 1253384 | tf_op jit(solution)/shard_map/ppermute | solution.py:21
  69.5 0.7 copy-done.18
  70.3 0.1 copy-done.13
  70.4 9.8 %shard_map.125 = (bf16[384,768]{1,0:T(8,128)(2,1)}, bf16[384,768]{1,0:T(8,128)(2,1)}, bf16[384,768]{1,0:T(8,128)(2,1)}) custom-call(s32[1]{0:T(128)} %bitcast.refs_0_, f32[768,128]{1,0:T(8,128)} %get-tuple-element.26.refs_1_, bf16[96,2048]{1,0:T(8,128)(2,1)} %copy-done.12, bf16[96,2048]{1,0:T(8,128)(2,1)} %copy-done.10, ...), custom_call_target="tpu_custom_call" | custom-call | flops 3623878656 | bytes 9059696 | tf_op jit(solution)/shard_map/pallas_call | solution.py:108
  80.2 0.0 copy-start.5
  80.2 0.7 copy-done.11
  81.0 0.1 copy-done.5
  81.1 2.2 %shard_map.123 = (bf16[24,2176]{1,0:T(8,128)(2,1)}, bf16[24,2176]{1,0:T(8,128)(2,1)}, bf16[24,2176]{1,0:T(8,128)(2,1)}, bf16[24,2176]{1,0:T(8,128)(2,1)}) custom-call(bf16[96,2048]{1,0:T(8,128)(2,1)} %get-tuple-element.27.refs_0_, bf16[96,2048]{1,0:T(8,128)(2,1)} %copy-done.11, bf16[96,2176]{1,0:T(8,128)(2,1)} %shard_map.122.refs_2_, bf16[96,2176]{1,0:T(8,128)(2,1)} %copy-done.5), custom_call_target="tpu_custom_call" | custom-call | flops 2000000 | bytes 5000 | tf_op jit(solution)/shard_map/pallas_call | solution.py:108
  83.3 0.1 collective-permute-start.26
  83.4 0.7 slice_bitcast_fusion.3
  84.1 2.6 %collective-permute-start.27 = (bf16[24,2176]{1,0:T(8,128)(2,1)}, bf16[24,2176]{1,0:T(8,128)(2,1)S(1)}, u32[]{:S(2)}, u32[]{:S(2)}) collective-permute-start(bf16[24,2176]{1,0:T(8,128)(2,1)} %get-tuple-element.33.refs_24_), channel_id=1, source_target_pairs={{0,8},{1,9},{2,10},{3,11},{4,12},{5,13},{6,14},{7,15},{8,0},{9,1},... | collective-permute-start | bytes 313352 | tf_op jit(solution)/shard_map/ppermute | solution.py:21
  86.7 1.8 %collective-permute-start.28 = (bf16[24,2176]{1,0:T(8,128)(2,1)}, bf16[24,2176]{1,0:T(8,128)(2,1)S(1)}, u32[]{:S(2)}, u32[]{:S(2)}) collective-permute-start(bf16[24,2176]{1,0:T(8,128)(2,1)} %get-tuple-element.34.refs_25_), channel_id=1, source_target_pairs={{0,12},{1,13},{2,14},{3,15},{4,8},{5,9},{6,10},{7,11},{8,4},{9,5},... | collective-permute-start | bytes 313352 | tf_op jit(solution)/shard_map/ppermute | solution.py:21
  88.5 1.7 %collective-permute-done.26 = bf16[24,2176]{1,0:T(8,128)(2,1)S(1)} collective-permute-done((bf16[24,2176]{1,0:T(8,128)(2,1)}, bf16[24,2176]{1,0:T(8,128)(2,1)S(1)}, u32[]{:S(2)}, u32[]{:S(2)}) %collective-permute-start.26) | collective-permute-done | bytes 104480 | tf_op jit(solution)/shard_map/ppermute | solution.py:21
  90.2 5.3 %collective-permute-done.27 = bf16[24,2176]{1,0:T(8,128)(2,1)S(1)} collective-permute-done((bf16[24,2176]{1,0:T(8,128)(2,1)}, bf16[24,2176]{1,0:T(8,128)(2,1)S(1)}, u32[]{:S(2)}, u32[]{:S(2)}) %collective-permute-start.27) | collective-permute-done | bytes 104480 | tf_op jit(solution)/shard_map/ppermute | solution.py:21
  95.5 1.6 %collective-permute-start.29 = (bf16[16,384]{1,0:T(8,128)(2,1)S(1)}, bf16[16,384]{1,0:T(8,128)(2,1)S(1)}, u32[]{:S(2)}, u32[]{:S(2)}) collective-permute-start(bf16[16,384]{1,0:T(8,128)(2,1)S(1)} %reshape.39), channel_id=1, source_target_pairs={{0,16},{16,0},{1,17},{17,1},{2,18},{18,2},{3,19},{19,3},{4,20},{20... | collective-permute-start | bytes 36872 | tf_op jit(solution)/shard_map/ppermute | solution.py:26
  97.0 7.2 %shard_map.126 = (bf16[1,1024,768]{2,1,0:T(8,128)(2,1)}, bf16[1,1024,768]{2,1,0:T(8,128)(2,1)}, bf16[1,384,2048]{2,1,0:T(8,128)(2,1)}) custom-call(s32[1]{0:T(128)} %bitcast.8.refs_0_, bf16[96,2048]{1,0:T(8,128)(2,1)} %copy-done.1, bf16[96,2048]{1,0:T(8,128)(2,1)} %collective-permute-done.19.refs_4_.refs_5_.refs_2_, ...), custom_call_target="tpu_custom_call" | custom-call | flops 3623878656 | bytes 9059696 | tf_op jit(solution)/shard_map/pallas_call | solution.py:108
  104.2 0.0 copy-start.14
  104.3 0.6 pad_maximum_fusion.1.refs_2_
  104.9 4.0 %shard_map.124 = (bf16[16,768]{1,0:T(8,128)(2,1)}, f32[16,2048]{1,0:T(8,128)}) custom-call(s32[1]{0:T(128)} %bitcast.refs_0_, f32[16,768]{1,0:T(8,128)} %get-tuple-element.35.refs_1_, bf16[2,16,384]{2,1,0:T(8,128)(2,1)} %pad_maximum_fusion.1.refs_2_, s32[1,384]{1,0:T(1,128)} %add.38.refs_2_.refs_3_, bf16[96,2048]{1,0:T(8,128)(2,1)} %copy-done.1, ...), custom_call_target="tpu_custom_call" | custom-call | flops 2000000 | bytes 5000 | tf_op jit(solution)/shard_map/pallas_call | solution.py:108
  108.9 1.5 %fusion = bf16[24,2048]{1,0:T(8,128)(2,1)} fusion(bf16[2048,16]{0,1:T(8,128)(2,1)S(1)} %copy-done.14, bf16[24,2176]{1,0:T(8,128)(2,1)S(1)} %collective-permute-done.28, bf16[24,2176]{1,0:T(8,128)(2,1)S(1)} %collective-permute-done.27, bf16[24,2176]{1,0:T(8,128)(2,1)S(1)} %collective-permute-done.26, bf16[24,2176]{1,0:T(8,128)(2,1)S(1)} %copy-done.17, ...), kind=kOutput, calls=%fused_computation.1 | convolution fusion | flops 2015232 | bytes 561152 | tf_op jit(solution)/shard_map/dot_general | solution.py:30
  (71 shorter events, 0.3 us)
Async XLA Ops:
  0.6 18.3 %collective-permute-start.8 = (bf16[24,2048]{1,0:T(8,128)(2,1)}, bf16[24,2048]{1,0:T(8,128)(2,1)S(1)}, u32[]{:S(2)}, u32[]{:S(2)}) collective-permute-start(bf16[24,2048]{1,0:T(8,128)(2,1)} %refs_1_.1), channel_id=1, source_target_pairs={{0,8},{1,9},{2,10},{3,11},{4,12},{5,13},{6,14},{7,15},{8,0},{9,1},... | collective-permute-start | bytes 294920 | tf_op jit(solution)/shard_map/ppermute | solution.py:21
  4.7 13.5 %collective-permute-start.7 = (bf16[24,2048]{1,0:T(8,128)(2,1)}, bf16[24,2048]{1,0:T(8,128)(2,1)S(1)}, u32[]{:S(2)}, u32[]{:S(2)}) collective-permute-start(bf16[24,2048]{1,0:T(8,128)(2,1)} %refs_1_.1), channel_id=1, source_target_pairs={{0,4},{1,5},{2,6},{3,7},{4,0},{5,1},{6,2},{7,3},{8,12},{9,13},{10,... | collective-permute-start | bytes 294920 | tf_op jit(solution)/shard_map/ppermute | solution.py:21
  6.3 12.6 %collective-permute-start.9 = (bf16[24,2048]{1,0:T(8,128)(2,1)}, bf16[24,2048]{1,0:T(8,128)(2,1)S(1)}, u32[]{:S(2)}, u32[]{:S(2)}) collective-permute-start(bf16[24,2048]{1,0:T(8,128)(2,1)} %refs_1_.1), channel_id=1, source_target_pairs={{0,12},{1,13},{2,14},{3,15},{4,8},{5,9},{6,10},{7,11},{8,4},{9,5},... | collective-permute-start | bytes 294920 | tf_op jit(solution)/shard_map/ppermute | solution.py:21
  9.5 3.8 %collective-permute-start = (bf16[24,128]{1,0:T(8,128)(2,1)}, bf16[24,128]{1,0:T(8,128)(2,1)S(1)}, u32[]{:S(2)}, u32[]{:S(2)}) collective-permute-start(bf16[24,128]{1,0:T(8,128)(2,1)} %shard_map.119), channel_id=1, source_target_pairs={{0,16},{16,0},{1,17},{17,1},{2,18},{18,2},{3,19},{19,3},{4,20},{20... | collective-permute-start | bytes 18440 | tf_op jit(solution)/shard_map/ppermute | solution.py:26
  14.4 7.8 %collective-permute-start.3 = (bf16[24,2176]{1,0:T(8,128)(2,1)S(1)}, bf16[24,2176]{1,0:T(8,128)(2,1)S(1)}, u32[]{:S(2)}, u32[]{:S(2)}) collective-permute-start(bf16[24,2176]{1,0:T(8,128)(2,1)S(1)} %concatenate.9), channel_id=1, source_target_pairs={{0,12},{1,13},{2,14},{3,15},{4,8},{5,9},{6,10},{7,11},{8,4},{9,5},... | collective-permute-start | bytes 313352 | tf_op jit(solution)/shard_map/ppermute | solution.py:21
  18.2 6.9 %collective-permute-start.2 = (bf16[24,2176]{1,0:T(8,128)(2,1)S(1)}, bf16[24,2176]{1,0:T(8,128)(2,1)S(1)}, u32[]{:S(2)}, u32[]{:S(2)}) collective-permute-start(bf16[24,2176]{1,0:T(8,128)(2,1)S(1)} %concatenate.9), channel_id=1, source_target_pairs={{0,8},{1,9},{2,10},{3,11},{4,12},{5,13},{6,14},{7,15},{8,0},{9,1},... | collective-permute-start | bytes 313352 | tf_op jit(solution)/shard_map/ppermute | solution.py:21
  18.2 6.9 %collective-permute-start.1 = (bf16[24,2176]{1,0:T(8,128)(2,1)S(1)}, bf16[24,2176]{1,0:T(8,128)(2,1)S(1)}, u32[]{:S(2)}, u32[]{:S(2)}) collective-permute-start(bf16[24,2176]{1,0:T(8,128)(2,1)S(1)} %concatenate.9), channel_id=1, source_target_pairs={{0,4},{1,5},{2,6},{3,7},{4,0},{5,1},{6,2},{7,3},{8,12},{9,13},{10,... | collective-permute-start | bytes 313352 | tf_op jit(solution)/shard_map/ppermute | solution.py:21
  18.9 30.0 %copy-start.1 = (bf16[96,2048]{1,0:T(8,128)(2,1)}, bf16[96,2048]{1,0:T(8,128)(2,1)S(1)}, u32[]{:S(2)}) copy-start(bf16[96,2048]{1,0:T(8,128)(2,1)S(1)} %constant_dynamic-update-slice_fusion.refs_3_.refs_4_.refs_1_) | copy-start | bytes 1179652
  18.9 9.4 %collective-permute-start.14 = (bf16[96,2048]{1,0:T(8,128)(2,1)S(1)}, bf16[96,2048]{1,0:T(8,128)(2,1)}, u32[]{:S(2)}, u32[]{:S(2)}) collective-permute-start(bf16[96,2048]{1,0:T(8,128)(2,1)S(1)} %constant_dynamic-update-slice_fusion.refs_3_.refs_4_.refs_1_), channel_id=1, source_target_pairs={{0,2},{1,3},{2,0},{3,1},{4,6},{5,7},{6,4},{7,5},{8,10},{9,11},{10,... | collective-permute-start | bytes 1179656 | tf_op jit(solution)/shard_map/ppermute | solution.py:21
  20.7 8.2 %collective-permute-start.10 = (bf16[96,2048]{1,0:T(8,128)(2,1)S(1)}, bf16[96,2048]{1,0:T(8,128)(2,1)S(1)}, u32[]{:S(2)}, u32[]{:S(2)}) collective-permute-start(bf16[96,2048]{1,0:T(8,128)(2,1)S(1)} %constant_dynamic-update-slice_fusion.refs_3_.refs_4_.refs_1_), channel_id=1, source_target_pairs={{0,16},{16,0},{1,17},{17,1},{2,18},{18,2},{3,19},{19,3},{4,20},{20... | collective-permute-start | bytes 1179656 | tf_op jit(solution)/shard_map/ppermute | solution.py:26
  25.2 18.1 %copy-start = (bf16[96,2176]{1,0:T(8,128)(2,1)}, bf16[96,2176]{1,0:T(8,128)(2,1)S(1)}, u32[]{:S(2)}) copy-start(bf16[96,2176]{1,0:T(8,128)(2,1)S(1)} %pad_maximum_fusion.refs_1_.refs_7_.refs_9_) | copy-start | bytes 1253380
  25.2 11.4 %collective-permute-start.5 = (bf16[96,2176]{1,0:T(8,128)(2,1)S(1)}, bf16[96,2176]{1,0:T(8,128)(2,1)S(1)}, u32[]{:S(2)}, u32[]{:S(2)}) collective-permute-start(bf16[96,2176]{1,0:T(8,128)(2,1)S(1)} %pad_maximum_fusion.refs_1_.refs_7_.refs_9_), channel_id=1, source_target_pairs={{0,2},{1,3},{2,0},{3,1},{4,6},{5,7},{6,4},{7,5},{8,10},{9,11},{10,... | collective-permute-start | bytes 1253384 | tf_op jit(solution)/shard_map/ppermute | solution.py:21
  26.7 11.5 %collective-permute-start.4 = (bf16[96,2176]{1,0:T(8,128)(2,1)S(1)}, bf16[96,2176]{1,0:T(8,128)(2,1)S(1)}, u32[]{:S(2)}, u32[]{:S(2)}) collective-permute-start(bf16[96,2176]{1,0:T(8,128)(2,1)S(1)} %pad_maximum_fusion.refs_1_.refs_7_.refs_9_), channel_id=1, source_target_pairs={{0,1},{1,0},{2,3},{3,2},{4,5},{5,4},{6,7},{7,6},{8,9},{9,8},{10,11... | collective-permute-start | bytes 1253384 | tf_op jit(solution)/shard_map/ppermute | solution.py:21
  28.3 1.9 %collective-permute-start.15 = (bf16[96,2048]{1,0:T(8,128)(2,1)}, bf16[96,2048]{1,0:T(8,128)(2,1)S(1)}, u32[]{:S(2)}, u32[]{:S(2)}) collective-permute-start(bf16[96,2048]{1,0:T(8,128)(2,1)} %collective-permute-done.14.refs_5_.refs_6_.refs_3_), channel_id=1, source_target_pairs={{0,1},{1,0},{2,3},{3,2},{4,5},{5,4},{6,7},{7,6},{8,9},{9,8},{10,11... | collective-permute-start | bytes 1179656 | tf_op jit(solution)/shard_map/ppermute | solution.py:21
  28.9 9.2 %copy-start.12 = (bf16[96,2048]{1,0:T(8,128)(2,1)}, bf16[96,2048]{1,0:T(8,128)(2,1)S(1)}, u32[]{:S(2)}) copy-start(bf16[96,2048]{1,0:T(8,128)(2,1)S(1)} %collective-permute-done.10.refs_8_.refs_2_.refs_5_) | copy-start | bytes 1179652
  28.9 9.2 %collective-permute-start.11 = (bf16[96,2048]{1,0:T(8,128)(2,1)S(1)}, bf16[96,2048]{1,0:T(8,128)(2,1)S(1)}, u32[]{:S(2)}, u32[]{:S(2)}) collective-permute-start(bf16[96,2048]{1,0:T(8,128)(2,1)S(1)} %collective-permute-done.10.refs_8_.refs_2_.refs_5_), channel_id=1, source_target_pairs={{0,1},{1,0},{2,3},{3,2},{4,5},{5,4},{6,7},{7,6},{8,9},{9,8},{10,11... | collective-permute-start | bytes 1179656 | tf_op jit(solution)/shard_map/ppermute | solution.py:21
  30.3 18.7 %copy-start.9 = (bf16[96,2048]{1,0:T(8,128)(2,1)}, bf16[96,2048]{1,0:T(8,128)(2,1)S(1)}, u32[]{:S(2)}) copy-start(bf16[96,2048]{1,0:T(8,128)(2,1)S(1)} %collective-permute-done.15.refs_6_.refs_7_.refs_4_) | copy-start | bytes 1179652
  30.3 8.4 %collective-permute-start.16 = (bf16[16,128]{1,0:T(8,128)(2,1)S(1)}, bf16[16,128]{1,0:T(8,128)(2,1)S(1)}, u32[]{:S(2)}, u32[]{:S(2)}) collective-permute-start(bf16[16,128]{1,0:T(8,128)(2,1)S(1)} %slice.55), channel_id=1, source_target_pairs={{0,1},{1,0},{2,3},{3,2},{4,5},{5,4},{6,7},{7,6},{8,9},{9,8},{10,11... | collective-permute-start | bytes 12296 | tf_op jit(solution)/shard_map/ppermute | solution.py:21
  30.4 15.8 %collective-permute-start.19 = (bf16[96,2048]{1,0:T(8,128)(2,1)S(1)}, bf16[96,2048]{1,0:T(8,128)(2,1)}, u32[]{:S(2)}, u32[]{:S(2)}) collective-permute-start(bf16[96,2048]{1,0:T(8,128)(2,1)S(1)} %constant_dynamic-update-slice_fusion.refs_3_.refs_4_.refs_1_), channel_id=1, source_target_pairs={{0,1},{1,0},{2,3},{3,2},{4,5},{5,4},{6,7},{7,6},{8,9},{9,8},{10,11... | collective-permute-start | bytes 1179656 | tf_op jit(solution)/shard_map/ppermute | solution.py:21
  36.6 6.7 %copy-start.2 = (bf16[96,2176]{1,0:T(8,128)(2,1)}, bf16[96,2176]{1,0:T(8,128)(2,1)S(1)}, u32[]{:S(2)}) copy-start(bf16[96,2176]{1,0:T(8,128)(2,1)S(1)} %collective-permute-done.5.refs_3_.refs_9_.refs_11_) | copy-start | bytes 1253380
  36.6 12.4 %collective-permute-start.20 = (bf16[96,2048]{1,0:T(8,128)(2,1)}, bf16[96,2048]{1,0:T(8,128)(2,1)}, u32[]{:S(2)}, u32[]{:S(2)}) collective-permute-start(bf16[96,2048]{1,0:T(8,128)(2,1)} %collective-permute-done.14.refs_5_.refs_6_.refs_3_), channel_id=1, source_target_pairs={{0,16},{16,0},{1,17},{17,1},{2,18},{18,2},{3,19},{19,3},{4,20},{20... | collective-permute-start | bytes 1179656 | tf_op jit(solution)/shard_map/ppermute | solution.py:26
  38.1 3.1 %copy-start.10 = (bf16[96,2048]{1,0:T(8,128)(2,1)}, bf16[96,2048]{1,0:T(8,128)(2,1)S(1)}, u32[]{:S(2)}) copy-start(bf16[96,2048]{1,0:T(8,128)(2,1)S(1)} %collective-permute-done.11.refs_9_.refs_3_.refs_6_) | copy-start | bytes 1179652
  38.1 5.2 %collective-permute-start.6 = (bf16[96,2176]{1,0:T(8,128)(2,1)S(1)}, bf16[96,2176]{1,0:T(8,128)(2,1)S(1)}, u32[]{:S(2)}, u32[]{:S(2)}) collective-permute-start(bf16[96,2176]{1,0:T(8,128)(2,1)S(1)} %collective-permute-done.5.refs_3_.refs_9_.refs_11_), channel_id=1, source_target_pairs={{0,1},{1,0},{2,3},{3,2},{4,5},{5,4},{6,7},{7,6},{8,9},{9,8},{10,11... | collective-permute-start | bytes 1253384 | tf_op jit(solution)/shard_map/ppermute | solution.py:21
  38.2 5.1 %copy-start.3 = (bf16[96,2176]{1,0:T(8,128)(2,1)}, bf16[96,2176]{1,0:T(8,128)(2,1)S(1)}, u32[]{:S(2)}) copy-start(bf16[96,2176]{1,0:T(8,128)(2,1)S(1)} %collective-permute-done.4.refs_2_.refs_8_.refs_10_) | copy-start | bytes 1253380
  38.2 1.7 %collective-permute-start.12 = (bf16[16,128]{1,0:T(8,128)(2,1)S(1)}, bf16[16,128]{1,0:T(8,128)(2,1)S(1)}, u32[]{:S(2)}, u32[]{:S(2)}) collective-permute-start(bf16[16,128]{1,0:T(8,128)(2,1)S(1)} %slice.54), channel_id=1, source_target_pairs={{0,1},{1,0},{2,3},{3,2},{4,5},{5,4},{6,7},{7,6},{8,9},{9,8},{10,11... | collective-permute-start | bytes 12296 | tf_op jit(solution)/shard_map/ppermute | solution.py:21
  38.7 1.3 %collective-permute-start.17 = (bf16[16,128]{1,0:T(8,128)(2,1)S(1)}, bf16[16,128]{1,0:T(8,128)(2,1)S(1)}, u32[]{:S(2)}, u32[]{:S(2)}) collective-permute-start(bf16[16,128]{1,0:T(8,128)(2,1)S(1)} %collective-permute-done.16), channel_id=1, source_target_pairs={{0,1},{1,0},{2,3},{3,2},{4,5},{5,4},{6,7},{7,6},{8,9},{9,8},{10,11... | collective-permute-start | bytes 12296 | tf_op jit(solution)/shard_map/ppermute | solution.py:21
  39.9 1.3 %collective-permute-start.13 = (bf16[16,128]{1,0:T(8,128)(2,1)S(1)}, bf16[16,128]{1,0:T(8,128)(2,1)S(1)}, u32[]{:S(2)}, u32[]{:S(2)}) collective-permute-start(bf16[16,128]{1,0:T(8,128)(2,1)S(1)} %collective-permute-done.12), channel_id=1, source_target_pairs={{0,1},{1,0},{2,3},{3,2},{4,5},{5,4},{6,7},{7,6},{8,9},{9,8},{10,11... | collective-permute-start | bytes 12296 | tf_op jit(solution)/shard_map/ppermute | solution.py:21
  40.0 1.7 %collective-permute-start.18 = (bf16[16,128]{1,0:T(8,128)(2,1)S(1)}, bf16[16,128]{1,0:T(8,128)(2,1)S(1)}, u32[]{:S(2)}, u32[]{:S(2)}) collective-permute-start(bf16[16,128]{1,0:T(8,128)(2,1)S(1)} %collective-permute-done.17), channel_id=1, source_target_pairs={{0,1},{1,0},{2,3},{3,2},{4,5},{5,4},{6,7},{7,6},{8,9},{9,8},{10,11... | collective-permute-start | bytes 12296 | tf_op jit(solution)/shard_map/ppermute | solution.py:21
  41.2 2.1 %copy-start.15 = (bf16[16,128]{1,0:T(8,128)(2,1)}, bf16[16,128]{1,0:T(8,128)(2,1)S(1)}, u32[]{:S(2)}) copy-start(bf16[16,128]{1,0:T(8,128)(2,1)S(1)} %collective-permute-done.13.refs_5_) | copy-start | bytes 12292
  41.2 21.5 %collective-permute-start.23 = (bf16[96,2176]{1,0:T(8,128)(2,1)S(1)}, bf16[96,2176]{1,0:T(8,128)(2,1)S(1)}, u32[]{:S(2)}, u32[]{:S(2)}) collective-permute-start(bf16[96,2176]{1,0:T(8,128)(2,1)S(1)} %pad_maximum_fusion.refs_1_.refs_7_.refs_9_), channel_id=1, source_target_pairs={{0,16},{16,0},{1,17},{17,1},{2,18},{18,2},{3,19},{19,3},{4,20},{20... | collective-permute-start | bytes 1253384 | tf_op jit(solution)/shard_map/ppermute | solution.py:26
  41.8 1.5 %copy-start.16 = (bf16[16,128]{1,0:T(8,128)(2,1)}, bf16[16,128]{1,0:T(8,128)(2,1)S(1)}, u32[]{:S(2)}) copy-start(bf16[16,128]{1,0:T(8,128)(2,1)S(1)} %collective-permute-done.18.refs_6_) | copy-start | bytes 12292
  41.8 22.8 %collective-permute-start.24 = (bf16[96,2176]{1,0:T(8,128)(2,1)S(1)}, bf16[96,2176]{1,0:T(8,128)(2,1)S(1)}, u32[]{:S(2)}, u32[]{:S(2)}) collective-permute-start(bf16[96,2176]{1,0:T(8,128)(2,1)S(1)} %collective-permute-done.5.refs_3_.refs_9_.refs_11_), channel_id=1, source_target_pairs={{0,16},{16,0},{1,17},{17,1},{2,18},{18,2},{3,19},{19,3},{4,20},{20... | collective-permute-start | bytes 1253384 | tf_op jit(solution)/shard_map/ppermute | solution.py:26
  43.3 0.8 copy-start.4
  62.6 2.5 %collective-permute-start.22 = (bf16[96,2176]{1,0:T(8,128)(2,1)}, bf16[96,2176]{1,0:T(8,128)(2,1)S(1)}, u32[]{:S(2)}, u32[]{:S(2)}) collective-permute-start(bf16[96,2176]{1,0:T(8,128)(2,1)} %get-tuple-element.30), channel_id=1, source_target_pairs={{0,1},{1,0},{2,3},{3,2},{4,5},{5,4},{6,7},{7,6},{8,9},{9,8},{10,11... | collective-permute-start | bytes 1253384 | tf_op jit(solution)/shard_map/ppermute | solution.py:21
  62.7 2.4 %copy-start.6 = (bf16[96,2176]{1,0:T(8,128)(2,1)}, bf16[96,2176]{1,0:T(8,128)(2,1)S(1)}, u32[]{:S(2)}) copy-start(bf16[96,2176]{1,0:T(8,128)(2,1)S(1)} %collective-permute-done.23.refs_2_.refs_6_.refs_13_) | copy-start | bytes 1253380
  62.7 6.8 %collective-permute-start.31 = (bf16[96,2176]{1,0:T(8,128)(2,1)S(1)}, bf16[96,2176]{1,0:T(8,128)(2,1)S(1)}, u32[]{:S(2)}, u32[]{:S(2)}) collective-permute-start(bf16[96,2176]{1,0:T(8,128)(2,1)S(1)} %collective-permute-done.23.refs_2_.refs_6_.refs_13_), channel_id=1, source_target_pairs={{0,1},{1,0},{2,3},{3,2},{4,5},{5,4},{6,7},{7,6},{8,9},{9,8},{10,11... | collective-permute-start | bytes 1253384 | tf_op jit(solution)/shard_map/ppermute | solution.py:21
  64.6 0.8 copy-start.7
  64.6 4.9 %collective-permute-start.32 = (bf16[96,2176]{1,0:T(8,128)(2,1)S(1)}, bf16[96,2176]{1,0:T(8,128)(2,1)}, u32[]{:S(2)}, u32[]{:S(2)}) collective-permute-start(bf16[96,2176]{1,0:T(8,128)(2,1)S(1)} %collective-permute-done.24.refs_3_.refs_8_.refs_15_), channel_id=1, source_target_pairs={{0,1},{1,0},{2,3},{3,2},{4,5},{5,4},{6,7},{7,6},{8,9},{9,8},{10,11... | collective-permute-start | bytes 1253384 | tf_op jit(solution)/shard_map/ppermute | solution.py:21
  64.6 4.9 %collective-permute-start.30 = (bf16[96,2048]{1,0:T(8,128)(2,1)}, bf16[96,2048]{1,0:T(8,128)(2,1)S(1)}, u32[]{:S(2)}, u32[]{:S(2)}) collective-permute-start(bf16[96,2048]{1,0:T(8,128)(2,1)} %collective-permute-done.20.refs_14_.refs_10_.refs_4_.refs_7_), channel_id=1, source_target_pairs={{0,1},{1,0},{2,3},{3,2},{4,5},{5,4},{6,7},{7,6},{8,9},{9,8},{10,11... | collective-permute-start | bytes 1179656 | tf_op jit(solution)/shard_map/ppermute | solution.py:21
  65.1 0.8 copy-start.8
  67.9 12.4 %collective-permute-start.25 = (bf16[96,2176]{1,0:T(8,128)(2,1)}, bf16[96,2176]{1,0:T(8,128)(2,1)S(1)}, u32[]{:S(2)}, u32[]{:S(2)}) collective-permute-start(bf16[96,2176]{1,0:T(8,128)(2,1)} %shard_map.122.refs_2_), channel_id=1, source_target_pairs={{0,2},{1,3},{2,0},{3,1},{4,6},{5,7},{6,4},{7,5},{8,10},{9,11},{10,... | collective-permute-start | bytes 1253384 | tf_op jit(solution)/shard_map/ppermute | solution.py:21
  69.5 10.7 %collective-permute-start.21 = (bf16[96,2048]{1,0:T(8,128)(2,1)}, bf16[96,2048]{1,0:T(8,128)(2,1)S(1)}, u32[]{:S(2)}, u32[]{:S(2)}) collective-permute-start(bf16[96,2048]{1,0:T(8,128)(2,1)} %get-tuple-element.28), channel_id=1, source_target_pairs={{0,1},{1,0},{2,3},{3,2},{4,5},{5,4},{6,7},{7,6},{8,9},{9,8},{10,11... | collective-permute-start | bytes 1179656 | tf_op jit(solution)/shard_map/ppermute | solution.py:21
  69.5 0.8 copy-start.18
  69.5 0.9 copy-start.13
  80.2 0.7 copy-start.11
  80.2 0.9 copy-start.5
  83.3 6.8 %collective-permute-start.26 = (bf16[24,2176]{1,0:T(8,128)(2,1)}, bf16[24,2176]{1,0:T(8,128)(2,1)S(1)}, u32[]{:S(2)}, u32[]{:S(2)}) collective-permute-start(bf16[24,2176]{1,0:T(8,128)(2,1)} %get-tuple-element.32.refs_23_), channel_id=1, source_target_pairs={{0,4},{1,5},{2,6},{3,7},{4,0},{5,1},{6,2},{7,3},{8,12},{9,13},{10,... | collective-permute-start | bytes 313352 | tf_op jit(solution)/shard_map/ppermute | solution.py:21
  84.1 11.4 %collective-permute-start.27 = (bf16[24,2176]{1,0:T(8,128)(2,1)}, bf16[24,2176]{1,0:T(8,128)(2,1)S(1)}, u32[]{:S(2)}, u32[]{:S(2)}) collective-permute-start(bf16[24,2176]{1,0:T(8,128)(2,1)} %get-tuple-element.33.refs_24_), channel_id=1, source_target_pairs={{0,8},{1,9},{2,10},{3,11},{4,12},{5,13},{6,14},{7,15},{8,0},{9,1},... | collective-permute-start | bytes 313352 | tf_op jit(solution)/shard_map/ppermute | solution.py:21
  86.7 8.8 %collective-permute-start.28 = (bf16[24,2176]{1,0:T(8,128)(2,1)}, bf16[24,2176]{1,0:T(8,128)(2,1)S(1)}, u32[]{:S(2)}, u32[]{:S(2)}) collective-permute-start(bf16[24,2176]{1,0:T(8,128)(2,1)} %get-tuple-element.34.refs_25_), channel_id=1, source_target_pairs={{0,12},{1,13},{2,14},{3,15},{4,8},{5,9},{6,10},{7,11},{8,4},{9,5},... | collective-permute-start | bytes 313352 | tf_op jit(solution)/shard_map/ppermute | solution.py:21
  95.5 8.8 %collective-permute-start.29 = (bf16[16,384]{1,0:T(8,128)(2,1)S(1)}, bf16[16,384]{1,0:T(8,128)(2,1)S(1)}, u32[]{:S(2)}, u32[]{:S(2)}) collective-permute-start(bf16[16,384]{1,0:T(8,128)(2,1)S(1)} %reshape.39), channel_id=1, source_target_pairs={{0,16},{16,0},{1,17},{17,1},{2,18},{18,2},{3,19},{19,3},{4,20},{20... | collective-permute-start | bytes 36872 | tf_op jit(solution)/shard_map/ppermute | solution.py:26
  104.2 4.7 %copy-start.14 = (bf16[2048,16]{0,1:T(8,128)(2,1)S(1)}, bf16[2048,16]{0,1:T(8,128)(2,1)}, u32[]{:S(2)}) copy-start(bf16[2048,16]{0,1:T(8,128)(2,1)} %param.11) | copy-start | bytes 196612
  104.2 4.7 %copy-start.17 = (bf16[24,2176]{1,0:T(8,128)(2,1)S(1)}, bf16[24,2176]{1,0:T(8,128)(2,1)}, u32[]{:S(2)}) copy-start(bf16[24,2176]{1,0:T(8,128)(2,1)} %get-tuple-element.31) | copy-start | bytes 313348

commit v5 on v4

--- a/solution.py
+++ b/solution.py
@@ -59,8 +59,16 @@
     return -(-value // unit) * unit
 
 
-def pack_kernel(ids_ref, tok_ref, router_ref, out):
+def pack_kernel(slots, me_ref, ids_ref, tok_ref, router_ref, out, place_ref):
     experts = router_ref.shape[0]
+    rows = tok_ref.shape[0]
+    at = lax.broadcasted_iota(jnp.int32, place_ref.shape, 1)
+    place = jnp.zeros(place_ref.shape, jnp.int32)
+    for index, offset in enumerate(slots):
+        first = index * rows
+        here = (at >= first) & (at < first + rows)
+        place = jnp.where(here, (me_ref[0] ^ offset) * rows + at - first, place)
+    place_ref[...] = place
     rest = contract(tok_ref[...], router_ref[...], 1, 1)
     lane = lax.broadcasted_iota(jnp.int32, out.shape, 1)
     packed = jnp.zeros(out.shape, jnp.float32)
@@ -77,7 +85,8 @@
 
 
 def gate_kernel(parts, experts, me_ref, *refs):
-    grad, gate_ref, logits_ref, packed, sems = (refs[:parts], *refs[parts:])
+    grad, gate_out, logits_out = (refs[:parts], *refs[parts : parts + 2])
+    packed, gate_ref, logits_ref, sems = refs[parts + 2 :]
     copies = Copies(sems)
     extra = packed.shape[1]
     wait(copies.stack(grad, packed, pl.ds(grad[0].shape[1] - extra, extra)))
@@ -89,10 +98,12 @@
         columns.append(terms[0] + terms[1] + terms[2])
     logits = jnp.concatenate(columns, axis=1)
     logits_ref[...] = logits
+    results = [copies.start(logits_ref, logits_out)]
     gates = experts * balancer_forward_pass(logits)[0][-1]
     row = lax.broadcasted_iota(jnp.int32, gates.shape, 0)
     mine = jnp.sum(jnp.where(row == me_ref[0], gates, 0.0), axis=0, keepdims=True)
     gate_ref[...] = jnp.transpose(jnp.broadcast_to(mine, (LANES, gates.shape[1])))
+    wait([*results, copies.start(gate_ref, gate_out)])
 
 
 def kernel_call(
@@ -260,7 +271,7 @@
     return pl.ds(start if isinstance(index, int) else pl.multiple_of(start, ROW_TILE), ROW_TILE)
 
 
-def expert_kernel(parts, me_ref, gate_ref, place_ref, *refs):
+def expert_kernel(parts, me_ref, place_ref, gate_all, *refs):
     tok, grad, sources = (refs[:parts], refs[parts : 2 * parts], refs[2 * parts : 2 * parts + 3])
     refs = refs[2 * parts + 3 :]
     sum_outs, scaled_outs = (refs[:parts], refs[parts : parts + 3])
@@ -272,12 +283,12 @@
     ff_width = wd.shape[0]
     blocks = project_start(copies, tok, rows_in, sources, (wg, wu))
     grad_here = copies.stack(grad, rows_grad)
+    grad_here.append(copies.start(gate_all.at[pl.ds(0, rows), :], gate))
     down = Tiles(copies, sources[2].at[0], wd, 0, FF_TILE)
     project(blocks, rows_in, (gate_pre, up_pre), (wg, wu))
     backward(grad_here, rows_grad, hidden_grad, down)
-    gate[...] = mask_of(me_ref, rows_grad[:, width : width + LANES])
-    column[...] = gate[...]
-    gate[...] *= gate_ref[:rows, :]
+    column[...] = mask_of(me_ref, rows_grad[:, width : width + LANES])
+    gate[...] *= column[...]
 
     def terms(index):
         cut = row_cut(index)
@@ -326,8 +337,8 @@
     half = jnp.bfloat16
     narrow = pltpu.VMEM((rows, ff_width), half)
     return kernel_call(
-        functools.partial(expert_kernel, len(tok)), (me,), (gate, place),
-        (*tok, *grad, *weights),
+        functools.partial(expert_kernel, len(tok)), (me,), (place,),
+        (gate, *tok, *grad, *weights),
         [shape(part.shape[0], width + LANES * (at > 1)) for at, part in enumerate(tok)]
         + [shape(rows, ff_width)] * 3,
         [pltpu.VMEM((rows, width), half), pltpu.VMEM((rows, grad[0].shape[1]), half)]
@@ -336,7 +347,7 @@
         + [narrow] * 5 + [pltpu.VMEM((rows, width + LANES), half)]
         + [pltpu.VMEM((rows, LANES), jnp.float32)] * 2,
         2 * len(tok) + (len(tok) + 2) * len(tiles(width, 2 * FF_TILE))
-        + len(tiles(ff_width, FF_TILE)) + 3,
+        + len(tiles(ff_width, FF_TILE)) + 4,
         len(tok) + 3, after, 5 * rows * width * ff_width,
     )
 
@@ -360,7 +371,7 @@
     return jnp.where(row == place_ref[...], 1.0, 0.0).astype(jnp.bfloat16)
 
 
-def near_kernel(pieces, keep, got, out, keep_here, got_here, total, sems):
+def near_kernel(pieces, keep, got, out, score_out, keep_here, got_here, total, sems):
     copies = Copies(sems)
     wait([copies.start(keep, keep_here), copies.start(got, got_here)])
     width = total.shape[1] - LANES
@@ -369,11 +380,14 @@
     ).astype(total.dtype)
     scores = first_rows(keep_here[: 2 * SUBLANES, width:], pieces)
     scores += first_rows(got_here[: 2 * SUBLANES, width:], pieces)
-    total[:, width:] = placed(scores, total.shape[0]).astype(total.dtype)
+    block = placed(scores, total.shape[0]).astype(total.dtype)
+    total[:, width:] = block
+    score_out[...] = block[: score_out.shape[0]]
     wait([copies.start(total, out)])
 
 
-def ready_kernel(pieces, keep, got, near, across, *refs):
+def ready_kernel(pieces, others, *refs):
+    other_scores, (keep, got, near, across, *refs) = (refs[:others], refs[others:])
     outs, refs = (refs[: len(refs) - 6], refs[len(refs) - 6 :])
     keep_here, got_here, near_here, across_here, made, sems = refs
     copies = Copies(sems)
@@ -388,7 +402,10 @@
     width = keep_here.shape[1]
     scores = first_rows(near_here[: 4 * SUBLANES, width:], 2 * pieces)
     scores += first_rows(across_here[: 4 * SUBLANES, width:], 2 * pieces)
-    block = placed(scores, rows)
+    for other in other_scores:
+        scores += first_rows(other[...], 2 * pieces)
+    blocks = [placed(scores[at : at + rows], rows) for at in range(0, len(scores), rows)]
+    block = jnp.concatenate(blocks, axis=1)
     total = keep_here[...].astype(jnp.float32) + got_here[...].astype(jnp.float32)
     total += across_here[:, :width].astype(jnp.float32)
     results = []
@@ -399,7 +416,7 @@
     wait(results)
 
 
-def others_kernel(parts, start, me_ref, gate_ref, *refs):
+def others_kernel(parts, start, me_ref, gate_all, *refs):
     tok, grad, sources = (refs[:parts], refs[parts : 2 * parts], refs[2 * parts : 2 * parts + 3])
     outs, refs = (refs[2 * parts + 3 : 2 * parts + 6], refs[2 * parts + 6 :])
     rows_in, rows_grad, gate_pre, up_pre, hidden_grad, wg, wu, wd, hs, gs, us, gate, sems = refs
@@ -408,11 +425,11 @@
     ff_width = wd.shape[0]
     blocks = project_start(copies, tok, rows_in, sources, (wg, wu))
     grad_here = copies.stack(grad, rows_grad)
+    grad_here.append(copies.start(gate_all.at[pl.ds(start, rows), :], gate))
     down = Tiles(copies, sources[2].at[0], wd, 0, FF_TILE)
     project(blocks, rows_in, (gate_pre, up_pre), (wg, wu))
     backward(grad_here, rows_grad, hidden_grad, down)
-    gate[...] = mask_of(me_ref, rows_grad[:, width : width + LANES])
-    gate[...] *= gate_ref[start : start + rows, :]
+    gate[...] *= mask_of(me_ref, rows_grad[:, width : width + LANES])
 
     def terms(index):
         cut = row_cut(index)
@@ -430,14 +447,15 @@
     width, ff_width = weights[0].shape[1:]
     half = jnp.bfloat16
     return kernel_call(
-        functools.partial(others_kernel, len(tok), start), (me,), (gate,), (*tok, *grad, *weights),
+        functools.partial(others_kernel, len(tok), start), (me,), (),
+        (gate, *tok, *grad, *weights),
         [shape(rows, ff_width)] * 3,
         [pltpu.VMEM((rows, width), half), pltpu.VMEM((rows, grad[0].shape[1]), half)]
         + [pltpu.VMEM((rows, ff_width), jnp.float32)] * 3
         + [pltpu.VMEM((width, ff_width), half)] * 2 + [pltpu.VMEM((ff_width, width), half)]
         + [pltpu.VMEM((rows, ff_width), half)] * 3 + [pltpu.VMEM((rows, LANES), jnp.float32)],
         len(tok) + (len(tok) + 2) * len(tiles(width, 2 * FF_TILE))
-        + len(tiles(ff_width, FF_TILE)) + 3,
+        + len(tiles(ff_width, FF_TILE)) + 4,
         3, after, 3 * rows * width * ff_width,
     )
 
@@ -522,10 +540,12 @@
 
 
 def router_kernel(parts, me_ref, *refs):
-    logits_ref, score_ref, place_ref, *tok = refs[: 3 + parts]
-    grad_ref, router_ref, rows, sems = refs[3 + parts :]
+    score_ref, place_ref, logits_all, *tok = refs[: 3 + parts]
+    grad_ref, router_ref, rows, logits_ref, sems = refs[3 + parts :]
     copies = Copies(sems)
+    logits_here = copies.start(logits_all, logits_ref)
     rows_here = copies.stack(tok, rows)
+    logits_here.wait()
     logits = logits_ref[...]
     experts = logits.shape[0]
     row = lax.broadcasted_iota(jnp.int32, (experts, experts), 0)
@@ -557,9 +577,10 @@
         return jnp.concatenate([array] + [swap_expert(array, 4 * k) for k in range(1, far)], axis=0)
 
     tok_line = along(tokens)
-    (packed,) = kernel_call(
-        pack_kernel, (), (expert_ids, tokens, router_weight.T), (),
-        [shape(tok_rows, round_up(4 * experts, LANES))], (), 0,
+    slots = [4 * j + 2 * i + k for i in range(2) for k in range(2) for j in range(far)]
+    packed, place = kernel_call(
+        functools.partial(pack_kernel, slots), (me,), (expert_ids, tokens, router_weight.T), (),
+        [shape(tok_rows, round_up(4 * experts, LANES)), shape(1, 2 * chunk, jnp.int32)], (), 0,
     )
     columns = [out_grad, packed[:, : 4 * experts]]
     for offset in range(1, groups):
@@ -587,46 +608,52 @@
 
     moved_tok = moved((tok_line, tok_next), 1) if at_once else []
     moved_grad = moved((grad_line, grad_next), 1) if at_once else []
-    early = []
-    if at_once:
-        for part, hops in ((moved_tok[1], 2), (tok_parts[3], 3)):
-            corner = part[: 2 * SUBLANES, :LANES]
-            for _ in range(hops):
-                corner = swap_expert(corner, 1)
-            early.append(corner)
+    early = [part[: 2 * SUBLANES, :LANES] for part in moved_tok[1:2]]
     extra = grad_line.shape[1] - width
+    wide = jnp.float32
+    all_rows = 2 * chunk * groups
     gate, logits = kernel_call(
         functools.partial(gate_kernel, len(grad_parts), experts), (me,), (), grad_parts,
-        [shape(2 * chunk * groups, LANES, jnp.float32), shape(experts, 2 * chunk * groups, jnp.float32)],
-        [pltpu.VMEM((2 * chunk, extra), jnp.bfloat16)], len(grad_parts), 0, early,
-    )
-    slots = [4 * j + 2 * i + k for i in range(2) for k in range(2) for j in range(far)]
-    slots = jnp.array(slots, jnp.int32) ^ me
-    place = slots[:, None] * tok_rows + jnp.arange(tok_rows, dtype=jnp.int32)[None, :]
-    place = place.reshape(1, 2 * chunk)
+        [shape(all_rows, LANES, wide), shape(experts, all_rows, wide)],
+        [
+            pltpu.VMEM((2 * chunk, extra), jnp.bfloat16), pltpu.VMEM((all_rows, LANES), wide),
+            pltpu.VMEM((experts, all_rows), wide),
+        ],
+        len(grad_parts) + 2, 2, early,
+    )
     pieces = round_up(2 * chunk, LANES) // LANES
 
     keep0, send0, keep1, send1, *scaled = expert_call(
-        me, gate, place, tok_parts, grad_parts, weights, moved_tok[2:3]
+        me, gate, place, tok_parts, grad_parts, weights, moved_tok[3:4]
     )
     given = [scaled]
     got1, got0 = (swap_expert(send1, 1), swap_expert(send0, 1))
-    (near,) = kernel_call(
-        functools.partial(near_kernel, pieces), (), (), (keep1, got1), [shape(*keep1.shape)],
+    near, near_score = kernel_call(
+        functools.partial(near_kernel, pieces), (), (), (keep1, got1),
+        [shape(*keep1.shape), shape(round_up(2 * pieces, 2 * SUBLANES), LANES)],
         [pltpu.VMEM(keep1.shape, keep1.dtype)] * 3, 3, 1, moved_grad[0::2],
     )
+    other_scores = []
+    for offset in range(1, groups):
+        moved_score = swap_group(near_score, offset)
+        other_scores += [moved_score, swap_expert(moved_score, 2)]
     across = swap_expert(near, 2)
+    count = 4 * pieces * groups
+    behind = round_up(count, tok_rows) // tok_rows * LANES
     ready = kernel_call(
-        functools.partial(ready_kernel, pieces), (), (), (keep0, got0, near, across),
-        [shape(tok_rows, width + LANES)] * far,
+        functools.partial(ready_kernel, pieces, len(other_scores)), (), other_scores,
+        (keep0, got0, near, across), [shape(tok_rows, width + behind)] * far,
         [pltpu.VMEM(keep0.shape, keep0.dtype)] * 2 + [pltpu.VMEM(near.shape, near.dtype)] * 2
-        + [pltpu.VMEM((far, tok_rows, width + LANES), near.dtype)], 4 + far, far,
+        + [pltpu.VMEM((far, tok_rows, width + behind), near.dtype)], 4 + far, far,
     )
     arrived = [ready[0]] + [swap_expert(ready[k], 4 * k) for k in range(1, far)]
     row_sum = sum(part[:, :width].astype(jnp.float32) for part in arrived)
-    score = jnp.stack([part[: 4 * pieces, width:] for part in arrived])
-    score = score.reshape(experts, pieces * LANES)
-    score = jnp.stack([score] + [swap_group(score, offset) for offset in range(1, groups)])
+    score = [
+        jnp.concatenate([part[:, at : at + LANES] for at in range(width, width + behind, LANES)])
+        for part in arrived
+    ]
+    score = jnp.stack([part[:count].reshape(groups, 4, pieces * LANES) for part in score], axis=1)
+    score = score.reshape(groups, experts, pieces * LANES)
     to_send = ready[1:]
 
     token_rows = list(tok_parts)
@@ -651,9 +678,11 @@
     final = [t.astype(jnp.bfloat16) for t in totals]
 
     logit_grad, grad_router = kernel_call(
-        functools.partial(router_kernel, len(token_rows)), (me,), (logits, score, place), token_rows,
+        functools.partial(router_kernel, len(token_rows)), (me,), (score, place),
+        (logits, *token_rows),
         [shape(*logits.shape), shape(experts, width, jnp.float32)],
-        [pltpu.VMEM((logits.shape[1], width), jnp.bfloat16)], len(token_rows),
+        [pltpu.VMEM((logits.shape[1], width), jnp.bfloat16), pltpu.VMEM(logits.shape, wide)],
+        len(token_rows) + 1,
     )
     row_sum = row_sum + contract(logit_grad[:, :tok_rows], router_weight, 0, 1)
     return (row_sum.astype(jnp.bfloat16), grad_router.T, *final)

time: 111 us -> 103 us (0.928)
  waiting for transfers between devices: 25.1 us -> 16.8 us
  other arithmetic: 1.38 us -> 0.06 us
  starting transfers between devices: 30.6 us -> 31.8 us
    ppermute x27 -> x23, waiting for transfers between devices: 19.2 us -> 11.8 us  [swap_expert(): return lax.ppermute(array, 'expert', [(i, i ^ offset) for i in range(size)])]
    ppermute x27 -> x23, starting transfers between devices: 22.3 us -> 23.6 us  [swap_expert(): return lax.ppermute(array, 'expert', [(i, i ^ offset) for i in range(size)])]
    unnamed x42 -> x50, local copies, waits for them, and re-layouts: 5.53 us -> 6.66 us
  transfers between devices with their start and end apart: 33 -> 29, of which waited for: 11 -> 9; matrix products, arithmetic and copies ran while one was open for 5% -> 4% of each run, Pallas kernels for 33% -> 35%
where the time goes in v5:
time: 103 us
  Pallas kernels  42.7 us (41%)
  starting transfers between devices  31.8 us (31%)
  waiting for transfers between devices  16.8 us (16%)
  local copies, waits for them, and re-layouts  9 us (9%)
  matrix products  1.53 us (1%)
  between operations  1.03 us (1%)
    pallas_call x8, Pallas kernels, kernel_call(): pl.pallas_call(body, in_specs=[pl.BlockSpec(memory_space=pltpu.SMEM)] * l...  42.7 us
    ppermute x23, starting transfers between devices, swap_expert(): return lax.ppermute(array, 'expert', [(i, i ^ offset) for i in range(size)])  23.6 us
    ppermute x23, waiting for transfers between devices, swap_expert(): return lax.ppermute(array, 'expert', [(i, i ^ offset) for i in range(size)])  11.8 us
    ppermute x6, starting transfers between devices, swap_group(): return lax.ppermute(array, 'dp', [(i, i ^ offset) for i in range(size)])  8.24 us
    unnamed x50, local copies, waits for them, and re-layouts  6.66 us
    ppermute x6, waiting for transfers between devices, swap_group(): return lax.ppermute(array, 'dp', [(i, i ^ offset) for i in range(size)])  4.98 us
  transfers between devices with their start and end apart: 29, of which 9 were waited for; matrix products, arithmetic and copies ran while one was open for 4% of the time, Pallas kernels for 35%

profile of v5, /device:TPU:0, one launch (start us, length us, event | category | flops | bytes accessed | tf_op | source)
XLA Modules:
  0.0 102.9 jit_solution(6062976049370925161)
XLA Ops:
  0.6 4.1 %collective-permute-start.8 = (bf16[24,2048]{1,0:T(8,128)(2,1)}, bf16[24,2048]{1,0:T(8,128)(2,1)S(1)}, u32[]{:S(2)}, u32[]{:S(2)}) collective-permute-start(bf16[24,2048]{1,0:T(8,128)(2,1)} %refs_2_.1), channel_id=1, source_target_pairs={{0,8},{1,9},{2,10},{3,11},{4,12},{5,13},{6,14},{7,15},{8,0},{9,1},... | collective-permute-start | bytes 294920 | tf_op jit(solution)/shard_map/ppermute | solution.py:21
  4.7 1.6 %collective-permute-start.7 = (bf16[24,2048]{1,0:T(8,128)(2,1)}, bf16[24,2048]{1,0:T(8,128)(2,1)S(1)}, u32[]{:S(2)}, u32[]{:S(2)}) collective-permute-start(bf16[24,2048]{1,0:T(8,128)(2,1)} %refs_2_.1), channel_id=1, source_target_pairs={{0,4},{1,5},{2,6},{3,7},{4,0},{5,1},{6,2},{7,3},{8,12},{9,13},{10,... | collective-permute-start | bytes 294920 | tf_op jit(solution)/shard_map/ppermute | solution.py:21
  6.3 1.4 %copy.12.refs_1_ = s32[24,8]{1,0:T(8,128)} copy(s32[24,8]{0,1:T(8,128)} %param.9) | data formatting | bytes 1536 | tf_op args[2]
  7.7 1.8 %shard_map.110 = (bf16[24,128]{1,0:T(8,128)(2,1)}, s32[1,384]{1,0:T(1,128)}) custom-call(s32[1]{0:T(128)} %bitcast.refs_0_, s32[24,8]{1,0:T(8,128)} %copy.12.refs_1_, bf16[24,2048]{1,0:T(8,128)(2,1)} %refs_2_.1, bf16[16,2048]{1,0:T(8,128)(2,1)} %bitcast.10), custom_call_target="tpu_custom_call" | custom-call | flops 2000000 | bytes 5000 | tf_op jit(solution)/shard_map/pallas_call | solution.py:119
  9.5 1.7 %collective-permute-start = (bf16[24,128]{1,0:T(8,128)(2,1)}, bf16[24,128]{1,0:T(8,128)(2,1)S(1)}, u32[]{:S(2)}, u32[]{:S(2)}) collective-permute-start(bf16[24,128]{1,0:T(8,128)(2,1)} %get-tuple-element.31), channel_id=1, source_target_pairs={{0,16},{16,0},{1,17},{17,1},{2,18},{18,2},{3,19},{19,3},{4,20},{20... | collective-permute-start | bytes 18440 | tf_op jit(solution)/shard_map/ppermute | solution.py:26
  11.2 0.9 constant_dynamic-update-slice_fusion.3
  12.1 1.2 %collective-permute-done = bf16[24,128]{1,0:T(8,128)(2,1)S(1)} collective-permute-done((bf16[24,128]{1,0:T(8,128)(2,1)}, bf16[24,128]{1,0:T(8,128)(2,1)S(1)}, u32[]{:S(2)}, u32[]{:S(2)}) %collective-permute-start) | collective-permute-done | bytes 6176 | tf_op jit(solution)/shard_map/ppermute | solution.py:26
  13.3 0.1 slice.48
  13.4 1.0 concatenate.9
  14.4 3.9 %collective-permute-start.3 = (bf16[24,2176]{1,0:T(8,128)(2,1)S(1)}, bf16[24,2176]{1,0:T(8,128)(2,1)S(1)}, u32[]{:S(2)}, u32[]{:S(2)}) collective-permute-start(bf16[24,2176]{1,0:T(8,128)(2,1)S(1)} %concatenate.9), channel_id=1, source_target_pairs={{0,12},{1,13},{2,14},{3,15},{4,8},{5,9},{6,10},{7,11},{8,4},{9,5},... | collective-permute-start | bytes 313352 | tf_op jit(solution)/shard_map/ppermute | solution.py:21
  18.2 0.0 collective-permute-start.2
  18.2 0.0 collective-permute-done.7
  18.2 0.6 collective-permute-start.1
  18.9 0.0 collective-permute-done.8
  19.0 1.7 %collective-permute-start.13 = (bf16[96,2048]{1,0:T(8,128)(2,1)S(1)}, bf16[96,2048]{1,0:T(8,128)(2,1)S(1)}, u32[]{:S(2)}, u32[]{:S(2)}) collective-permute-start(bf16[96,2048]{1,0:T(8,128)(2,1)S(1)} %constant_dynamic-update-slice_fusion.refs_3_.refs_4_.refs_1_), channel_id=1, source_target_pairs={{0,2},{1,3},{2,0},{3,1},{4,6},{5,7},{6,4},{7,5},{8,10},{9,11},{10,... | collective-permute-start | bytes 1179656 | tf_op jit(solution)/shard_map/ppermute | solution.py:21
  20.7 1.5 %collective-permute-start.10 = (bf16[96,2048]{1,0:T(8,128)(2,1)S(1)}, bf16[96,2048]{1,0:T(8,128)(2,1)S(1)}, u32[]{:S(2)}, u32[]{:S(2)}) collective-permute-start(bf16[96,2048]{1,0:T(8,128)(2,1)S(1)} %constant_dynamic-update-slice_fusion.refs_3_.refs_4_.refs_1_), channel_id=1, source_target_pairs={{0,16},{16,0},{1,17},{17,1},{2,18},{18,2},{3,19},{19,3},{4,20},{20... | collective-permute-start | bytes 1179656 | tf_op jit(solution)/shard_map/ppermute | solution.py:26
  22.2 2.9 %collective-permute-done.2 = bf16[24,2176]{1,0:T(8,128)(2,1)S(1)} collective-permute-done((bf16[24,2176]{1,0:T(8,128)(2,1)S(1)}, bf16[24,2176]{1,0:T(8,128)(2,1)S(1)}, u32[]{:S(2)}, u32[]{:S(2)}) %collective-permute-start.2) | collective-permute-done | bytes 104480 | tf_op jit(solution)/shard_map/ppermute | solution.py:21
  25.1 0.0 collective-permute-done.1
  25.2 1.5 %collective-permute-start.5 = (bf16[96,2176]{1,0:T(8,128)(2,1)S(1)}, bf16[96,2176]{1,0:T(8,128)(2,1)S(1)}, u32[]{:S(2)}, u32[]{:S(2)}) collective-permute-start(bf16[96,2176]{1,0:T(8,128)(2,1)S(1)} %pad_maximum_fusion.refs_1_.refs_7_.refs_9_), channel_id=1, source_target_pairs={{0,2},{1,3},{2,0},{3,1},{4,6},{5,7},{6,4},{7,5},{8,10},{9,11},{10,... | collective-permute-start | bytes 1253384 | tf_op jit(solution)/shard_map/ppermute | solution.py:21
  26.7 1.5 %collective-permute-done.13.refs_5_.refs_6_.refs_3_ = bf16[96,2048]{1,0:T(8,128)(2,1)S(1)} collective-permute-done((bf16[96,2048]{1,0:T(8,128)(2,1)S(1)}, bf16[96,2048]{1,0:T(8,128)(2,1)S(1)}, u32[]{:S(2)}, u32[]{:S(2)}) %collective-permute-start.13) | collective-permute-done | bytes 393248 | tf_op jit(solution)/shard_map/ppermute | solution.py:21
  28.2 1.5 %collective-permute-start.15 = (bf16[96,2048]{1,0:T(8,128)(2,1)S(1)}, bf16[96,2048]{1,0:T(8,128)(2,1)S(1)}, u32[]{:S(2)}, u32[]{:S(2)}) collective-permute-start(bf16[96,2048]{1,0:T(8,128)(2,1)S(1)} %collective-permute-done.13.refs_5_.refs_6_.refs_3_), channel_id=1, source_target_pairs={{0,16},{16,0},{1,17},{17,1},{2,18},{18,2},{3,19},{19,3},{4,20},{20... | collective-permute-start | bytes 1179656 | tf_op jit(solution)/shard_map/ppermute | solution.py:26
  29.8 0.0 collective-permute-done.10.refs_8_.refs_2_.refs_5_
  29.8 0.0 collective-permute-start.11
  29.8 0.5 collective-permute-start.4
  30.3 6.3 %collective-permute-done.5.refs_3_.refs_9_.refs_11_ = bf16[96,2176]{1,0:T(8,128)(2,1)S(1)} collective-permute-done((bf16[96,2176]{1,0:T(8,128)(2,1)S(1)}, bf16[96,2176]{1,0:T(8,128)(2,1)S(1)}, u32[]{:S(2)}, u32[]{:S(2)}) %collective-permute-start.5) | collective-permute-done | bytes 417824 | tf_op jit(solution)/shard_map/ppermute | solution.py:21
  36.6 0.5 collective-permute-start.12
  37.1 0.2 collective-permute-done.15.refs_10_.refs_4_.refs_7_
  37.3 0.5 collective-permute-start.16
  37.8 0.6 slice.49.refs_5_
  38.4 1.6 %collective-permute-start.18 = (bf16[96,2176]{1,0:T(8,128)(2,1)S(1)}, bf16[96,2176]{1,0:T(8,128)(2,1)S(1)}, u32[]{:S(2)}, u32[]{:S(2)}) collective-permute-start(bf16[96,2176]{1,0:T(8,128)(2,1)S(1)} %pad_maximum_fusion.refs_1_.refs_7_.refs_9_), channel_id=1, source_target_pairs={{0,16},{16,0},{1,17},{17,1},{2,18},{18,2},{3,19},{19,3},{4,20},{20... | collective-permute-start | bytes 1253384 | tf_op jit(solution)/shard_map/ppermute | solution.py:26
  40.0 0.5 collective-permute-start.19
  40.5 0.2 copy-done.4
  40.8 2.2 %shard_map.111 = (f32[768,128]{1,0:T(8,128)}, f32[16,768]{1,0:T(8,128)}) custom-call(s32[1]{0:T(128)} %bitcast.refs_0_, bf16[96,2176]{1,0:T(8,128)(2,1)} %copy-done, bf16[96,2176]{1,0:T(8,128)(2,1)} %copy-done.3, bf16[96,2176]{1,0:T(8,128)(2,1)} %copy-done.2, bf16[96,2176]{1,0:T(8,128)(2,1)} %copy-done.4, bf16[16,128]{1,0:T(8,128)(2,1)} %slice.49.refs_5_), custom_call_target="tpu_custom_call" | custom-call | flops 2000000 | bytes 5000 | tf_op jit(solution)/shard_map/pallas_call | solution.py:119
  43.0 0.7 copy-done.14
  43.7 0.1 copy-done.15
  43.8 0.2 copy-done.16
  44.0 13.4 %shard_map.112 = (bf16[96,2048]{1,0:T(8,128)(2,1)}, bf16[96,2048]{1,0:T(8,128)(2,1)}, bf16[96,2176]{1,0:T(8,128)(2,1)}, bf16[96,2176]{1,0:T(8,128)(2,1)}, bf16[3...) custom-call(s32[1]{0:T(128)} %bitcast.refs_0_, ...), custom_call_target="tpu_custom_call" | custom-call | flops 6039797760 | bytes 15099494 | tf_op jit(solution)/shard_map/pallas_call | solution.py:119
  57.4 0.1 collective-permute-start.17
  57.5 0.5 collective-permute-start.27
  58.0 1.1 %collective-permute-done.19.refs_3_.refs_8_.refs_15_ = bf16[96,2176]{1,0:T(8,128)(2,1)S(1)} collective-permute-done((bf16[96,2176]{1,0:T(8,128)(2,1)S(1)}, bf16[96,2176]{1,0:T(8,128)(2,1)S(1)}, u32[]{:S(2)}, u32[]{:S(2)}) %collective-permute-start.19) | collective-permute-done | bytes 417824 | tf_op jit(solution)/shard_map/ppermute | solution.py:26
  59.1 0.3 collective-permute-done.17.refs_1_
  59.4 0.4 copy-done.6
  59.9 0.3 copy-done.8
  60.2 2.6 %shard_map.113 = (bf16[96,2176]{1,0:T(8,128)(2,1)}, bf16[16,128]{1,0:T(8,128)(2,1)}) custom-call(bf16[96,2176]{1,0:T(8,128)(2,1)} %get-tuple-element.33.refs_0_, bf16[96,2176]{1,0:T(8,128)(2,1)} %copy-done.8, bf16[96,2176]{1,0:T(8,128)(2,1)} %copy-done.5, bf16[96,2176]{1,0:T(8,128)(2,1)} %copy-done.6), custom_call_target="tpu_custom_call" | custom-call | flops 2000000 | bytes 5000 | tf_op jit(solution)/shard_map/pallas_call | solution.py:119
  62.8 1.4 %collective-permute-start.23 = (bf16[96,2176]{1,0:T(8,128)(2,1)}, bf16[96,2176]{1,0:T(8,128)(2,1)S(1)}, u32[]{:S(2)}, u32[]{:S(2)}) collective-permute-start(bf16[96,2176]{1,0:T(8,128)(2,1)} %get-tuple-element.38.refs_4_), channel_id=1, source_target_pairs={{0,2},{1,3},{2,0},{3,1},{4,6},{5,7},{6,4},{7,5},{8,10},{9,11},{10,... | collective-permute-start | bytes 1253384 | tf_op jit(solution)/shard_map/ppermute | solution.py:21
  64.2 1.4 %collective-permute-start.20 = (bf16[16,128]{1,0:T(8,128)(2,1)}, bf16[16,128]{1,0:T(8,128)(2,1)S(1)}, u32[]{:S(2)}, u32[]{:S(2)}) collective-permute-start(bf16[16,128]{1,0:T(8,128)(2,1)} %get-tuple-element.35), channel_id=1, source_target_pairs={{0,16},{16,0},{1,17},{17,1},{2,18},{18,2},{3,19},{19,3},{4,20},{20... | collective-permute-start | bytes 12296 | tf_op jit(solution)/shard_map/ppermute | solution.py:26
  65.6 2.4 %collective-permute-done.20.refs_0_ = bf16[16,128]{1,0:T(8,128)(2,1)S(1)} collective-permute-done((bf16[16,128]{1,0:T(8,128)(2,1)}, bf16[16,128]{1,0:T(8,128)(2,1)S(1)}, u32[]{:S(2)}, u32[]{:S(2)}) %collective-permute-start.20) | collective-permute-done | bytes 4128 | tf_op jit(solution)/shard_map/ppermute | solution.py:26
  68.0 0.7 collective-permute-start.21
  68.7 0.8 copy-done.21
  69.5 0.7 copy-done.22
  70.2 8.8 %shard_map.116 = (bf16[384,768]{1,0:T(8,128)(2,1)}, bf16[384,768]{1,0:T(8,128)(2,1)}, bf16[384,768]{1,0:T(8,128)(2,1)}) custom-call(s32[1]{0:T(128)} %bitcast.refs_0_, f32[768,128]{1,0:T(8,128)} %get-tuple-element.32.refs_2_.refs_1_, bf16[96,2048]{1,0:T(8,128)(2,1)} %copy-done.12, bf16[96,2048]{1,0:T(8,128)(2,1)} %copy-done.9, bf16[96,2048]{1,0:T(8,128)(2,1)} %copy-done.13, ...), custom_call_target="tpu_custom_call" | custom-call | flops 3623878656 | bytes 9059696 | tf_op jit(solution)/shard_map/pallas_call | solution.py:119
  79.0 0.0 copy-start.10
  79.1 0.0 copy-start.7
  79.1 0.7 copy-done.10
  79.8 0.1 copy-done.7
  79.9 2.9 %shard_map.114 = (bf16[24,2176]{1,0:T(8,128)(2,1)}, bf16[24,2176]{1,0:T(8,128)(2,1)}, bf16[24,2176]{1,0:T(8,128)(2,1)}, bf16[24,2176]{1,0:T(8,128)(2,1)}) custom-call(bf16[16,128]{1,0:T(8,128)(2,1)} %copy-done.18, bf16[16,128]{1,0:T(8,128)(2,1)} %copy-done.19, bf16[96,2048]{1,0:T(8,128)(2,1)} %get-tuple-element.36.refs_2_, bf16[96,2048]{1,0:T(8,128)(2,1)} %copy-done.10, ...), custom_call_target="tpu_custom_call" | custom-call | flops 2000000 | bytes 5000 | tf_op jit(solution)/shard_map/pallas_call | solution.py:119
  82.8 2.8 %collective-permute-start.24 = (bf16[24,2176]{1,0:T(8,128)(2,1)}, bf16[24,2176]{1,0:T(8,128)(2,1)S(1)}, u32[]{:S(2)}, u32[]{:S(2)}) collective-permute-start(bf16[24,2176]{1,0:T(8,128)(2,1)} %get-tuple-element.40.refs_23_), channel_id=1, source_target_pairs={{0,4},{1,5},{2,6},{3,7},{4,0},{5,1},{6,2},{7,3},{8,12},{9,13},{10,... | collective-permute-start | bytes 313352 | tf_op jit(solution)/shard_map/ppermute | solution.py:21
  85.6 3.1 %collective-permute-start.25 = (bf16[24,2176]{1,0:T(8,128)(2,1)}, bf16[24,2176]{1,0:T(8,128)(2,1)S(1)}, u32[]{:S(2)}, u32[]{:S(2)}) collective-permute-start(bf16[24,2176]{1,0:T(8,128)(2,1)} %get-tuple-element.41.refs_24_), channel_id=1, source_target_pairs={{0,8},{1,9},{2,10},{3,11},{4,12},{5,13},{6,14},{7,15},{8,0},{9,1},... | collective-permute-start | bytes 313352 | tf_op jit(solution)/shard_map/ppermute | solution.py:21
  88.8 7.2 %shard_map.117 = (bf16[1,1024,768]{2,1,0:T(8,128)(2,1)}, bf16[1,1024,768]{2,1,0:T(8,128)(2,1)}, bf16[1,384,2048]{2,1,0:T(8,128)(2,1)}) custom-call(s32[1]{0:T(128)} %bitcast.7.refs_0_, bf16[96,2048]{1,0:T(8,128)(2,1)} %copy-done.1, bf16[96,2048]{1,0:T(8,128)(2,1)} %copy-done.14, bf16[96,2048]{1,0:T(8,128)(2,1)} %copy-done.11, bf16[96,2048]{1,0:T(8,128)(2,1)} %copy-done.15, ...), custom_call_target="tpu_custom_call" | custom-call | flops 3623878656 | bytes 9059696 | tf_op jit(solution)/shard_map/pallas_call | solution.py:119
  96.0 0.0 copy-start.17
  96.1 0.7 collective-permute-done.25
  96.8 0.6 reshape.13.refs_1_
  97.5 3.8 %shard_map.115 = (bf16[16,768]{1,0:T(8,128)(2,1)}, f32[16,2048]{1,0:T(8,128)}) custom-call(s32[1]{0:T(128)} %bitcast.refs_0_, bf16[2,16,384]{2,1,0:T(8,128)(2,1)} %reshape.13.refs_1_, s32[1,384]{1,0:T(1,128)} %get-tuple-element.30.refs_1_.refs_2_, f32[16,768]{1,0:T(8,128)} %get-tuple-element.43.refs_3_, bf16[96,2048]{1,0:T(8,128)(2,1)} %copy-done.1, ...), custom_call_target="tpu_custom_call" | custom-call | flops 2000000 | bytes 5000 | tf_op jit(solution)/shard_map/pallas_call | solution.py:119
  101.3 1.5 %fusion = bf16[24,2048]{1,0:T(8,128)(2,1)} fusion(bf16[2048,16]{0,1:T(8,128)(2,1)S(1)} %copy-done.17, bf16[24,2176]{1,0:T(8,128)(2,1)S(1)} %collective-permute-done.26, bf16[24,2176]{1,0:T(8,128)(2,1)S(1)} %collective-permute-done.25, bf16[24,2176]{1,0:T(8,128)(2,1)S(1)} %collective-permute-done.24, bf16[24,2176]{1,0:T(8,128)(2,1)S(1)} %copy-done.20, ...), kind=kOutput, calls=%fused_computation.1 | convolution fusion | flops 2015232 | bytes 561152 | tf_op jit(solution)/shard_map/dot_general | solution.py:30
  (69 shorter events, 0.3 us)
Async XLA Ops:
  0.6 18.3 %collective-permute-start.8 = (bf16[24,2048]{1,0:T(8,128)(2,1)}, bf16[24,2048]{1,0:T(8,128)(2,1)S(1)}, u32[]{:S(2)}, u32[]{:S(2)}) collective-permute-start(bf16[24,2048]{1,0:T(8,128)(2,1)} %refs_2_.1), channel_id=1, source_target_pairs={{0,8},{1,9},{2,10},{3,11},{4,12},{5,13},{6,14},{7,15},{8,0},{9,1},... | collective-permute-start | bytes 294920 | tf_op jit(solution)/shard_map/ppermute | solution.py:21
  4.7 13.5 %collective-permute-start.7 = (bf16[24,2048]{1,0:T(8,128)(2,1)}, bf16[24,2048]{1,0:T(8,128)(2,1)S(1)}, u32[]{:S(2)}, u32[]{:S(2)}) collective-permute-start(bf16[24,2048]{1,0:T(8,128)(2,1)} %refs_2_.1), channel_id=1, source_target_pairs={{0,4},{1,5},{2,6},{3,7},{4,0},{5,1},{6,2},{7,3},{8,12},{9,13},{10,... | collective-permute-start | bytes 294920 | tf_op jit(solution)/shard_map/ppermute | solution.py:21
  6.3 12.6 %collective-permute-start.9 = (bf16[24,2048]{1,0:T(8,128)(2,1)}, bf16[24,2048]{1,0:T(8,128)(2,1)S(1)}, u32[]{:S(2)}, u32[]{:S(2)}) collective-permute-start(bf16[24,2048]{1,0:T(8,128)(2,1)} %refs_2_.1), channel_id=1, source_target_pairs={{0,12},{1,13},{2,14},{3,15},{4,8},{5,9},{6,10},{7,11},{8,4},{9,5},... | collective-permute-start | bytes 294920 | tf_op jit(solution)/shard_map/ppermute | solution.py:21
  9.5 3.8 %collective-permute-start = (bf16[24,128]{1,0:T(8,128)(2,1)}, bf16[24,128]{1,0:T(8,128)(2,1)S(1)}, u32[]{:S(2)}, u32[]{:S(2)}) collective-permute-start(bf16[24,128]{1,0:T(8,128)(2,1)} %get-tuple-element.31), channel_id=1, source_target_pairs={{0,16},{16,0},{1,17},{17,1},{2,18},{18,2},{3,19},{19,3},{4,20},{20... | collective-permute-start | bytes 18440 | tf_op jit(solution)/shard_map/ppermute | solution.py:26
  14.4 7.8 %collective-permute-start.3 = (bf16[24,2176]{1,0:T(8,128)(2,1)S(1)}, bf16[24,2176]{1,0:T(8,128)(2,1)S(1)}, u32[]{:S(2)}, u32[]{:S(2)}) collective-permute-start(bf16[24,2176]{1,0:T(8,128)(2,1)S(1)} %concatenate.9), channel_id=1, source_target_pairs={{0,12},{1,13},{2,14},{3,15},{4,8},{5,9},{6,10},{7,11},{8,4},{9,5},... | collective-permute-start | bytes 313352 | tf_op jit(solution)/shard_map/ppermute | solution.py:21
  18.2 6.9 %collective-permute-start.2 = (bf16[24,2176]{1,0:T(8,128)(2,1)S(1)}, bf16[24,2176]{1,0:T(8,128)(2,1)S(1)}, u32[]{:S(2)}, u32[]{:S(2)}) collective-permute-start(bf16[24,2176]{1,0:T(8,128)(2,1)S(1)} %concatenate.9), channel_id=1, source_target_pairs={{0,8},{1,9},{2,10},{3,11},{4,12},{5,13},{6,14},{7,15},{8,0},{9,1},... | collective-permute-start | bytes 313352 | tf_op jit(solution)/shard_map/ppermute | solution.py:21
  18.2 6.9 %collective-permute-start.1 = (bf16[24,2176]{1,0:T(8,128)(2,1)S(1)}, bf16[24,2176]{1,0:T(8,128)(2,1)S(1)}, u32[]{:S(2)}, u32[]{:S(2)}) collective-permute-start(bf16[24,2176]{1,0:T(8,128)(2,1)S(1)} %concatenate.9), channel_id=1, source_target_pairs={{0,4},{1,5},{2,6},{3,7},{4,0},{5,1},{6,2},{7,3},{8,12},{9,13},{10,... | collective-permute-start | bytes 313352 | tf_op jit(solution)/shard_map/ppermute | solution.py:21
  18.9 24.1 %copy-start.1 = (bf16[96,2048]{1,0:T(8,128)(2,1)}, bf16[96,2048]{1,0:T(8,128)(2,1)S(1)}, u32[]{:S(2)}) copy-start(bf16[96,2048]{1,0:T(8,128)(2,1)S(1)} %constant_dynamic-update-slice_fusion.refs_3_.refs_4_.refs_1_) | copy-start | bytes 1179652
  19.0 9.3 %collective-permute-start.13 = (bf16[96,2048]{1,0:T(8,128)(2,1)S(1)}, bf16[96,2048]{1,0:T(8,128)(2,1)S(1)}, u32[]{:S(2)}, u32[]{:S(2)}) collective-permute-start(bf16[96,2048]{1,0:T(8,128)(2,1)S(1)} %constant_dynamic-update-slice_fusion.refs_3_.refs_4_.refs_1_), channel_id=1, source_target_pairs={{0,2},{1,3},{2,0},{3,1},{4,6},{5,7},{6,4},{7,5},{8,10},{9,11},{10,... | collective-permute-start | bytes 1179656 | tf_op jit(solution)/shard_map/ppermute | solution.py:21
  20.7 9.1 %collective-permute-start.10 = (bf16[96,2048]{1,0:T(8,128)(2,1)S(1)}, bf16[96,2048]{1,0:T(8,128)(2,1)S(1)}, u32[]{:S(2)}, u32[]{:S(2)}) collective-permute-start(bf16[96,2048]{1,0:T(8,128)(2,1)S(1)} %constant_dynamic-update-slice_fusion.refs_3_.refs_4_.refs_1_), channel_id=1, source_target_pairs={{0,16},{16,0},{1,17},{17,1},{2,18},{18,2},{3,19},{19,3},{4,20},{20... | collective-permute-start | bytes 1179656 | tf_op jit(solution)/shard_map/ppermute | solution.py:26
  25.2 15.3 %copy-start = (bf16[96,2176]{1,0:T(8,128)(2,1)}, bf16[96,2176]{1,0:T(8,128)(2,1)S(1)}, u32[]{:S(2)}) copy-start(bf16[96,2176]{1,0:T(8,128)(2,1)S(1)} %pad_maximum_fusion.refs_1_.refs_7_.refs_9_) | copy-start | bytes 1253380
  25.2 11.4 %collective-permute-start.5 = (bf16[96,2176]{1,0:T(8,128)(2,1)S(1)}, bf16[96,2176]{1,0:T(8,128)(2,1)S(1)}, u32[]{:S(2)}, u32[]{:S(2)}) collective-permute-start(bf16[96,2176]{1,0:T(8,128)(2,1)S(1)} %pad_maximum_fusion.refs_1_.refs_7_.refs_9_), channel_id=1, source_target_pairs={{0,2},{1,3},{2,0},{3,1},{4,6},{5,7},{6,4},{7,5},{8,10},{9,11},{10,... | collective-permute-start | bytes 1253384 | tf_op jit(solution)/shard_map/ppermute | solution.py:21
  28.2 14.8 %copy-start.11 = (bf16[96,2048]{1,0:T(8,128)(2,1)}, bf16[96,2048]{1,0:T(8,128)(2,1)S(1)}, u32[]{:S(2)}) copy-start(bf16[96,2048]{1,0:T(8,128)(2,1)S(1)} %collective-permute-done.13.refs_5_.refs_6_.refs_3_) | copy-start | bytes 1179652
  28.2 9.1 %collective-permute-start.15 = (bf16[96,2048]{1,0:T(8,128)(2,1)S(1)}, bf16[96,2048]{1,0:T(8,128)(2,1)S(1)}, u32[]{:S(2)}, u32[]{:S(2)}) collective-permute-start(bf16[96,2048]{1,0:T(8,128)(2,1)S(1)} %collective-permute-done.13.refs_5_.refs_6_.refs_3_), channel_id=1, source_target_pairs={{0,16},{16,0},{1,17},{17,1},{2,18},{18,2},{3,19},{19,3},{4,20},{20... | collective-permute-start | bytes 1179656 | tf_op jit(solution)/shard_map/ppermute | solution.py:26
  29.8 8.6 %copy-start.12 = (bf16[96,2048]{1,0:T(8,128)(2,1)}, bf16[96,2048]{1,0:T(8,128)(2,1)S(1)}, u32[]{:S(2)}) copy-start(bf16[96,2048]{1,0:T(8,128)(2,1)S(1)} %collective-permute-done.10.refs_8_.refs_2_.refs_5_) | copy-start | bytes 1179652
  29.8 7.5 %collective-permute-start.11 = (bf16[96,2048]{1,0:T(8,128)(2,1)S(1)}, bf16[96,2048]{1,0:T(8,128)(2,1)S(1)}, u32[]{:S(2)}, u32[]{:S(2)}) collective-permute-start(bf16[96,2048]{1,0:T(8,128)(2,1)S(1)} %collective-permute-done.10.refs_8_.refs_2_.refs_5_), channel_id=1, source_target_pairs={{0,1},{1,0},{2,3},{3,2},{4,5},{5,4},{6,7},{7,6},{8,9},{9,8},{10,11... | collective-permute-start | bytes 1179656 | tf_op jit(solution)/shard_map/ppermute | solution.py:21
  29.8 8.6 %collective-permute-start.4 = (bf16[96,2176]{1,0:T(8,128)(2,1)S(1)}, bf16[96,2176]{1,0:T(8,128)(2,1)S(1)}, u32[]{:S(2)}, u32[]{:S(2)}) collective-permute-start(bf16[96,2176]{1,0:T(8,128)(2,1)S(1)} %pad_maximum_fusion.refs_1_.refs_7_.refs_9_), channel_id=1, source_target_pairs={{0,1},{1,0},{2,3},{3,2},{4,5},{5,4},{6,7},{7,6},{8,9},{9,8},{10,11... | collective-permute-start | bytes 1253384 | tf_op jit(solution)/shard_map/ppermute | solution.py:21
  36.6 3.9 %copy-start.2 = (bf16[96,2176]{1,0:T(8,128)(2,1)}, bf16[96,2176]{1,0:T(8,128)(2,1)S(1)}, u32[]{:S(2)}) copy-start(bf16[96,2176]{1,0:T(8,128)(2,1)S(1)} %collective-permute-done.5.refs_3_.refs_9_.refs_11_) | copy-start | bytes 1253380
  36.6 3.4 %collective-permute-start.6 = (bf16[96,2176]{1,0:T(8,128)(2,1)S(1)}, bf16[96,2176]{1,0:T(8,128)(2,1)S(1)}, u32[]{:S(2)}, u32[]{:S(2)}) collective-permute-start(bf16[96,2176]{1,0:T(8,128)(2,1)S(1)} %collective-permute-done.5.refs_3_.refs_9_.refs_11_), channel_id=1, source_target_pairs={{0,1},{1,0},{2,3},{3,2},{4,5},{5,4},{6,7},{7,6},{8,9},{9,8},{10,11... | collective-permute-start | bytes 1253384 | tf_op jit(solution)/shard_map/ppermute | solution.py:21
  36.6 6.4 %collective-permute-start.12 = (bf16[96,2048]{1,0:T(8,128)(2,1)S(1)}, bf16[96,2048]{1,0:T(8,128)(2,1)S(1)}, u32[]{:S(2)}, u32[]{:S(2)}) collective-permute-start(bf16[96,2048]{1,0:T(8,128)(2,1)S(1)} %constant_dynamic-update-slice_fusion.refs_3_.refs_4_.refs_1_), channel_id=1, source_target_pairs={{0,1},{1,0},{2,3},{3,2},{4,5},{5,4},{6,7},{7,6},{8,9},{9,8},{10,11... | collective-permute-start | bytes 1179656 | tf_op jit(solution)/shard_map/ppermute | solution.py:21
  37.3 20.1 %copy-start.13 = (bf16[96,2048]{1,0:T(8,128)(2,1)}, bf16[96,2048]{1,0:T(8,128)(2,1)S(1)}, u32[]{:S(2)}) copy-start(bf16[96,2048]{1,0:T(8,128)(2,1)S(1)} %collective-permute-done.15.refs_10_.refs_4_.refs_7_) | copy-start | bytes 1179652
  37.3 5.7 %collective-permute-start.14 = (bf16[96,2048]{1,0:T(8,128)(2,1)S(1)}, bf16[96,2048]{1,0:T(8,128)(2,1)S(1)}, u32[]{:S(2)}, u32[]{:S(2)}) collective-permute-start(bf16[96,2048]{1,0:T(8,128)(2,1)S(1)} %collective-permute-done.13.refs_5_.refs_6_.refs_3_), channel_id=1, source_target_pairs={{0,1},{1,0},{2,3},{3,2},{4,5},{5,4},{6,7},{7,6},{8,9},{9,8},{10,11... | collective-permute-start | bytes 1179656 | tf_op jit(solution)/shard_map/ppermute | solution.py:21
  37.3 20.1 %copy-start.9 = (bf16[96,2048]{1,0:T(8,128)(2,1)}, bf16[96,2048]{1,0:T(8,128)(2,1)S(1)}, u32[]{:S(2)}) copy-start(bf16[96,2048]{1,0:T(8,128)(2,1)S(1)} %collective-permute-done.11.refs_9_.refs_3_.refs_6_) | copy-start | bytes 1179652
  37.3 5.7 %collective-permute-start.16 = (bf16[96,2048]{1,0:T(8,128)(2,1)S(1)}, bf16[96,2048]{1,0:T(8,128)(2,1)S(1)}, u32[]{:S(2)}, u32[]{:S(2)}) collective-permute-start(bf16[96,2048]{1,0:T(8,128)(2,1)S(1)} %collective-permute-done.15.refs_10_.refs_4_.refs_7_), channel_id=1, source_target_pairs={{0,1},{1,0},{2,3},{3,2},{4,5},{5,4},{6,7},{7,6},{8,9},{9,8},{10,11... | collective-permute-start | bytes 1179656 | tf_op jit(solution)/shard_map/ppermute | solution.py:21
  38.4 2.1 %copy-start.3 = (bf16[96,2176]{1,0:T(8,128)(2,1)}, bf16[96,2176]{1,0:T(8,128)(2,1)S(1)}, u32[]{:S(2)}) copy-start(bf16[96,2176]{1,0:T(8,128)(2,1)S(1)} %collective-permute-done.4.refs_2_.refs_8_.refs_10_) | copy-start | bytes 1253380
  38.4 19.0 %collective-permute-start.18 = (bf16[96,2176]{1,0:T(8,128)(2,1)S(1)}, bf16[96,2176]{1,0:T(8,128)(2,1)S(1)}, u32[]{:S(2)}, u32[]{:S(2)}) collective-permute-start(bf16[96,2176]{1,0:T(8,128)(2,1)S(1)} %pad_maximum_fusion.refs_1_.refs_7_.refs_9_), channel_id=1, source_target_pairs={{0,16},{16,0},{1,17},{17,1},{2,18},{18,2},{3,19},{19,3},{4,20},{20... | collective-permute-start | bytes 1253384 | tf_op jit(solution)/shard_map/ppermute | solution.py:26
  40.0 0.8 copy-start.4
  40.0 19.1 %collective-permute-start.19 = (bf16[96,2176]{1,0:T(8,128)(2,1)S(1)}, bf16[96,2176]{1,0:T(8,128)(2,1)S(1)}, u32[]{:S(2)}, u32[]{:S(2)}) collective-permute-start(bf16[96,2176]{1,0:T(8,128)(2,1)S(1)} %collective-permute-done.5.refs_3_.refs_9_.refs_11_), channel_id=1, source_target_pairs={{0,16},{16,0},{1,17},{17,1},{2,18},{18,2},{3,19},{19,3},{4,20},{20... | collective-permute-start | bytes 1253384 | tf_op jit(solution)/shard_map/ppermute | solution.py:26
  42.9 0.8 copy-start.14
  43.0 0.9 copy-start.15
  43.0 1.0 copy-start.16
  57.4 2.0 %collective-permute-start.17 = (bf16[96,2176]{1,0:T(8,128)(2,1)}, bf16[96,2176]{1,0:T(8,128)(2,1)S(1)}, u32[]{:S(2)}, u32[]{:S(2)}) collective-permute-start(bf16[96,2176]{1,0:T(8,128)(2,1)} %get-tuple-element.34), channel_id=1, source_target_pairs={{0,1},{1,0},{2,3},{3,2},{4,5},{5,4},{6,7},{7,6},{8,9},{9,8},{10,11... | collective-permute-start | bytes 1253384 | tf_op jit(solution)/shard_map/ppermute | solution.py:21
  57.5 1.9 %copy-start.5 = (bf16[96,2176]{1,0:T(8,128)(2,1)}, bf16[96,2176]{1,0:T(8,128)(2,1)S(1)}, u32[]{:S(2)}) copy-start(bf16[96,2176]{1,0:T(8,128)(2,1)S(1)} %collective-permute-done.18.refs_2_.refs_6_.refs_13_) | copy-start | bytes 1253380
  57.5 11.2 %collective-permute-start.27 = (bf16[96,2176]{1,0:T(8,128)(2,1)S(1)}, bf16[96,2176]{1,0:T(8,128)(2,1)S(1)}, u32[]{:S(2)}, u32[]{:S(2)}) collective-permute-start(bf16[96,2176]{1,0:T(8,128)(2,1)S(1)} %collective-permute-done.18.refs_2_.refs_6_.refs_13_), channel_id=1, source_target_pairs={{0,1},{1,0},{2,3},{3,2},{4,5},{5,4},{6,7},{7,6},{8,9},{9,8},{10,11... | collective-permute-start | bytes 1253384 | tf_op jit(solution)/shard_map/ppermute | solution.py:21
  59.1 0.8 copy-start.6
  59.1 9.6 %collective-permute-start.28 = (bf16[96,2176]{1,0:T(8,128)(2,1)S(1)}, bf16[96,2176]{1,0:T(8,128)(2,1)S(1)}, u32[]{:S(2)}, u32[]{:S(2)}) collective-permute-start(bf16[96,2176]{1,0:T(8,128)(2,1)S(1)} %collective-permute-done.19.refs_3_.refs_8_.refs_15_), channel_id=1, source_target_pairs={{0,1},{1,0},{2,3},{3,2},{4,5},{5,4},{6,7},{7,6},{8,9},{9,8},{10,11... | collective-permute-start | bytes 1253384 | tf_op jit(solution)/shard_map/ppermute | solution.py:21
  59.4 0.8 copy-start.8
  62.8 16.3 %collective-permute-start.23 = (bf16[96,2176]{1,0:T(8,128)(2,1)}, bf16[96,2176]{1,0:T(8,128)(2,1)S(1)}, u32[]{:S(2)}, u32[]{:S(2)}) collective-permute-start(bf16[96,2176]{1,0:T(8,128)(2,1)} %get-tuple-element.38.refs_4_), channel_id=1, source_target_pairs={{0,2},{1,3},{2,0},{3,1},{4,6},{5,7},{6,4},{7,5},{8,10},{9,11},{10,... | collective-permute-start | bytes 1253384 | tf_op jit(solution)/shard_map/ppermute | solution.py:21
  64.2 14.9 %collective-permute-start.22 = (bf16[96,2048]{1,0:T(8,128)(2,1)}, bf16[96,2048]{1,0:T(8,128)(2,1)S(1)}, u32[]{:S(2)}, u32[]{:S(2)}) collective-permute-start(bf16[96,2048]{1,0:T(8,128)(2,1)} %get-tuple-element.37), channel_id=1, source_target_pairs={{0,1},{1,0},{2,3},{3,2},{4,5},{5,4},{6,7},{7,6},{8,9},{9,8},{10,11... | collective-permute-start | bytes 1179656 | tf_op jit(solution)/shard_map/ppermute | solution.py:21
  64.2 3.8 %collective-permute-start.20 = (bf16[16,128]{1,0:T(8,128)(2,1)}, bf16[16,128]{1,0:T(8,128)(2,1)S(1)}, u32[]{:S(2)}, u32[]{:S(2)}) collective-permute-start(bf16[16,128]{1,0:T(8,128)(2,1)} %get-tuple-element.35), channel_id=1, source_target_pairs={{0,16},{16,0},{1,17},{17,1},{2,18},{18,2},{3,19},{19,3},{4,20},{20... | collective-permute-start | bytes 12296 | tf_op jit(solution)/shard_map/ppermute | solution.py:26
  68.0 11.0 %copy-start.18 = (bf16[16,128]{1,0:T(8,128)(2,1)}, bf16[16,128]{1,0:T(8,128)(2,1)S(1)}, u32[]{:S(2)}) copy-start(bf16[16,128]{1,0:T(8,128)(2,1)S(1)} %collective-permute-done.20.refs_0_) | copy-start | bytes 12292
  68.0 11.1 %collective-permute-start.21 = (bf16[16,128]{1,0:T(8,128)(2,1)S(1)}, bf16[16,128]{1,0:T(8,128)(2,1)S(1)}, u32[]{:S(2)}, u32[]{:S(2)}) collective-permute-start(bf16[16,128]{1,0:T(8,128)(2,1)S(1)} %collective-permute-done.20.refs_0_), channel_id=1, source_target_pairs={{0,2},{1,3},{2,0},{3,1},{4,6},{5,7},{6,4},{7,5},{8,10},{9,11},{10,... | collective-permute-start | bytes 12296 | tf_op jit(solution)/shard_map/ppermute | solution.py:21
  68.7 0.8 copy-start.21
  69.5 0.7 copy-start.22
  79.0 0.7 copy-start.10
  79.0 0.7 copy-start.19
  79.1 0.8 copy-start.7
  82.8 13.2 %collective-permute-start.24 = (bf16[24,2176]{1,0:T(8,128)(2,1)}, bf16[24,2176]{1,0:T(8,128)(2,1)S(1)}, u32[]{:S(2)}, u32[]{:S(2)}) collective-permute-start(bf16[24,2176]{1,0:T(8,128)(2,1)} %get-tuple-element.40.refs_23_), channel_id=1, source_target_pairs={{0,4},{1,5},{2,6},{3,7},{4,0},{5,1},{6,2},{7,3},{8,12},{9,13},{10,... | collective-permute-start | bytes 313352 | tf_op jit(solution)/shard_map/ppermute | solution.py:21
  85.6 11.1 %collective-permute-start.25 = (bf16[24,2176]{1,0:T(8,128)(2,1)}, bf16[24,2176]{1,0:T(8,128)(2,1)S(1)}, u32[]{:S(2)}, u32[]{:S(2)}) collective-permute-start(bf16[24,2176]{1,0:T(8,128)(2,1)} %get-tuple-element.41.refs_24_), channel_id=1, source_target_pairs={{0,8},{1,9},{2,10},{3,11},{4,12},{5,13},{6,14},{7,15},{8,0},{9,1},... | collective-permute-start | bytes 313352 | tf_op jit(solution)/shard_map/ppermute | solution.py:21
  88.8 8.0 %collective-permute-start.26 = (bf16[24,2176]{1,0:T(8,128)(2,1)}, bf16[24,2176]{1,0:T(8,128)(2,1)S(1)}, u32[]{:S(2)}, u32[]{:S(2)}) collective-permute-start(bf16[24,2176]{1,0:T(8,128)(2,1)} %get-tuple-element.42.refs_25_), channel_id=1, source_target_pairs={{0,12},{1,13},{2,14},{3,15},{4,8},{5,9},{6,10},{7,11},{8,4},{9,5},... | collective-permute-start | bytes 313352 | tf_op jit(solution)/shard_map/ppermute | solution.py:21
  88.8 7.2 %copy-start.20 = (bf16[24,2176]{1,0:T(8,128)(2,1)S(1)}, bf16[24,2176]{1,0:T(8,128)(2,1)}, u32[]{:S(2)}) copy-start(bf16[24,2176]{1,0:T(8,128)(2,1)} %get-tuple-element.39) | copy-start | bytes 313348
  96.0 5.3 %copy-start.17 = (bf16[2048,16]{0,1:T(8,128)(2,1)S(1)}, bf16[2048,16]{0,1:T(8,128)(2,1)}, u32[]{:S(2)}) copy-start(bf16[2048,16]{0,1:T(8,128)(2,1)} %param.10) | copy-start | bytes 196612

commit v6 on v5

--- a/solution.py
+++ b/solution.py
@@ -12,7 +12,8 @@
 SUBLANES = 8
 FF_TILE = 256
 ROW_TILE = 32
-GRANT = 56 << 20
+GRANT = 53 << 20
+SMALL_GRANT = 24 << 20
 ROWS_AT_ONCE = 1024
 
 
@@ -107,7 +108,7 @@
 
 
 def kernel_call(
-    kernel, scalars, small, large, out_shape, scratch, copies, large_outs=0, after=(), macs=10**6
+    kernel, scalars, small, large, out_shape, scratch, copies, large_outs=0, after=(), macs=10**6, grant=GRANT
 ):
     whole = pl.BlockSpec(memory_space=pltpu.VMEM)
     outside = pl.BlockSpec(memory_space=pltpu.HBM)
@@ -124,7 +125,7 @@
         out_specs=[outside] * large_outs + [whole] * (len(out_shape) - large_outs),
         out_shape=out_shape,
         scratch_shapes=[*scratch] + [pltpu.SemaphoreType.DMA((copies,))] * (copies > 0),
-        compiler_params=pltpu.CompilerParams(vmem_limit_bytes=GRANT),
+        compiler_params=pltpu.CompilerParams(vmem_limit_bytes=grant),
         cost_estimate=pl.CostEstimate(
             flops=2 * macs, bytes_accessed=macs // 200, transcendentals=macs // 10000
         ),
@@ -631,7 +632,7 @@
     near, near_score = kernel_call(
         functools.partial(near_kernel, pieces), (), (), (keep1, got1),
         [shape(*keep1.shape), shape(round_up(2 * pieces, 2 * SUBLANES), LANES)],
-        [pltpu.VMEM(keep1.shape, keep1.dtype)] * 3, 3, 1, moved_grad[0::2],
+        [pltpu.VMEM(keep1.shape, keep1.dtype)] * 3, 3, 1, moved_grad[0::2], grant=SMALL_GRANT,
     )
     other_scores = []
     for offset in range(1, groups):
@@ -644,7 +645,7 @@
         functools.partial(ready_kernel, pieces, len(other_scores)), (), other_scores,
         (keep0, got0, near, across), [shape(tok_rows, width + behind)] * far,
         [pltpu.VMEM(keep0.shape, keep0.dtype)] * 2 + [pltpu.VMEM(near.shape, near.dtype)] * 2
-        + [pltpu.VMEM((far, tok_rows, width + behind), near.dtype)], 4 + far, far,
+        + [pltpu.VMEM((far, tok_rows, width + behind), near.dtype)], 4 + far, far, grant=SMALL_GRANT,
     )
     arrived = [ready[0]] + [swap_expert(ready[k], 4 * k) for k in range(1, far)]
     row_sum = sum(part[:, :width].astype(jnp.float32) for part in arrived)

time: 103 us -> 95.5 us (0.927)
  Pallas kernels: 42.7 us -> 36.1 us
  local copies, waits for them, and re-layouts: 9 us -> 7.75 us
    pallas_call x8, Pallas kernels: 42.7 us -> 36.1 us  [kernel_call(): pl.pallas_call(body, in_specs=[pl.BlockSpec(memory_space=pltpu.SMEM)] * l...]
    ppermute x6, waiting for transfers between devices: 4.98 us -> 6.12 us  [swap_group(): return lax.ppermute(array, 'dp', [(i, i ^ offset) for i in range(size)])]
    unnamed x50 -> x48, local copies, waits for them, and re-layouts: 6.66 us -> 6.6 us
  transfers between devices with their start and end apart: 29 -> 29, of which waited for: 9 -> 8; matrix products, arithmetic and copies ran while one was open for 4% -> 2% of each run, Pallas kernels for 35% -> 33%
where the time goes in v6:
time: 95.5 us; the launch traced here: 95 us
  Pallas kernels  36.1 us (38%)
  starting transfers between devices  31.9 us (33%)
  waiting for transfers between devices  17.3 us (18%)
  local copies, waits for them, and re-layouts  7.75 us (8%)
  between operations  1.03 us (1%)
    pallas_call x8, Pallas kernels, kernel_call(): pl.pallas_call(body, in_specs=[pl.BlockSpec(memory_space=pltpu.SMEM)] * l...  36.1 us
    ppermute x23, starting transfers between devices, swap_expert(): return lax.ppermute(array, 'expert', [(i, i ^ offset) for i in range(size)])  23.6 us
    ppermute x23, waiting for transfers between devices, swap_expert(): return lax.ppermute(array, 'expert', [(i, i ^ offset) for i in range(size)])  11.2 us
    ppermute x6, starting transfers between devices, swap_group(): return lax.ppermute(array, 'dp', [(i, i ^ offset) for i in range(size)])  8.32 us
    unnamed x48, local copies, waits for them, and re-layouts  6.6 us
    ppermute x6, waiting for transfers between devices, swap_group(): return lax.ppermute(array, 'dp', [(i, i ^ offset) for i in range(size)])  6.12 us
  transfers between devices with their start and end apart: 29, of which 8 were waited for; matrix products, arithmetic and copies ran while one was open for 2% of the time, Pallas kernels for 33%

profile of v6, /device:TPU:0, one launch (start us, length us, event | category | flops | bytes accessed | tf_op | source)
XLA Modules:
  0.0 95.0 jit_solution(10034091761100302309)
XLA Ops:
  0.6 4.1 %collective-permute-start.8 = (bf16[24,2048]{1,0:T(8,128)(2,1)}, bf16[24,2048]{1,0:T(8,128)(2,1)S(1)}, u32[]{:S(2)}, u32[]{:S(2)}) collective-permute-start(bf16[24,2048]{1,0:T(8,128)(2,1)} %refs_2_.1), channel_id=1, source_target_pairs={{0,8},{1,9},{2,10},{3,11},{4,12},{5,13},{6,14},{7,15},{8,0},{9,1},... | collective-permute-start | bytes 294920 | tf_op jit(solution)/shard_map/ppermute | solution.py:22
  4.7 1.6 %collective-permute-start.7 = (bf16[24,2048]{1,0:T(8,128)(2,1)}, bf16[24,2048]{1,0:T(8,128)(2,1)S(1)}, u32[]{:S(2)}, u32[]{:S(2)}) collective-permute-start(bf16[24,2048]{1,0:T(8,128)(2,1)} %refs_2_.1), channel_id=1, source_target_pairs={{0,4},{1,5},{2,6},{3,7},{4,0},{5,1},{6,2},{7,3},{8,12},{9,13},{10,... | collective-permute-start | bytes 294920 | tf_op jit(solution)/shard_map/ppermute | solution.py:22
  6.3 0.0 collective-permute-start.9
  6.3 0.8 copy.12.refs_1_
  7.1 0.9 copy-done.6
  8.0 0.8 copy-done.10
  8.8 0.3 shard_map.110
  9.1 1.7 %collective-permute-start = (bf16[24,128]{1,0:T(8,128)(2,1)S(1)}, bf16[24,128]{1,0:T(8,128)(2,1)S(1)}, u32[]{:S(2)}, u32[]{:S(2)}) collective-permute-start(bf16[24,128]{1,0:T(8,128)(2,1)S(1)} %get-tuple-element.31), channel_id=1, source_target_pairs={{0,16},{16,0},{1,17},{17,1},{2,18},{18,2},{3,19},{19,3},{4,20},{20... | collective-permute-start | bytes 18440 | tf_op jit(solution)/shard_map/ppermute | solution.py:27
  10.8 1.9 %collective-permute-done = bf16[24,128]{1,0:T(8,128)(2,1)S(1)} collective-permute-done((bf16[24,128]{1,0:T(8,128)(2,1)S(1)}, bf16[24,128]{1,0:T(8,128)(2,1)S(1)}, u32[]{:S(2)}, u32[]{:S(2)}) %collective-permute-start) | collective-permute-done | bytes 6176 | tf_op jit(solution)/shard_map/ppermute | solution.py:27
  12.7 0.1 slice.48
  12.8 1.0 %concatenate.9 = bf16[24,2176]{1,0:T(8,128)(2,1)S(1)} concatenate(bf16[24,2048]{1,0:T(8,128)(2,1)} %param.8, bf16[24,64]{1,0:T(8,128)(2,1)S(1)} %bitcast.11, bf16[24,48]{1,0:T(8,128)(2,1)S(1)} %slice.48, bf16[24,16]{1,0:T(8,128)(2,1)S(1)} %broadcast_in_dim.10), dimensions={1} | concatenate | bytes 208896 | tf_op jit(solution)/shard_map/concatenate | solution.py:591
  13.8 3.9 %collective-permute-start.3 = (bf16[24,2176]{1,0:T(8,128)(2,1)S(1)}, bf16[24,2176]{1,0:T(8,128)(2,1)S(1)}, u32[]{:S(2)}, u32[]{:S(2)}) collective-permute-start(bf16[24,2176]{1,0:T(8,128)(2,1)S(1)} %concatenate.9), channel_id=1, source_target_pairs={{0,12},{1,13},{2,14},{3,15},{4,8},{5,9},{6,10},{7,11},{8,4},{9,5},... | collective-permute-start | bytes 313352 | tf_op jit(solution)/shard_map/ppermute | solution.py:22
  17.7 0.0 collective-permute-start.2
  17.7 0.0 collective-permute-done.7
  17.7 0.6 collective-permute-start.1
  18.3 0.0 collective-permute-done.8
  18.4 1.7 %collective-permute-start.13 = (bf16[96,2048]{1,0:T(8,128)(2,1)S(1)}, bf16[96,2048]{1,0:T(8,128)(2,1)S(1)}, u32[]{:S(2)}, u32[]{:S(2)}) collective-permute-start(bf16[96,2048]{1,0:T(8,128)(2,1)S(1)} %constant_dynamic-update-slice_fusion.refs_3_.refs_4_.refs_1_), channel_id=1, source_target_pairs={{0,2},{1,3},{2,0},{3,1},{4,6},{5,7},{6,4},{7,5},{8,10},{9,11},{10,... | collective-permute-start | bytes 1179656 | tf_op jit(solution)/shard_map/ppermute | solution.py:22
  20.1 1.5 %collective-permute-start.10 = (bf16[96,2048]{1,0:T(8,128)(2,1)S(1)}, bf16[96,2048]{1,0:T(8,128)(2,1)S(1)}, u32[]{:S(2)}, u32[]{:S(2)}) collective-permute-start(bf16[96,2048]{1,0:T(8,128)(2,1)S(1)} %constant_dynamic-update-slice_fusion.refs_3_.refs_4_.refs_1_), channel_id=1, source_target_pairs={{0,16},{16,0},{1,17},{17,1},{2,18},{18,2},{3,19},{19,3},{4,20},{20... | collective-permute-start | bytes 1179656 | tf_op jit(solution)/shard_map/ppermute | solution.py:27
  21.6 2.9 %collective-permute-done.2 = bf16[24,2176]{1,0:T(8,128)(2,1)S(1)} collective-permute-done((bf16[24,2176]{1,0:T(8,128)(2,1)S(1)}, bf16[24,2176]{1,0:T(8,128)(2,1)S(1)}, u32[]{:S(2)}, u32[]{:S(2)}) %collective-permute-start.2) | collective-permute-done | bytes 104480 | tf_op jit(solution)/shard_map/ppermute | solution.py:22
  24.5 0.0 collective-permute-done.1
  24.6 1.5 %collective-permute-start.5 = (bf16[96,2176]{1,0:T(8,128)(2,1)S(1)}, bf16[96,2176]{1,0:T(8,128)(2,1)S(1)}, u32[]{:S(2)}, u32[]{:S(2)}) collective-permute-start(bf16[96,2176]{1,0:T(8,128)(2,1)S(1)} %pad_maximum_fusion.refs_1_.refs_7_.refs_9_), channel_id=1, source_target_pairs={{0,2},{1,3},{2,0},{3,1},{4,6},{5,7},{6,4},{7,5},{8,10},{9,11},{10,... | collective-permute-start | bytes 1253384 | tf_op jit(solution)/shard_map/ppermute | solution.py:22
  26.1 1.5 %collective-permute-done.13.refs_5_.refs_6_.refs_3_ = bf16[96,2048]{1,0:T(8,128)(2,1)S(1)} collective-permute-done((bf16[96,2048]{1,0:T(8,128)(2,1)S(1)}, bf16[96,2048]{1,0:T(8,128)(2,1)S(1)}, u32[]{:S(2)}, u32[]{:S(2)}) %collective-permute-start.13) | collective-permute-done | bytes 393248 | tf_op jit(solution)/shard_map/ppermute | solution.py:22
  27.7 1.5 %collective-permute-start.15 = (bf16[96,2048]{1,0:T(8,128)(2,1)S(1)}, bf16[96,2048]{1,0:T(8,128)(2,1)S(1)}, u32[]{:S(2)}, u32[]{:S(2)}) collective-permute-start(bf16[96,2048]{1,0:T(8,128)(2,1)S(1)} %collective-permute-done.13.refs_5_.refs_6_.refs_3_), channel_id=1, source_target_pairs={{0,16},{16,0},{1,17},{17,1},{2,18},{18,2},{3,19},{19,3},{4,20},{20... | collective-permute-start | bytes 1179656 | tf_op jit(solution)/shard_map/ppermute | solution.py:27
  29.2 0.0 collective-permute-done.10.refs_8_.refs_2_.refs_5_
  29.2 0.5 collective-permute-start.4
  29.7 6.3 %collective-permute-done.5.refs_3_.refs_9_.refs_11_ = bf16[96,2176]{1,0:T(8,128)(2,1)S(1)} collective-permute-done((bf16[96,2176]{1,0:T(8,128)(2,1)S(1)}, bf16[96,2176]{1,0:T(8,128)(2,1)S(1)}, u32[]{:S(2)}, u32[]{:S(2)}) %collective-permute-start.5) | collective-permute-done | bytes 417824 | tf_op jit(solution)/shard_map/ppermute | solution.py:22
  36.0 0.5 collective-permute-start.12
  36.5 0.2 collective-permute-done.15.refs_10_.refs_4_.refs_7_
  36.7 0.0 collective-permute-start.14
  36.7 0.0 collective-permute-done.11.refs_9_.refs_3_.refs_6_
  36.7 0.5 collective-permute-start.16
  37.2 1.6 %collective-permute-start.18 = (bf16[96,2176]{1,0:T(8,128)(2,1)S(1)}, bf16[96,2176]{1,0:T(8,128)(2,1)S(1)}, u32[]{:S(2)}, u32[]{:S(2)}) collective-permute-start(bf16[96,2176]{1,0:T(8,128)(2,1)S(1)} %pad_maximum_fusion.refs_1_.refs_7_.refs_9_), channel_id=1, source_target_pairs={{0,16},{16,0},{1,17},{17,1},{2,18},{18,2},{3,19},{19,3},{4,20},{20... | collective-permute-start | bytes 1253384 | tf_op jit(solution)/shard_map/ppermute | solution.py:27
  38.8 0.0 collective-permute-done.6.refs_4_.refs_10_.refs_12_
  38.8 0.5 collective-permute-start.19
  39.3 0.2 copy-done.16
  39.6 1.7 %shard_map.111 = (f32[768,128]{1,0:T(8,128)S(1)}, f32[16,768]{1,0:T(8,128)S(1)}) custom-call(s32[1]{0:T(128)} %bitcast.refs_0_, bf16[96,2176]{1,0:T(8,128)(2,1)S(1)} %pad_maximum_fusion.refs_1_.refs_7_.refs_9_, bf16[96,2176]{1,0:T(8,128)(2,1)} %copy-done.15, bf16[96,2176]{1,0:T(8,128)(2,1)} %copy-done.14, bf16[96,2176]{1,0:T(8,128)(2,1)} %copy-done.16, ...), custom_call_target="tpu_custom_call" | custom-call | flops 2000000 | bytes 5000 | tf_op jit(solution)/shard_map/pallas_call | solution.py:120
  41.2 0.0 copy-start.12
  41.2 0.7 copy-done.12
  42.1 0.7 copy-done.8
  42.8 0.1 copy-done.20
  42.9 0.1 copy-done.21
  43.0 12.4 %shard_map.112 = (bf16[96,2048]{1,0:T(8,128)(2,1)S(1)}, bf16[96,2048]{1,0:T(8,128)(2,1)}, bf16[96,2176]{1,0:T(8,128)(2,1)}, bf16[96,2176]{1,0:T(8,128)(2,1)}, bf...) custom-call(s32[1]{0:T(128)} %bitcast.refs_0_, ...), custom_call_target="tpu_custom_call" | custom-call | flops 6039797760 | bytes 15099494 | tf_op jit(solution)/shard_map/pallas_call | solution.py:120
  55.4 0.1 collective-permute-start.17
  55.5 0.5 collective-permute-start.27
  56.0 1.9 %collective-permute-done.19.refs_3_.refs_8_.refs_15_ = bf16[96,2176]{1,0:T(8,128)(2,1)S(1)} collective-permute-done((bf16[96,2176]{1,0:T(8,128)(2,1)S(1)}, bf16[96,2176]{1,0:T(8,128)(2,1)S(1)}, u32[]{:S(2)}, u32[]{:S(2)}) %collective-permute-start.19) | collective-permute-done | bytes 417824 | tf_op jit(solution)/shard_map/ppermute | solution.py:27
  57.9 0.0 copy-start.5
  57.9 1.1 %copy-done.5 = bf16[96,2176]{1,0:T(8,128)(2,1)S(1)} copy-done((bf16[96,2176]{1,0:T(8,128)(2,1)S(1)}, bf16[96,2176]{1,0:T(8,128)(2,1)}, u32[]{:S(2)}) %copy-start.5) | copy-done | bytes 417816
  59.1 0.8 shard_map.113
  59.8 1.4 %collective-permute-start.23 = (bf16[96,2176]{1,0:T(8,128)(2,1)S(1)}, bf16[96,2176]{1,0:T(8,128)(2,1)S(1)}, u32[]{:S(2)}, u32[]{:S(2)}) collective-permute-start(bf16[96,2176]{1,0:T(8,128)(2,1)S(1)} %get-tuple-element.38.refs_4_), channel_id=1, source_target_pairs={{0,2},{1,3},{2,0},{3,1},{4,6},{5,7},{6,4},{7,5},{8,10},{9,11},{10,... | collective-permute-start | bytes 1253384 | tf_op jit(solution)/shard_map/ppermute | solution.py:22
  61.2 0.1 collective-permute-start.22
  61.3 1.5 %collective-permute-start.20 = (bf16[16,128]{1,0:T(8,128)(2,1)S(1)}, bf16[16,128]{1,0:T(8,128)(2,1)S(1)}, u32[]{:S(2)}, u32[]{:S(2)}) collective-permute-start(bf16[16,128]{1,0:T(8,128)(2,1)S(1)} %get-tuple-element.35), channel_id=1, source_target_pairs={{0,16},{16,0},{1,17},{17,1},{2,18},{18,2},{3,19},{19,3},{4,20},{20... | collective-permute-start | bytes 12296 | tf_op jit(solution)/shard_map/ppermute | solution.py:27
  62.8 2.1 %collective-permute-done.20.refs_0_ = bf16[16,128]{1,0:T(8,128)(2,1)S(1)} collective-permute-done((bf16[16,128]{1,0:T(8,128)(2,1)S(1)}, bf16[16,128]{1,0:T(8,128)(2,1)S(1)}, u32[]{:S(2)}, u32[]{:S(2)}) %collective-permute-start.20) | collective-permute-done | bytes 4128 | tf_op jit(solution)/shard_map/ppermute | solution.py:27
  64.9 0.7 collective-permute-start.21
  65.6 0.0 copy-start.13
  65.7 1.0 %copy-done.13 = f32[768,128]{1,0:T(8,128)S(1)} copy-done((f32[768,128]{1,0:T(8,128)S(1)}, f32[768,128]{1,0:T(8,128)}, u32[]{:S(2)}) %copy-start.13) | copy-done | bytes 393240
  66.6 8.8 %shard_map.116 = (bf16[384,768]{1,0:T(8,128)(2,1)}, bf16[384,768]{1,0:T(8,128)(2,1)}, bf16[384,768]{1,0:T(8,128)(2,1)}) custom-call(s32[1]{0:T(128)} %bitcast.refs_0_, f32[768,128]{1,0:T(8,128)S(1)} %copy-done.13, bf16[96,2048]{1,0:T(8,128)(2,1)S(1)} %collective-permute-done.10.refs_8_.refs_2_.refs_5_, bf16[96,2048]{1,0:T(8,128)(2,1)} %copy-done.17, ...), custom_call_target="tpu_custom_call" | custom-call | flops 3623878656 | bytes 9059696 | tf_op jit(solution)/shard_map/pallas_call | solution.py:120
  75.4 1.7 %shard_map.114 = (bf16[24,2176]{1,0:T(8,128)(2,1)S(1)}, bf16[24,2176]{1,0:T(8,128)(2,1)S(1)}, bf16[24,2176]{1,0:T(8,128)(2,1)S(1)}, bf16[24,2176]{1,0:T(8,128)(2,1)S(1)}) custom-call(bf16[16,128]{1,0:T(8,128)(2,1)S(1)} %collective-permute-done.20.refs_0_, bf16[16,128]{1,0:T(8,128)(2,1)S(1)} %collective-permute-done.21.refs_1_, ...), custom_call_target="tpu_custom_call" | custom-call | flops 2000000 | bytes 5000 | tf_op jit(solution)/shard_map/pallas_call | solution.py:120
  77.1 2.8 %collective-permute-start.24 = (bf16[24,2176]{1,0:T(8,128)(2,1)S(1)}, bf16[24,2176]{1,0:T(8,128)(2,1)S(1)}, u32[]{:S(2)}, u32[]{:S(2)}) collective-permute-start(bf16[24,2176]{1,0:T(8,128)(2,1)S(1)} %get-tuple-element.40.refs_23_), channel_id=1, source_target_pairs={{0,4},{1,5},{2,6},{3,7},{4,0},{5,1},{6,2},{7,3},{8,12},{9,13},{10,... | collective-permute-start | bytes 313352 | tf_op jit(solution)/shard_map/ppermute | solution.py:22
  79.9 3.1 %collective-permute-start.25 = (bf16[24,2176]{1,0:T(8,128)(2,1)S(1)}, bf16[24,2176]{1,0:T(8,128)(2,1)S(1)}, u32[]{:S(2)}, u32[]{:S(2)}) collective-permute-start(bf16[24,2176]{1,0:T(8,128)(2,1)S(1)} %get-tuple-element.41.refs_24_), channel_id=1, source_target_pairs={{0,8},{1,9},{2,10},{3,11},{4,12},{5,13},{6,14},{7,15},{8,0},{9,1},... | collective-permute-start | bytes 313352 | tf_op jit(solution)/shard_map/ppermute | solution.py:22
  83.1 7.2 %shard_map.117 = (bf16[1,1024,768]{2,1,0:T(8,128)(2,1)}, bf16[1,1024,768]{2,1,0:T(8,128)(2,1)}, bf16[1,384,2048]{2,1,0:T(8,128)(2,1)}) custom-call(s32[1]{0:T(128)} %bitcast.7.refs_0_, bf16[96,2048]{1,0:T(8,128)(2,1)S(1)} %copy-done.2, bf16[96,2048]{1,0:T(8,128)(2,1)} %copy-done.8, bf16[96,2048]{1,0:T(8,128)(2,1)} %copy-done.18, ...), custom_call_target="tpu_custom_call" | custom-call | flops 3623878656 | bytes 9059696 | tf_op jit(solution)/shard_map/pallas_call | solution.py:120
  90.3 0.0 copy-start.11
  90.4 0.4 collective-permute-done.25
  90.9 3.3 %shard_map.115 = (bf16[16,768]{1,0:T(8,128)(2,1)S(1)}, f32[16,2048]{1,0:T(8,128)}) custom-call(s32[1]{0:T(128)} %bitcast.refs_0_, bf16[2,16,384]{2,1,0:T(8,128)(2,1)S(1)} %reshape.13.refs_1_, s32[1,384]{1,0:T(1,128)S(1)} %get-tuple-element.30.refs_1_.refs_2_, f32[16,768]{1,0:T(8,128)S(1)} %get-tuple-element.43.refs_3_, bf16[96,2048]{1,0:T(8,128)(2,1)S(1)} %copy-done.2, ...), custom_call_target="tpu_custom_call" | custom-call | flops 2000000 | bytes 5000 | tf_op jit(solution)/shard_map/pallas_call | solution.py:120
  94.2 0.8 fusion
  (67 shorter events, 0.3 us)
Async XLA Ops:
  0.6 17.7 %collective-permute-start.8 = (bf16[24,2048]{1,0:T(8,128)(2,1)}, bf16[24,2048]{1,0:T(8,128)(2,1)S(1)}, u32[]{:S(2)}, u32[]{:S(2)}) collective-permute-start(bf16[24,2048]{1,0:T(8,128)(2,1)} %refs_2_.1), channel_id=1, source_target_pairs={{0,8},{1,9},{2,10},{3,11},{4,12},{5,13},{6,14},{7,15},{8,0},{9,1},... | collective-permute-start | bytes 294920 | tf_op jit(solution)/shard_map/ppermute | solution.py:22
  4.7 12.9 %collective-permute-start.7 = (bf16[24,2048]{1,0:T(8,128)(2,1)}, bf16[24,2048]{1,0:T(8,128)(2,1)S(1)}, u32[]{:S(2)}, u32[]{:S(2)}) collective-permute-start(bf16[24,2048]{1,0:T(8,128)(2,1)} %refs_2_.1), channel_id=1, source_target_pairs={{0,4},{1,5},{2,6},{3,7},{4,0},{5,1},{6,2},{7,3},{8,12},{9,13},{10,... | collective-permute-start | bytes 294920 | tf_op jit(solution)/shard_map/ppermute | solution.py:22
  6.3 12.0 %collective-permute-start.9 = (bf16[24,2048]{1,0:T(8,128)(2,1)}, bf16[24,2048]{1,0:T(8,128)(2,1)S(1)}, u32[]{:S(2)}, u32[]{:S(2)}) collective-permute-start(bf16[24,2048]{1,0:T(8,128)(2,1)} %refs_2_.1), channel_id=1, source_target_pairs={{0,12},{1,13},{2,14},{3,15},{4,8},{5,9},{6,10},{7,11},{8,4},{9,5},... | collective-permute-start | bytes 294920 | tf_op jit(solution)/shard_map/ppermute | solution.py:22
  7.1 0.9 copy-start.6
  8.0 0.8 copy-start.10
  9.1 3.6 %collective-permute-start = (bf16[24,128]{1,0:T(8,128)(2,1)S(1)}, bf16[24,128]{1,0:T(8,128)(2,1)S(1)}, u32[]{:S(2)}, u32[]{:S(2)}) collective-permute-start(bf16[24,128]{1,0:T(8,128)(2,1)S(1)} %get-tuple-element.31), channel_id=1, source_target_pairs={{0,16},{16,0},{1,17},{17,1},{2,18},{18,2},{3,19},{19,3},{4,20},{20... | collective-permute-start | bytes 18440 | tf_op jit(solution)/shard_map/ppermute | solution.py:27
  13.8 7.8 %collective-permute-start.3 = (bf16[24,2176]{1,0:T(8,128)(2,1)S(1)}, bf16[24,2176]{1,0:T(8,128)(2,1)S(1)}, u32[]{:S(2)}, u32[]{:S(2)}) collective-permute-start(bf16[24,2176]{1,0:T(8,128)(2,1)S(1)} %concatenate.9), channel_id=1, source_target_pairs={{0,12},{1,13},{2,14},{3,15},{4,8},{5,9},{6,10},{7,11},{8,4},{9,5},... | collective-permute-start | bytes 313352 | tf_op jit(solution)/shard_map/ppermute | solution.py:22
  17.7 6.9 %collective-permute-start.2 = (bf16[24,2176]{1,0:T(8,128)(2,1)S(1)}, bf16[24,2176]{1,0:T(8,128)(2,1)S(1)}, u32[]{:S(2)}, u32[]{:S(2)}) collective-permute-start(bf16[24,2176]{1,0:T(8,128)(2,1)S(1)} %concatenate.9), channel_id=1, source_target_pairs={{0,8},{1,9},{2,10},{3,11},{4,12},{5,13},{6,14},{7,15},{8,0},{9,1},... | collective-permute-start | bytes 313352 | tf_op jit(solution)/shard_map/ppermute | solution.py:22
  17.7 6.9 %collective-permute-start.1 = (bf16[24,2176]{1,0:T(8,128)(2,1)S(1)}, bf16[24,2176]{1,0:T(8,128)(2,1)S(1)}, u32[]{:S(2)}, u32[]{:S(2)}) collective-permute-start(bf16[24,2176]{1,0:T(8,128)(2,1)S(1)} %concatenate.9), channel_id=1, source_target_pairs={{0,4},{1,5},{2,6},{3,7},{4,0},{5,1},{6,2},{7,3},{8,12},{9,13},{10,... | collective-permute-start | bytes 313352 | tf_op jit(solution)/shard_map/ppermute | solution.py:22
  18.4 23.7 %copy-start.1 = (bf16[96,2048]{1,0:T(8,128)(2,1)}, bf16[96,2048]{1,0:T(8,128)(2,1)S(1)}, u32[]{:S(2)}) copy-start(bf16[96,2048]{1,0:T(8,128)(2,1)S(1)} %constant_dynamic-update-slice_fusion.refs_3_.refs_4_.refs_1_) | copy-start | bytes 1179652
  18.4 9.3 %collective-permute-start.13 = (bf16[96,2048]{1,0:T(8,128)(2,1)S(1)}, bf16[96,2048]{1,0:T(8,128)(2,1)S(1)}, u32[]{:S(2)}, u32[]{:S(2)}) collective-permute-start(bf16[96,2048]{1,0:T(8,128)(2,1)S(1)} %constant_dynamic-update-slice_fusion.refs_3_.refs_4_.refs_1_), channel_id=1, source_target_pairs={{0,2},{1,3},{2,0},{3,1},{4,6},{5,7},{6,4},{7,5},{8,10},{9,11},{10,... | collective-permute-start | bytes 1179656 | tf_op jit(solution)/shard_map/ppermute | solution.py:22
  20.1 9.1 %collective-permute-start.10 = (bf16[96,2048]{1,0:T(8,128)(2,1)S(1)}, bf16[96,2048]{1,0:T(8,128)(2,1)S(1)}, u32[]{:S(2)}, u32[]{:S(2)}) collective-permute-start(bf16[96,2048]{1,0:T(8,128)(2,1)S(1)} %constant_dynamic-update-slice_fusion.refs_3_.refs_4_.refs_1_), channel_id=1, source_target_pairs={{0,16},{16,0},{1,17},{17,1},{2,18},{18,2},{3,19},{19,3},{4,20},{20... | collective-permute-start | bytes 1179656 | tf_op jit(solution)/shard_map/ppermute | solution.py:27
  24.6 17.5 %copy-start = (bf16[96,2176]{1,0:T(8,128)(2,1)}, bf16[96,2176]{1,0:T(8,128)(2,1)S(1)}, u32[]{:S(2)}) copy-start(bf16[96,2176]{1,0:T(8,128)(2,1)S(1)} %pad_maximum_fusion.refs_1_.refs_7_.refs_9_) | copy-start | bytes 1253380
  24.6 11.4 %collective-permute-start.5 = (bf16[96,2176]{1,0:T(8,128)(2,1)S(1)}, bf16[96,2176]{1,0:T(8,128)(2,1)S(1)}, u32[]{:S(2)}, u32[]{:S(2)}) collective-permute-start(bf16[96,2176]{1,0:T(8,128)(2,1)S(1)} %pad_maximum_fusion.refs_1_.refs_7_.refs_9_), channel_id=1, source_target_pairs={{0,2},{1,3},{2,0},{3,1},{4,6},{5,7},{6,4},{7,5},{8,10},{9,11},{10,... | collective-permute-start | bytes 1253384 | tf_op jit(solution)/shard_map/ppermute | solution.py:22
  27.7 14.4 %copy-start.18 = (bf16[96,2048]{1,0:T(8,128)(2,1)}, bf16[96,2048]{1,0:T(8,128)(2,1)S(1)}, u32[]{:S(2)}) copy-start(bf16[96,2048]{1,0:T(8,128)(2,1)S(1)} %collective-permute-done.13.refs_5_.refs_6_.refs_3_) | copy-start | bytes 1179652
  27.7 9.1 %collective-permute-start.15 = (bf16[96,2048]{1,0:T(8,128)(2,1)S(1)}, bf16[96,2048]{1,0:T(8,128)(2,1)S(1)}, u32[]{:S(2)}, u32[]{:S(2)}) collective-permute-start(bf16[96,2048]{1,0:T(8,128)(2,1)S(1)} %collective-permute-done.13.refs_5_.refs_6_.refs_3_), channel_id=1, source_target_pairs={{0,16},{16,0},{1,17},{17,1},{2,18},{18,2},{3,19},{19,3},{4,20},{20... | collective-permute-start | bytes 1179656 | tf_op jit(solution)/shard_map/ppermute | solution.py:27
  29.2 36.4 %copy-start.7 = (bf16[96,2048]{1,0:T(8,128)(2,1)}, bf16[96,2048]{1,0:T(8,128)(2,1)S(1)}, u32[]{:S(2)}) copy-start(bf16[96,2048]{1,0:T(8,128)(2,1)S(1)} %collective-permute-done.10.refs_8_.refs_2_.refs_5_) | copy-start | bytes 1179652
  29.2 7.5 %collective-permute-start.11 = (bf16[96,2048]{1,0:T(8,128)(2,1)S(1)}, bf16[96,2048]{1,0:T(8,128)(2,1)S(1)}, u32[]{:S(2)}, u32[]{:S(2)}) collective-permute-start(bf16[96,2048]{1,0:T(8,128)(2,1)S(1)} %collective-permute-done.10.refs_8_.refs_2_.refs_5_), channel_id=1, source_target_pairs={{0,1},{1,0},{2,3},{3,2},{4,5},{5,4},{6,7},{7,6},{8,9},{9,8},{10,11... | collective-permute-start | bytes 1179656 | tf_op jit(solution)/shard_map/ppermute | solution.py:22
  29.2 8.0 %collective-permute-start.4 = (bf16[96,2176]{1,0:T(8,128)(2,1)S(1)}, bf16[96,2176]{1,0:T(8,128)(2,1)S(1)}, u32[]{:S(2)}, u32[]{:S(2)}) collective-permute-start(bf16[96,2176]{1,0:T(8,128)(2,1)S(1)} %pad_maximum_fusion.refs_1_.refs_7_.refs_9_), channel_id=1, source_target_pairs={{0,1},{1,0},{2,3},{3,2},{4,5},{5,4},{6,7},{7,6},{8,9},{9,8},{10,11... | collective-permute-start | bytes 1253384 | tf_op jit(solution)/shard_map/ppermute | solution.py:22
  36.0 3.3 %copy-start.14 = (bf16[96,2176]{1,0:T(8,128)(2,1)}, bf16[96,2176]{1,0:T(8,128)(2,1)S(1)}, u32[]{:S(2)}) copy-start(bf16[96,2176]{1,0:T(8,128)(2,1)S(1)} %collective-permute-done.5.refs_3_.refs_9_.refs_11_) | copy-start | bytes 1253380
  36.0 2.8 %collective-permute-start.6 = (bf16[96,2176]{1,0:T(8,128)(2,1)S(1)}, bf16[96,2176]{1,0:T(8,128)(2,1)S(1)}, u32[]{:S(2)}, u32[]{:S(2)}) collective-permute-start(bf16[96,2176]{1,0:T(8,128)(2,1)S(1)} %collective-permute-done.5.refs_3_.refs_9_.refs_11_), channel_id=1, source_target_pairs={{0,1},{1,0},{2,3},{3,2},{4,5},{5,4},{6,7},{7,6},{8,9},{9,8},{10,11... | collective-permute-start | bytes 1253384 | tf_op jit(solution)/shard_map/ppermute | solution.py:22
  36.0 6.0 %collective-permute-start.12 = (bf16[96,2048]{1,0:T(8,128)(2,1)S(1)}, bf16[96,2048]{1,0:T(8,128)(2,1)S(1)}, u32[]{:S(2)}, u32[]{:S(2)}) collective-permute-start(bf16[96,2048]{1,0:T(8,128)(2,1)S(1)} %constant_dynamic-update-slice_fusion.refs_3_.refs_4_.refs_1_), channel_id=1, source_target_pairs={{0,1},{1,0},{2,3},{3,2},{4,5},{5,4},{6,7},{7,6},{8,9},{9,8},{10,11... | collective-permute-start | bytes 1179656 | tf_op jit(solution)/shard_map/ppermute | solution.py:22
  36.7 5.3 %copy-start.19 = (bf16[96,2048]{1,0:T(8,128)(2,1)}, bf16[96,2048]{1,0:T(8,128)(2,1)S(1)}, u32[]{:S(2)}) copy-start(bf16[96,2048]{1,0:T(8,128)(2,1)S(1)} %collective-permute-done.15.refs_10_.refs_4_.refs_7_) | copy-start | bytes 1179652
  36.7 5.3 %collective-permute-start.14 = (bf16[96,2048]{1,0:T(8,128)(2,1)S(1)}, bf16[96,2048]{1,0:T(8,128)(2,1)S(1)}, u32[]{:S(2)}, u32[]{:S(2)}) collective-permute-start(bf16[96,2048]{1,0:T(8,128)(2,1)S(1)} %collective-permute-done.13.refs_5_.refs_6_.refs_3_), channel_id=1, source_target_pairs={{0,1},{1,0},{2,3},{3,2},{4,5},{5,4},{6,7},{7,6},{8,9},{9,8},{10,11... | collective-permute-start | bytes 1179656 | tf_op jit(solution)/shard_map/ppermute | solution.py:22
  36.7 5.3 %copy-start.17 = (bf16[96,2048]{1,0:T(8,128)(2,1)}, bf16[96,2048]{1,0:T(8,128)(2,1)S(1)}, u32[]{:S(2)}) copy-start(bf16[96,2048]{1,0:T(8,128)(2,1)S(1)} %collective-permute-done.11.refs_9_.refs_3_.refs_6_) | copy-start | bytes 1179652
  36.7 5.3 %collective-permute-start.16 = (bf16[96,2048]{1,0:T(8,128)(2,1)S(1)}, bf16[96,2048]{1,0:T(8,128)(2,1)S(1)}, u32[]{:S(2)}, u32[]{:S(2)}) collective-permute-start(bf16[96,2048]{1,0:T(8,128)(2,1)S(1)} %collective-permute-done.15.refs_10_.refs_4_.refs_7_), channel_id=1, source_target_pairs={{0,1},{1,0},{2,3},{3,2},{4,5},{5,4},{6,7},{7,6},{8,9},{9,8},{10,11... | collective-permute-start | bytes 1179656 | tf_op jit(solution)/shard_map/ppermute | solution.py:22
  37.2 2.1 %copy-start.15 = (bf16[96,2176]{1,0:T(8,128)(2,1)}, bf16[96,2176]{1,0:T(8,128)(2,1)S(1)}, u32[]{:S(2)}) copy-start(bf16[96,2176]{1,0:T(8,128)(2,1)S(1)} %collective-permute-done.4.refs_2_.refs_8_.refs_10_) | copy-start | bytes 1253380
  37.2 18.3 %collective-permute-start.18 = (bf16[96,2176]{1,0:T(8,128)(2,1)S(1)}, bf16[96,2176]{1,0:T(8,128)(2,1)S(1)}, u32[]{:S(2)}, u32[]{:S(2)}) collective-permute-start(bf16[96,2176]{1,0:T(8,128)(2,1)S(1)} %pad_maximum_fusion.refs_1_.refs_7_.refs_9_), channel_id=1, source_target_pairs={{0,16},{16,0},{1,17},{17,1},{2,18},{18,2},{3,19},{19,3},{4,20},{20... | collective-permute-start | bytes 1253384 | tf_op jit(solution)/shard_map/ppermute | solution.py:27
  38.8 0.8 copy-start.16
  38.8 19.1 %collective-permute-start.19 = (bf16[96,2176]{1,0:T(8,128)(2,1)S(1)}, bf16[96,2176]{1,0:T(8,128)(2,1)S(1)}, u32[]{:S(2)}, u32[]{:S(2)}) collective-permute-start(bf16[96,2176]{1,0:T(8,128)(2,1)S(1)} %collective-permute-done.5.refs_3_.refs_9_.refs_11_), channel_id=1, source_target_pairs={{0,16},{16,0},{1,17},{17,1},{2,18},{18,2},{3,19},{19,3},{4,20},{20... | collective-permute-start | bytes 1253384 | tf_op jit(solution)/shard_map/ppermute | solution.py:27
  41.2 0.7 copy-start.12
  42.0 0.8 copy-start.8
  42.0 0.9 copy-start.20
  42.0 1.0 %copy-start.21 = (bf16[96,2048]{1,0:T(8,128)(2,1)}, bf16[96,2048]{1,0:T(8,128)(2,1)S(1)}, u32[]{:S(2)}) copy-start(bf16[96,2048]{1,0:T(8,128)(2,1)S(1)} %collective-permute-done.16.refs_14_.refs_11_.refs_5_.refs_8_) | copy-start | bytes 1179652
  55.4 2.5 %collective-permute-start.17 = (bf16[96,2176]{1,0:T(8,128)(2,1)}, bf16[96,2176]{1,0:T(8,128)(2,1)S(1)}, u32[]{:S(2)}, u32[]{:S(2)}) collective-permute-start(bf16[96,2176]{1,0:T(8,128)(2,1)} %get-tuple-element.34), channel_id=1, source_target_pairs={{0,1},{1,0},{2,3},{3,2},{4,5},{5,4},{6,7},{7,6},{8,9},{9,8},{10,11... | collective-permute-start | bytes 1253384 | tf_op jit(solution)/shard_map/ppermute | solution.py:22
  55.5 10.1 %copy-start.3 = (bf16[96,2176]{1,0:T(8,128)(2,1)}, bf16[96,2176]{1,0:T(8,128)(2,1)S(1)}, u32[]{:S(2)}) copy-start(bf16[96,2176]{1,0:T(8,128)(2,1)S(1)} %collective-permute-done.18.refs_2_.refs_6_.refs_13_) | copy-start | bytes 1253380
  55.5 10.1 %collective-permute-start.27 = (bf16[96,2176]{1,0:T(8,128)(2,1)S(1)}, bf16[96,2176]{1,0:T(8,128)(2,1)}, u32[]{:S(2)}, u32[]{:S(2)}) collective-permute-start(bf16[96,2176]{1,0:T(8,128)(2,1)S(1)} %collective-permute-done.18.refs_2_.refs_6_.refs_13_), channel_id=1, source_target_pairs={{0,1},{1,0},{2,3},{3,2},{4,5},{5,4},{6,7},{7,6},{8,9},{9,8},{10,11... | collective-permute-start | bytes 1253384 | tf_op jit(solution)/shard_map/ppermute | solution.py:22
  57.9 7.8 %copy-start.4 = (bf16[96,2176]{1,0:T(8,128)(2,1)}, bf16[96,2176]{1,0:T(8,128)(2,1)S(1)}, u32[]{:S(2)}) copy-start(bf16[96,2176]{1,0:T(8,128)(2,1)S(1)} %collective-permute-done.19.refs_3_.refs_8_.refs_15_) | copy-start | bytes 1253380
  57.9 7.7 %collective-permute-start.28 = (bf16[96,2176]{1,0:T(8,128)(2,1)S(1)}, bf16[96,2176]{1,0:T(8,128)(2,1)}, u32[]{:S(2)}, u32[]{:S(2)}) collective-permute-start(bf16[96,2176]{1,0:T(8,128)(2,1)S(1)} %collective-permute-done.19.refs_3_.refs_8_.refs_15_), channel_id=1, source_target_pairs={{0,1},{1,0},{2,3},{3,2},{4,5},{5,4},{6,7},{7,6},{8,9},{9,8},{10,11... | collective-permute-start | bytes 1253384 | tf_op jit(solution)/shard_map/ppermute | solution.py:22
  57.9 1.2 %copy-start.5 = (bf16[96,2176]{1,0:T(8,128)(2,1)S(1)}, bf16[96,2176]{1,0:T(8,128)(2,1)}, u32[]{:S(2)}) copy-start(bf16[96,2176]{1,0:T(8,128)(2,1)} %get-tuple-element.33.refs_0_) | copy-start | bytes 1253380
  59.8 15.6 %collective-permute-start.23 = (bf16[96,2176]{1,0:T(8,128)(2,1)S(1)}, bf16[96,2176]{1,0:T(8,128)(2,1)S(1)}, u32[]{:S(2)}, u32[]{:S(2)}) collective-permute-start(bf16[96,2176]{1,0:T(8,128)(2,1)S(1)} %get-tuple-element.38.refs_4_), channel_id=1, source_target_pairs={{0,2},{1,3},{2,0},{3,1},{4,6},{5,7},{6,4},{7,5},{8,10},{9,11},{10,... | collective-permute-start | bytes 1253384 | tf_op jit(solution)/shard_map/ppermute | solution.py:22
  61.2 14.2 %collective-permute-start.22 = (bf16[96,2048]{1,0:T(8,128)(2,1)}, bf16[96,2048]{1,0:T(8,128)(2,1)S(1)}, u32[]{:S(2)}, u32[]{:S(2)}) collective-permute-start(bf16[96,2048]{1,0:T(8,128)(2,1)} %get-tuple-element.37), channel_id=1, source_target_pairs={{0,1},{1,0},{2,3},{3,2},{4,5},{5,4},{6,7},{7,6},{8,9},{9,8},{10,11... | collective-permute-start | bytes 1179656 | tf_op jit(solution)/shard_map/ppermute | solution.py:22
  61.3 3.6 %collective-permute-start.20 = (bf16[16,128]{1,0:T(8,128)(2,1)S(1)}, bf16[16,128]{1,0:T(8,128)(2,1)S(1)}, u32[]{:S(2)}, u32[]{:S(2)}) collective-permute-start(bf16[16,128]{1,0:T(8,128)(2,1)S(1)} %get-tuple-element.35), channel_id=1, source_target_pairs={{0,16},{16,0},{1,17},{17,1},{2,18},{18,2},{3,19},{19,3},{4,20},{20... | collective-permute-start | bytes 12296 | tf_op jit(solution)/shard_map/ppermute | solution.py:27
  62.8 20.3 %copy-start.2 = (bf16[96,2048]{1,0:T(8,128)(2,1)S(1)}, bf16[96,2048]{1,0:T(8,128)(2,1)}, u32[]{:S(2)}) copy-start(bf16[96,2048]{1,0:T(8,128)(2,1)} %copy-done.1) | copy-start | bytes 1179652
  64.9 10.5 %collective-permute-start.21 = (bf16[16,128]{1,0:T(8,128)(2,1)S(1)}, bf16[16,128]{1,0:T(8,128)(2,1)S(1)}, u32[]{:S(2)}, u32[]{:S(2)}) collective-permute-start(bf16[16,128]{1,0:T(8,128)(2,1)S(1)} %collective-permute-done.20.refs_0_), channel_id=1, source_target_pairs={{0,2},{1,3},{2,0},{3,1},{4,6},{5,7},{6,4},{7,5},{8,10},{9,11},{10,... | collective-permute-start | bytes 12296 | tf_op jit(solution)/shard_map/ppermute | solution.py:22
  65.6 1.0 %copy-start.13 = (f32[768,128]{1,0:T(8,128)S(1)}, f32[768,128]{1,0:T(8,128)}, u32[]{:S(2)}) copy-start(f32[768,128]{1,0:T(8,128)} %copy-done.12) | copy-start | bytes 1179652
  77.1 13.2 %collective-permute-start.24 = (bf16[24,2176]{1,0:T(8,128)(2,1)S(1)}, bf16[24,2176]{1,0:T(8,128)(2,1)S(1)}, u32[]{:S(2)}, u32[]{:S(2)}) collective-permute-start(bf16[24,2176]{1,0:T(8,128)(2,1)S(1)} %get-tuple-element.40.refs_23_), channel_id=1, source_target_pairs={{0,4},{1,5},{2,6},{3,7},{4,0},{5,1},{6,2},{7,3},{8,12},{9,13},{10,... | collective-permute-start | bytes 313352 | tf_op jit(solution)/shard_map/ppermute | solution.py:22
  79.9 10.8 %collective-permute-start.25 = (bf16[24,2176]{1,0:T(8,128)(2,1)S(1)}, bf16[24,2176]{1,0:T(8,128)(2,1)S(1)}, u32[]{:S(2)}, u32[]{:S(2)}) collective-permute-start(bf16[24,2176]{1,0:T(8,128)(2,1)S(1)} %get-tuple-element.41.refs_24_), channel_id=1, source_target_pairs={{0,8},{1,9},{2,10},{3,11},{4,12},{5,13},{6,14},{7,15},{8,0},{9,1},... | collective-permute-start | bytes 313352 | tf_op jit(solution)/shard_map/ppermute | solution.py:22
  83.1 7.7 %collective-permute-start.26 = (bf16[24,2176]{1,0:T(8,128)(2,1)S(1)}, bf16[24,2176]{1,0:T(8,128)(2,1)S(1)}, u32[]{:S(2)}, u32[]{:S(2)}) collective-permute-start(bf16[24,2176]{1,0:T(8,128)(2,1)S(1)} %get-tuple-element.42.refs_25_), channel_id=1, source_target_pairs={{0,12},{1,13},{2,14},{3,15},{4,8},{5,9},{6,10},{7,11},{8,4},{9,5},... | collective-permute-start | bytes 313352 | tf_op jit(solution)/shard_map/ppermute | solution.py:22
  83.1 7.8 %copy-start.9 = (bf16[96,2048]{1,0:T(8,128)(2,1)S(1)}, bf16[96,2048]{1,0:T(8,128)(2,1)}, u32[]{:S(2)}) copy-start(bf16[96,2048]{1,0:T(8,128)(2,1)} %copy-done.8) | copy-start | bytes 1179652
  90.3 3.9 %copy-start.11 = (bf16[2048,16]{0,1:T(8,128)(2,1)S(1)}, bf16[2048,16]{0,1:T(8,128)(2,1)}, u32[]{:S(2)}) copy-start(bf16[2048,16]{0,1:T(8,128)(2,1)} %param.10) | copy-start | bytes 196612

commit v7 on v6

--- a/solution.py
+++ b/solution.py
@@ -14,6 +14,7 @@
 ROW_TILE = 32
 GRANT = 53 << 20
 SMALL_GRANT = 24 << 20
+OTHERS_GRANT = 54 << 20
 ROWS_AT_ONCE = 1024
 
 
@@ -457,7 +458,7 @@
         + [pltpu.VMEM((rows, ff_width), half)] * 3 + [pltpu.VMEM((rows, LANES), jnp.float32)],
         len(tok) + (len(tok) + 2) * len(tiles(width, 2 * FF_TILE))
         + len(tiles(ff_width, FF_TILE)) + 4,
-        3, after, 3 * rows * width * ff_width,
+        3, after, rows * width * ff_width, OTHERS_GRANT,
     )
 
 

time: 95.5 us -> 94.5 us (0.990)
  local copies, waits for them, and re-layouts: 7.75 us -> 6.76 us
    unnamed x48 -> x46, local copies, waits for them, and re-layouts: 6.6 us -> 5.61 us
where the time goes in v7:
time: 94.5 us; the launch traced here: 94.1 us
  Pallas kernels  36.1 us (38%)
  starting transfers between devices  31.9 us (34%)
  waiting for transfers between devices  17.3 us (18%)
  local copies, waits for them, and re-layouts  6.76 us (7%)
  between operations  1.02 us (1%)
    pallas_call x8, Pallas kernels, kernel_call(): pl.pallas_call(body, in_specs=[pl.BlockSpec(memory_space=pltpu.SMEM)] * l...  36.1 us
    ppermute x23, starting transfers between devices, swap_expert(): return lax.ppermute(array, 'expert', [(i, i ^ offset) for i in range(size)])  23.6 us
    ppermute x23, waiting for transfers between devices, swap_expert(): return lax.ppermute(array, 'expert', [(i, i ^ offset) for i in range(size)])  11.2 us
    ppermute x6, starting transfers between devices, swap_group(): return lax.ppermute(array, 'dp', [(i, i ^ offset) for i in range(size)])  8.32 us
    ppermute x6, waiting for transfers between devices, swap_group(): return lax.ppermute(array, 'dp', [(i, i ^ offset) for i in range(size)])  6.1 us
    unnamed x46, local copies, waits for them, and re-layouts  5.61 us
  transfers between devices with their start and end apart: 29, of which 8 were waited for; matrix products, arithmetic and copies ran while one was open for 2% of the time, Pallas kernels for 33%

profile of v7, /device:TPU:0, one launch (start us, length us, event | category | flops | bytes accessed | tf_op | source)
XLA Modules:
  0.0 94.1 jit_solution(7343919142383509114)
XLA Ops:
  0.6 4.1 %collective-permute-start.8 = (bf16[24,2048]{1,0:T(8,128)(2,1)}, bf16[24,2048]{1,0:T(8,128)(2,1)S(1)}, u32[]{:S(2)}, u32[]{:S(2)}) collective-permute-start(bf16[24,2048]{1,0:T(8,128)(2,1)} %refs_2_.1), channel_id=1, source_target_pairs={{0,8},{1,9},{2,10},{3,11},{4,12},{5,13},{6,14},{7,15},{8,0},{9,1},... | collective-permute-start | bytes 294920 | tf_op jit(solution)/shard_map/ppermute | solution.py:23
  4.7 1.6 %collective-permute-start.7 = (bf16[24,2048]{1,0:T(8,128)(2,1)}, bf16[24,2048]{1,0:T(8,128)(2,1)S(1)}, u32[]{:S(2)}, u32[]{:S(2)}) collective-permute-start(bf16[24,2048]{1,0:T(8,128)(2,1)} %refs_2_.1), channel_id=1, source_target_pairs={{0,4},{1,5},{2,6},{3,7},{4,0},{5,1},{6,2},{7,3},{8,12},{9,13},{10,... | collective-permute-start | bytes 294920 | tf_op jit(solution)/shard_map/ppermute | solution.py:23
  6.3 0.0 collective-permute-start.9
  6.3 0.8 copy.12.refs_1_
  7.1 0.9 copy-done.7
  8.0 0.8 copy-done.10
  8.8 0.3 shard_map.110
  9.1 1.7 %collective-permute-start = (bf16[24,128]{1,0:T(8,128)(2,1)S(1)}, bf16[24,128]{1,0:T(8,128)(2,1)S(1)}, u32[]{:S(2)}, u32[]{:S(2)}) collective-permute-start(bf16[24,128]{1,0:T(8,128)(2,1)S(1)} %get-tuple-element.31), channel_id=1, source_target_pairs={{0,16},{16,0},{1,17},{17,1},{2,18},{18,2},{3,19},{19,3},{4,20},{20... | collective-permute-start | bytes 18440 | tf_op jit(solution)/shard_map/ppermute | solution.py:28
  10.8 1.9 %collective-permute-done = bf16[24,128]{1,0:T(8,128)(2,1)S(1)} collective-permute-done((bf16[24,128]{1,0:T(8,128)(2,1)S(1)}, bf16[24,128]{1,0:T(8,128)(2,1)S(1)}, u32[]{:S(2)}, u32[]{:S(2)}) %collective-permute-start) | collective-permute-done | bytes 6176 | tf_op jit(solution)/shard_map/ppermute | solution.py:28
  12.7 0.1 slice.48
  12.8 1.0 %concatenate.9 = bf16[24,2176]{1,0:T(8,128)(2,1)S(1)} concatenate(bf16[24,2048]{1,0:T(8,128)(2,1)} %param.8, bf16[24,64]{1,0:T(8,128)(2,1)S(1)} %bitcast.11, bf16[24,48]{1,0:T(8,128)(2,1)S(1)} %slice.48, bf16[24,16]{1,0:T(8,128)(2,1)S(1)} %broadcast_in_dim.10), dimensions={1} | concatenate | bytes 208896 | tf_op jit(solution)/shard_map/concatenate | solution.py:592
  13.8 3.9 %collective-permute-start.3 = (bf16[24,2176]{1,0:T(8,128)(2,1)S(1)}, bf16[24,2176]{1,0:T(8,128)(2,1)S(1)}, u32[]{:S(2)}, u32[]{:S(2)}) collective-permute-start(bf16[24,2176]{1,0:T(8,128)(2,1)S(1)} %concatenate.9), channel_id=1, source_target_pairs={{0,12},{1,13},{2,14},{3,15},{4,8},{5,9},{6,10},{7,11},{8,4},{9,5},... | collective-permute-start | bytes 313352 | tf_op jit(solution)/shard_map/ppermute | solution.py:23
  17.7 0.6 collective-permute-start.1
  18.3 0.0 collective-permute-done.9
  18.4 1.7 %collective-permute-start.13 = (bf16[96,2048]{1,0:T(8,128)(2,1)S(1)}, bf16[96,2048]{1,0:T(8,128)(2,1)S(1)}, u32[]{:S(2)}, u32[]{:S(2)}) collective-permute-start(bf16[96,2048]{1,0:T(8,128)(2,1)S(1)} %constant_dynamic-update-slice_fusion.refs_3_.refs_4_.refs_1_), channel_id=1, source_target_pairs={{0,2},{1,3},{2,0},{3,1},{4,6},{5,7},{6,4},{7,5},{8,10},{9,11},{10,... | collective-permute-start | bytes 1179656 | tf_op jit(solution)/shard_map/ppermute | solution.py:23
  20.1 1.5 %collective-permute-start.10 = (bf16[96,2048]{1,0:T(8,128)(2,1)S(1)}, bf16[96,2048]{1,0:T(8,128)(2,1)S(1)}, u32[]{:S(2)}, u32[]{:S(2)}) collective-permute-start(bf16[96,2048]{1,0:T(8,128)(2,1)S(1)} %constant_dynamic-update-slice_fusion.refs_3_.refs_4_.refs_1_), channel_id=1, source_target_pairs={{0,16},{16,0},{1,17},{17,1},{2,18},{18,2},{3,19},{19,3},{4,20},{20... | collective-permute-start | bytes 1179656 | tf_op jit(solution)/shard_map/ppermute | solution.py:28
  21.6 0.0 collective-permute-done.3
  21.6 2.9 %collective-permute-done.2 = bf16[24,2176]{1,0:T(8,128)(2,1)S(1)} collective-permute-done((bf16[24,2176]{1,0:T(8,128)(2,1)S(1)}, bf16[24,2176]{1,0:T(8,128)(2,1)S(1)}, u32[]{:S(2)}, u32[]{:S(2)}) %collective-permute-start.2) | collective-permute-done | bytes 104480 | tf_op jit(solution)/shard_map/ppermute | solution.py:23
  24.6 1.5 %collective-permute-start.5 = (bf16[96,2176]{1,0:T(8,128)(2,1)S(1)}, bf16[96,2176]{1,0:T(8,128)(2,1)S(1)}, u32[]{:S(2)}, u32[]{:S(2)}) collective-permute-start(bf16[96,2176]{1,0:T(8,128)(2,1)S(1)} %pad_maximum_fusion.refs_1_.refs_7_.refs_9_), channel_id=1, source_target_pairs={{0,2},{1,3},{2,0},{3,1},{4,6},{5,7},{6,4},{7,5},{8,10},{9,11},{10,... | collective-permute-start | bytes 1253384 | tf_op jit(solution)/shard_map/ppermute | solution.py:23
  26.1 1.5 %collective-permute-done.13.refs_5_.refs_6_.refs_3_ = bf16[96,2048]{1,0:T(8,128)(2,1)S(1)} collective-permute-done((bf16[96,2048]{1,0:T(8,128)(2,1)S(1)}, bf16[96,2048]{1,0:T(8,128)(2,1)S(1)}, u32[]{:S(2)}, u32[]{:S(2)}) %collective-permute-start.13) | collective-permute-done | bytes 393248 | tf_op jit(solution)/shard_map/ppermute | solution.py:23
  27.7 1.5 %collective-permute-start.15 = (bf16[96,2048]{1,0:T(8,128)(2,1)S(1)}, bf16[96,2048]{1,0:T(8,128)(2,1)S(1)}, u32[]{:S(2)}, u32[]{:S(2)}) collective-permute-start(bf16[96,2048]{1,0:T(8,128)(2,1)S(1)} %collective-permute-done.13.refs_5_.refs_6_.refs_3_), channel_id=1, source_target_pairs={{0,16},{16,0},{1,17},{17,1},{2,18},{18,2},{3,19},{19,3},{4,20},{20... | collective-permute-start | bytes 1179656 | tf_op jit(solution)/shard_map/ppermute | solution.py:28
  29.2 0.0 collective-permute-done.10.refs_8_.refs_2_.refs_5_
  29.2 0.0 collective-permute-start.11
  29.2 0.5 collective-permute-start.4
  29.7 6.3 %collective-permute-done.5.refs_3_.refs_9_.refs_11_ = bf16[96,2176]{1,0:T(8,128)(2,1)S(1)} collective-permute-done((bf16[96,2176]{1,0:T(8,128)(2,1)S(1)}, bf16[96,2176]{1,0:T(8,128)(2,1)S(1)}, u32[]{:S(2)}, u32[]{:S(2)}) %collective-permute-start.5) | collective-permute-done | bytes 417824 | tf_op jit(solution)/shard_map/ppermute | solution.py:23
  36.0 0.0 collective-permute-start.6
  36.0 0.5 collective-permute-start.12
  36.5 0.2 collective-permute-done.15.refs_10_.refs_4_.refs_7_
  36.7 0.5 collective-permute-start.16
  37.2 0.0 collective-permute-done.4.refs_2_.refs_8_.refs_10_
  37.2 1.6 %collective-permute-start.18 = (bf16[96,2176]{1,0:T(8,128)(2,1)S(1)}, bf16[96,2176]{1,0:T(8,128)(2,1)S(1)}, u32[]{:S(2)}, u32[]{:S(2)}) collective-permute-start(bf16[96,2176]{1,0:T(8,128)(2,1)S(1)} %pad_maximum_fusion.refs_1_.refs_7_.refs_9_), channel_id=1, source_target_pairs={{0,16},{16,0},{1,17},{17,1},{2,18},{18,2},{3,19},{19,3},{4,20},{20... | collective-permute-start | bytes 1253384 | tf_op jit(solution)/shard_map/ppermute | solution.py:28
  38.8 0.5 collective-permute-start.19
  39.3 0.2 copy-done.18
  39.6 1.7 %shard_map.111 = (f32[768,128]{1,0:T(8,128)S(1)}, f32[16,768]{1,0:T(8,128)S(1)}) custom-call(s32[1]{0:T(128)} %bitcast.refs_0_, bf16[96,2176]{1,0:T(8,128)(2,1)S(1)} %pad_maximum_fusion.refs_1_.refs_7_.refs_9_, bf16[96,2176]{1,0:T(8,128)(2,1)} %copy-done.17, bf16[96,2176]{1,0:T(8,128)(2,1)} %copy-done.16, bf16[96,2176]{1,0:T(8,128)(2,1)} %copy-done.18, ...), custom_call_target="tpu_custom_call" | custom-call | flops 2000000 | bytes 5000 | tf_op jit(solution)/shard_map/pallas_call | solution.py:121
  41.2 0.0 copy-start.6
  41.2 0.7 copy-done.6
  42.0 0.0 collective-permute-done.12.refs_4_.refs_5_.refs_2_
  42.0 0.0 collective-permute-done.16.refs_14_.refs_11_.refs_5_.refs_8_
  42.1 0.7 copy-done.8
  42.7 0.1 copy-done.20
  42.9 0.1 copy-done.15
  43.0 12.4 %shard_map.112 = (bf16[96,2048]{1,0:T(8,128)(2,1)S(1)}, bf16[96,2048]{1,0:T(8,128)(2,1)}, bf16[96,2176]{1,0:T(8,128)(2,1)}, bf16[96,2176]{1,0:T(8,128)(2,1)}, bf...) custom-call(s32[1]{0:T(128)} %bitcast.refs_0_, ...), custom_call_target="tpu_custom_call" | custom-call | flops 6039797760 | bytes 15099494 | tf_op jit(solution)/shard_map/pallas_call | solution.py:121
  55.4 0.1 collective-permute-start.17
  55.5 0.0 collective-permute-done.18.refs_2_.refs_6_.refs_13_
  55.5 0.5 collective-permute-start.27
  56.0 1.9 %collective-permute-done.19.refs_3_.refs_8_.refs_15_ = bf16[96,2176]{1,0:T(8,128)(2,1)S(1)} collective-permute-done((bf16[96,2176]{1,0:T(8,128)(2,1)S(1)}, bf16[96,2176]{1,0:T(8,128)(2,1)S(1)}, u32[]{:S(2)}, u32[]{:S(2)}) %collective-permute-start.19) | collective-permute-done | bytes 417824 | tf_op jit(solution)/shard_map/ppermute | solution.py:28
  57.9 0.0 collective-permute-start.28
  57.9 0.0 copy-start.5
  57.9 1.1 %copy-done.5 = bf16[96,2176]{1,0:T(8,128)(2,1)S(1)} copy-done((bf16[96,2176]{1,0:T(8,128)(2,1)S(1)}, bf16[96,2176]{1,0:T(8,128)(2,1)}, u32[]{:S(2)}) %copy-start.5) | copy-done | bytes 417816
  59.1 0.8 shard_map.113
  59.8 1.4 %collective-permute-start.23 = (bf16[96,2176]{1,0:T(8,128)(2,1)S(1)}, bf16[96,2176]{1,0:T(8,128)(2,1)S(1)}, u32[]{:S(2)}, u32[]{:S(2)}) collective-permute-start(bf16[96,2176]{1,0:T(8,128)(2,1)S(1)} %get-tuple-element.38.refs_4_), channel_id=1, source_target_pairs={{0,2},{1,3},{2,0},{3,1},{4,6},{5,7},{6,4},{7,5},{8,10},{9,11},{10,... | collective-permute-start | bytes 1253384 | tf_op jit(solution)/shard_map/ppermute | solution.py:23
  61.2 0.1 collective-permute-start.22
  61.3 1.5 %collective-permute-start.20 = (bf16[16,128]{1,0:T(8,128)(2,1)S(1)}, bf16[16,128]{1,0:T(8,128)(2,1)S(1)}, u32[]{:S(2)}, u32[]{:S(2)}) collective-permute-start(bf16[16,128]{1,0:T(8,128)(2,1)S(1)} %get-tuple-element.35), channel_id=1, source_target_pairs={{0,16},{16,0},{1,17},{17,1},{2,18},{18,2},{3,19},{19,3},{4,20},{20... | collective-permute-start | bytes 12296 | tf_op jit(solution)/shard_map/ppermute | solution.py:28
  62.8 2.1 %collective-permute-done.20.refs_0_ = bf16[16,128]{1,0:T(8,128)(2,1)S(1)} collective-permute-done((bf16[16,128]{1,0:T(8,128)(2,1)S(1)}, bf16[16,128]{1,0:T(8,128)(2,1)S(1)}, u32[]{:S(2)}, u32[]{:S(2)}) %collective-permute-start.20) | collective-permute-done | bytes 4128 | tf_op jit(solution)/shard_map/ppermute | solution.py:28
  64.9 0.7 collective-permute-start.21
  65.6 8.8 %shard_map.116 = (bf16[384,768]{1,0:T(8,128)(2,1)}, bf16[384,768]{1,0:T(8,128)(2,1)}, bf16[384,768]{1,0:T(8,128)(2,1)}) custom-call(s32[1]{0:T(128)} %bitcast.refs_0_, f32[768,128]{1,0:T(8,128)} %copy-done.6, bf16[96,2048]{1,0:T(8,128)(2,1)} %copy-done.13, bf16[96,2048]{1,0:T(8,128)(2,1)} %copy-done.12, bf16[96,2048]{1,0:T(8,128)(2,1)} %copy-done.14, ...), custom_call_target="tpu_custom_call" | custom-call | flops 1207959552 | bytes 3019898 | tf_op jit(solution)/shard_map/pallas_call | solution.py:121
  74.5 1.7 %shard_map.114 = (bf16[24,2176]{1,0:T(8,128)(2,1)S(1)}, bf16[24,2176]{1,0:T(8,128)(2,1)S(1)}, bf16[24,2176]{1,0:T(8,128)(2,1)S(1)}, bf16[24,2176]{1,0:T(8,128)(2,1)S(1)}) custom-call(bf16[16,128]{1,0:T(8,128)(2,1)S(1)} %collective-permute-done.20.refs_0_, bf16[16,128]{1,0:T(8,128)(2,1)S(1)} %collective-permute-done.21.refs_1_, ...), custom_call_target="tpu_custom_call" | custom-call | flops 2000000 | bytes 5000 | tf_op jit(solution)/shard_map/pallas_call | solution.py:121
  76.2 2.8 %collective-permute-start.24 = (bf16[24,2176]{1,0:T(8,128)(2,1)S(1)}, bf16[24,2176]{1,0:T(8,128)(2,1)S(1)}, u32[]{:S(2)}, u32[]{:S(2)}) collective-permute-start(bf16[24,2176]{1,0:T(8,128)(2,1)S(1)} %get-tuple-element.40.refs_23_), channel_id=1, source_target_pairs={{0,4},{1,5},{2,6},{3,7},{4,0},{5,1},{6,2},{7,3},{8,12},{9,13},{10,... | collective-permute-start | bytes 313352 | tf_op jit(solution)/shard_map/ppermute | solution.py:23
  79.0 3.1 %collective-permute-start.25 = (bf16[24,2176]{1,0:T(8,128)(2,1)S(1)}, bf16[24,2176]{1,0:T(8,128)(2,1)S(1)}, u32[]{:S(2)}, u32[]{:S(2)}) collective-permute-start(bf16[24,2176]{1,0:T(8,128)(2,1)S(1)} %get-tuple-element.41.refs_24_), channel_id=1, source_target_pairs={{0,8},{1,9},{2,10},{3,11},{4,12},{5,13},{6,14},{7,15},{8,0},{9,1},... | collective-permute-start | bytes 313352 | tf_op jit(solution)/shard_map/ppermute | solution.py:23
  82.1 7.2 %shard_map.117 = (bf16[1,1024,768]{2,1,0:T(8,128)(2,1)}, bf16[1,1024,768]{2,1,0:T(8,128)(2,1)}, bf16[1,384,2048]{2,1,0:T(8,128)(2,1)}) custom-call(s32[1]{0:T(128)} %bitcast.7.refs_0_, bf16[96,2048]{1,0:T(8,128)(2,1)S(1)} %copy-done.4, bf16[96,2048]{1,0:T(8,128)(2,1)} %copy-done.8, bf16[96,2048]{1,0:T(8,128)(2,1)} %copy-done.19, ...), custom_call_target="tpu_custom_call" | custom-call | flops 3623878656 | bytes 9059696 | tf_op jit(solution)/shard_map/pallas_call | solution.py:121
  89.3 0.0 copy-start.11
  89.4 0.4 collective-permute-done.25
  89.9 3.3 %shard_map.115 = (bf16[16,768]{1,0:T(8,128)(2,1)S(1)}, f32[16,2048]{1,0:T(8,128)}) custom-call(s32[1]{0:T(128)} %bitcast.refs_0_, bf16[2,16,384]{2,1,0:T(8,128)(2,1)S(1)} %reshape.13.refs_1_, s32[1,384]{1,0:T(1,128)S(1)} %get-tuple-element.30.refs_1_.refs_2_, f32[16,768]{1,0:T(8,128)S(1)} %get-tuple-element.43.refs_3_, bf16[96,2048]{1,0:T(8,128)(2,1)S(1)} %copy-done.4, ...), custom_call_target="tpu_custom_call" | custom-call | flops 2000000 | bytes 5000 | tf_op jit(solution)/shard_map/pallas_call | solution.py:121
  93.2 0.8 fusion
  (65 shorter events, 0.3 us)
Async XLA Ops:
  0.6 17.7 %collective-permute-start.8 = (bf16[24,2048]{1,0:T(8,128)(2,1)}, bf16[24,2048]{1,0:T(8,128)(2,1)S(1)}, u32[]{:S(2)}, u32[]{:S(2)}) collective-permute-start(bf16[24,2048]{1,0:T(8,128)(2,1)} %refs_2_.1), channel_id=1, source_target_pairs={{0,8},{1,9},{2,10},{3,11},{4,12},{5,13},{6,14},{7,15},{8,0},{9,1},... | collective-permute-start | bytes 294920 | tf_op jit(solution)/shard_map/ppermute | solution.py:23
  4.7 12.9 %collective-permute-start.7 = (bf16[24,2048]{1,0:T(8,128)(2,1)}, bf16[24,2048]{1,0:T(8,128)(2,1)S(1)}, u32[]{:S(2)}, u32[]{:S(2)}) collective-permute-start(bf16[24,2048]{1,0:T(8,128)(2,1)} %refs_2_.1), channel_id=1, source_target_pairs={{0,4},{1,5},{2,6},{3,7},{4,0},{5,1},{6,2},{7,3},{8,12},{9,13},{10,... | collective-permute-start | bytes 294920 | tf_op jit(solution)/shard_map/ppermute | solution.py:23
  6.3 12.0 %collective-permute-start.9 = (bf16[24,2048]{1,0:T(8,128)(2,1)}, bf16[24,2048]{1,0:T(8,128)(2,1)S(1)}, u32[]{:S(2)}, u32[]{:S(2)}) collective-permute-start(bf16[24,2048]{1,0:T(8,128)(2,1)} %refs_2_.1), channel_id=1, source_target_pairs={{0,12},{1,13},{2,14},{3,15},{4,8},{5,9},{6,10},{7,11},{8,4},{9,5},... | collective-permute-start | bytes 294920 | tf_op jit(solution)/shard_map/ppermute | solution.py:23
  7.1 0.9 copy-start.7
  8.0 0.8 copy-start.10
  9.1 3.6 %collective-permute-start = (bf16[24,128]{1,0:T(8,128)(2,1)S(1)}, bf16[24,128]{1,0:T(8,128)(2,1)S(1)}, u32[]{:S(2)}, u32[]{:S(2)}) collective-permute-start(bf16[24,128]{1,0:T(8,128)(2,1)S(1)} %get-tuple-element.31), channel_id=1, source_target_pairs={{0,16},{16,0},{1,17},{17,1},{2,18},{18,2},{3,19},{19,3},{4,20},{20... | collective-permute-start | bytes 18440 | tf_op jit(solution)/shard_map/ppermute | solution.py:28
  13.8 7.8 %collective-permute-start.3 = (bf16[24,2176]{1,0:T(8,128)(2,1)S(1)}, bf16[24,2176]{1,0:T(8,128)(2,1)S(1)}, u32[]{:S(2)}, u32[]{:S(2)}) collective-permute-start(bf16[24,2176]{1,0:T(8,128)(2,1)S(1)} %concatenate.9), channel_id=1, source_target_pairs={{0,12},{1,13},{2,14},{3,15},{4,8},{5,9},{6,10},{7,11},{8,4},{9,5},... | collective-permute-start | bytes 313352 | tf_op jit(solution)/shard_map/ppermute | solution.py:23
  17.7 6.9 %collective-permute-start.2 = (bf16[24,2176]{1,0:T(8,128)(2,1)S(1)}, bf16[24,2176]{1,0:T(8,128)(2,1)S(1)}, u32[]{:S(2)}, u32[]{:S(2)}) collective-permute-start(bf16[24,2176]{1,0:T(8,128)(2,1)S(1)} %concatenate.9), channel_id=1, source_target_pairs={{0,8},{1,9},{2,10},{3,11},{4,12},{5,13},{6,14},{7,15},{8,0},{9,1},... | collective-permute-start | bytes 313352 | tf_op jit(solution)/shard_map/ppermute | solution.py:23
  17.7 6.9 %collective-permute-start.1 = (bf16[24,2176]{1,0:T(8,128)(2,1)S(1)}, bf16[24,2176]{1,0:T(8,128)(2,1)S(1)}, u32[]{:S(2)}, u32[]{:S(2)}) collective-permute-start(bf16[24,2176]{1,0:T(8,128)(2,1)S(1)} %concatenate.9), channel_id=1, source_target_pairs={{0,4},{1,5},{2,6},{3,7},{4,0},{5,1},{6,2},{7,3},{8,12},{9,13},{10,... | collective-permute-start | bytes 313352 | tf_op jit(solution)/shard_map/ppermute | solution.py:23
  18.4 23.7 %copy-start.3 = (bf16[96,2048]{1,0:T(8,128)(2,1)}, bf16[96,2048]{1,0:T(8,128)(2,1)S(1)}, u32[]{:S(2)}) copy-start(bf16[96,2048]{1,0:T(8,128)(2,1)S(1)} %constant_dynamic-update-slice_fusion.refs_3_.refs_4_.refs_1_) | copy-start | bytes 1179652
  18.4 9.3 %collective-permute-start.13 = (bf16[96,2048]{1,0:T(8,128)(2,1)S(1)}, bf16[96,2048]{1,0:T(8,128)(2,1)S(1)}, u32[]{:S(2)}, u32[]{:S(2)}) collective-permute-start(bf16[96,2048]{1,0:T(8,128)(2,1)S(1)} %constant_dynamic-update-slice_fusion.refs_3_.refs_4_.refs_1_), channel_id=1, source_target_pairs={{0,2},{1,3},{2,0},{3,1},{4,6},{5,7},{6,4},{7,5},{8,10},{9,11},{10,... | collective-permute-start | bytes 1179656 | tf_op jit(solution)/shard_map/ppermute | solution.py:23
  20.1 9.1 %collective-permute-start.10 = (bf16[96,2048]{1,0:T(8,128)(2,1)S(1)}, bf16[96,2048]{1,0:T(8,128)(2,1)S(1)}, u32[]{:S(2)}, u32[]{:S(2)}) collective-permute-start(bf16[96,2048]{1,0:T(8,128)(2,1)S(1)} %constant_dynamic-update-slice_fusion.refs_3_.refs_4_.refs_1_), channel_id=1, source_target_pairs={{0,16},{16,0},{1,17},{17,1},{2,18},{18,2},{3,19},{19,3},{4,20},{20... | collective-permute-start | bytes 1179656 | tf_op jit(solution)/shard_map/ppermute | solution.py:28
  24.6 17.5 %copy-start.2 = (bf16[96,2176]{1,0:T(8,128)(2,1)}, bf16[96,2176]{1,0:T(8,128)(2,1)S(1)}, u32[]{:S(2)}) copy-start(bf16[96,2176]{1,0:T(8,128)(2,1)S(1)} %pad_maximum_fusion.refs_1_.refs_7_.refs_9_) | copy-start | bytes 1253380
  24.6 11.4 %collective-permute-start.5 = (bf16[96,2176]{1,0:T(8,128)(2,1)S(1)}, bf16[96,2176]{1,0:T(8,128)(2,1)S(1)}, u32[]{:S(2)}, u32[]{:S(2)}) collective-permute-start(bf16[96,2176]{1,0:T(8,128)(2,1)S(1)} %pad_maximum_fusion.refs_1_.refs_7_.refs_9_), channel_id=1, source_target_pairs={{0,2},{1,3},{2,0},{3,1},{4,6},{5,7},{6,4},{7,5},{8,10},{9,11},{10,... | collective-permute-start | bytes 1253384 | tf_op jit(solution)/shard_map/ppermute | solution.py:23
  27.7 14.4 %copy-start.19 = (bf16[96,2048]{1,0:T(8,128)(2,1)}, bf16[96,2048]{1,0:T(8,128)(2,1)S(1)}, u32[]{:S(2)}) copy-start(bf16[96,2048]{1,0:T(8,128)(2,1)S(1)} %collective-permute-done.13.refs_5_.refs_6_.refs_3_) | copy-start | bytes 1179652
  27.7 9.1 %collective-permute-start.15 = (bf16[96,2048]{1,0:T(8,128)(2,1)S(1)}, bf16[96,2048]{1,0:T(8,128)(2,1)S(1)}, u32[]{:S(2)}, u32[]{:S(2)}) collective-permute-start(bf16[96,2048]{1,0:T(8,128)(2,1)S(1)} %collective-permute-done.13.refs_5_.refs_6_.refs_3_), channel_id=1, source_target_pairs={{0,16},{16,0},{1,17},{17,1},{2,18},{18,2},{3,19},{19,3},{4,20},{20... | collective-permute-start | bytes 1179656 | tf_op jit(solution)/shard_map/ppermute | solution.py:28
  29.2 12.8 %copy-start.13 = (bf16[96,2048]{1,0:T(8,128)(2,1)}, bf16[96,2048]{1,0:T(8,128)(2,1)S(1)}, u32[]{:S(2)}) copy-start(bf16[96,2048]{1,0:T(8,128)(2,1)S(1)} %collective-permute-done.10.refs_8_.refs_2_.refs_5_) | copy-start | bytes 1179652
  29.2 7.5 %collective-permute-start.11 = (bf16[96,2048]{1,0:T(8,128)(2,1)S(1)}, bf16[96,2048]{1,0:T(8,128)(2,1)S(1)}, u32[]{:S(2)}, u32[]{:S(2)}) collective-permute-start(bf16[96,2048]{1,0:T(8,128)(2,1)S(1)} %collective-permute-done.10.refs_8_.refs_2_.refs_5_), channel_id=1, source_target_pairs={{0,1},{1,0},{2,3},{3,2},{4,5},{5,4},{6,7},{7,6},{8,9},{9,8},{10,11... | collective-permute-start | bytes 1179656 | tf_op jit(solution)/shard_map/ppermute | solution.py:23
  29.2 8.0 %collective-permute-start.4 = (bf16[96,2176]{1,0:T(8,128)(2,1)S(1)}, bf16[96,2176]{1,0:T(8,128)(2,1)S(1)}, u32[]{:S(2)}, u32[]{:S(2)}) collective-permute-start(bf16[96,2176]{1,0:T(8,128)(2,1)S(1)} %pad_maximum_fusion.refs_1_.refs_7_.refs_9_), channel_id=1, source_target_pairs={{0,1},{1,0},{2,3},{3,2},{4,5},{5,4},{6,7},{7,6},{8,9},{9,8},{10,11... | collective-permute-start | bytes 1253384 | tf_op jit(solution)/shard_map/ppermute | solution.py:23
  36.0 3.3 %copy-start.16 = (bf16[96,2176]{1,0:T(8,128)(2,1)}, bf16[96,2176]{1,0:T(8,128)(2,1)S(1)}, u32[]{:S(2)}) copy-start(bf16[96,2176]{1,0:T(8,128)(2,1)S(1)} %collective-permute-done.5.refs_3_.refs_9_.refs_11_) | copy-start | bytes 1253380
  36.0 2.8 %collective-permute-start.6 = (bf16[96,2176]{1,0:T(8,128)(2,1)S(1)}, bf16[96,2176]{1,0:T(8,128)(2,1)S(1)}, u32[]{:S(2)}, u32[]{:S(2)}) collective-permute-start(bf16[96,2176]{1,0:T(8,128)(2,1)S(1)} %collective-permute-done.5.refs_3_.refs_9_.refs_11_), channel_id=1, source_target_pairs={{0,1},{1,0},{2,3},{3,2},{4,5},{5,4},{6,7},{7,6},{8,9},{9,8},{10,11... | collective-permute-start | bytes 1253384 | tf_op jit(solution)/shard_map/ppermute | solution.py:23
  36.0 6.0 %collective-permute-start.12 = (bf16[96,2048]{1,0:T(8,128)(2,1)S(1)}, bf16[96,2048]{1,0:T(8,128)(2,1)S(1)}, u32[]{:S(2)}, u32[]{:S(2)}) collective-permute-start(bf16[96,2048]{1,0:T(8,128)(2,1)S(1)} %constant_dynamic-update-slice_fusion.refs_3_.refs_4_.refs_1_), channel_id=1, source_target_pairs={{0,1},{1,0},{2,3},{3,2},{4,5},{5,4},{6,7},{7,6},{8,9},{9,8},{10,11... | collective-permute-start | bytes 1179656 | tf_op jit(solution)/shard_map/ppermute | solution.py:23
  36.7 18.7 %copy-start.14 = (bf16[96,2048]{1,0:T(8,128)(2,1)}, bf16[96,2048]{1,0:T(8,128)(2,1)S(1)}, u32[]{:S(2)}) copy-start(bf16[96,2048]{1,0:T(8,128)(2,1)S(1)} %collective-permute-done.15.refs_10_.refs_4_.refs_7_) | copy-start | bytes 1179652
  36.7 5.3 %collective-permute-start.14 = (bf16[96,2048]{1,0:T(8,128)(2,1)S(1)}, bf16[96,2048]{1,0:T(8,128)(2,1)S(1)}, u32[]{:S(2)}, u32[]{:S(2)}) collective-permute-start(bf16[96,2048]{1,0:T(8,128)(2,1)S(1)} %collective-permute-done.13.refs_5_.refs_6_.refs_3_), channel_id=1, source_target_pairs={{0,1},{1,0},{2,3},{3,2},{4,5},{5,4},{6,7},{7,6},{8,9},{9,8},{10,11... | collective-permute-start | bytes 1179656 | tf_op jit(solution)/shard_map/ppermute | solution.py:23
  36.7 18.7 %copy-start.12 = (bf16[96,2048]{1,0:T(8,128)(2,1)}, bf16[96,2048]{1,0:T(8,128)(2,1)S(1)}, u32[]{:S(2)}) copy-start(bf16[96,2048]{1,0:T(8,128)(2,1)S(1)} %collective-permute-done.11.refs_9_.refs_3_.refs_6_) | copy-start | bytes 1179652
  36.7 5.3 %collective-permute-start.16 = (bf16[96,2048]{1,0:T(8,128)(2,1)S(1)}, bf16[96,2048]{1,0:T(8,128)(2,1)S(1)}, u32[]{:S(2)}, u32[]{:S(2)}) collective-permute-start(bf16[96,2048]{1,0:T(8,128)(2,1)S(1)} %collective-permute-done.15.refs_10_.refs_4_.refs_7_), channel_id=1, source_target_pairs={{0,1},{1,0},{2,3},{3,2},{4,5},{5,4},{6,7},{7,6},{8,9},{9,8},{10,11... | collective-permute-start | bytes 1179656 | tf_op jit(solution)/shard_map/ppermute | solution.py:23
  37.2 2.1 %copy-start.17 = (bf16[96,2176]{1,0:T(8,128)(2,1)}, bf16[96,2176]{1,0:T(8,128)(2,1)S(1)}, u32[]{:S(2)}) copy-start(bf16[96,2176]{1,0:T(8,128)(2,1)S(1)} %collective-permute-done.4.refs_2_.refs_8_.refs_10_) | copy-start | bytes 1253380
  37.2 18.3 %collective-permute-start.18 = (bf16[96,2176]{1,0:T(8,128)(2,1)S(1)}, bf16[96,2176]{1,0:T(8,128)(2,1)S(1)}, u32[]{:S(2)}, u32[]{:S(2)}) collective-permute-start(bf16[96,2176]{1,0:T(8,128)(2,1)S(1)} %pad_maximum_fusion.refs_1_.refs_7_.refs_9_), channel_id=1, source_target_pairs={{0,16},{16,0},{1,17},{17,1},{2,18},{18,2},{3,19},{19,3},{4,20},{20... | collective-permute-start | bytes 1253384 | tf_op jit(solution)/shard_map/ppermute | solution.py:28
  38.8 0.8 copy-start.18
  38.8 19.1 %collective-permute-start.19 = (bf16[96,2176]{1,0:T(8,128)(2,1)S(1)}, bf16[96,2176]{1,0:T(8,128)(2,1)S(1)}, u32[]{:S(2)}, u32[]{:S(2)}) collective-permute-start(bf16[96,2176]{1,0:T(8,128)(2,1)S(1)} %collective-permute-done.5.refs_3_.refs_9_.refs_11_), channel_id=1, source_target_pairs={{0,16},{16,0},{1,17},{17,1},{2,18},{18,2},{3,19},{19,3},{4,20},{20... | collective-permute-start | bytes 1253384 | tf_op jit(solution)/shard_map/ppermute | solution.py:28
  41.2 0.7 copy-start.6
  42.0 0.7 copy-start.8
  42.0 0.9 copy-start.20
  42.0 1.0 %copy-start.15 = (bf16[96,2048]{1,0:T(8,128)(2,1)}, bf16[96,2048]{1,0:T(8,128)(2,1)S(1)}, u32[]{:S(2)}) copy-start(bf16[96,2048]{1,0:T(8,128)(2,1)S(1)} %collective-permute-done.16.refs_14_.refs_11_.refs_5_.refs_8_) | copy-start | bytes 1179652
  55.4 2.5 %collective-permute-start.17 = (bf16[96,2176]{1,0:T(8,128)(2,1)}, bf16[96,2176]{1,0:T(8,128)(2,1)S(1)}, u32[]{:S(2)}, u32[]{:S(2)}) collective-permute-start(bf16[96,2176]{1,0:T(8,128)(2,1)} %get-tuple-element.34), channel_id=1, source_target_pairs={{0,1},{1,0},{2,3},{3,2},{4,5},{5,4},{6,7},{7,6},{8,9},{9,8},{10,11... | collective-permute-start | bytes 1253384 | tf_op jit(solution)/shard_map/ppermute | solution.py:23
  55.5 10.1 %copy-start = (bf16[96,2176]{1,0:T(8,128)(2,1)}, bf16[96,2176]{1,0:T(8,128)(2,1)S(1)}, u32[]{:S(2)}) copy-start(bf16[96,2176]{1,0:T(8,128)(2,1)S(1)} %collective-permute-done.18.refs_2_.refs_6_.refs_13_) | copy-start | bytes 1253380
  55.5 10.1 %collective-permute-start.27 = (bf16[96,2176]{1,0:T(8,128)(2,1)S(1)}, bf16[96,2176]{1,0:T(8,128)(2,1)}, u32[]{:S(2)}, u32[]{:S(2)}) collective-permute-start(bf16[96,2176]{1,0:T(8,128)(2,1)S(1)} %collective-permute-done.18.refs_2_.refs_6_.refs_13_), channel_id=1, source_target_pairs={{0,1},{1,0},{2,3},{3,2},{4,5},{5,4},{6,7},{7,6},{8,9},{9,8},{10,11... | collective-permute-start | bytes 1253384 | tf_op jit(solution)/shard_map/ppermute | solution.py:23
  57.9 7.7 %copy-start.1 = (bf16[96,2176]{1,0:T(8,128)(2,1)}, bf16[96,2176]{1,0:T(8,128)(2,1)S(1)}, u32[]{:S(2)}) copy-start(bf16[96,2176]{1,0:T(8,128)(2,1)S(1)} %collective-permute-done.19.refs_3_.refs_8_.refs_15_) | copy-start | bytes 1253380
  57.9 7.7 %collective-permute-start.28 = (bf16[96,2176]{1,0:T(8,128)(2,1)S(1)}, bf16[96,2176]{1,0:T(8,128)(2,1)}, u32[]{:S(2)}, u32[]{:S(2)}) collective-permute-start(bf16[96,2176]{1,0:T(8,128)(2,1)S(1)} %collective-permute-done.19.refs_3_.refs_8_.refs_15_), channel_id=1, source_target_pairs={{0,1},{1,0},{2,3},{3,2},{4,5},{5,4},{6,7},{7,6},{8,9},{9,8},{10,11... | collective-permute-start | bytes 1253384 | tf_op jit(solution)/shard_map/ppermute | solution.py:23
  57.9 1.2 %copy-start.5 = (bf16[96,2176]{1,0:T(8,128)(2,1)S(1)}, bf16[96,2176]{1,0:T(8,128)(2,1)}, u32[]{:S(2)}) copy-start(bf16[96,2176]{1,0:T(8,128)(2,1)} %get-tuple-element.33.refs_0_) | copy-start | bytes 1253380
  59.8 14.6 %collective-permute-start.23 = (bf16[96,2176]{1,0:T(8,128)(2,1)S(1)}, bf16[96,2176]{1,0:T(8,128)(2,1)S(1)}, u32[]{:S(2)}, u32[]{:S(2)}) collective-permute-start(bf16[96,2176]{1,0:T(8,128)(2,1)S(1)} %get-tuple-element.38.refs_4_), channel_id=1, source_target_pairs={{0,2},{1,3},{2,0},{3,1},{4,6},{5,7},{6,4},{7,5},{8,10},{9,11},{10,... | collective-permute-start | bytes 1253384 | tf_op jit(solution)/shard_map/ppermute | solution.py:23
  61.2 13.2 %collective-permute-start.22 = (bf16[96,2048]{1,0:T(8,128)(2,1)}, bf16[96,2048]{1,0:T(8,128)(2,1)S(1)}, u32[]{:S(2)}, u32[]{:S(2)}) collective-permute-start(bf16[96,2048]{1,0:T(8,128)(2,1)} %get-tuple-element.37), channel_id=1, source_target_pairs={{0,1},{1,0},{2,3},{3,2},{4,5},{5,4},{6,7},{7,6},{8,9},{9,8},{10,11... | collective-permute-start | bytes 1179656 | tf_op jit(solution)/shard_map/ppermute | solution.py:23
  61.3 3.6 %collective-permute-start.20 = (bf16[16,128]{1,0:T(8,128)(2,1)S(1)}, bf16[16,128]{1,0:T(8,128)(2,1)S(1)}, u32[]{:S(2)}, u32[]{:S(2)}) collective-permute-start(bf16[16,128]{1,0:T(8,128)(2,1)S(1)} %get-tuple-element.35), channel_id=1, source_target_pairs={{0,16},{16,0},{1,17},{17,1},{2,18},{18,2},{3,19},{19,3},{4,20},{20... | collective-permute-start | bytes 12296 | tf_op jit(solution)/shard_map/ppermute | solution.py:28
  62.8 19.3 %copy-start.4 = (bf16[96,2048]{1,0:T(8,128)(2,1)S(1)}, bf16[96,2048]{1,0:T(8,128)(2,1)}, u32[]{:S(2)}) copy-start(bf16[96,2048]{1,0:T(8,128)(2,1)} %copy-done.3) | copy-start | bytes 1179652
  64.9 9.5 %collective-permute-start.21 = (bf16[16,128]{1,0:T(8,128)(2,1)S(1)}, bf16[16,128]{1,0:T(8,128)(2,1)S(1)}, u32[]{:S(2)}, u32[]{:S(2)}) collective-permute-start(bf16[16,128]{1,0:T(8,128)(2,1)S(1)} %collective-permute-done.20.refs_0_), channel_id=1, source_target_pairs={{0,2},{1,3},{2,0},{3,1},{4,6},{5,7},{6,4},{7,5},{8,10},{9,11},{10,... | collective-permute-start | bytes 12296 | tf_op jit(solution)/shard_map/ppermute | solution.py:23
  76.2 13.2 %collective-permute-start.24 = (bf16[24,2176]{1,0:T(8,128)(2,1)S(1)}, bf16[24,2176]{1,0:T(8,128)(2,1)S(1)}, u32[]{:S(2)}, u32[]{:S(2)}) collective-permute-start(bf16[24,2176]{1,0:T(8,128)(2,1)S(1)} %get-tuple-element.40.refs_23_), channel_id=1, source_target_pairs={{0,4},{1,5},{2,6},{3,7},{4,0},{5,1},{6,2},{7,3},{8,12},{9,13},{10,... | collective-permute-start | bytes 313352 | tf_op jit(solution)/shard_map/ppermute | solution.py:23
  79.0 10.8 %collective-permute-start.25 = (bf16[24,2176]{1,0:T(8,128)(2,1)S(1)}, bf16[24,2176]{1,0:T(8,128)(2,1)S(1)}, u32[]{:S(2)}, u32[]{:S(2)}) collective-permute-start(bf16[24,2176]{1,0:T(8,128)(2,1)S(1)} %get-tuple-element.41.refs_24_), channel_id=1, source_target_pairs={{0,8},{1,9},{2,10},{3,11},{4,12},{5,13},{6,14},{7,15},{8,0},{9,1},... | collective-permute-start | bytes 313352 | tf_op jit(solution)/shard_map/ppermute | solution.py:23
  82.1 7.7 %collective-permute-start.26 = (bf16[24,2176]{1,0:T(8,128)(2,1)S(1)}, bf16[24,2176]{1,0:T(8,128)(2,1)S(1)}, u32[]{:S(2)}, u32[]{:S(2)}) collective-permute-start(bf16[24,2176]{1,0:T(8,128)(2,1)S(1)} %get-tuple-element.42.refs_25_), channel_id=1, source_target_pairs={{0,12},{1,13},{2,14},{3,15},{4,8},{5,9},{6,10},{7,11},{8,4},{9,5},... | collective-permute-start | bytes 313352 | tf_op jit(solution)/shard_map/ppermute | solution.py:23
  82.1 7.8 %copy-start.9 = (bf16[96,2048]{1,0:T(8,128)(2,1)S(1)}, bf16[96,2048]{1,0:T(8,128)(2,1)}, u32[]{:S(2)}) copy-start(bf16[96,2048]{1,0:T(8,128)(2,1)} %copy-done.8) | copy-start | bytes 1179652
  89.3 3.9 %copy-start.11 = (bf16[2048,16]{0,1:T(8,128)(2,1)S(1)}, bf16[2048,16]{0,1:T(8,128)(2,1)}, u32[]{:S(2)}) copy-start(bf16[2048,16]{0,1:T(8,128)(2,1)} %param.10) | copy-start | bytes 196612

commit v8 on v7

--- a/solution.py
+++ b/solution.py
@@ -61,7 +61,9 @@
     return -(-value // unit) * unit
 
 
-def pack_kernel(slots, me_ref, ids_ref, tok_ref, router_ref, out, place_ref):
+def pack_kernel(slots, me_ref, ids_ref, tok, router, out, place_ref, tok_ref, router_ref, sems):
+    copies = Copies(sems)
+    operands_here = [copies.start(tok, tok_ref), copies.start(router, router_ref)]
     experts = router_ref.shape[0]
     rows = tok_ref.shape[0]
     at = lax.broadcasted_iota(jnp.int32, place_ref.shape, 1)
@@ -71,6 +73,7 @@
         here = (at >= first) & (at < first + rows)
         place = jnp.where(here, (me_ref[0] ^ offset) * rows + at - first, place)
     place_ref[...] = place
+    wait(operands_here)
     rest = contract(tok_ref[...], router_ref[...], 1, 1)
     lane = lax.broadcasted_iota(jnp.int32, out.shape, 1)
     packed = jnp.zeros(out.shape, jnp.float32)
@@ -581,8 +584,10 @@
     tok_line = along(tokens)
     slots = [4 * j + 2 * i + k for i in range(2) for k in range(2) for j in range(far)]
     packed, place = kernel_call(
-        functools.partial(pack_kernel, slots), (me,), (expert_ids, tokens, router_weight.T), (),
-        [shape(tok_rows, round_up(4 * experts, LANES)), shape(1, 2 * chunk, jnp.int32)], (), 0,
+        functools.partial(pack_kernel, slots), (me,), (expert_ids,),
+        (tokens, router_weight.T),
+        [shape(tok_rows, round_up(4 * experts, LANES)), shape(1, 2 * chunk, jnp.int32)],
+        [pltpu.VMEM(tokens.shape, tokens.dtype), pltpu.VMEM((experts, width), tokens.dtype)], 2,
     )
     columns = [out_grad, packed[:, : 4 * experts]]
     for offset in range(1, groups):

time: 94.5 us -> 94.7 us (level)
  no operation moved by 1% of the time
where the time goes in v8:
time: 94.7 us; the launch traced here: 94.4 us
  Pallas kernels  36.5 us (39%)
  starting transfers between devices  32 us (34%)
  waiting for transfers between devices  17.2 us (18%)
  local copies, waits for them, and re-layouts  6.75 us (7%)
  between operations  1.03 us (1%)
    pallas_call x8, Pallas kernels, kernel_call(): pl.pallas_call(body, in_specs=[pl.BlockSpec(memory_space=pltpu.SMEM)] * l...  36.5 us
    ppermute x23, starting transfers between devices, swap_expert(): return lax.ppermute(array, 'expert', [(i, i ^ offset) for i in range(size)])  23.6 us
    ppermute x23, waiting for transfers between devices, swap_expert(): return lax.ppermute(array, 'expert', [(i, i ^ offset) for i in range(size)])  11.1 us
    ppermute x6, starting transfers between devices, swap_group(): return lax.ppermute(array, 'dp', [(i, i ^ offset) for i in range(size)])  8.38 us
    ppermute x6, waiting for transfers between devices, swap_group(): return lax.ppermute(array, 'dp', [(i, i ^ offset) for i in range(size)])  6.12 us
    unnamed x46, local copies, waits for them, and re-layouts  5.6 us
  transfers between devices with their start and end apart: 29, of which 8 were waited for; matrix products, arithmetic and copies ran while one was open for 2% of the time, Pallas kernels for 33%

profile of v8, /device:TPU:0, one launch (start us, length us, event | category | flops | bytes accessed | tf_op | source)
XLA Modules:
  0.0 94.4 jit_solution(5189907509319545365)
XLA Ops:
  0.6 4.1 %collective-permute-start.8 = (bf16[24,2048]{1,0:T(8,128)(2,1)}, bf16[24,2048]{1,0:T(8,128)(2,1)S(1)}, u32[]{:S(2)}, u32[]{:S(2)}) collective-permute-start(bf16[24,2048]{1,0:T(8,128)(2,1)} %refs_2_.1), channel_id=1, source_target_pairs={{0,8},{1,9},{2,10},{3,11},{4,12},{5,13},{6,14},{7,15},{8,0},{9,1},... | collective-permute-start | bytes 294920 | tf_op jit(solution)/shard_map/ppermute | solution.py:23
  4.7 1.6 %collective-permute-start.7 = (bf16[24,2048]{1,0:T(8,128)(2,1)}, bf16[24,2048]{1,0:T(8,128)(2,1)S(1)}, u32[]{:S(2)}, u32[]{:S(2)}) collective-permute-start(bf16[24,2048]{1,0:T(8,128)(2,1)} %refs_2_.1), channel_id=1, source_target_pairs={{0,4},{1,5},{2,6},{3,7},{4,0},{5,1},{6,2},{7,3},{8,12},{9,13},{10,... | collective-permute-start | bytes 294920 | tf_op jit(solution)/shard_map/ppermute | solution.py:23
  6.3 0.0 collective-permute-start.9
  6.3 0.8 copy.12.refs_1_
  7.1 0.9 copy-done.7
  8.0 0.8 copy-done.10
  8.8 0.5 shard_map.110
  9.3 1.8 %collective-permute-start = (bf16[24,128]{1,0:T(8,128)(2,1)S(1)}, bf16[24,128]{1,0:T(8,128)(2,1)S(1)}, u32[]{:S(2)}, u32[]{:S(2)}) collective-permute-start(bf16[24,128]{1,0:T(8,128)(2,1)S(1)} %get-tuple-element.31), channel_id=1, source_target_pairs={{0,16},{16,0},{1,17},{17,1},{2,18},{18,2},{3,19},{19,3},{4,20},{20... | collective-permute-start | bytes 18440 | tf_op jit(solution)/shard_map/ppermute | solution.py:28
  11.1 1.9 %collective-permute-done = bf16[24,128]{1,0:T(8,128)(2,1)S(1)} collective-permute-done((bf16[24,128]{1,0:T(8,128)(2,1)S(1)}, bf16[24,128]{1,0:T(8,128)(2,1)S(1)}, u32[]{:S(2)}, u32[]{:S(2)}) %collective-permute-start) | collective-permute-done | bytes 6176 | tf_op jit(solution)/shard_map/ppermute | solution.py:28
  13.0 0.1 slice.48
  13.1 1.0 %concatenate.9 = bf16[24,2176]{1,0:T(8,128)(2,1)S(1)} concatenate(bf16[24,2048]{1,0:T(8,128)(2,1)} %param.8, bf16[24,64]{1,0:T(8,128)(2,1)S(1)} %bitcast.11, bf16[24,48]{1,0:T(8,128)(2,1)S(1)} %slice.48, bf16[24,16]{1,0:T(8,128)(2,1)S(1)} %broadcast_in_dim.10), dimensions={1} | concatenate | bytes 208896 | tf_op jit(solution)/shard_map/concatenate | solution.py:597
  14.1 3.9 %collective-permute-start.3 = (bf16[24,2176]{1,0:T(8,128)(2,1)S(1)}, bf16[24,2176]{1,0:T(8,128)(2,1)S(1)}, u32[]{:S(2)}, u32[]{:S(2)}) collective-permute-start(bf16[24,2176]{1,0:T(8,128)(2,1)S(1)} %concatenate.9), channel_id=1, source_target_pairs={{0,12},{1,13},{2,14},{3,15},{4,8},{5,9},{6,10},{7,11},{8,4},{9,5},... | collective-permute-start | bytes 313352 | tf_op jit(solution)/shard_map/ppermute | solution.py:23
  18.0 0.0 collective-permute-done.7
  18.0 0.6 collective-permute-start.1
  18.6 0.0 collective-permute-done.8
  18.6 0.0 collective-permute-done.9
  18.7 1.7 %collective-permute-start.13 = (bf16[96,2048]{1,0:T(8,128)(2,1)S(1)}, bf16[96,2048]{1,0:T(8,128)(2,1)S(1)}, u32[]{:S(2)}, u32[]{:S(2)}) collective-permute-start(bf16[96,2048]{1,0:T(8,128)(2,1)S(1)} %constant_dynamic-update-slice_fusion.refs_3_.refs_4_.refs_1_), channel_id=1, source_target_pairs={{0,2},{1,3},{2,0},{3,1},{4,6},{5,7},{6,4},{7,5},{8,10},{9,11},{10,... | collective-permute-start | bytes 1179656 | tf_op jit(solution)/shard_map/ppermute | solution.py:23
  20.4 1.5 %collective-permute-start.10 = (bf16[96,2048]{1,0:T(8,128)(2,1)S(1)}, bf16[96,2048]{1,0:T(8,128)(2,1)S(1)}, u32[]{:S(2)}, u32[]{:S(2)}) collective-permute-start(bf16[96,2048]{1,0:T(8,128)(2,1)S(1)} %constant_dynamic-update-slice_fusion.refs_3_.refs_4_.refs_1_), channel_id=1, source_target_pairs={{0,16},{16,0},{1,17},{17,1},{2,18},{18,2},{3,19},{19,3},{4,20},{20... | collective-permute-start | bytes 1179656 | tf_op jit(solution)/shard_map/ppermute | solution.py:28
  21.9 2.9 %collective-permute-done.2 = bf16[24,2176]{1,0:T(8,128)(2,1)S(1)} collective-permute-done((bf16[24,2176]{1,0:T(8,128)(2,1)S(1)}, bf16[24,2176]{1,0:T(8,128)(2,1)S(1)}, u32[]{:S(2)}, u32[]{:S(2)}) %collective-permute-start.2) | collective-permute-done | bytes 104480 | tf_op jit(solution)/shard_map/ppermute | solution.py:23
  24.9 1.5 %collective-permute-start.5 = (bf16[96,2176]{1,0:T(8,128)(2,1)S(1)}, bf16[96,2176]{1,0:T(8,128)(2,1)S(1)}, u32[]{:S(2)}, u32[]{:S(2)}) collective-permute-start(bf16[96,2176]{1,0:T(8,128)(2,1)S(1)} %pad_maximum_fusion.refs_1_.refs_7_.refs_9_), channel_id=1, source_target_pairs={{0,2},{1,3},{2,0},{3,1},{4,6},{5,7},{6,4},{7,5},{8,10},{9,11},{10,... | collective-permute-start | bytes 1253384 | tf_op jit(solution)/shard_map/ppermute | solution.py:23
  26.4 1.5 %collective-permute-done.13.refs_5_.refs_6_.refs_3_ = bf16[96,2048]{1,0:T(8,128)(2,1)S(1)} collective-permute-done((bf16[96,2048]{1,0:T(8,128)(2,1)S(1)}, bf16[96,2048]{1,0:T(8,128)(2,1)S(1)}, u32[]{:S(2)}, u32[]{:S(2)}) %collective-permute-start.13) | collective-permute-done | bytes 393248 | tf_op jit(solution)/shard_map/ppermute | solution.py:23
  27.9 1.5 %collective-permute-start.15 = (bf16[96,2048]{1,0:T(8,128)(2,1)S(1)}, bf16[96,2048]{1,0:T(8,128)(2,1)S(1)}, u32[]{:S(2)}, u32[]{:S(2)}) collective-permute-start(bf16[96,2048]{1,0:T(8,128)(2,1)S(1)} %collective-permute-done.13.refs_5_.refs_6_.refs_3_), channel_id=1, source_target_pairs={{0,16},{16,0},{1,17},{17,1},{2,18},{18,2},{3,19},{19,3},{4,20},{20... | collective-permute-start | bytes 1179656 | tf_op jit(solution)/shard_map/ppermute | solution.py:28
  29.5 0.0 collective-permute-done.10.refs_8_.refs_2_.refs_5_
  29.5 0.0 collective-permute-start.11
  29.5 0.5 collective-permute-start.4
  30.0 6.3 %collective-permute-done.5.refs_3_.refs_9_.refs_11_ = bf16[96,2176]{1,0:T(8,128)(2,1)S(1)} collective-permute-done((bf16[96,2176]{1,0:T(8,128)(2,1)S(1)}, bf16[96,2176]{1,0:T(8,128)(2,1)S(1)}, u32[]{:S(2)}, u32[]{:S(2)}) %collective-permute-start.5) | collective-permute-done | bytes 417824 | tf_op jit(solution)/shard_map/ppermute | solution.py:23
  36.3 0.0 collective-permute-start.6
  36.3 0.5 collective-permute-start.12
  36.8 0.2 collective-permute-done.15.refs_10_.refs_4_.refs_7_
  37.0 0.0 collective-permute-start.14
  37.0 0.0 collective-permute-done.11.refs_9_.refs_3_.refs_6_
  37.0 0.5 collective-permute-start.16
  37.5 0.0 collective-permute-done.4.refs_2_.refs_8_.refs_10_
  37.5 1.5 %collective-permute-start.18 = (bf16[96,2176]{1,0:T(8,128)(2,1)S(1)}, bf16[96,2176]{1,0:T(8,128)(2,1)S(1)}, u32[]{:S(2)}, u32[]{:S(2)}) collective-permute-start(bf16[96,2176]{1,0:T(8,128)(2,1)S(1)} %pad_maximum_fusion.refs_1_.refs_7_.refs_9_), channel_id=1, source_target_pairs={{0,16},{16,0},{1,17},{17,1},{2,18},{18,2},{3,19},{19,3},{4,20},{20... | collective-permute-start | bytes 1253384 | tf_op jit(solution)/shard_map/ppermute | solution.py:28
  39.1 0.5 collective-permute-start.19
  39.6 0.2 copy-done.18
  39.8 1.7 %shard_map.111 = (f32[768,128]{1,0:T(8,128)S(1)}, f32[16,768]{1,0:T(8,128)S(1)}) custom-call(s32[1]{0:T(128)} %bitcast.refs_0_, bf16[96,2176]{1,0:T(8,128)(2,1)S(1)} %pad_maximum_fusion.refs_1_.refs_7_.refs_9_, bf16[96,2176]{1,0:T(8,128)(2,1)} %copy-done.17, bf16[96,2176]{1,0:T(8,128)(2,1)} %copy-done.16, bf16[96,2176]{1,0:T(8,128)(2,1)} %copy-done.18, ...), custom_call_target="tpu_custom_call" | custom-call | flops 2000000 | bytes 5000 | tf_op jit(solution)/shard_map/pallas_call | solution.py:124
  41.5 0.0 copy-start.6
  41.5 0.7 copy-done.6
  42.3 0.0 collective-permute-done.12.refs_4_.refs_5_.refs_2_
  42.3 0.7 copy-done.8
  43.0 0.1 copy-done.20
  43.1 0.1 copy-done.15
  43.3 12.4 %shard_map.112 = (bf16[96,2048]{1,0:T(8,128)(2,1)S(1)}, bf16[96,2048]{1,0:T(8,128)(2,1)}, bf16[96,2176]{1,0:T(8,128)(2,1)}, bf16[96,2176]{1,0:T(8,128)(2,1)}, bf...) custom-call(s32[1]{0:T(128)} %bitcast.refs_0_, ...), custom_call_target="tpu_custom_call" | custom-call | flops 6039797760 | bytes 15099494 | tf_op jit(solution)/shard_map/pallas_call | solution.py:124
  55.7 0.1 collective-permute-start.17
  55.8 0.5 collective-permute-start.27
  56.3 1.9 %collective-permute-done.19.refs_3_.refs_8_.refs_15_ = bf16[96,2176]{1,0:T(8,128)(2,1)S(1)} collective-permute-done((bf16[96,2176]{1,0:T(8,128)(2,1)S(1)}, bf16[96,2176]{1,0:T(8,128)(2,1)S(1)}, u32[]{:S(2)}, u32[]{:S(2)}) %collective-permute-start.19) | collective-permute-done | bytes 417824 | tf_op jit(solution)/shard_map/ppermute | solution.py:28
  58.2 0.0 copy-start.5
  58.2 1.1 %copy-done.5 = bf16[96,2176]{1,0:T(8,128)(2,1)S(1)} copy-done((bf16[96,2176]{1,0:T(8,128)(2,1)S(1)}, bf16[96,2176]{1,0:T(8,128)(2,1)}, u32[]{:S(2)}) %copy-start.5) | copy-done | bytes 417816
  59.3 0.8 shard_map.113
  60.1 1.4 %collective-permute-start.23 = (bf16[96,2176]{1,0:T(8,128)(2,1)S(1)}, bf16[96,2176]{1,0:T(8,128)(2,1)S(1)}, u32[]{:S(2)}, u32[]{:S(2)}) collective-permute-start(bf16[96,2176]{1,0:T(8,128)(2,1)S(1)} %get-tuple-element.38.refs_4_), channel_id=1, source_target_pairs={{0,2},{1,3},{2,0},{3,1},{4,6},{5,7},{6,4},{7,5},{8,10},{9,11},{10,... | collective-permute-start | bytes 1253384 | tf_op jit(solution)/shard_map/ppermute | solution.py:23
  61.5 0.1 collective-permute-start.22
  61.6 1.5 %collective-permute-start.20 = (bf16[16,128]{1,0:T(8,128)(2,1)S(1)}, bf16[16,128]{1,0:T(8,128)(2,1)S(1)}, u32[]{:S(2)}, u32[]{:S(2)}) collective-permute-start(bf16[16,128]{1,0:T(8,128)(2,1)S(1)} %get-tuple-element.35), channel_id=1, source_target_pairs={{0,16},{16,0},{1,17},{17,1},{2,18},{18,2},{3,19},{19,3},{4,20},{20... | collective-permute-start | bytes 12296 | tf_op jit(solution)/shard_map/ppermute | solution.py:28
  63.1 2.1 %collective-permute-done.20.refs_0_ = bf16[16,128]{1,0:T(8,128)(2,1)S(1)} collective-permute-done((bf16[16,128]{1,0:T(8,128)(2,1)S(1)}, bf16[16,128]{1,0:T(8,128)(2,1)S(1)}, u32[]{:S(2)}, u32[]{:S(2)}) %collective-permute-start.20) | collective-permute-done | bytes 4128 | tf_op jit(solution)/shard_map/ppermute | solution.py:28
  65.2 0.7 collective-permute-start.21
  65.9 8.8 %shard_map.116 = (bf16[384,768]{1,0:T(8,128)(2,1)}, bf16[384,768]{1,0:T(8,128)(2,1)}, bf16[384,768]{1,0:T(8,128)(2,1)}) custom-call(s32[1]{0:T(128)} %bitcast.refs_0_, f32[768,128]{1,0:T(8,128)} %copy-done.6, bf16[96,2048]{1,0:T(8,128)(2,1)} %copy-done.13, bf16[96,2048]{1,0:T(8,128)(2,1)} %copy-done.12, bf16[96,2048]{1,0:T(8,128)(2,1)} %copy-done.14, ...), custom_call_target="tpu_custom_call" | custom-call | flops 1207959552 | bytes 3019898 | tf_op jit(solution)/shard_map/pallas_call | solution.py:124
  74.8 1.7 %shard_map.114 = (bf16[24,2176]{1,0:T(8,128)(2,1)S(1)}, bf16[24,2176]{1,0:T(8,128)(2,1)S(1)}, bf16[24,2176]{1,0:T(8,128)(2,1)S(1)}, bf16[24,2176]{1,0:T(8,128)(2,1)S(1)}) custom-call(bf16[16,128]{1,0:T(8,128)(2,1)S(1)} %collective-permute-done.20.refs_0_, bf16[16,128]{1,0:T(8,128)(2,1)S(1)} %collective-permute-done.21.refs_1_, ...), custom_call_target="tpu_custom_call" | custom-call | flops 2000000 | bytes 5000 | tf_op jit(solution)/shard_map/pallas_call | solution.py:124
  76.5 2.8 %collective-permute-start.24 = (bf16[24,2176]{1,0:T(8,128)(2,1)S(1)}, bf16[24,2176]{1,0:T(8,128)(2,1)S(1)}, u32[]{:S(2)}, u32[]{:S(2)}) collective-permute-start(bf16[24,2176]{1,0:T(8,128)(2,1)S(1)} %get-tuple-element.40.refs_23_), channel_id=1, source_target_pairs={{0,4},{1,5},{2,6},{3,7},{4,0},{5,1},{6,2},{7,3},{8,12},{9,13},{10,... | collective-permute-start | bytes 313352 | tf_op jit(solution)/shard_map/ppermute | solution.py:23
  79.3 3.1 %collective-permute-start.25 = (bf16[24,2176]{1,0:T(8,128)(2,1)S(1)}, bf16[24,2176]{1,0:T(8,128)(2,1)S(1)}, u32[]{:S(2)}, u32[]{:S(2)}) collective-permute-start(bf16[24,2176]{1,0:T(8,128)(2,1)S(1)} %get-tuple-element.41.refs_24_), channel_id=1, source_target_pairs={{0,8},{1,9},{2,10},{3,11},{4,12},{5,13},{6,14},{7,15},{8,0},{9,1},... | collective-permute-start | bytes 313352 | tf_op jit(solution)/shard_map/ppermute | solution.py:23
  82.4 7.3 %shard_map.117 = (bf16[1,1024,768]{2,1,0:T(8,128)(2,1)}, bf16[1,1024,768]{2,1,0:T(8,128)(2,1)}, bf16[1,384,2048]{2,1,0:T(8,128)(2,1)}) custom-call(s32[1]{0:T(128)} %bitcast.7.refs_0_, bf16[96,2048]{1,0:T(8,128)(2,1)S(1)} %copy-done.4, bf16[96,2048]{1,0:T(8,128)(2,1)} %copy-done.8, bf16[96,2048]{1,0:T(8,128)(2,1)} %copy-done.19, ...), custom_call_target="tpu_custom_call" | custom-call | flops 3623878656 | bytes 9059696 | tf_op jit(solution)/shard_map/pallas_call | solution.py:124
  89.8 0.0 copy-start.11
  89.8 0.3 collective-permute-done.25
  90.2 3.3 %shard_map.115 = (bf16[16,768]{1,0:T(8,128)(2,1)S(1)}, f32[16,2048]{1,0:T(8,128)}) custom-call(s32[1]{0:T(128)} %bitcast.refs_0_, bf16[2,16,384]{2,1,0:T(8,128)(2,1)S(1)} %reshape.13.refs_1_, s32[1,384]{1,0:T(1,128)S(1)} %get-tuple-element.30.refs_1_.refs_2_, f32[16,768]{1,0:T(8,128)S(1)} %get-tuple-element.43.refs_3_, bf16[96,2048]{1,0:T(8,128)(2,1)S(1)} %copy-done.4, ...), custom_call_target="tpu_custom_call" | custom-call | flops 2000000 | bytes 5000 | tf_op jit(solution)/shard_map/pallas_call | solution.py:124
  93.5 0.8 fusion
  (65 shorter events, 0.3 us)
Async XLA Ops:
  0.6 18.0 %collective-permute-start.8 = (bf16[24,2048]{1,0:T(8,128)(2,1)}, bf16[24,2048]{1,0:T(8,128)(2,1)S(1)}, u32[]{:S(2)}, u32[]{:S(2)}) collective-permute-start(bf16[24,2048]{1,0:T(8,128)(2,1)} %refs_2_.1), channel_id=1, source_target_pairs={{0,8},{1,9},{2,10},{3,11},{4,12},{5,13},{6,14},{7,15},{8,0},{9,1},... | collective-permute-start | bytes 294920 | tf_op jit(solution)/shard_map/ppermute | solution.py:23
  4.7 13.2 %collective-permute-start.7 = (bf16[24,2048]{1,0:T(8,128)(2,1)}, bf16[24,2048]{1,0:T(8,128)(2,1)S(1)}, u32[]{:S(2)}, u32[]{:S(2)}) collective-permute-start(bf16[24,2048]{1,0:T(8,128)(2,1)} %refs_2_.1), channel_id=1, source_target_pairs={{0,4},{1,5},{2,6},{3,7},{4,0},{5,1},{6,2},{7,3},{8,12},{9,13},{10,... | collective-permute-start | bytes 294920 | tf_op jit(solution)/shard_map/ppermute | solution.py:23
  6.3 12.3 %collective-permute-start.9 = (bf16[24,2048]{1,0:T(8,128)(2,1)}, bf16[24,2048]{1,0:T(8,128)(2,1)S(1)}, u32[]{:S(2)}, u32[]{:S(2)}) collective-permute-start(bf16[24,2048]{1,0:T(8,128)(2,1)} %refs_2_.1), channel_id=1, source_target_pairs={{0,12},{1,13},{2,14},{3,15},{4,8},{5,9},{6,10},{7,11},{8,4},{9,5},... | collective-permute-start | bytes 294920 | tf_op jit(solution)/shard_map/ppermute | solution.py:23
  7.1 0.9 copy-start.7
  8.0 0.8 copy-start.10
  9.3 3.7 %collective-permute-start = (bf16[24,128]{1,0:T(8,128)(2,1)S(1)}, bf16[24,128]{1,0:T(8,128)(2,1)S(1)}, u32[]{:S(2)}, u32[]{:S(2)}) collective-permute-start(bf16[24,128]{1,0:T(8,128)(2,1)S(1)} %get-tuple-element.31), channel_id=1, source_target_pairs={{0,16},{16,0},{1,17},{17,1},{2,18},{18,2},{3,19},{19,3},{4,20},{20... | collective-permute-start | bytes 18440 | tf_op jit(solution)/shard_map/ppermute | solution.py:28
  14.1 7.8 %collective-permute-start.3 = (bf16[24,2176]{1,0:T(8,128)(2,1)S(1)}, bf16[24,2176]{1,0:T(8,128)(2,1)S(1)}, u32[]{:S(2)}, u32[]{:S(2)}) collective-permute-start(bf16[24,2176]{1,0:T(8,128)(2,1)S(1)} %concatenate.9), channel_id=1, source_target_pairs={{0,12},{1,13},{2,14},{3,15},{4,8},{5,9},{6,10},{7,11},{8,4},{9,5},... | collective-permute-start | bytes 313352 | tf_op jit(solution)/shard_map/ppermute | solution.py:23
  18.0 6.9 %collective-permute-start.2 = (bf16[24,2176]{1,0:T(8,128)(2,1)S(1)}, bf16[24,2176]{1,0:T(8,128)(2,1)S(1)}, u32[]{:S(2)}, u32[]{:S(2)}) collective-permute-start(bf16[24,2176]{1,0:T(8,128)(2,1)S(1)} %concatenate.9), channel_id=1, source_target_pairs={{0,8},{1,9},{2,10},{3,11},{4,12},{5,13},{6,14},{7,15},{8,0},{9,1},... | collective-permute-start | bytes 313352 | tf_op jit(solution)/shard_map/ppermute | solution.py:23
  18.0 6.9 %collective-permute-start.1 = (bf16[24,2176]{1,0:T(8,128)(2,1)S(1)}, bf16[24,2176]{1,0:T(8,128)(2,1)S(1)}, u32[]{:S(2)}, u32[]{:S(2)}) collective-permute-start(bf16[24,2176]{1,0:T(8,128)(2,1)S(1)} %concatenate.9), channel_id=1, source_target_pairs={{0,4},{1,5},{2,6},{3,7},{4,0},{5,1},{6,2},{7,3},{8,12},{9,13},{10,... | collective-permute-start | bytes 313352 | tf_op jit(solution)/shard_map/ppermute | solution.py:23
  18.7 23.7 %copy-start.3 = (bf16[96,2048]{1,0:T(8,128)(2,1)}, bf16[96,2048]{1,0:T(8,128)(2,1)S(1)}, u32[]{:S(2)}) copy-start(bf16[96,2048]{1,0:T(8,128)(2,1)S(1)} %constant_dynamic-update-slice_fusion.refs_3_.refs_4_.refs_1_) | copy-start | bytes 1179652
  18.7 9.3 %collective-permute-start.13 = (bf16[96,2048]{1,0:T(8,128)(2,1)S(1)}, bf16[96,2048]{1,0:T(8,128)(2,1)S(1)}, u32[]{:S(2)}, u32[]{:S(2)}) collective-permute-start(bf16[96,2048]{1,0:T(8,128)(2,1)S(1)} %constant_dynamic-update-slice_fusion.refs_3_.refs_4_.refs_1_), channel_id=1, source_target_pairs={{0,2},{1,3},{2,0},{3,1},{4,6},{5,7},{6,4},{7,5},{8,10},{9,11},{10,... | collective-permute-start | bytes 1179656 | tf_op jit(solution)/shard_map/ppermute | solution.py:23
  20.4 9.1 %collective-permute-start.10 = (bf16[96,2048]{1,0:T(8,128)(2,1)S(1)}, bf16[96,2048]{1,0:T(8,128)(2,1)S(1)}, u32[]{:S(2)}, u32[]{:S(2)}) collective-permute-start(bf16[96,2048]{1,0:T(8,128)(2,1)S(1)} %constant_dynamic-update-slice_fusion.refs_3_.refs_4_.refs_1_), channel_id=1, source_target_pairs={{0,16},{16,0},{1,17},{17,1},{2,18},{18,2},{3,19},{19,3},{4,20},{20... | collective-permute-start | bytes 1179656 | tf_op jit(solution)/shard_map/ppermute | solution.py:28
  24.9 17.5 %copy-start.2 = (bf16[96,2176]{1,0:T(8,128)(2,1)}, bf16[96,2176]{1,0:T(8,128)(2,1)S(1)}, u32[]{:S(2)}) copy-start(bf16[96,2176]{1,0:T(8,128)(2,1)S(1)} %pad_maximum_fusion.refs_1_.refs_7_.refs_9_) | copy-start | bytes 1253380
  24.9 11.4 %collective-permute-start.5 = (bf16[96,2176]{1,0:T(8,128)(2,1)S(1)}, bf16[96,2176]{1,0:T(8,128)(2,1)S(1)}, u32[]{:S(2)}, u32[]{:S(2)}) collective-permute-start(bf16[96,2176]{1,0:T(8,128)(2,1)S(1)} %pad_maximum_fusion.refs_1_.refs_7_.refs_9_), channel_id=1, source_target_pairs={{0,2},{1,3},{2,0},{3,1},{4,6},{5,7},{6,4},{7,5},{8,10},{9,11},{10,... | collective-permute-start | bytes 1253384 | tf_op jit(solution)/shard_map/ppermute | solution.py:23
  27.9 14.4 %copy-start.19 = (bf16[96,2048]{1,0:T(8,128)(2,1)}, bf16[96,2048]{1,0:T(8,128)(2,1)S(1)}, u32[]{:S(2)}) copy-start(bf16[96,2048]{1,0:T(8,128)(2,1)S(1)} %collective-permute-done.13.refs_5_.refs_6_.refs_3_) | copy-start | bytes 1179652
  27.9 9.1 %collective-permute-start.15 = (bf16[96,2048]{1,0:T(8,128)(2,1)S(1)}, bf16[96,2048]{1,0:T(8,128)(2,1)S(1)}, u32[]{:S(2)}, u32[]{:S(2)}) collective-permute-start(bf16[96,2048]{1,0:T(8,128)(2,1)S(1)} %collective-permute-done.13.refs_5_.refs_6_.refs_3_), channel_id=1, source_target_pairs={{0,16},{16,0},{1,17},{17,1},{2,18},{18,2},{3,19},{19,3},{4,20},{20... | collective-permute-start | bytes 1179656 | tf_op jit(solution)/shard_map/ppermute | solution.py:28
  29.5 12.8 %copy-start.13 = (bf16[96,2048]{1,0:T(8,128)(2,1)}, bf16[96,2048]{1,0:T(8,128)(2,1)S(1)}, u32[]{:S(2)}) copy-start(bf16[96,2048]{1,0:T(8,128)(2,1)S(1)} %collective-permute-done.10.refs_8_.refs_2_.refs_5_) | copy-start | bytes 1179652
  29.5 7.5 %collective-permute-start.11 = (bf16[96,2048]{1,0:T(8,128)(2,1)S(1)}, bf16[96,2048]{1,0:T(8,128)(2,1)S(1)}, u32[]{:S(2)}, u32[]{:S(2)}) collective-permute-start(bf16[96,2048]{1,0:T(8,128)(2,1)S(1)} %collective-permute-done.10.refs_8_.refs_2_.refs_5_), channel_id=1, source_target_pairs={{0,1},{1,0},{2,3},{3,2},{4,5},{5,4},{6,7},{7,6},{8,9},{9,8},{10,11... | collective-permute-start | bytes 1179656 | tf_op jit(solution)/shard_map/ppermute | solution.py:23
  29.5 8.0 %collective-permute-start.4 = (bf16[96,2176]{1,0:T(8,128)(2,1)S(1)}, bf16[96,2176]{1,0:T(8,128)(2,1)S(1)}, u32[]{:S(2)}, u32[]{:S(2)}) collective-permute-start(bf16[96,2176]{1,0:T(8,128)(2,1)S(1)} %pad_maximum_fusion.refs_1_.refs_7_.refs_9_), channel_id=1, source_target_pairs={{0,1},{1,0},{2,3},{3,2},{4,5},{5,4},{6,7},{7,6},{8,9},{9,8},{10,11... | collective-permute-start | bytes 1253384 | tf_op jit(solution)/shard_map/ppermute | solution.py:23
  36.3 3.3 %copy-start.16 = (bf16[96,2176]{1,0:T(8,128)(2,1)}, bf16[96,2176]{1,0:T(8,128)(2,1)S(1)}, u32[]{:S(2)}) copy-start(bf16[96,2176]{1,0:T(8,128)(2,1)S(1)} %collective-permute-done.5.refs_3_.refs_9_.refs_11_) | copy-start | bytes 1253380
  36.3 2.8 %collective-permute-start.6 = (bf16[96,2176]{1,0:T(8,128)(2,1)S(1)}, bf16[96,2176]{1,0:T(8,128)(2,1)S(1)}, u32[]{:S(2)}, u32[]{:S(2)}) collective-permute-start(bf16[96,2176]{1,0:T(8,128)(2,1)S(1)} %collective-permute-done.5.refs_3_.refs_9_.refs_11_), channel_id=1, source_target_pairs={{0,1},{1,0},{2,3},{3,2},{4,5},{5,4},{6,7},{7,6},{8,9},{9,8},{10,11... | collective-permute-start | bytes 1253384 | tf_op jit(solution)/shard_map/ppermute | solution.py:23
  36.3 6.0 %collective-permute-start.12 = (bf16[96,2048]{1,0:T(8,128)(2,1)S(1)}, bf16[96,2048]{1,0:T(8,128)(2,1)S(1)}, u32[]{:S(2)}, u32[]{:S(2)}) collective-permute-start(bf16[96,2048]{1,0:T(8,128)(2,1)S(1)} %constant_dynamic-update-slice_fusion.refs_3_.refs_4_.refs_1_), channel_id=1, source_target_pairs={{0,1},{1,0},{2,3},{3,2},{4,5},{5,4},{6,7},{7,6},{8,9},{9,8},{10,11... | collective-permute-start | bytes 1179656 | tf_op jit(solution)/shard_map/ppermute | solution.py:23
  37.0 18.7 %copy-start.14 = (bf16[96,2048]{1,0:T(8,128)(2,1)}, bf16[96,2048]{1,0:T(8,128)(2,1)S(1)}, u32[]{:S(2)}) copy-start(bf16[96,2048]{1,0:T(8,128)(2,1)S(1)} %collective-permute-done.15.refs_10_.refs_4_.refs_7_) | copy-start | bytes 1179652
  37.0 5.3 %collective-permute-start.14 = (bf16[96,2048]{1,0:T(8,128)(2,1)S(1)}, bf16[96,2048]{1,0:T(8,128)(2,1)S(1)}, u32[]{:S(2)}, u32[]{:S(2)}) collective-permute-start(bf16[96,2048]{1,0:T(8,128)(2,1)S(1)} %collective-permute-done.13.refs_5_.refs_6_.refs_3_), channel_id=1, source_target_pairs={{0,1},{1,0},{2,3},{3,2},{4,5},{5,4},{6,7},{7,6},{8,9},{9,8},{10,11... | collective-permute-start | bytes 1179656 | tf_op jit(solution)/shard_map/ppermute | solution.py:23
  37.0 18.7 %copy-start.12 = (bf16[96,2048]{1,0:T(8,128)(2,1)}, bf16[96,2048]{1,0:T(8,128)(2,1)S(1)}, u32[]{:S(2)}) copy-start(bf16[96,2048]{1,0:T(8,128)(2,1)S(1)} %collective-permute-done.11.refs_9_.refs_3_.refs_6_) | copy-start | bytes 1179652
  37.0 5.3 %collective-permute-start.16 = (bf16[96,2048]{1,0:T(8,128)(2,1)S(1)}, bf16[96,2048]{1,0:T(8,128)(2,1)S(1)}, u32[]{:S(2)}, u32[]{:S(2)}) collective-permute-start(bf16[96,2048]{1,0:T(8,128)(2,1)S(1)} %collective-permute-done.15.refs_10_.refs_4_.refs_7_), channel_id=1, source_target_pairs={{0,1},{1,0},{2,3},{3,2},{4,5},{5,4},{6,7},{7,6},{8,9},{9,8},{10,11... | collective-permute-start | bytes 1179656 | tf_op jit(solution)/shard_map/ppermute | solution.py:23
  37.5 2.1 %copy-start.17 = (bf16[96,2176]{1,0:T(8,128)(2,1)}, bf16[96,2176]{1,0:T(8,128)(2,1)S(1)}, u32[]{:S(2)}) copy-start(bf16[96,2176]{1,0:T(8,128)(2,1)S(1)} %collective-permute-done.4.refs_2_.refs_8_.refs_10_) | copy-start | bytes 1253380
  37.5 18.3 %collective-permute-start.18 = (bf16[96,2176]{1,0:T(8,128)(2,1)S(1)}, bf16[96,2176]{1,0:T(8,128)(2,1)S(1)}, u32[]{:S(2)}, u32[]{:S(2)}) collective-permute-start(bf16[96,2176]{1,0:T(8,128)(2,1)S(1)} %pad_maximum_fusion.refs_1_.refs_7_.refs_9_), channel_id=1, source_target_pairs={{0,16},{16,0},{1,17},{17,1},{2,18},{18,2},{3,19},{19,3},{4,20},{20... | collective-permute-start | bytes 1253384 | tf_op jit(solution)/shard_map/ppermute | solution.py:28
  39.1 0.8 copy-start.18
  39.1 19.1 %collective-permute-start.19 = (bf16[96,2176]{1,0:T(8,128)(2,1)S(1)}, bf16[96,2176]{1,0:T(8,128)(2,1)S(1)}, u32[]{:S(2)}, u32[]{:S(2)}) collective-permute-start(bf16[96,2176]{1,0:T(8,128)(2,1)S(1)} %collective-permute-done.5.refs_3_.refs_9_.refs_11_), channel_id=1, source_target_pairs={{0,16},{16,0},{1,17},{17,1},{2,18},{18,2},{3,19},{19,3},{4,20},{20... | collective-permute-start | bytes 1253384 | tf_op jit(solution)/shard_map/ppermute | solution.py:28
  41.5 0.7 copy-start.6
  42.3 0.7 copy-start.8
  42.3 0.9 copy-start.20
  42.3 1.0 %copy-start.15 = (bf16[96,2048]{1,0:T(8,128)(2,1)}, bf16[96,2048]{1,0:T(8,128)(2,1)S(1)}, u32[]{:S(2)}) copy-start(bf16[96,2048]{1,0:T(8,128)(2,1)S(1)} %collective-permute-done.16.refs_14_.refs_11_.refs_5_.refs_8_) | copy-start | bytes 1179652
  55.7 2.5 %collective-permute-start.17 = (bf16[96,2176]{1,0:T(8,128)(2,1)}, bf16[96,2176]{1,0:T(8,128)(2,1)S(1)}, u32[]{:S(2)}, u32[]{:S(2)}) collective-permute-start(bf16[96,2176]{1,0:T(8,128)(2,1)} %get-tuple-element.34), channel_id=1, source_target_pairs={{0,1},{1,0},{2,3},{3,2},{4,5},{5,4},{6,7},{7,6},{8,9},{9,8},{10,11... | collective-permute-start | bytes 1253384 | tf_op jit(solution)/shard_map/ppermute | solution.py:23
  55.8 10.1 %copy-start = (bf16[96,2176]{1,0:T(8,128)(2,1)}, bf16[96,2176]{1,0:T(8,128)(2,1)S(1)}, u32[]{:S(2)}) copy-start(bf16[96,2176]{1,0:T(8,128)(2,1)S(1)} %collective-permute-done.18.refs_2_.refs_6_.refs_13_) | copy-start | bytes 1253380
  55.8 10.1 %collective-permute-start.27 = (bf16[96,2176]{1,0:T(8,128)(2,1)S(1)}, bf16[96,2176]{1,0:T(8,128)(2,1)}, u32[]{:S(2)}, u32[]{:S(2)}) collective-permute-start(bf16[96,2176]{1,0:T(8,128)(2,1)S(1)} %collective-permute-done.18.refs_2_.refs_6_.refs_13_), channel_id=1, source_target_pairs={{0,1},{1,0},{2,3},{3,2},{4,5},{5,4},{6,7},{7,6},{8,9},{9,8},{10,11... | collective-permute-start | bytes 1253384 | tf_op jit(solution)/shard_map/ppermute | solution.py:23
  58.2 7.7 %copy-start.1 = (bf16[96,2176]{1,0:T(8,128)(2,1)}, bf16[96,2176]{1,0:T(8,128)(2,1)S(1)}, u32[]{:S(2)}) copy-start(bf16[96,2176]{1,0:T(8,128)(2,1)S(1)} %collective-permute-done.19.refs_3_.refs_8_.refs_15_) | copy-start | bytes 1253380
  58.2 7.7 %collective-permute-start.28 = (bf16[96,2176]{1,0:T(8,128)(2,1)S(1)}, bf16[96,2176]{1,0:T(8,128)(2,1)}, u32[]{:S(2)}, u32[]{:S(2)}) collective-permute-start(bf16[96,2176]{1,0:T(8,128)(2,1)S(1)} %collective-permute-done.19.refs_3_.refs_8_.refs_15_), channel_id=1, source_target_pairs={{0,1},{1,0},{2,3},{3,2},{4,5},{5,4},{6,7},{7,6},{8,9},{9,8},{10,11... | collective-permute-start | bytes 1253384 | tf_op jit(solution)/shard_map/ppermute | solution.py:23
  58.2 1.2 %copy-start.5 = (bf16[96,2176]{1,0:T(8,128)(2,1)S(1)}, bf16[96,2176]{1,0:T(8,128)(2,1)}, u32[]{:S(2)}) copy-start(bf16[96,2176]{1,0:T(8,128)(2,1)} %get-tuple-element.33.refs_0_) | copy-start | bytes 1253380
  60.1 14.6 %collective-permute-start.23 = (bf16[96,2176]{1,0:T(8,128)(2,1)S(1)}, bf16[96,2176]{1,0:T(8,128)(2,1)S(1)}, u32[]{:S(2)}, u32[]{:S(2)}) collective-permute-start(bf16[96,2176]{1,0:T(8,128)(2,1)S(1)} %get-tuple-element.38.refs_4_), channel_id=1, source_target_pairs={{0,2},{1,3},{2,0},{3,1},{4,6},{5,7},{6,4},{7,5},{8,10},{9,11},{10,... | collective-permute-start | bytes 1253384 | tf_op jit(solution)/shard_map/ppermute | solution.py:23
  61.5 13.2 %collective-permute-start.22 = (bf16[96,2048]{1,0:T(8,128)(2,1)}, bf16[96,2048]{1,0:T(8,128)(2,1)S(1)}, u32[]{:S(2)}, u32[]{:S(2)}) collective-permute-start(bf16[96,2048]{1,0:T(8,128)(2,1)} %get-tuple-element.37), channel_id=1, source_target_pairs={{0,1},{1,0},{2,3},{3,2},{4,5},{5,4},{6,7},{7,6},{8,9},{9,8},{10,11... | collective-permute-start | bytes 1179656 | tf_op jit(solution)/shard_map/ppermute | solution.py:23
  61.6 3.6 %collective-permute-start.20 = (bf16[16,128]{1,0:T(8,128)(2,1)S(1)}, bf16[16,128]{1,0:T(8,128)(2,1)S(1)}, u32[]{:S(2)}, u32[]{:S(2)}) collective-permute-start(bf16[16,128]{1,0:T(8,128)(2,1)S(1)} %get-tuple-element.35), channel_id=1, source_target_pairs={{0,16},{16,0},{1,17},{17,1},{2,18},{18,2},{3,19},{19,3},{4,20},{20... | collective-permute-start | bytes 12296 | tf_op jit(solution)/shard_map/ppermute | solution.py:28
  63.1 19.3 %copy-start.4 = (bf16[96,2048]{1,0:T(8,128)(2,1)S(1)}, bf16[96,2048]{1,0:T(8,128)(2,1)}, u32[]{:S(2)}) copy-start(bf16[96,2048]{1,0:T(8,128)(2,1)} %copy-done.3) | copy-start | bytes 1179652
  65.2 9.5 %collective-permute-start.21 = (bf16[16,128]{1,0:T(8,128)(2,1)S(1)}, bf16[16,128]{1,0:T(8,128)(2,1)S(1)}, u32[]{:S(2)}, u32[]{:S(2)}) collective-permute-start(bf16[16,128]{1,0:T(8,128)(2,1)S(1)} %collective-permute-done.20.refs_0_), channel_id=1, source_target_pairs={{0,2},{1,3},{2,0},{3,1},{4,6},{5,7},{6,4},{7,5},{8,10},{9,11},{10,... | collective-permute-start | bytes 12296 | tf_op jit(solution)/shard_map/ppermute | solution.py:23
  76.5 13.3 %collective-permute-start.24 = (bf16[24,2176]{1,0:T(8,128)(2,1)S(1)}, bf16[24,2176]{1,0:T(8,128)(2,1)S(1)}, u32[]{:S(2)}, u32[]{:S(2)}) collective-permute-start(bf16[24,2176]{1,0:T(8,128)(2,1)S(1)} %get-tuple-element.40.refs_23_), channel_id=1, source_target_pairs={{0,4},{1,5},{2,6},{3,7},{4,0},{5,1},{6,2},{7,3},{8,12},{9,13},{10,... | collective-permute-start | bytes 313352 | tf_op jit(solution)/shard_map/ppermute | solution.py:23
  79.3 10.8 %collective-permute-start.25 = (bf16[24,2176]{1,0:T(8,128)(2,1)S(1)}, bf16[24,2176]{1,0:T(8,128)(2,1)S(1)}, u32[]{:S(2)}, u32[]{:S(2)}) collective-permute-start(bf16[24,2176]{1,0:T(8,128)(2,1)S(1)} %get-tuple-element.41.refs_24_), channel_id=1, source_target_pairs={{0,8},{1,9},{2,10},{3,11},{4,12},{5,13},{6,14},{7,15},{8,0},{9,1},... | collective-permute-start | bytes 313352 | tf_op jit(solution)/shard_map/ppermute | solution.py:23
  82.4 7.7 %collective-permute-start.26 = (bf16[24,2176]{1,0:T(8,128)(2,1)S(1)}, bf16[24,2176]{1,0:T(8,128)(2,1)S(1)}, u32[]{:S(2)}, u32[]{:S(2)}) collective-permute-start(bf16[24,2176]{1,0:T(8,128)(2,1)S(1)} %get-tuple-element.42.refs_25_), channel_id=1, source_target_pairs={{0,12},{1,13},{2,14},{3,15},{4,8},{5,9},{6,10},{7,11},{8,4},{9,5},... | collective-permute-start | bytes 313352 | tf_op jit(solution)/shard_map/ppermute | solution.py:23
  82.4 7.8 %copy-start.9 = (bf16[96,2048]{1,0:T(8,128)(2,1)S(1)}, bf16[96,2048]{1,0:T(8,128)(2,1)}, u32[]{:S(2)}) copy-start(bf16[96,2048]{1,0:T(8,128)(2,1)} %copy-done.8) | copy-start | bytes 1179652
  89.8 3.7 %copy-start.11 = (bf16[2048,16]{0,1:T(8,128)(2,1)S(1)}, bf16[2048,16]{0,1:T(8,128)(2,1)}, u32[]{:S(2)}) copy-start(bf16[2048,16]{0,1:T(8,128)(2,1)} %param.10) | copy-start | bytes 196612
